TPU v7x, 32 devices: a whole 2x2x4 slice. The times are simulated.
32 devices in a mesh: groups: 2 (over x), section: 8 (over z, y), tp: 2 (over core).
Axes of the slice: x: 2, y: 2, z: 4, core: 2. Of those that a mesh axis runs over, the one named last changes fastest.
Arguments:
- prompts: bfloat16 [12288, 12288], P(('groups', 'section'), 'tp'), parts along dimension 0, may hold values from -6 to 6
- decode_hidden: bfloat16 [2048, 12288], P(('groups', 'section'), 'tp'), parts along dimension 0, may hold values from -6 to 6
- queries: bfloat16 [2048, 6144], P(('groups', 'section'), 'tp'), parts along dimension 0, may hold values from -12 to 12
- kv_cache: bfloat16 [2048, 32, 1024], P(('groups', 'section'), None, 'tp'), parts along dimension 0, may hold values from -12 to 12
- cache_len: int32 [2048], P(('groups', 'section')), parts along dimension 0, may hold values from 2 to 32, as said below
- span_len: int32 [16, 12], P('groups'), parts along dimension 0, may hold values from 1 to 64, 576 in all within a row
- target_row: int32 [16, 12], P('groups'), parts along dimension 0, may hold values from 0 to 1023, as said below
- w_kv: bfloat16 [12288, 1024], P('tp'), may hold values from -0.0546875 to 0.0546875
- kv_scale: float32 [1024], replicated, may hold values from 0.5 to 2
Outputs:
- attended: bfloat16 [2048, 6144], P(('groups', 'section'), 'tp'), parts along dimension 0
There are 2 independent parts, one for each index of `groups`. A program takes and returns all parts, laid end to end along the dimension named above; an argument that names none is the same for every part. Nothing has to cross between parts.
Inputs may be any that keep to these rules, and one draw needn't show every extreme that they name: target_row[s, r] // 128 is the decode section of section s's r-th request and target_row[s, r] % 128 its row there. No two requests name the same decode row. A section sends at most 2 of its requests to one decode section, and exactly 2 to some decode section. `cache_len`: every section has a decode row with exactly 32 valid positions.
All inputs are finite; a program needn't handle non-finite values.
Results may differ from a plain program's by a relative error of at most 0.0059.
Values may be sent and summed in bfloat16 or wider, within the bound.
No kernel may reach another device: no remote copies, remote signals or barrier semaphores. Data moves between devices by JAX's collectives and lax.ppermute only.
A program may use at most 128 MiB of HBM per device.

v0:
```python
import jax
import jax.numpy as jnp
from jax import lax
from jax.sharding import PartitionSpec as P

HD = 128


masked_score = -1e30


def partial_kv(rows_in, w_kv, kv_scale):
    return jnp.dot(rows_in, w_kv, preferred_element_type=jnp.float32) * kv_scale


def attend(queries, cache_rows, own_kv, arrived, cache_len, new_len):
    row_count = queries.shape[0]
    kv_heads = own_kv.shape[1] // (2 * HD)
    group_size = queries.shape[1] // (kv_heads * HD)
    query_heads = queries.reshape(row_count, kv_heads, group_size, HD)
    cache_rows = cache_rows.reshape(row_count, cache_rows.shape[1], kv_heads, 2, HD)
    arrived = arrived.reshape(row_count, arrived.shape[1], kv_heads, 2, HD)
    own_kv = own_kv.reshape(row_count, kv_heads, 2, HD)
    score_scale = HD ** (-0.5)
    cache_scores = (
        jnp.einsum(
            "bhgd,bthd->bhgt",
            query_heads,
            cache_rows[:, :, :, 0],
            preferred_element_type=jnp.float32,
        )
        * score_scale
    )
    new_scores = (
        jnp.einsum(
            "bhgd,bthd->bhgt", query_heads, arrived[:, :, :, 0], preferred_element_type=jnp.float32
        )
        * score_scale
    )
    own_scores = (
        jnp.einsum(
            "bhgd,bhd->bhg", query_heads, own_kv[:, :, 0], preferred_element_type=jnp.float32
        )
        * score_scale
    )
    cache_valid = (jnp.arange(cache_rows.shape[1], dtype=jnp.int32)[None, :] < cache_len[:, None])[
        :, None, None, :
    ]
    new_valid = (jnp.arange(arrived.shape[1], dtype=jnp.int32)[None, :] < new_len[:, None])[
        :, None, None, :
    ]
    cache_scores = jnp.where(cache_valid, cache_scores, masked_score)
    new_scores = jnp.where(new_valid, new_scores, masked_score)
    largest = jnp.maximum(
        jnp.maximum(jnp.max(cache_scores, axis=3), jnp.max(new_scores, axis=3)), own_scores
    )
    cache_exp = jnp.exp(cache_scores - largest[..., None])
    new_exp = jnp.exp(new_scores - largest[..., None])
    own_exp = jnp.exp(own_scores - largest)
    denominator = jnp.sum(cache_exp, axis=3) + jnp.sum(new_exp, axis=3) + own_exp
    cache_weights = (cache_exp / denominator[..., None]).astype(jnp.bfloat16)
    new_weights = (new_exp / denominator[..., None]).astype(jnp.bfloat16)
    own_weights = (own_exp / denominator).astype(jnp.bfloat16)
    combined = jnp.einsum(
        "bhgt,bthd->bhgd", cache_weights, cache_rows[:, :, :, 1], preferred_element_type=jnp.float32
    )
    combined = combined + jnp.einsum(
        "bhgt,bthd->bhgd", new_weights, arrived[:, :, :, 1], preferred_element_type=jnp.float32
    )
    combined = (
        combined
        + own_weights.astype(jnp.float32)[..., None]
        * own_kv[:, :, 1].astype(jnp.float32)[:, :, None, :]
    )
    return combined.astype(jnp.bfloat16).reshape(row_count, kv_heads * group_size * HD)


def shards(
    prompts, decode_hidden, queries, kv_cache, cache_len, span_len, target_row, w_kv, kv_scale
):
    row_count = decode_hidden.shape[0]
    sections = lax.axis_size("section")
    position = lax.axis_index("section")
    request_count = span_len.shape[1]
    span_rows = prompts.shape[0] // request_count
    local_width = kv_cache.shape[2]
    flat_width = span_rows * local_width
    prompt_rows = prompts.shape[0]
    destination = target_row // row_count
    decode_slot = target_row % row_count
    landing_mask = (destination == position)[:, :, None] & (
        decode_slot[:, :, None] == jnp.arange(row_count, dtype=jnp.int32)[None, None, :]
    )
    new_len = jnp.sum(jnp.where(landing_mask, span_len[:, :, None], 0), axis=(0, 1))
    landing = landing_mask.astype(jnp.float32)
    partial_terms = jnp.concatenate(
        [partial_kv(prompts, w_kv, kv_scale), partial_kv(decode_hidden, w_kv, kv_scale)], 0
    )
    kv_rows = lax.psum_scatter(
        partial_terms.astype(jnp.bfloat16), "tp", scatter_dimension=1, tiled=True
    )
    packed = kv_rows[:prompt_rows].reshape(request_count, flat_width)
    everyone = lax.all_gather(packed, "section", axis=0, tiled=True)
    picker = landing.reshape(sections * request_count, row_count).T.astype(jnp.bfloat16)
    result_rows = jnp.dot(picker, everyone, preferred_element_type=jnp.float32)
    arrived = result_rows
    own_kv = kv_rows[prompt_rows:]
    arrived = arrived.astype(jnp.bfloat16).reshape(row_count, span_rows, local_width)
    return attend(queries, kv_cache, own_kv, arrived, cache_len, new_len)


def solution(mesh):
    in_specs = (
        P(("groups", "section"), "tp"),
        P(("groups", "section"), "tp"),
        P(("groups", "section"), "tp"),
        P(("groups", "section"), None, "tp"),
        P(("groups", "section")),
        P("groups", None),
        P("groups", None),
        P("tp", None),
        P(),
    )
    out_specs = P(("groups", "section"), "tp")
    return jax.shard_map(shards, mesh=mesh, in_specs=in_specs, out_specs=out_specs, check_vma=False)
```

profile of v0, /device:TPU:0, one launch (start us, length us, event | category | flops | bytes accessed | tf_op | source)
XLA Modules:
  0.0 232.9 jit_solution(12050102509844050073)
XLA Ops:
  6.5 14.7 %multiply_convert_fusion = bf16[768,1024]{1,0:T(8,128)(2,1)S(1)} fusion(bf16[768,6144]{1,0:T(8,128)(2,1)} %param.9, bf16[6144,1024]{1,0:T(8,128)(2,1)} %param.16, f32[1024]{0:T(1024)} %param.17), kind=kOutput, calls=%fused_computation.5 | convolution fusion | flops 9665249280 | bytes 23597056 | tf_op jit(solution)/shard_map/dot_general | solution.py:13
  21.3 1.8 fusion.12
  23.1 1.4 pad_maximum_fusion
  24.6 12.2 %reduce-scatter.2.cloned.1.call-done = bf16[896,512]{1,0:T(8,128)(2,1)} async-done(((bf16[896,1024]{1,0:T(8,128)(2,1)}), bf16[896,512]{1,0:T(8,128)(2,1)}) %reduce-scatter.2.cloned.1.call-update) | async-done | bytes 917520 | tf_op jit(solution)/shard_map/reduce_scatter | solution.py:99
  36.7 1.1 slice-done
  37.8 1.5 reshape.65
  40.2 1.1 copy.37
  41.4 8.1 %copy.35 = bf16[128,32,512]{0,2,1:T(8,128)(2,1)} copy(bf16[128,32,512]{2,1,0:T(8,128)(2,1)} %param.12) | data formatting | bytes 8388608 | tf_op args[3]
  49.4 5.2 %fusion.38 = (bf16[128,32,2,1,128]{0,4,3,2,1:T(8,128)(2,1)}, bf16[128,32,2,1,128]{0,4,3,2,1:T(8,128)(2,1)}) fusion(bf16[128,32,2,2,128]{0,4,3,2,1:T(8,128)(2,1)} %bitcast.46), kind=kLoop, calls=%fused_computation.68 | loop fusion | bytes 8388608 | tf_op jit(solution)/shard_map/slice | solution.py:65
  54.6 4.5 %copy.50 = bf16[128,32,2,1,128]{4,1,2,0,3:T(8,128)(2,1)} copy(bf16[128,32,2,1,128]{0,4,3,2,1:T(8,128)(2,1)} %get-tuple-element.10) | data formatting | bytes 4194304
  59.2 4.6 %copy.53 = bf16[128,32,2,1,128]{4,1,2,0,3:T(8,128)(2,1)} copy(bf16[128,32,2,1,128]{0,4,3,2,1:T(8,128)(2,1)} %get-tuple-element.9) | data formatting | bytes 4194304
  64.1 4.2 %fusion.7 = (f32[128,2,12]{2,1,0:T(2,128)S(1)}, f32[128,2,12,32]{3,2,1,0:T(8,128)}) fusion(pred[128,32]{1,0:T(8,128)(4,1)S(1)} %iota_compare_fusion.2, bf16[128,2,12,128]{3,2,1,0:T(8,128)(2,1)S(1)} %copy.37, bf16[128,32,2,1,128]{4,1,2,0,3:T(8,128)(2,1)} %copy.50), kind=kOutput, calls=%fused_computation.19 | convolution fusion | flops 25457664 | bytes 3293184 | tf_op jit(solution)/shard_map/bhgd,bthd->bhgt/dot_general | solution.py:26
  69.3 96.4 %all-gather.3.cloned.1.call-done = bf16[8,12,32768]{2,1,0:T(8,128)(2,1)} async-done(((bf16[1,12,32768]{2,1,0:T(8,128)(2,1)}), bf16[8,12,32768]{2,1,0:T(8,128)(2,1)}) %all-gather.3.cloned.1.call-update) | async-done | bytes 6291472 | tf_op jit(solution)/shard_map/all_gather | solution.py:103
  165.6 6.9 %reshape.66 = bf16[96,32768]{1,0:T(8,128)(2,1)} reshape(bf16[8,12,32768]{2,1,0:T(8,128)(2,1)} %all-gather.3.cloned.1.call-done) | data formatting | bytes 12582912
  172.5 8.3 %convolution_convert_fusion = bf16[128,32768]{1,0:T(8,128)(2,1)} fusion(bf16[96,32768]{1,0:T(8,128)(2,1)} %reshape.66, s32[96]{0:T(128)S(1)} %eq.36, pred[96]{0:T(512)(128)(4,1)S(1)} %and.31), kind=kOutput, calls=%fused_computation | convolution fusion | flops 809549824 | bytes 14680544 | tf_op jit(solution)/shard_map/dot_general | solution.py:105
  180.9 14.3 %reshape_reshape.3 = bf16[128,64,2,2,128]{4,3,2,1,0:T(2,128)(2,1)} reshape(bf16[128,32768]{1,0:T(8,128)(2,1)} %convolution_convert_fusion) | data formatting | bytes 16777216 | tf_op jit(solution)/shard_map/reshape;reshape | solution.py:22
  195.2 19.1 %fusion.37 = (bf16[128,64,2,1,128]{4,3,2,1,0:T(2,128)(2,1)S(1)}, bf16[128,64,2,1,128]{4,3,2,1,0:T(2,128)(2,1)S(1)}) fusion(bf16[128,64,2,2,128]{4,3,2,1,0:T(2,128)(2,1)} %reshape_reshape.3), kind=kLoop, calls=%fused_computation.67 | loop fusion | bytes 16777216 | tf_op jit(solution)/shard_map/slice | solution.py:36
  214.3 2.6 %bitcast_reduce_fusion = (f32[128,2,12]{2,1,0:T(2,128)S(1)}, f32[128,2,64,12]{2,3,1,0:T(8,128)S(1)}) fusion(pred[128,64]{1,0:T(8,128)(4,1)S(1)} %iota_compare_fusion.1, bf16[128,2,12,128]{3,2,1,0:T(8,128)(2,1)S(1)} %copy.37, bf16[128,64,2,1,128]{4,3,2,1,0:T(2,128)(2,1)S(1)} %get-tuple-element.7), kind=kOutput, calls=%fused_computation.9 | convolution fusion | flops 50918400 | bytes 5787648 | tf_op jit(solution)/shard_map/bhgd,bthd->bhgt/dot_general | solution.py:35
  217.0 1.4 fusion.11
  218.4 1.4 fusion.10
  220.0 2.0 fusion
  222.1 2.0 add_convert_fusion
  224.1 0.8 copy.46
  224.9 1.2 copy.47
  (44 shorter events, 2.5 us)
Async XLA Ops:
  6.5 14.7 %copy-start = (bf16[128,6144]{1,0:T(8,128)(2,1)S(1)}, bf16[128,6144]{1,0:T(8,128)(2,1)}, u32[]{:S(2)}) copy-start(bf16[128,6144]{1,0:T(8,128)(2,1)} %param.10) | copy-start | bytes 4718596
  6.5 14.7 %copy-start.7 = (f32[1024]{0:T(1024)S(1)}, f32[1024]{0:T(1024)}, u32[]{:S(2)}) copy-start(f32[1024]{0:T(1024)} %param.17) | copy-start | bytes 12292
  6.5 30.2 %reduce-scatter.2.cloned.1.call-start = ((), (), s32[]{:S(2)}) async-start(), calls=%async_computation.1 | async-start | bytes 2752512 | tf_op jit(solution)/shard_map/reduce_scatter | solution.py:99
  6.5 14.7 %copy-start.2 = (bf16[6144,1024]{1,0:T(8,128)(2,1)S(1)}, bf16[6144,1024]{1,0:T(8,128)(2,1)}, u32[]{:S(2)}) copy-start(bf16[6144,1024]{1,0:T(8,128)(2,1)} %param.16) | copy-start | bytes 37748740
  24.5 14.9 %copy-start.6 = (s32[8,12]{1,0:T(8,128)S(1)}, s32[8,12]{1,0:T(8,128)}, u32[]{:S(2)}) copy-start(s32[8,12]{1,0:T(8,128)} %param.15) | copy-start | bytes 1156
  24.5 15.3 %copy-start.8 = (s32[8,12]{1,0:T(8,128)S(1)}, s32[8,12]{1,0:T(8,128)}, u32[]{:S(2)}) copy-start(s32[8,12]{1,0:T(8,128)} %param.14) | copy-start | bytes 1156
  24.5 15.4 %copy-start.5 = (bf16[128,3072]{1,0:T(8,128)(2,1)S(1)}, bf16[128,3072]{1,0:T(8,128)(2,1)}, u32[]{:S(2)}) copy-start(bf16[128,3072]{1,0:T(8,128)(2,1)} %param.11) | copy-start | bytes 2359300
  24.5 141.1 %all-gather.3.cloned.1.call-start = ((), (), s32[]{:S(2)}) async-start(), calls=%async_computation.2 | async-start | bytes 9437184 | tf_op jit(solution)/shard_map/all_gather | solution.py:103
  36.7 1.1 slice-start
  59.2 4.8 %copy-start.9 = (s32[128]{0:T(128)S(1)}, s32[128]{0:T(128)}, u32[]{:S(2)}) copy-start(s32[128]{0:T(128)} %param.13) | copy-start | bytes 1540
  64.1 4.2 %slice-start.1 = ((bf16[896,512]{1,0:T(8,128)(2,1)}), bf16[128,512]{1,0:T(8,128)(2,1)S(1)}, s32[]{:S(2)}) async-start(bf16[896,512]{1,0:T(8,128)(2,1)} %reduce-scatter.2.cloned.1.call-done), calls=%async_computation.4 | async-start | bytes 262144 | tf_op jit(solution)/shard_map/slice | solution.py:107
  216.8 1.6 copy-start.3
  220.0 2.0 copy-start.4
  222.0 4.1 %copy-start.1 = (bf16[128,6144]{1,0:T(8,128)(2,1)S(1)}, bf16[128,6144]{1,0:T(8,128)(2,1)}, u32[]{:S(2)}) copy-start(bf16[128,6144]{1,0:T(8,128)(2,1)} %param.10) | copy-start | bytes 4718596
Sparse Core Ops, SparseCore 0:
  24.6 12.0 reduce-scatter.1
  39.5 126.0 all-gather.2
where the time goes:
time: 234 us; the launch traced here: 233 us
  waiting for transfers between devices  109 us (47%)
  local copies, waits for them, and re-layouts  69.5 us (30%)
  matrix products  36.3 us (16%)
  between operations  13.7 us (6%)
  other arithmetic  4.94 us (2%)
    all_gather x1, waiting for transfers between devices, shards(): everyone = lax.all_gather(packed, 'section', axis=0, tiled=True)  96.4 us
    unnamed x28, local copies, waits for them, and re-layouts  26.2 us
    slice x1, local copies, waits for them, and re-layouts, attend(): arrived[:, :, :, 0]  19.1 us
    dot_general x2, matrix products, partial_kv(): return jnp.dot(rows_in, w_kv, preferred_element_type=jnp.float32) * kv_scale  16.5 us
    another operation x1, local copies, waits for them, and re-layouts, attend(): arrived = arrived.reshape(row_count, arrived.shape[1], kv_heads, 2, HD)  14.3 us
    reduce_scatter x1, waiting for transfers between devices, shards(): lax.psum_scatter(partial_terms.astype(jnp.bfloat16), 'tp', scatter_dimens...  12.2 us
    dot_general x1, matrix products, shards(): result_rows = jnp.dot(picker, everyone, preferred_element_type=jnp.float32)  8.35 us
    slice x1, local copies, waits for them, and re-layouts, attend(): cache_rows[:, :, :, 1]  5.19 us
  transfers between devices with their start and end apart: 2, of which 2 were waited for; matrix products, arithmetic and copies ran while one was open for 13% of the time, Pallas kernels for 0%

commit v1 on v0

v1 whole, which is shorter than its diff:
```python
import functools
import math

import jax
import jax.numpy as jnp
from jax import lax
from jax.experimental import pallas as pl
from jax.experimental.pallas import tpu as pltpu
from jax.sharding import PartitionSpec as P

HD = 128
CAP = 2
STATS = 128
MASKED = -1e30
LOG2_SCALE = HD ** (-0.5) * math.log2(math.e)
F32 = jnp.float32
BF16 = jnp.bfloat16
VMEM_LIMIT = 56 * 1024 * 1024


def iota(shape, dim):
    return lax.broadcasted_iota(jnp.int32, shape, dim)


def decode_slots(target_ref, first_section, position, row_count):
    sections, requests = target_ref.shape
    slots = sections * CAP
    slot_id = iota((slots, requests), 0)
    table = jnp.zeros((slots, requests), jnp.int32)
    for step in range(sections):
        row = target_ref[pl.ds(lax.rem(first_section + step, sections), 1), :]
        table = jnp.where((slot_id >= step * CAP) & (slot_id < (step + 1) * CAP), row, table)
    local = table - position * row_count
    here = ((local >= 0) & (local < row_count)).astype(jnp.int32)
    member = lax.rem(iota((slots, 1), 0), CAP)
    earlier = jnp.zeros((slots, 1), jnp.int32)
    found = jnp.full((slots, 1), -1, jnp.int32)
    for r in range(requests):
        named = here[:, r : r + 1]
        found = jnp.where((named == 1) & (earlier == member), local[:, r : r + 1], found)
        earlier = earlier + named
    return found


def request_slots(target_ref, span_ref, position, row_count, padded):
    sections, requests = target_ref.shape
    target = target_ref[pl.ds(position, 1), :].astype(F32)
    span = span_ref[pl.ds(position, 1), :].astype(F32)
    section = jnp.zeros_like(target)
    for s in range(1, sections):
        section = section + (target >= s * row_count).astype(F32)
    diagonal = iota((padded, requests), 0) == iota((padded, requests), 1)
    section_col = jnp.sum(jnp.where(diagonal, section, 0.0), axis=1, keepdims=True)
    span_col = jnp.sum(jnp.where(diagonal, span, 0.0), axis=1, keepdims=True)
    real = iota((padded, 1), 0) < requests
    section_col = jnp.where(real, section_col, -1.0)
    square_0, square_1 = iota((padded, padded), 0), iota((padded, padded), 1)
    section_row = jnp.sum(jnp.where(square_0 == square_1, section_col, 0.0), axis=0, keepdims=True)
    before = (section_row == section_col) & (square_1 < square_0)
    rank_col = jnp.sum(before.astype(F32), axis=1, keepdims=True)
    slot_col = jnp.where(real, section_col * CAP + rank_col, -1.0)
    slot_row = jnp.sum(jnp.where(square_0 == square_1, slot_col, 0.0), axis=0, keepdims=True)
    return slot_col.astype(jnp.int32), slot_row.astype(jnp.int32), span_col.astype(jnp.int32)


def select_queries(place_ref, target_ref, queries_ref, out_ref):
    row_count = queries_ref.shape[0]
    rows = decode_slots(target_ref, 0, place_ref[0], row_count)
    pick = (iota((rows.shape[0], row_count), 1) == rows).astype(BF16)
    out_ref[...] = jnp.dot(pick, queries_ref[...], preferred_element_type=F32).astype(BF16)


def project(place_ref, prompts_ref, hidden_ref, w_ref, scale_ref, out_ref, total_ref):
    step = pl.program_id(0)
    prompt_rows = prompts_ref.shape[0]
    w = w_ref[...]
    prompt_part = jnp.dot(prompts_ref[...], w, preferred_element_type=F32)
    hidden_part = jnp.dot(hidden_ref[...], w, preferred_element_type=F32)

    @pl.when(step == 0)
    def _():
        total_ref[:prompt_rows] = prompt_part
        total_ref[prompt_rows:] = hidden_part

    @pl.when(step > 0)
    def _():
        total_ref[:prompt_rows] += prompt_part
        total_ref[prompt_rows:] += hidden_part

    @pl.when(step == pl.num_programs(0) - 1)
    def _():
        out_ref[...] = (total_ref[...] * scale_ref[...]).astype(BF16)


def split_bf16(x):
    high = x.astype(BF16).astype(F32)
    middle = (x - high).astype(BF16).astype(F32)
    return high, middle, (x - high - middle).astype(BF16).astype(F32)


def attend_arrived(place_ref, target_ref, span_ref, mine_ref, other_ref, queries_ref, out_ref):
    sections, requests = target_ref.shape
    padded = -(-requests // 16) * 16
    prompt_rows = mine_ref.shape[0]
    span_rows = prompt_rows // requests
    slots, width = queries_ref.shape
    group = width // HD
    slot_col, slot_row, span_col = request_slots(
        target_ref, span_ref, place_ref[0], place_ref[2], padded
    )
    from_slot = (iota((padded, slots), 1) == slot_col).astype(BF16)
    to_slot = (iota((slots, padded), 0) == slot_row).astype(BF16)
    rows = jnp.dot(from_slot, queries_ref[...], preferred_element_type=F32).astype(BF16)
    stacked = jnp.concatenate([rows[:, i * HD : (i + 1) * HD] for i in range(group)], axis=0)
    kv = (mine_ref[...].astype(F32) + other_ref[...].astype(F32)).astype(BF16)
    scores = lax.dot_general(
        stacked, kv[:, :HD], (((1,), (1,)), ((), ())), preferred_element_type=F32
    )
    key = iota((padded, prompt_rows), 1) - iota((padded, prompt_rows), 0) * span_rows
    valid = (key >= 0) & (key < span_col)
    bias = jnp.where(valid, 0.0, MASKED)
    scores = scores.reshape(group, padded, prompt_rows) * LOG2_SCALE + bias[None]
    largest = jnp.max(scores, axis=2, keepdims=True)
    weights = jnp.exp2(scores - largest)
    total = jnp.sum(weights, axis=2, keepdims=True)
    values = jnp.dot(
        weights.reshape(group * padded, prompt_rows).astype(BF16),
        kv[:, HD:],
        preferred_element_type=F32,
    ).reshape(group, padded, HD)
    values = values / total
    lse = largest + jnp.log2(total)
    lane = iota((padded, STATS), 1)
    stats = jnp.zeros((padded, STATS), F32)
    for i in range(group):
        for part, piece in enumerate(split_bf16(lse[i])):
            stats = jnp.where(lane == part * group + i, piece, stats)
    result = jnp.concatenate([values[i] for i in range(group)] + [stats], axis=1)
    out_ref[...] = jnp.dot(to_slot, result.astype(BF16), preferred_element_type=F32).astype(BF16)


def attend_cache(
    queries_ref, cache_ref, len_ref, mine_ref, other_ref, out_ref, stats_ref
):
    block_rows, cache_rows, width = cache_ref.shape
    kv_heads = width // (2 * HD)
    group = queries_ref.shape[1] // (kv_heads * HD)
    unit = 8
    queries = queries_ref[...].astype(F32)
    own = (mine_ref[...].astype(F32) + other_ref[...].astype(F32)).astype(BF16).astype(F32)
    shape = (unit, unit * cache_rows)
    key = iota(shape, 1) - iota(shape, 0) * cache_rows
    lane = iota((unit, STATS), 1)
    outs, all_stats = [], []
    for u in range(block_rows // unit):
        at = slice(u * unit, (u + 1) * unit)
        valid = (key >= 0) & (key < len_ref[at, :])
        bias = jnp.where(valid, 0.0, MASKED)
        stats = jnp.zeros((unit, STATS), F32)
        pieces = []
        for h in range(kv_heads):
            first = h * group
            q = jnp.stack(
                [queries[at, (first + i) * HD : (first + i + 1) * HD] for i in range(group)], axis=0
            )
            base = h * 2 * HD
            keys = cache_ref[at, :, base : base + HD].reshape(unit * cache_rows, HD)
            values = cache_ref[at, :, base + HD : base + 2 * HD].reshape(unit * cache_rows, HD)
            scores = lax.dot_general(
                q.reshape(group * unit, HD).astype(BF16),
                keys,
                (((1,), (1,)), ((), ())),
                preferred_element_type=F32,
            ).reshape(group, unit, unit * cache_rows)
            scores = scores * LOG2_SCALE + bias[None]
            own_key = own[at, base : base + HD]
            own_value = own[at, base + HD : base + 2 * HD]
            own_score = jnp.sum(q * own_key[None], axis=2, keepdims=True) * LOG2_SCALE
            largest = jnp.maximum(jnp.max(scores, axis=2, keepdims=True), own_score)
            weights = jnp.exp2(scores - largest)
            own_weight = jnp.exp2(own_score - largest)
            total = jnp.sum(weights, axis=2, keepdims=True) + own_weight
            result = jnp.dot(
                weights.reshape(group * unit, unit * cache_rows).astype(BF16),
                values,
                preferred_element_type=F32,
            ).reshape(group, unit, HD)
            result = (result + own_weight * own_value[None]) / total
            lse = largest + jnp.log2(total)
            pieces += [result[i] for i in range(group)]
            for i in range(group):
                stats = jnp.where(lane == first + i, lse[i], stats)
        outs.append(jnp.concatenate(pieces, axis=1))
        all_stats.append(stats)
    out_ref[...] = jnp.concatenate(outs, axis=0).astype(out_ref.dtype)
    stats_ref[...] = jnp.concatenate(all_stats, axis=0)


def merge(place_ref, target_ref, arrived_ref, cache_ref, stats_ref, out_ref, *, group):
    row_count = cache_ref.shape[0]
    head = pl.program_id(0)
    slots = arrived_ref.shape[0]
    rows = decode_slots(target_ref, 0, place_ref[0], row_count)
    pick = (iota((slots, row_count), 1) == rows).astype(BF16)
    has = lax.dot_general(
        pick, jnp.ones((slots, STATS), BF16), (((0,), (0,)), ((), ())), preferred_element_type=F32
    )
    arrived = lax.dot_general(
        pick, arrived_ref[...], (((0,), (0,)), ((), ())), preferred_element_type=F32
    )
    stats = stats_ref[...]
    first = arrived[:, group * HD :]
    for i in range(group):
        cache_lse = jnp.where(
            head == 0, stats[:, i : i + 1], stats[:, group + i : group + i + 1]
        )
        new_lse = (
            first[:, i : i + 1]
            + first[:, group + i : group + i + 1]
            + first[:, 2 * group + i : 2 * group + i + 1]
        )
        new_lse = jnp.where(has[:, :1] > 0.5, new_lse, MASKED)
        largest = jnp.maximum(cache_lse, new_lse)
        cache_weight = jnp.exp2(cache_lse - largest)
        new_weight = jnp.exp2(new_lse - largest)
        total = cache_weight + new_weight
        at = slice(i * HD, (i + 1) * HD)
        out_ref[:, at] = (
            cache_ref[:, at].astype(F32) * (cache_weight / total)
            + arrived[:, at] * (new_weight / total)
        ).astype(BF16)


def compiler_params():
    return pltpu.CompilerParams(vmem_limit_bytes=VMEM_LIMIT)


def whole(array):
    return pl.BlockSpec(array.shape, lambda *_: (0,) * array.ndim)


def shards(
    prompts, decode_hidden, queries, kv_cache, cache_len, span_len, target_row, w_kv, kv_scale
):
    row_count = decode_hidden.shape[0]
    prompt_rows, features = prompts.shape
    sections = lax.axis_size("section")
    tensor_parts = lax.axis_size("tp")
    local_width = kv_cache.shape[2]
    cache_rows = kv_cache.shape[1]
    kv_heads = local_width // (2 * HD)
    query_width = queries.shape[1]
    group = query_width // (kv_heads * HD)
    slots = sections * CAP
    all_rows = prompt_rows + row_count
    tp = lax.axis_index("tp")
    place = jnp.stack(
        [lax.axis_index("section"), tp, jnp.int32(row_count), tensor_parts - 1 - tp]
    ).astype(jnp.int32)
    scale = kv_scale.reshape(1, -1)
    lengths = cache_len.reshape(-1, 1)

    asked = pl.pallas_call(
        select_queries,
        grid_spec=pltpu.PrefetchScalarGridSpec(
            num_scalar_prefetch=1,
            grid=(1,),
            in_specs=[whole(target_row), whole(queries)],
            out_specs=pl.BlockSpec((slots, query_width), lambda *_: (0, 0)),
        ),
        out_shape=jax.ShapeDtypeStruct((slots, query_width), BF16),
        compiler_params=compiler_params(),
        name="select_queries",
    )(place, target_row, queries)
    asked = lax.all_to_all(asked, "section", 0, 0, tiled=True)

    depth = 1024

    def projected(which):
        return pl.pallas_call(
            project,
            grid_spec=pltpu.PrefetchScalarGridSpec(
                num_scalar_prefetch=1,
                grid=(features // depth,),
                in_specs=[
                    pl.BlockSpec((prompt_rows, depth), lambda k, place: (0, k)),
                    pl.BlockSpec((row_count, depth), lambda k, place: (0, k)),
                    pl.BlockSpec((depth, local_width), lambda k, place: (k, place[which])),
                    pl.BlockSpec((1, local_width), lambda k, place: (0, place[which])),
                ],
                out_specs=pl.BlockSpec((all_rows, local_width), lambda k, place: (0, 0)),
                scratch_shapes=[pltpu.VMEM((all_rows, local_width), F32)],
            ),
            out_shape=jax.ShapeDtypeStruct((all_rows, local_width), BF16),
            compiler_params=compiler_params(),
            name="project",
        )(place, prompts, decode_hidden, w_kv, scale)

    theirs = projected(3)
    other = lax.ppermute(theirs, "tp", [(0, 1), (1, 0)])
    mine = projected(1)

    head_width = group * HD
    answer_width = head_width + STATS
    answers = pl.pallas_call(
        attend_arrived,
        grid_spec=pltpu.PrefetchScalarGridSpec(
            num_scalar_prefetch=1,
            grid=(kv_heads,),
            in_specs=[
                whole(target_row),
                whole(span_len),
                pl.BlockSpec((prompt_rows, 2 * HD), lambda h, place: (0, h)),
                pl.BlockSpec((prompt_rows, 2 * HD), lambda h, place: (0, h)),
                pl.BlockSpec((slots, head_width), lambda h, place: (0, h)),
            ],
            out_specs=pl.BlockSpec((slots, answer_width), lambda h, place: (0, h)),
        ),
        out_shape=jax.ShapeDtypeStruct((slots, kv_heads * answer_width), BF16),
        compiler_params=compiler_params(),
        name="attend_arrived",
    )(place, target_row, span_len, mine, other, asked)
    answers = lax.all_to_all(answers, "section", 0, 0, tiled=True)

    block = 16
    own_block = prompt_rows // block
    cached, stats = pl.pallas_call(
        attend_cache,
        grid=(row_count // block,),
        in_specs=[
            pl.BlockSpec((block, query_width), lambda b: (b, 0)),
            pl.BlockSpec((block, cache_rows, local_width), lambda b: (b, 0, 0)),
            pl.BlockSpec((block, 1), lambda b: (b, 0)),
            pl.BlockSpec((block, local_width), lambda b: (own_block + b, 0)),
            pl.BlockSpec((block, local_width), lambda b: (own_block + b, 0)),
        ],
        out_specs=[
            pl.BlockSpec((block, query_width), lambda b: (b, 0)),
            pl.BlockSpec((block, STATS), lambda b: (b, 0)),
        ],
        out_shape=[
            jax.ShapeDtypeStruct((row_count, query_width), F32),
            jax.ShapeDtypeStruct((row_count, STATS), F32),
        ],
        compiler_params=compiler_params(),
        name="attend_cache",
    )(queries, kv_cache, lengths, mine, other)

    return pl.pallas_call(
        functools.partial(merge, group=group),
        grid_spec=pltpu.PrefetchScalarGridSpec(
            num_scalar_prefetch=1,
            grid=(kv_heads,),
            in_specs=[
                whole(target_row),
                pl.BlockSpec((slots, answer_width), lambda h, place: (0, h)),
                pl.BlockSpec((row_count, head_width), lambda h, place: (0, h)),
                whole(stats),
            ],
            out_specs=pl.BlockSpec((row_count, head_width), lambda h, place: (0, h)),
        ),
        out_shape=jax.ShapeDtypeStruct((row_count, query_width), BF16),
        compiler_params=compiler_params(),
        name="merge",
    )(place, target_row, answers, cached, stats)


def solution(mesh):
    in_specs = (
        P(("groups", "section"), "tp"),
        P(("groups", "section"), "tp"),
        P(("groups", "section"), "tp"),
        P(("groups", "section"), None, "tp"),
        P(("groups", "section")),
        P("groups", None),
        P("groups", None),
        P("tp", None),
        P(),
    )
    out_specs = P(("groups", "section"), "tp")
    return jax.shard_map(shards, mesh=mesh, in_specs=in_specs, out_specs=out_specs, check_vma=False)
```

time: 234 us -> 71.6 us (0.31)
  waiting for transfers between devices: 109 us -> 0.01 us
  local copies, waits for them, and re-layouts: 69.5 us -> 6.2 us
  Pallas kernels: 0 us -> 50.6 us
  matrix products: 36.3 us -> 0 us
  between operations: 13.7 us -> 0.02 us
  starting transfers between devices: 0.04 us -> 13.3 us
  other arithmetic: 4.94 us -> 0.59 us
    all_gather x1 -> x0, waiting for transfers between devices: 96.4 us -> none  [shards(): everyone = lax.all_gather(packed, 'section', axis=0, tiled=True)]
    pallas_call x0 -> x6, Pallas kernels: none -> 50.6 us  [the longest x2 25 us: projected(): pl.pallas_call(project, grid_spec=pltpu.PrefetchScalarGridSpec(num_scalar...]
    dot_general x8 -> x0, matrix products: 36.3 us -> none  [the longest x2 16.5 us: partial_kv(): return jnp.dot(rows_in, w_kv, preferred_element_type=jnp.float32) * kv_scale]
    slice x6 -> x0, local copies, waits for them, and re-layouts: 25.4 us -> none  [the longest x1 19.1 us: attend(): arrived[:, :, :, 0]]
    unnamed x28 -> x4, local copies, waits for them, and re-layouts: 26.2 us -> 0.94 us
    another operation x1 -> x0, local copies, waits for them, and re-layouts: 14.3 us -> none  [attend(): arrived = arrived.reshape(row_count, arrived.shape[1], kv_heads, 2, HD)]
    all_to_all x0 -> x2, starting transfers between devices: none -> 12.8 us  [the longest x1 6.83 us: shards(): asked = lax.all_to_all(asked, 'section', 0, 0, tiled=True)]
    reduce_scatter x1 -> x0, waiting for transfers between devices: 12.2 us -> none  [shards(): lax.psum_scatter(partial_terms.astype(jnp.bfloat16), 'tp', scatter_dimens...]
  transfers between devices with their start and end apart: 2 -> 3, of which waited for: 2 -> 0; matrix products, arithmetic and copies ran while one was open for 13% -> 1% of each run, Pallas kernels for 0% -> 37%
where the time goes in v1:
time: 71.6 us; the launch traced here: 70.7 us
  Pallas kernels  50.6 us (71%)
  starting transfers between devices  13.3 us (19%)
  local copies, waits for them, and re-layouts  6.2 us (9%)
    pallas_call x2, Pallas kernels, projected(): pl.pallas_call(project, grid_spec=pltpu.PrefetchScalarGridSpec(num_scalar...  25 us
    pallas_call x1, Pallas kernels, shards(): pl.pallas_call(attend_cache, grid=(row_count // block,), in_specs=[pl.Blo...  9.81 us
    pallas_call x1, Pallas kernels, shards(): pl.pallas_call(functools.partial(merge, group=group), grid_spec=pltpu.Pre...  8.02 us
    all_to_all x1, starting transfers between devices, shards(): asked = lax.all_to_all(asked, 'section', 0, 0, tiled=True)  6.83 us
    all_to_all x1, starting transfers between devices, shards(): answers = lax.all_to_all(answers, 'section', 0, 0, tiled=True)  5.99 us
    pallas_call x1, Pallas kernels, shards(): pl.pallas_call(attend_arrived, grid_spec=pltpu.PrefetchScalarGridSpec(num...  4.34 us
    pallas_call x1, Pallas kernels, shards(): pl.pallas_call(select_queries, grid_spec=pltpu.PrefetchScalarGridSpec(num...  3.49 us
    all_to_all x2, local copies, waits for them, and re-layouts, shards(): asked = lax.all_to_all(asked, 'section', 0, 0, tiled=True)  2.26 us
  transfers between devices with their start and end apart: 3, of which 0 were waited for; matrix products, arithmetic and copies ran while one was open for 1% of the time, Pallas kernels for 37%

profile of v1, /device:TPU:0, one launch (start us, length us, event | category | flops | bytes accessed | tf_op | source)
XLA Modules:
  0.0 70.7 jit_solution(15523375295624996796)
XLA Ops:
  0.0 0.6 pad_add_fusion.place_ref
  0.6 12.4 %project.3 = bf16[896,512]{1,0:T(8,128)(2,1)} custom-call(s32[4]{0:T(128)} %pad_add_fusion.place_ref, bf16[768,6144]{1,0:T(8,128)(2,1)} %prompts_ref.3, bf16[128,6144]{1,0:T(8,128)(2,1)} %hidden_ref.3, bf16[6144,1024]{1,0:T(8,128)(2,1)} %w_ref.3, f32[1,1024]{1,0:T(1,128)} %bitcast.5), custom_call_target="tpu_custom_call" | custom-call | tf_op jit(solution)/shard_map/project/pallas_call | solution.py:280
  13.0 0.5 collective-permute-start
  13.5 3.5 %select_queries.1 = bf16[16,3072]{1,0:T(8,128)(2,1)} custom-call(s32[4]{0:T(128)} %pad_add_fusion.place_ref, s32[8,12]{1,0:T(8,128)} %target_ref.5, bf16[128,3072]{1,0:T(8,128)(2,1)} %queries_ref.3), custom_call_target="tpu_custom_call" | custom-call | tf_op jit(solution)/shard_map/select_queries/pallas_call | solution.py:263
  17.0 1.6 %all_to_all.14 = bf16[8,2,3072]{2,1,0:T(2,128)(2,1)} reshape(bf16[16,3072]{1,0:T(8,128)(2,1)} %select_queries.1) | data formatting | bytes 196608 | tf_op jit(solution)/shard_map/all_to_all | solution.py:275
  18.5 6.8 %all-to-all-start = ((bf16[8,2,3072]{2,1,0:T(2,128)(2,1)}), bf16[8,2,3072]{2,1,0:T(2,128)(2,1)S(1)}, u32[]{:S(2)}, u32[]{:S(2)}) async-start(bf16[8,2,3072]{2,1,0:T(2,128)(2,1)} %all_to_all.14), calls=%async_computation | async-start | bytes 196608 | tf_op jit(solution)/shard_map/all_to_all | solution.py:275
  25.4 0.0 copy-start.1
  25.4 12.5 %project.2.mine_ref = bf16[896,512]{1,0:T(8,128)(2,1)} custom-call(s32[4]{0:T(128)} %pad_add_fusion.place_ref, bf16[768,6144]{1,0:T(8,128)(2,1)} %prompts_ref.3, bf16[128,6144]{1,0:T(8,128)(2,1)} %hidden_ref.3, bf16[6144,1024]{1,0:T(8,128)(2,1)} %w_ref.3, f32[1,1024]{1,0:T(1,128)} %bitcast.6), custom_call_target="tpu_custom_call" | custom-call | tf_op jit(solution)/shard_map/project/pallas_call | solution.py:280
  37.9 0.0 all-to-all-done
  37.9 0.7 all_to_all.16.queries_ref
  38.6 0.0 collective-permute-done.other_ref
  38.6 0.0 copy-start
  38.6 0.9 %copy-done = bf16[896,512]{1,0:T(8,128)(2,1)} copy-done((bf16[896,512]{1,0:T(8,128)(2,1)}, bf16[896,512]{1,0:T(8,128)(2,1)S(1)}, u32[]{:S(2)}) %copy-start) | copy-done | bytes 917528
  39.5 4.3 %attend_arrived.1 = bf16[16,3328]{1,0:T(8,128)(2,1)} custom-call(s32[4]{0:T(128)} %pad_add_fusion.place_ref, s32[8,12]{1,0:T(8,128)} %target_ref.5, s32[8,12]{1,0:T(8,128)} %span_ref.1, bf16[896,512]{1,0:T(8,128)(2,1)} %project.2.mine_ref, bf16[896,512]{1,0:T(8,128)(2,1)} %copy-done, bf16[16,3072]{1,0:T(8,128)(2,1)} %all_to_all.16.queries_ref), custom_call_target="tpu_custom_call" | custom-call | tf_op jit(solution)/shard_map/attend_arrived/pallas_call | solution.py:305
  43.9 1.6 %all_to_all.17 = bf16[8,2,3328]{2,1,0:T(2,128)(2,1)} reshape(bf16[16,3328]{1,0:T(8,128)(2,1)} %attend_arrived.1) | data formatting | bytes 212992 | tf_op jit(solution)/shard_map/all_to_all | solution.py:323
  45.4 6.0 %all-to-all-start.1 = ((bf16[8,2,3328]{2,1,0:T(2,128)(2,1)}), bf16[8,2,3328]{2,1,0:T(2,128)(2,1)S(1)}, u32[]{:S(2)}, u32[]{:S(2)}) async-start(bf16[8,2,3328]{2,1,0:T(2,128)(2,1)} %all_to_all.17), calls=%async_computation.1 | async-start | bytes 212992 | tf_op jit(solution)/shard_map/all_to_all | solution.py:323
  51.4 0.0 copy-done.1
  51.4 0.7 %copy.10.len_ref = s32[128,1]{1,0:T(8,128)} copy(s32[128,1]{0,1:T(1,128)S(1)} %bitcast.7) | data formatting | bytes 1024 | tf_op jit(solution)/shard_map/reshape | solution.py:261
  52.2 9.8 %attend_cache.1 = (f32[128,3072]{1,0:T(8,128)}, f32[128,128]{1,0:T(8,128)}) custom-call(bf16[128,3072]{1,0:T(8,128)(2,1)} %queries_ref.3, bf16[128,32,512]{2,1,0:T(8,128)(2,1)} %cache_ref.1, s32[128,1]{1,0:T(8,128)} %copy.10.len_ref, bf16[896,512]{1,0:T(8,128)(2,1)} %project.2.mine_ref, bf16[896,512]{1,0:T(8,128)(2,1)} %copy-done), custom_call_target="tpu_custom_call" | custom-call | tf_op jit(solution)/shard_map/attend_cache/pallas_call | solution.py:327
  62.0 0.0 all-to-all-done.1
  62.0 0.7 all_to_all.19.arrived_ref
  62.7 8.0 %merge.1 = bf16[128,3072]{1,0:T(8,128)(2,1)} custom-call(s32[4]{0:T(128)} %pad_add_fusion.place_ref, s32[8,12]{1,0:T(8,128)} %target_ref.5, bf16[16,3328]{1,0:T(8,128)(2,1)} %all_to_all.19.arrived_ref, f32[128,3072]{1,0:T(8,128)} %get-tuple-element.7.cache_ref, f32[128,128]{1,0:T(8,128)} %get-tuple-element.8.stats_ref), custom_call_target="tpu_custom_call" | custom-call | tf_op jit(solution)/shard_map/merge/pallas_call | solution.py:349
Async XLA Ops:
  13.0 25.6 %collective-permute-start = (bf16[896,512]{1,0:T(8,128)(2,1)}, bf16[896,512]{1,0:T(8,128)(2,1)S(1)}, u32[]{:S(2)}, u32[]{:S(2)}) collective-permute-start(bf16[896,512]{1,0:T(8,128)(2,1)} %project.3), channel_id=1, source_target_pairs={{0,1},{1,0},{2,3},{3,2},{4,5},{5,4},{6,7},{7,6},{8,9},{9,8},{10,11... | collective-permute-start | bytes 2752520 | tf_op jit(solution)/shard_map/ppermute | solution.py:300
  18.5 19.4 %all-to-all-start = ((bf16[8,2,3072]{2,1,0:T(2,128)(2,1)}), bf16[8,2,3072]{2,1,0:T(2,128)(2,1)S(1)}, u32[]{:S(2)}, u32[]{:S(2)}) async-start(bf16[8,2,3072]{2,1,0:T(2,128)(2,1)} %all_to_all.14), calls=%async_computation | async-start | bytes 196608 | tf_op jit(solution)/shard_map/all_to_all | solution.py:275
  25.4 26.1 %copy-start.1 = (s32[128]{0:T(128)S(1)}, s32[128]{0:T(128)}, u32[]{:S(2)}) copy-start(s32[128]{0:T(128)} %param.13) | copy-start | bytes 1540
  38.6 0.9 %copy-start = (bf16[896,512]{1,0:T(8,128)(2,1)}, bf16[896,512]{1,0:T(8,128)(2,1)S(1)}, u32[]{:S(2)}) copy-start(bf16[896,512]{1,0:T(8,128)(2,1)S(1)} %collective-permute-done.other_ref) | copy-start | bytes 2752516
  45.4 16.6 %all-to-all-start.1 = ((bf16[8,2,3328]{2,1,0:T(2,128)(2,1)}), bf16[8,2,3328]{2,1,0:T(2,128)(2,1)S(1)}, u32[]{:S(2)}, u32[]{:S(2)}) async-start(bf16[8,2,3328]{2,1,0:T(2,128)(2,1)} %all_to_all.17), calls=%async_computation.1 | async-start | bytes 212992 | tf_op jit(solution)/shard_map/all_to_all | solution.py:323

commit v2 on v0

v2 whole, which is shorter than its diff:
```python
import functools
import math

import jax
import jax.numpy as jnp
from jax import lax
from jax.experimental import pallas as pl
from jax.experimental.pallas import tpu as pltpu
from jax.sharding import PartitionSpec as P

HD = 128
CAP = 2
STATS = 128
MASKED = -1e30
LOG2_SCALE = HD ** (-0.5) * math.log2(math.e)
F32 = jnp.float32
BF16 = jnp.bfloat16


def iota(shape, dim):
    return lax.broadcasted_iota(jnp.int32, shape, dim)


def decode_slots(target_ref, position, row_count, section_major):
    sections, requests = target_ref.shape
    slots = sections * CAP
    slot = iota((slots, 1), 0)
    if section_major:
        table = jnp.zeros((slots, requests), jnp.int32)
        slot_id = iota((slots, requests), 0)
        for s in range(sections):
            mine = (slot_id >= s * CAP) & (slot_id < (s + 1) * CAP)
            table = jnp.where(mine, target_ref[s : s + 1, :], table)
        member = lax.rem(slot, CAP)
    else:
        table = jnp.concatenate([target_ref[...]] * CAP, axis=0)
        member = sum((slot >= j * sections).astype(jnp.int32) for j in range(1, CAP))
    local = table - position * row_count
    here = (local >= 0) & (local < row_count)
    square = (requests, requests)
    earlier = jnp.dot(
        here.astype(F32).astype(BF16),
        (iota(square, 0) < iota(square, 1)).astype(F32).astype(BF16),
        preferred_element_type=F32,
    )
    chosen = here & (earlier == member.astype(F32))
    return jnp.max(jnp.where(chosen, local.astype(F32), -1.0), axis=1, keepdims=True).astype(
        jnp.int32
    )


def request_slots(target_ref, span_ref, position, row_count, padded):
    sections, requests = target_ref.shape
    target = target_ref[pl.ds(position, 1), :].astype(F32)
    span = span_ref[pl.ds(position, 1), :].astype(F32)
    diagonal = iota((padded, requests), 0) == iota((padded, requests), 1)
    target_col = jnp.sum(jnp.where(diagonal, target, 0.0), axis=1, keepdims=True)
    span_col = jnp.sum(jnp.where(diagonal, span, 0.0), axis=1, keepdims=True)
    section_row = jnp.zeros_like(target)
    section_col = jnp.zeros_like(target_col)
    for s in range(1, sections):
        section_row = section_row + (target >= s * row_count).astype(F32)
        section_col = section_col + (target_col >= s * row_count).astype(F32)
    before = (section_row == section_col) & (
        iota((padded, requests), 1) < iota((padded, requests), 0)
    )
    rank_col = jnp.sum(before.astype(F32), axis=1, keepdims=True)
    section_col = jnp.where(iota((padded, 1), 0) < requests, section_col, -1.0)
    return section_col.astype(jnp.int32), rank_col.astype(jnp.int32), span_col.astype(jnp.int32)


def select_queries(place_ref, target_ref, queries_ref, out_ref):
    row_count = queries_ref.shape[0]
    rows = decode_slots(target_ref, place_ref[0], row_count, False)
    pick = (iota((rows.shape[0], row_count), 1) == rows).astype(F32).astype(BF16)
    out_ref[...] = jnp.dot(pick, queries_ref[...], preferred_element_type=F32).astype(BF16)


def project_first(
    place_ref,
    prompts_ref,
    hidden_ref,
    w_ref,
    scale_ref,
    out_ref,
    rows_ref,
    w_mine_ref,
    w_theirs_ref,
    total_ref,
    row_sems,
    hidden_sems,
    theirs_sems,
    mine_sems,
    *,
    edges,
):
    prompt_rows = prompts_ref.shape[0]
    width = out_ref.shape[1]
    theirs = pl.ds(pl.multiple_of(place_ref[2] * width, width), width)
    mine = pl.ds(pl.multiple_of(place_ref[1] * width, width), width)
    chunks = [slice(a, b) for a, b in zip(edges[:-1], edges[1:])]
    waits = []
    for c, at in enumerate(chunks):
        copies = [
            pltpu.make_async_copy(
                w_ref.at[at, theirs], w_theirs_ref.at[at, :], theirs_sems.at[c]
            ),
            pltpu.make_async_copy(
                prompts_ref.at[:, at], rows_ref.at[:prompt_rows, at], row_sems.at[c]
            ),
            pltpu.make_async_copy(
                hidden_ref.at[:, at], rows_ref.at[prompt_rows:, at], hidden_sems.at[c]
            ),
        ]
        for copy in copies:
            copy.start()
        waits.append(copies)
    later = []
    for c, at in enumerate(chunks):
        copy = pltpu.make_async_copy(w_ref.at[at, mine], w_mine_ref.at[at, :], mine_sems.at[c])
        copy.start()
        later.append(copy)
    for c, at in enumerate(chunks):
        for copy in waits[c]:
            copy.wait()
        part = jnp.dot(rows_ref[:, at], w_theirs_ref[at, :], preferred_element_type=F32)
        if c == 0:
            total_ref[...] = part
        elif c < len(chunks) - 1:
            total_ref[...] += part
        else:
            out_ref[...] = ((total_ref[...] + part) * scale_ref[...]).astype(BF16)
    for copy in later:
        copy.wait()


def project_second(place_ref, rows_ref, w_ref, scale_ref, out_ref, *, block):
    for m in range(0, rows_ref.shape[0], block):
        at = slice(m, m + block)
        total = jnp.dot(rows_ref[at, :], w_ref[...], preferred_element_type=F32)
        out_ref[at, :] = (total * scale_ref[...]).astype(BF16)


def split_bf16(x):
    high = x.astype(BF16).astype(F32)
    middle = (x - high).astype(BF16).astype(F32)
    return high, middle, (x - high - middle).astype(BF16).astype(F32)


def attend_arrived(
    place_ref, target_ref, span_ref, mine_ref, other_ref, asked_ref, out_ref, *, row_count
):
    sections, requests = target_ref.shape
    slots = sections * CAP
    padded = -(-requests // 16) * 16
    position = place_ref[0]
    prompt_rows = mine_ref.shape[0] - row_count
    span_rows = prompt_rows // requests
    kv_heads = mine_ref.shape[1] // (2 * HD)
    group = asked_ref.shape[1] // (kv_heads * HD)
    section_col, rank_col, span_col = request_slots(
        target_ref, span_ref, position, row_count, padded
    )
    asked_at = jnp.where(
        section_col >= 0, section_col * slots + rank_col * sections + position, -1
    )
    from_asked = (iota((padded, asked_ref.shape[0]), 1) == asked_at).astype(F32).astype(BF16)
    answer_at = jnp.where(section_col >= 0, section_col * CAP + rank_col, -1)
    to_slot = (iota((padded, slots), 1) == answer_at).astype(F32).astype(BF16)
    key = iota((padded, prompt_rows), 1) - iota((padded, prompt_rows), 0) * span_rows
    bias = jnp.where((key >= 0) & (key < span_col), 0.0, MASKED)
    rows = jnp.dot(from_asked, asked_ref[...], preferred_element_type=F32).astype(BF16)
    kv = (
        mine_ref[:prompt_rows, :].astype(F32) + other_ref[:prompt_rows, :].astype(F32)
    ).astype(BF16)
    scores = []
    for h in range(kv_heads):
        stacked = jnp.concatenate(
            [rows[:, (h * group + i) * HD : (h * group + i + 1) * HD] for i in range(group)],
            axis=0,
        )
        keys = kv[:, h * 2 * HD : (h * 2 + 1) * HD]
        scores.append(
            lax.dot_general(
                stacked, keys, (((1,), (1,)), ((), ())), preferred_element_type=F32
            )
        )
    scores = [
        x.reshape(group, padded, prompt_rows) * LOG2_SCALE + bias[None] for x in scores
    ]
    largest = [jnp.max(x, axis=2, keepdims=True) for x in scores]
    weights = [jnp.exp2(x - y) for x, y in zip(scores, largest)]
    totals = [jnp.sum(x, axis=2, keepdims=True) for x in weights]
    lane = iota((padded, STATS), 1)
    lse = jnp.zeros((padded, STATS), F32)
    pieces = []
    for h in range(kv_heads):
        values = jnp.dot(
            weights[h].reshape(group * padded, prompt_rows).astype(BF16),
            kv[:, (h * 2 + 1) * HD : (h * 2 + 2) * HD],
            preferred_element_type=F32,
        ).reshape(group, padded, HD)
        values = values / totals[h]
        head_lse = largest[h] + jnp.log2(totals[h])
        for i in range(group):
            pieces.append(values[i])
            lse = jnp.where(lane == h * group + i, head_lse[i], lse)
    result = jnp.concatenate(pieces + list(split_bf16(lse)), axis=1).astype(BF16)
    answers = lax.dot_general(
        to_slot, result, (((0,), (0,)), ((), ())), preferred_element_type=F32
    ).astype(BF16)
    for s in range(sections):
        out_ref[s] = answers[s * CAP : (s + 1) * CAP]


def attend_cache(queries_ref, cache_ref, len_ref, mine_ref, other_ref, out_ref, stats_ref):
    block_rows, cache_rows, width = cache_ref.shape
    kv_heads = width // (2 * HD)
    group = queries_ref.shape[1] // (kv_heads * HD)
    unit = 8
    keys_of = unit * cache_rows
    queries = queries_ref[...].astype(F32)
    own = (mine_ref[...].astype(F32) + other_ref[...].astype(F32)).astype(BF16).astype(F32)
    key = iota((unit, keys_of), 1) - iota((unit, keys_of), 0) * cache_rows
    lengths = len_ref[...].astype(F32)
    row_count = lengths.shape[1]
    first_row = pl.program_id(0) * block_rows
    lane = iota((unit, STATS), 1)
    ones = jnp.ones((keys_of, HD), BF16)
    units = range(block_rows // unit)
    pairs = [(u, h) for u in units for h in range(kv_heads)]
    bias = []
    for u in units:
        row = iota((unit, row_count), 0) + (first_row + u * unit)
        length = jnp.sum(
            jnp.where(iota((unit, row_count), 1) == row, lengths, 0.0), axis=1, keepdims=True
        ).astype(jnp.int32)
        bias.append(jnp.where((key >= 0) & (key < length), 0.0, MASKED))
    q, scores, own_scores = [], [], []
    for u, h in pairs:
        at = slice(u * unit, (u + 1) * unit)
        q.append(
            jnp.stack(
                [
                    queries[at, (h * group + i) * HD : (h * group + i + 1) * HD]
                    for i in range(group)
                ],
                axis=0,
            )
        )
        keys = cache_ref[at, :, h * 2 * HD : (h * 2 + 1) * HD].reshape(keys_of, HD)
        scores.append(
            lax.dot_general(
                q[-1].reshape(group * unit, HD).astype(BF16),
                keys,
                (((1,), (1,)), ((), ())),
                preferred_element_type=F32,
            ).reshape(group, unit, keys_of)
        )
    for n, (u, h) in enumerate(pairs):
        at = slice(u * unit, (u + 1) * unit)
        own_key = own[at, h * 2 * HD : (h * 2 + 1) * HD]
        own_scores.append(jnp.sum(q[n] * own_key[None], axis=2, keepdims=True) * LOG2_SCALE)
    scores = [scores[n] * LOG2_SCALE + bias[u][None] for n, (u, h) in enumerate(pairs)]
    largest = [
        jnp.maximum(jnp.max(x, axis=2, keepdims=True), y) for x, y in zip(scores, own_scores)
    ]
    weights = [jnp.exp2(x - y).astype(BF16) for x, y in zip(scores, largest)]
    own_weights = [jnp.exp2(x - y) for x, y in zip(own_scores, largest)]
    sums = []
    for n, (u, h) in enumerate(pairs):
        at = slice(u * unit, (u + 1) * unit)
        values = cache_ref[at, :, (h * 2 + 1) * HD : (h * 2 + 2) * HD].reshape(keys_of, HD)
        sums.append(
            jnp.dot(
                weights[n].reshape(group * unit, keys_of),
                jnp.concatenate([values, ones], axis=1),
                preferred_element_type=F32,
            ).reshape(group, unit, 2 * HD)
        )
    pieces = [[] for _ in units]
    stats = [jnp.zeros((unit, STATS), F32) for _ in units]
    for n, (u, h) in enumerate(pairs):
        at = slice(u * unit, (u + 1) * unit)
        own_value = own[at, (h * 2 + 1) * HD : (h * 2 + 2) * HD]
        total = sums[n][:, :, HD:] + own_weights[n]
        result = (sums[n][:, :, :HD] + own_weights[n] * own_value[None]) / total
        lse = largest[n] + jnp.log2(total)
        for i in range(group):
            pieces[u].append(result[i])
            stats[u] = jnp.where(lane == h * group + i, lse[i], stats[u])
    out_ref[...] = jnp.concatenate(
        [jnp.concatenate(x, axis=1) for x in pieces], axis=0
    ).astype(out_ref.dtype)
    stats_ref[...] = jnp.concatenate(stats, axis=0)


def merge(place_ref, target_ref, arrived_ref, cached_ref, stats_ref, out_ref):
    row_count, width = cached_ref.shape
    heads = width // HD
    sections = arrived_ref.shape[0]
    slots = sections * CAP
    rows = decode_slots(target_ref, place_ref[0], row_count, True)
    pick_f32 = (iota((slots, row_count), 1) == rows).astype(F32)
    pick = pick_f32.astype(BF16)
    transposed = (((0,), (0,)), ((), ()))
    has = lax.dot_general(
        pick, jnp.ones((slots, HD), BF16), transposed, preferred_element_type=F32
    )
    cached = jnp.dot(pick, cached_ref[...], preferred_element_type=F32)
    cached_lse = jnp.dot(
        pick_f32, stats_ref[...], preferred_element_type=F32, precision=lax.Precision.HIGHEST
    )
    arrived = jnp.concatenate([arrived_ref[s].astype(F32) for s in range(sections)], axis=0)
    arrived_lse = (
        arrived[:, width : width + STATS]
        + arrived[:, width + STATS : width + 2 * STATS]
        + arrived[:, width + 2 * STATS :]
    )
    largest = jnp.maximum(cached_lse, arrived_lse)
    cached_weight = jnp.exp2(cached_lse - largest)
    arrived_weight = jnp.exp2(arrived_lse - largest)
    total = cached_weight + arrived_weight
    cached_weight = cached_weight / total
    arrived_weight = arrived_weight / total
    merged = jnp.concatenate(
        [
            cached[:, i * HD : (i + 1) * HD] * cached_weight[:, i : i + 1]
            + arrived[:, i * HD : (i + 1) * HD] * arrived_weight[:, i : i + 1]
            for i in range(heads)
        ],
        axis=1,
    ).astype(BF16)
    placed = lax.dot_general(pick, merged, transposed, preferred_element_type=F32)
    for i in range(heads):
        at = slice(i * HD, (i + 1) * HD)
        out_ref[:, at] = jnp.where(
            has > 0.5, placed[:, at], cached_ref[:, at].astype(F32)
        ).astype(BF16)


def compiler_params(megabytes):
    return pltpu.CompilerParams(vmem_limit_bytes=megabytes * 1024 * 1024)


SCALARS = pl.BlockSpec(memory_space=pltpu.SMEM)
RESIDENT = pl.BlockSpec(memory_space=pltpu.VMEM)
REMAINS = pl.BlockSpec(memory_space=pl.ANY)


def in_vmem(x):
    return pltpu.with_memory_space_constraint(x, pltpu.VMEM)


def shards(
    prompts, decode_hidden, queries, kv_cache, cache_len, span_len, target_row, w_kv, kv_scale
):
    row_count = decode_hidden.shape[0]
    prompt_rows, features = prompts.shape
    sections = lax.axis_size("section")
    local_width = kv_cache.shape[2]
    cache_rows = kv_cache.shape[1]
    kv_heads = local_width // (2 * HD)
    query_width = queries.shape[1]
    slots = sections * CAP
    all_rows = prompt_rows + row_count
    tp = lax.axis_index("tp")
    place = jnp.stack([lax.axis_index("section"), tp, 1 - tp]).astype(jnp.int32)
    scale = kv_scale.reshape(1, -1)
    lengths = cache_len.reshape(1, -1)

    asked = pl.pallas_call(
        select_queries,
        in_specs=[SCALARS, RESIDENT, RESIDENT],
        out_specs=RESIDENT,
        out_shape=jax.ShapeDtypeStruct((slots, query_width), BF16),
        compiler_params=compiler_params(16),
        name="select_queries",
    )(place, target_row, queries)
    asked = lax.all_gather(asked, "section", axis=0, tiled=True)

    depth = 512
    edges = tuple(range(0, features + 1, depth))
    count = len(edges) - 1
    theirs, rows, w_mine = pl.pallas_call(
        functools.partial(project_first, edges=edges),
        grid_spec=pltpu.PrefetchScalarGridSpec(
            num_scalar_prefetch=1,
            grid=(1,),
            in_specs=[
                REMAINS,
                REMAINS,
                REMAINS,
                pl.BlockSpec((1, local_width), lambda k, place: (0, place[2])),
            ],
            out_specs=[RESIDENT, RESIDENT, RESIDENT],
            scratch_shapes=[
                pltpu.VMEM((features, local_width), BF16),
                pltpu.VMEM((all_rows, local_width), F32),
                pltpu.SemaphoreType.DMA((count,)),
                pltpu.SemaphoreType.DMA((count,)),
                pltpu.SemaphoreType.DMA((count,)),
                pltpu.SemaphoreType.DMA((count,)),
            ],
        ),
        out_shape=[
            jax.ShapeDtypeStruct((all_rows, local_width), BF16),
            pltpu.VMEM((all_rows, features), BF16),
            pltpu.VMEM((features, local_width), BF16),
        ],
        compiler_params=compiler_params(16),
        name="project_first",
    )(place, prompts, decode_hidden, w_kv, scale)
    other = lax.ppermute(theirs, "tp", [(0, 1), (1, 0)])
    mine = pl.pallas_call(
        functools.partial(project_second, block=all_rows // 2),
        grid_spec=pltpu.PrefetchScalarGridSpec(
            num_scalar_prefetch=1,
            grid=(1,),
            in_specs=[
                RESIDENT,
                RESIDENT,
                pl.BlockSpec((1, local_width), lambda k, place: (0, place[1])),
            ],
            out_specs=RESIDENT,
        ),
        out_shape=pltpu.VMEM((all_rows, local_width), BF16),
        compiler_params=compiler_params(16),
        name="project_second",
    )(place, in_vmem(rows), in_vmem(w_mine), scale)

    answer_width = query_width + 3 * STATS
    answers = pl.pallas_call(
        functools.partial(attend_arrived, row_count=row_count),
        in_specs=[SCALARS] + [RESIDENT] * 5,
        out_specs=RESIDENT,
        out_shape=jax.ShapeDtypeStruct((sections, CAP, answer_width), BF16),
        compiler_params=compiler_params(24),
        name="attend_arrived",
    )(place, target_row, span_len, in_vmem(mine), in_vmem(other), asked)
    answers = lax.all_to_all(answers, "section", 0, 0)

    block = 32
    own_block = prompt_rows // block
    cached, stats = pl.pallas_call(
        attend_cache,
        grid=(row_count // block,),
        in_specs=[
            pl.BlockSpec((block, query_width), lambda b: (b, 0)),
            pl.BlockSpec((block, cache_rows, local_width), lambda b: (b, 0, 0)),
            pl.BlockSpec((1, row_count), lambda b: (0, 0)),
            pl.BlockSpec((block, local_width), lambda b: (own_block + b, 0)),
            pl.BlockSpec((block, local_width), lambda b: (own_block + b, 0)),
        ],
        out_specs=[
            pl.BlockSpec((block, query_width), lambda b: (b, 0)),
            pl.BlockSpec((block, STATS), lambda b: (b, 0)),
        ],
        out_shape=[
            jax.ShapeDtypeStruct((row_count, query_width), BF16),
            jax.ShapeDtypeStruct((row_count, STATS), F32),
        ],
        compiler_params=compiler_params(24),
        name="attend_cache",
    )(queries, kv_cache, lengths, mine, other)

    return pl.pallas_call(
        merge,
        in_specs=[SCALARS] + [RESIDENT] * 4,
        out_specs=RESIDENT,
        out_shape=jax.ShapeDtypeStruct((row_count, query_width), BF16),
        compiler_params=compiler_params(24),
        name="merge",
    )(place, target_row, in_vmem(answers), cached, stats)


def solution(mesh):
    in_specs = (
        P(("groups", "section"), "tp"),
        P(("groups", "section"), "tp"),
        P(("groups", "section"), "tp"),
        P(("groups", "section"), None, "tp"),
        P(("groups", "section")),
        P("groups", None),
        P("groups", None),
        P("tp", None),
        P(),
    )
    out_specs = P(("groups", "section"), "tp")
    return jax.shard_map(shards, mesh=mesh, in_specs=in_specs, out_specs=out_specs, check_vma=False)
```

time: 234 us -> 74.8 us (0.32)
  waiting for transfers between devices: 109 us -> 2.06 us
  local copies, waits for them, and re-layouts: 69.5 us -> 9.44 us
  matrix products: 36.3 us -> 0 us
  blocking collectives: 0 us -> 33.5 us
  Pallas kernels: 0 us -> 23.2 us
  between operations: 13.7 us -> 0.08 us
  starting transfers between devices: 0.04 us -> 6.03 us
  other arithmetic: 4.94 us -> 0.08 us
    all_gather x1 -> x0, waiting for transfers between devices: 96.4 us -> none  [shards(): everyone = lax.all_gather(packed, 'section', axis=0, tiled=True)]
    dot_general x8 -> x0, matrix products: 36.3 us -> none  [the longest x2 16.5 us: partial_kv(): return jnp.dot(rows_in, w_kv, preferred_element_type=jnp.float32) * kv_scale]
    all_gather x0 -> x1, blocking collectives: none -> 33.5 us  [shards(): asked = lax.all_gather(asked, 'section', axis=0, tiled=True)]
    slice x6 -> x0, local copies, waits for them, and re-layouts: 25.4 us -> none  [the longest x1 19.1 us: attend(): arrived[:, :, :, 0]]
    pallas_call x0 -> x6, Pallas kernels: none -> 23.2 us  [the longest x1 8.89 us: shards(): pl.pallas_call(functools.partial(project_first, edges=edges), grid_spec=p...]
    unnamed x28 -> x20, local copies, waits for them, and re-layouts: 26.2 us -> 9.44 us
    another operation x1 -> x0, local copies, waits for them, and re-layouts: 14.3 us -> none  [attend(): arrived = arrived.reshape(row_count, arrived.shape[1], kv_heads, 2, HD)]
    reduce_scatter x1 -> x0, waiting for transfers between devices: 12.2 us -> none  [shards(): lax.psum_scatter(partial_terms.astype(jnp.bfloat16), 'tp', scatter_dimens...]
  transfers between devices with their start and end apart: 2 -> 2, of which waited for: 2 -> 1; matrix products, arithmetic and copies ran while one was open for 13% -> 0% of each run, Pallas kernels for 0% -> 13%
where the time goes in v2:
time: 74.8 us; the launch traced here: 74.4 us
  blocking collectives  33.5 us (45%)
  Pallas kernels  23.2 us (31%)
  local copies, waits for them, and re-layouts  9.44 us (13%)
  starting transfers between devices  6.03 us (8%)
  waiting for transfers between devices  2.06 us (3%)
    all_gather x1, blocking collectives, shards(): asked = lax.all_gather(asked, 'section', axis=0, tiled=True)  33.5 us
    unnamed x20, local copies, waits for them, and re-layouts  9.44 us
    pallas_call x1, Pallas kernels, shards(): pl.pallas_call(functools.partial(project_first, edges=edges), grid_spec=p...  8.89 us
    pallas_call x1, Pallas kernels, shards(): pl.pallas_call(functools.partial(project_second, block=all_rows // 2), gr...  6.36 us
    all_to_all x1, starting transfers between devices, shards(): answers = lax.all_to_all(answers, 'section', 0, 0)  5.51 us
    pallas_call x1, Pallas kernels, shards(): pl.pallas_call(merge, in_specs=[SCALARS] + [RESIDENT] * 4, out_specs=RESI...  2.39 us
    pallas_call x1, Pallas kernels, shards(): pl.pallas_call(attend_cache, grid=(row_count // block,), in_specs=[pl.Blo...  2.32 us
    pallas_call x1, Pallas kernels, shards(): pl.pallas_call(functools.partial(attend_arrived, row_count=row_count), in...  2.29 us
  transfers between devices with their start and end apart: 2, of which 1 were waited for; matrix products, arithmetic and copies ran while one was open for 0% of the time, Pallas kernels for 13%

profile of v2, /device:TPU:0, one launch (start us, length us, event | category | flops | bytes accessed | tf_op | source)
XLA Modules:
  0.0 74.4 jit_solution(12034422055880396667)
XLA Ops:
  0.0 0.1 pad_add_fusion.place_ref
  0.1 3.7 %copy-done = bf16[768,6144]{1,0:T(8,128)(2,1)S(1)} copy-done((bf16[768,6144]{1,0:T(8,128)(2,1)S(1)}, bf16[768,6144]{1,0:T(8,128)(2,1)}, u32[]{:S(2)}) %copy-start) | copy-done | bytes 9437208
  3.8 1.4 %copy-done.3 = bf16[128,6144]{1,0:T(8,128)(2,1)S(1)} copy-done((bf16[128,6144]{1,0:T(8,128)(2,1)S(1)}, bf16[128,6144]{1,0:T(8,128)(2,1)}, u32[]{:S(2)}) %copy-start.3) | copy-done | bytes 1572888
  5.2 0.7 copy-done.7
  5.9 8.9 %project_first.1 = (bf16[896,512]{1,0:T(8,128)(2,1)S(1)}, bf16[896,6144]{1,0:T(8,128)(2,1)S(1)}, bf16[6144,512]{1,0:T(8,128)(2,1)S(1)}) custom-call(s32[3]{0:T(128)S(1)} %pad_add_fusion.place_ref, bf16[768,6144]{1,0:T(8,128)(2,1)S(1)} %copy-done, bf16[128,6144]{1,0:T(8,128)(2,1)S(1)} %copy-done.3, bf16[6144,1024]{1,0:T(8,128)(2,1)} %w_ref.1, ...), custom_call_target="tpu_custom_call" | custom-call | tf_op jit(solution)/shard_map/project_first/pallas_call | solution.py:385
  14.8 0.0 copy-start.2
  14.8 0.0 copy-start.6
  14.8 0.5 collective-permute-start
  15.3 6.4 %project_second.1.mine_ref = bf16[896,512]{1,0:T(8,128)(2,1)S(1)} custom-call(s32[3]{0:T(128)S(1)} %pad_add_fusion.place_ref, bf16[896,6144]{1,0:T(8,128)(2,1)S(1)} %get-tuple-element.10.rows_ref, bf16[6144,512]{1,0:T(8,128)(2,1)S(1)} %get-tuple-element.11.w_ref, f32[1,1024]{1,0:T(1,128)S(1)} %bitcast.6), custom_call_target="tpu_custom_call" | custom-call | tf_op jit(solution)/shard_map/project_second/pallas_call | solution.py:415
  21.7 0.0 copy-done.2
  21.7 0.0 copy-done.6
  21.7 0.9 %select_queries.1 = bf16[16,3072]{1,0:T(8,128)(2,1)S(1)} custom-call(s32[3]{0:T(128)S(1)} %pad_add_fusion.place_ref, s32[8,12]{1,0:T(8,128)S(1)} %copy-done.6, bf16[128,3072]{1,0:T(8,128)(2,1)S(1)} %copy-done.2), custom_call_target="tpu_custom_call" | custom-call | tf_op jit(solution)/shard_map/select_queries/pallas_call | solution.py:372
  22.6 33.5 %all_gather.3.asked_ref = bf16[128,3072]{1,0:T(8,128)(2,1)S(1)} all-gather(bf16[16,3072]{1,0:T(8,128)(2,1)S(1)} %select_queries.1), channel_id=1, replica_groups=mesh['groups'=2,'section'=8,'tp'=2] {'section'}, dimensions={0}, use_global_device_ids=true | all-gather | bytes 884736 | tf_op jit(solution)/shard_map/all_gather | solution.py:380
  56.2 0.0 collective-permute-done.other_ref
  56.2 0.0 copy-done.8
  56.2 2.3 %attend_arrived.1 = bf16[8,2,3456]{2,1,0:T(2,128)(2,1)} custom-call(s32[3]{0:T(128)S(1)} %pad_add_fusion.place_ref, s32[8,12]{1,0:T(8,128)S(1)} %copy-done.6, s32[8,12]{1,0:T(8,128)S(1)} %copy-done.8, bf16[896,512]{1,0:T(8,128)(2,1)S(1)} %project_second.1.mine_ref, bf16[896,512]{1,0:T(8,128)(2,1)S(1)} %collective-permute-done.other_ref, ...), custom_call_target="tpu_custom_call" | custom-call | tf_op jit(solution)/shard_map/attend_arrived/pallas_call | solution.py:433
  58.5 5.5 %all-to-all-start = ((bf16[8,2,3456]{2,1,0:T(2,128)(2,1)}), bf16[8,2,3456]{2,1,0:T(2,128)(2,1)S(1)}, u32[]{:S(2)}, u32[]{:S(2)}) async-start(bf16[8,2,3456]{2,1,0:T(2,128)(2,1)} %attend_arrived.1), calls=%async_computation | async-start | bytes 221184 | tf_op jit(solution)/shard_map/all_to_all | solution.py:441
  64.0 0.0 copy-start.1
  64.0 2.2 %copy-done.1 = bf16[128,32,512]{2,1,0:T(8,128)(2,1)S(1)} copy-done((bf16[128,32,512]{2,1,0:T(8,128)(2,1)S(1)}, bf16[128,32,512]{2,1,0:T(8,128)(2,1)}, u32[]{:S(2)}) %copy-start.1) | copy-done | bytes 4194328
  66.2 2.3 %attend_cache.1 = (bf16[128,3072]{1,0:T(8,128)(2,1)S(1)}, f32[128,128]{1,0:T(8,128)S(1)}) custom-call(bf16[128,3072]{1,0:T(8,128)(2,1)S(1)} %copy-done.2, bf16[128,32,512]{2,1,0:T(8,128)(2,1)S(1)} %copy-done.1, s32[1,128]{1,0:T(1,128)S(1)} %bitcast.7, bf16[896,512]{1,0:T(8,128)(2,1)S(1)} %project_second.1.mine_ref, ...), custom_call_target="tpu_custom_call" | custom-call | tf_op jit(solution)/shard_map/attend_cache/pallas_call | solution.py:445
  68.5 0.6 copy-done.4
  69.1 2.1 %all-to-all-done.arrived_ref = bf16[8,2,3456]{2,1,0:T(2,128)(2,1)S(1)} async-done(((bf16[8,2,3456]{2,1,0:T(2,128)(2,1)}), bf16[8,2,3456]{2,1,0:T(2,128)(2,1)S(1)}, u32[]{:S(2)}, u32[]{:S(2)}) %all-to-all-start) | async-done | bytes 110624 | tf_op jit(solution)/shard_map/all_to_all | solution.py:441
  71.2 0.8 %copy-done.5 = f32[128,128]{1,0:T(8,128)S(1)} copy-done((f32[128,128]{1,0:T(8,128)S(1)}, f32[128,128]{1,0:T(8,128)}, u32[]{:S(2)}) %copy-start.5) | copy-done | bytes 65560
  72.0 2.4 %merge.1 = bf16[128,3072]{1,0:T(8,128)(2,1)} custom-call(s32[3]{0:T(128)S(1)} %pad_add_fusion.place_ref, s32[8,12]{1,0:T(8,128)S(1)} %copy-done.6, bf16[8,2,3456]{2,1,0:T(2,128)(2,1)S(1)} %all-to-all-done.arrived_ref, bf16[128,3072]{1,0:T(8,128)(2,1)S(1)} %get-tuple-element.13.cached_ref, f32[128,128]{1,0:T(8,128)S(1)} %copy-done.5), custom_call_target="tpu_custom_call" | custom-call | tf_op jit(solution)/shard_map/merge/pallas_call | solution.py:467
  (8 shorter events, 0.0 us)
Async XLA Ops:
  0.1 3.7 %copy-start = (bf16[768,6144]{1,0:T(8,128)(2,1)S(1)}, bf16[768,6144]{1,0:T(8,128)(2,1)}, u32[]{:S(2)}) copy-start(bf16[768,6144]{1,0:T(8,128)(2,1)} %prompts_ref.1) | copy-start | bytes 28311556
  3.8 1.4 %copy-start.3 = (bf16[128,6144]{1,0:T(8,128)(2,1)S(1)}, bf16[128,6144]{1,0:T(8,128)(2,1)}, u32[]{:S(2)}) copy-start(bf16[128,6144]{1,0:T(8,128)(2,1)} %hidden_ref.1) | copy-start | bytes 4718596
  5.2 0.7 copy-start.7
  14.8 6.9 %copy-start.2 = (bf16[128,3072]{1,0:T(8,128)(2,1)S(1)}, bf16[128,3072]{1,0:T(8,128)(2,1)}, u32[]{:S(2)}) copy-start(bf16[128,3072]{1,0:T(8,128)(2,1)} %queries_ref.3) | copy-start | bytes 2359300
  14.8 6.9 %copy-start.6 = (s32[8,12]{1,0:T(8,128)S(1)}, s32[8,12]{1,0:T(8,128)}, u32[]{:S(2)}) copy-start(s32[8,12]{1,0:T(8,128)} %target_ref.5) | copy-start | bytes 1156
  14.8 41.4 %collective-permute-start = (bf16[896,512]{1,0:T(8,128)(2,1)S(1)}, bf16[896,512]{1,0:T(8,128)(2,1)S(1)}, u32[]{:S(2)}, u32[]{:S(2)}) collective-permute-start(bf16[896,512]{1,0:T(8,128)(2,1)S(1)} %get-tuple-element.12), channel_id=1, source_target_pairs={{0,1},{1,0},{2,3},{3,2},{4,5},{5,4},{6,7},{7,6},{8,9},{9,8},{10,11... | collective-permute-start | bytes 2752520 | tf_op jit(solution)/shard_map/ppermute | solution.py:414
  15.3 40.9 %copy-start.8 = (s32[8,12]{1,0:T(8,128)S(1)}, s32[8,12]{1,0:T(8,128)}, u32[]{:S(2)}) copy-start(s32[8,12]{1,0:T(8,128)} %span_ref.1) | copy-start | bytes 1156
  15.3 48.7 %copy-start.9 = (s32[128]{0:T(128)S(1)}, s32[128]{0:T(128)}, u32[]{:S(2)}) copy-start(s32[128]{0:T(128)} %param.13) | copy-start | bytes 1540
  58.5 12.7 %all-to-all-start = ((bf16[8,2,3456]{2,1,0:T(2,128)(2,1)}), bf16[8,2,3456]{2,1,0:T(2,128)(2,1)S(1)}, u32[]{:S(2)}, u32[]{:S(2)}) async-start(bf16[8,2,3456]{2,1,0:T(2,128)(2,1)} %attend_arrived.1), calls=%async_computation | async-start | bytes 221184 | tf_op jit(solution)/shard_map/all_to_all | solution.py:441
  64.0 2.2 %copy-start.1 = (bf16[128,32,512]{2,1,0:T(8,128)(2,1)S(1)}, bf16[128,32,512]{2,1,0:T(8,128)(2,1)}, u32[]{:S(2)}) copy-start(bf16[128,32,512]{2,1,0:T(8,128)(2,1)} %cache_ref.1) | copy-start | bytes 12582916
  68.5 0.6 copy-start.4
  71.2 0.8 %copy-start.5 = (f32[128,128]{1,0:T(8,128)S(1)}, f32[128,128]{1,0:T(8,128)}, u32[]{:S(2)}) copy-start(f32[128,128]{1,0:T(8,128)} %copy-done.4) | copy-start | bytes 196612

commit v3 on v2

v3 whole, which is shorter than its diff:
```python
import functools
import math

import jax
import jax.numpy as jnp
from jax import lax
from jax.experimental import pallas as pl
from jax.experimental.pallas import tpu as pltpu
from jax.sharding import PartitionSpec as P

HD = 128
CAP = 2
STATS = 128
MASKED = -1e30
LOG2_SCALE = HD ** (-0.5) * math.log2(math.e)
F32 = jnp.float32
BF16 = jnp.bfloat16
TRANSPOSED = (((0,), (0,)), ((), ()))


def iota(shape, dim):
    return lax.broadcasted_iota(jnp.int32, shape, dim)


def one_hot(shape, dim, index):
    return (iota(shape, dim) == index).astype(F32).astype(BF16)


def select_queries(target_ref, queries_ref, pick_ref, *asked_refs):
    sections, requests = target_ref.shape
    row_count = queries_ref.shape[0]
    slots = sections * CAP
    position = lax.axis_index("section")
    slot_id = iota((slots, requests), 0)
    table = jnp.zeros((slots, requests), jnp.int32)
    for k in range(sections):
        row = target_ref[pl.ds(lax.rem(position + k, sections), 1), :]
        table = jnp.where((slot_id >= k * CAP) & (slot_id < (k + 1) * CAP), row, table)
    local = table - position * row_count
    here = (local >= 0) & (local < row_count)
    square = (requests, requests)
    earlier = jnp.dot(
        here.astype(F32).astype(BF16),
        (iota(square, 0) < iota(square, 1)).astype(F32).astype(BF16),
        preferred_element_type=F32,
    )
    chosen = here & (earlier == lax.rem(slot_id, CAP).astype(F32))
    row = jnp.max(jnp.where(chosen, local.astype(F32), -1.0), axis=1, keepdims=True)
    pick = one_hot((slots, row_count), 1, row.astype(jnp.int32))
    pick_ref[...] = pick
    asked = jnp.dot(pick, queries_ref[...], preferred_element_type=F32).astype(BF16)
    for k in range(sections):
        asked_refs[k][...] = asked[k * CAP : (k + 1) * CAP]


def project_first(
    prompts_ref,
    hidden_ref,
    w_ref,
    scale_ref,
    after_ref,
    out_ref,
    rows_ref,
    w_mine_ref,
    w_theirs_ref,
    total_ref,
    scale_here_ref,
    row_sems,
    hidden_sems,
    theirs_sems,
    mine_sems,
    scale_sem,
    *,
    edges,
):
    prompt_rows = prompts_ref.shape[0]
    width = out_ref.shape[1]
    tp = lax.axis_index("tp")
    theirs = pl.ds(pl.multiple_of((1 - tp) * width, width), width)
    mine = pl.ds(pl.multiple_of(tp * width, width), width)
    chunks = [slice(a, b) for a, b in zip(edges[:-1], edges[1:])]
    waits = []
    for c, at in enumerate(chunks):
        copies = [
            pltpu.make_async_copy(
                w_ref.at[at, theirs], w_theirs_ref.at[at, :], theirs_sems.at[c]
            ),
            pltpu.make_async_copy(
                prompts_ref.at[:, at], rows_ref.at[:prompt_rows, at], row_sems.at[c]
            ),
            pltpu.make_async_copy(
                hidden_ref.at[:, at], rows_ref.at[prompt_rows:, at], hidden_sems.at[c]
            ),
        ]
        for copy in copies:
            copy.start()
        waits.append(copies)
    later = [
        pltpu.make_async_copy(w_ref.at[at, mine], w_mine_ref.at[at, :], mine_sems.at[c])
        for c, at in enumerate(chunks)
    ]
    later.append(pltpu.make_async_copy(scale_ref.at[:, theirs], scale_here_ref, scale_sem))
    for copy in later:
        copy.start()
    for c, at in enumerate(chunks):
        for copy in waits[c]:
            copy.wait()
        part = jnp.dot(rows_ref[:, at], w_theirs_ref[at, :], preferred_element_type=F32)
        if c == 0:
            total_ref[...] = part
        elif c < len(chunks) - 1:
            total_ref[...] += part
        else:
            later[-1].wait()
            out_ref[...] = ((total_ref[...] + part) * scale_here_ref[...]).astype(BF16)
    for copy in later[:-1]:
        copy.wait()


def project_second(
    rows_ref,
    w_ref,
    scale_ref,
    cache_ref,
    queries_ref,
    out_ref,
    cache_here_ref,
    queries_here_ref,
    scale_here_ref,
    scale_sem,
    cache_sem,
    queries_sem,
    *,
    block,
):
    width = out_ref.shape[1]
    mine = pl.ds(pl.multiple_of(lax.axis_index("tp") * width, width), width)
    copies = [
        pltpu.make_async_copy(scale_ref.at[:, mine], scale_here_ref, scale_sem),
        pltpu.make_async_copy(queries_ref, queries_here_ref, queries_sem),
        pltpu.make_async_copy(cache_ref, cache_here_ref, cache_sem),
    ]
    for copy in copies:
        copy.start()
    for m in range(0, rows_ref.shape[0], block):
        at = slice(m, m + block)
        total = jnp.dot(rows_ref[at, :], w_ref[...], preferred_element_type=F32)
        if m == 0:
            copies[0].wait()
        out_ref[at, :] = (total * scale_here_ref[...]).astype(BF16)
    for copy in copies[1:]:
        copy.wait()


def split_bf16(x):
    high = x.astype(BF16).astype(F32)
    middle = (x - high).astype(BF16).astype(F32)
    return high, middle, (x - high - middle).astype(BF16).astype(F32)


def request_slots(target_ref, span_ref, row_count, padded):
    sections, requests = target_ref.shape
    position = lax.axis_index("section")
    target = target_ref[pl.ds(position, 1), :].astype(F32)
    span = span_ref[pl.ds(position, 1), :].astype(F32)
    diagonal = iota((padded, requests), 0) == iota((padded, requests), 1)
    target_col = jnp.sum(jnp.where(diagonal, target, 0.0), axis=1, keepdims=True)
    span_col = jnp.sum(jnp.where(diagonal, span, 0.0), axis=1, keepdims=True)
    section_row = jnp.zeros_like(target)
    section_col = jnp.zeros_like(target_col)
    for s in range(1, sections):
        section_row = section_row + (target >= s * row_count).astype(F32)
        section_col = section_col + (target_col >= s * row_count).astype(F32)
    before = (section_row == section_col) & (
        iota((padded, requests), 1) < iota((padded, requests), 0)
    )
    rank_col = jnp.sum(before.astype(F32), axis=1, keepdims=True).astype(jnp.int32)
    back = position - section_col.astype(jnp.int32)
    back = jnp.where(back < 0, back + sections, back)
    real = iota((padded, 1), 0) < requests
    return jnp.where(real, back * CAP + rank_col, -1), span_col.astype(jnp.int32)


def attend_arrived(target_ref, span_ref, mine_ref, other_ref, *refs, row_count):
    sections, requests = target_ref.shape
    asked_refs, out_refs = refs[:sections], refs[sections:]
    slots = sections * CAP
    padded = -(-requests // 16) * 16
    prompt_rows = mine_ref.shape[0] - row_count
    span_rows = prompt_rows // requests
    kv_heads = mine_ref.shape[1] // (2 * HD)
    group = asked_refs[0].shape[1] // (kv_heads * HD)
    slot_col, span_col = request_slots(target_ref, span_ref, row_count, padded)
    slot_of = one_hot((padded, slots), 1, slot_col)
    key = iota((padded, prompt_rows), 1) - iota((padded, prompt_rows), 0) * span_rows
    bias = jnp.where((key >= 0) & (key < span_col), 0.0, MASKED)
    asked = jnp.concatenate([ref[...].astype(F32) for ref in asked_refs], axis=0).astype(BF16)
    rows = jnp.dot(slot_of, asked, preferred_element_type=F32).astype(BF16)
    kv = (
        mine_ref[:prompt_rows, :].astype(F32) + other_ref[:prompt_rows, :].astype(F32)
    ).astype(BF16)
    scores = []
    for h in range(kv_heads):
        stacked = jnp.concatenate(
            [rows[:, (h * group + i) * HD : (h * group + i + 1) * HD] for i in range(group)],
            axis=0,
        )
        keys = kv[:, h * 2 * HD : (h * 2 + 1) * HD]
        scores.append(
            lax.dot_general(
                stacked, keys, (((1,), (1,)), ((), ())), preferred_element_type=F32
            )
        )
    scores = [
        x.reshape(group, padded, prompt_rows) * LOG2_SCALE + bias[None] for x in scores
    ]
    largest = [jnp.max(x, axis=2, keepdims=True) for x in scores]
    weights = [jnp.exp2(x - y) for x, y in zip(scores, largest)]
    totals = [jnp.sum(x, axis=2, keepdims=True) for x in weights]
    lane = iota((padded, STATS), 1)
    lse = jnp.zeros((padded, STATS), F32)
    pieces = []
    for h in range(kv_heads):
        values = jnp.dot(
            weights[h].reshape(group * padded, prompt_rows).astype(BF16),
            kv[:, (h * 2 + 1) * HD : (h * 2 + 2) * HD],
            preferred_element_type=F32,
        ).reshape(group, padded, HD)
        values = values / totals[h]
        head_lse = largest[h] + jnp.log2(totals[h])
        for i in range(group):
            pieces.append(values[i])
            lse = jnp.where(lane == h * group + i, head_lse[i], lse)
    result = jnp.concatenate(pieces + list(split_bf16(lse)), axis=1).astype(BF16)
    answers = lax.dot_general(slot_of, result, TRANSPOSED, preferred_element_type=F32).astype(BF16)
    for k in range(sections):
        out_refs[k][...] = answers[k * CAP : (k + 1) * CAP]


def attend_cache(
    queries_ref,
    cache_ref,
    len_ref,
    mine_ref,
    other_ref,
    pick_ref,
    after_ref,
    out_ref,
    slot_out_ref,
    slot_lse_ref,
    *,
    block_rows,
):
    row_count, cache_rows, width = cache_ref.shape
    kv_heads = width // (2 * HD)
    group = queries_ref.shape[1] // (kv_heads * HD)
    unit = 8
    keys_of = unit * cache_rows
    first_row = pl.multiple_of(pl.program_id(0) * block_rows, block_rows)
    block = pl.ds(first_row, block_rows)
    own_block = pl.ds(first_row + (mine_ref.shape[0] - row_count), block_rows)
    queries = queries_ref[block, :].astype(F32)
    own = mine_ref[own_block, :].astype(F32) + other_ref[own_block, :].astype(F32)
    own = own.astype(BF16).astype(F32)
    key = iota((unit, keys_of), 1) - iota((unit, keys_of), 0) * cache_rows
    lengths = len_ref[...].astype(F32)
    lane = iota((unit, STATS), 1)
    ones = jnp.ones((keys_of, HD), BF16)
    units = range(block_rows // unit)

    def rows_of(u):
        return pl.ds(first_row + u * unit, unit)

    pairs = [(u, h) for u in units for h in range(kv_heads)]
    bias = []
    for u in units:
        row = iota((unit, row_count), 0) + (first_row + u * unit)
        length = jnp.sum(
            jnp.where(iota((unit, row_count), 1) == row, lengths, 0.0), axis=1, keepdims=True
        ).astype(jnp.int32)
        bias.append(jnp.where((key >= 0) & (key < length), 0.0, MASKED))
    q, scores, own_scores = [], [], []
    for u, h in pairs:
        at = slice(u * unit, (u + 1) * unit)
        q.append(
            jnp.stack(
                [
                    queries[at, (h * group + i) * HD : (h * group + i + 1) * HD]
                    for i in range(group)
                ],
                axis=0,
            )
        )
        keys = cache_ref[rows_of(u), :, h * 2 * HD : (h * 2 + 1) * HD].reshape(keys_of, HD)
        scores.append(
            lax.dot_general(
                q[-1].reshape(group * unit, HD).astype(BF16),
                keys,
                (((1,), (1,)), ((), ())),
                preferred_element_type=F32,
            ).reshape(group, unit, keys_of)
        )
    for n, (u, h) in enumerate(pairs):
        at = slice(u * unit, (u + 1) * unit)
        own_key = own[at, h * 2 * HD : (h * 2 + 1) * HD]
        own_scores.append(jnp.sum(q[n] * own_key[None], axis=2, keepdims=True) * LOG2_SCALE)
    scores = [scores[n] * LOG2_SCALE + bias[u][None] for n, (u, h) in enumerate(pairs)]
    largest = [
        jnp.maximum(jnp.max(x, axis=2, keepdims=True), y) for x, y in zip(scores, own_scores)
    ]
    weights = [jnp.exp2(x - y).astype(BF16) for x, y in zip(scores, largest)]
    own_weights = [jnp.exp2(x - y) for x, y in zip(own_scores, largest)]
    sums = []
    for n, (u, h) in enumerate(pairs):
        at = slice(u * unit, (u + 1) * unit)
        values = cache_ref[rows_of(u), :, (h * 2 + 1) * HD : (h * 2 + 2) * HD].reshape(keys_of, HD)
        sums.append(
            jnp.dot(
                weights[n].reshape(group * unit, keys_of),
                jnp.concatenate([values, ones], axis=1),
                preferred_element_type=F32,
            ).reshape(group, unit, 2 * HD)
        )
    pieces = [[] for _ in units]
    stats = [jnp.zeros((unit, STATS), F32) for _ in units]
    for n, (u, h) in enumerate(pairs):
        at = slice(u * unit, (u + 1) * unit)
        own_value = own[at, (h * 2 + 1) * HD : (h * 2 + 2) * HD]
        total = sums[n][:, :, HD:] + own_weights[n]
        result = (sums[n][:, :, :HD] + own_weights[n] * own_value[None]) / total
        lse = largest[n] + jnp.log2(total)
        for i in range(group):
            pieces[u].append(result[i])
            stats[u] = jnp.where(lane == h * group + i, lse[i], stats[u])
    out = jnp.concatenate([jnp.concatenate(x, axis=1) for x in pieces], axis=0).astype(BF16)
    out_ref[block, :] = out
    pick = pick_ref[...]
    here = iota((row_count, block_rows), 0) == iota((row_count, block_rows), 1) + first_row
    pick = jnp.dot(pick, here.astype(F32).astype(BF16), preferred_element_type=F32).astype(BF16)
    slot_out = jnp.dot(pick, out, preferred_element_type=F32)
    lse = jnp.concatenate(stats, axis=0)
    slot_lse = sum(
        jnp.dot(pick, part.astype(BF16), preferred_element_type=F32) for part in split_bf16(lse)
    )

    @pl.when(pl.program_id(0) == 0)
    def _():
        slot_out_ref[...] = slot_out
        slot_lse_ref[...] = slot_lse

    @pl.when(pl.program_id(0) > 0)
    def _():
        slot_out_ref[...] += slot_out
        slot_lse_ref[...] += slot_lse


def merge(pick_ref, cached_ref, slot_out_ref, slot_lse_ref, *refs):
    arrived_refs, out_ref = refs[:-1], refs[-1]
    width = cached_ref.shape[1]
    pick = pick_ref[...]
    arrived = jnp.concatenate([ref[...].astype(F32) for ref in arrived_refs], axis=0)
    arrived_lse = (
        arrived[:, width : width + STATS]
        + arrived[:, width + STATS : width + 2 * STATS]
        + arrived[:, width + 2 * STATS :]
    )
    cached_lse = slot_lse_ref[...]
    largest = jnp.maximum(cached_lse, arrived_lse)
    cached_weight = jnp.exp2(cached_lse - largest)
    arrived_weight = jnp.exp2(arrived_lse - largest)
    total = cached_weight + arrived_weight
    cached_weight = cached_weight / total
    arrived_weight = arrived_weight / total
    has = lax.dot_general(
        pick, jnp.ones((pick.shape[0], HD), BF16), TRANSPOSED, preferred_element_type=F32
    )
    for i in range(width // HD):
        at = slice(i * HD, (i + 1) * HD)
        merged = (
            slot_out_ref[:, at] * cached_weight[:, i : i + 1]
            + arrived[:, at] * arrived_weight[:, i : i + 1]
        )
        placed = lax.dot_general(
            pick, merged.astype(BF16), TRANSPOSED, preferred_element_type=F32
        )
        out_ref[:, at] = jnp.where(has > 0.5, placed, cached_ref[:, at].astype(F32)).astype(BF16)


def compiler_params(megabytes):
    return pltpu.CompilerParams(vmem_limit_bytes=megabytes * 1024 * 1024)


RESIDENT = pl.BlockSpec(memory_space=pltpu.VMEM)
REMAINS = pl.BlockSpec(memory_space=pl.ANY)


def in_vmem(x):
    return pltpu.with_memory_space_constraint(x, pltpu.VMEM)


def in_hbm(x):
    return pltpu.with_memory_space_constraint(x, pltpu.HBM)


def shards(
    prompts, decode_hidden, queries, kv_cache, cache_len, span_len, target_row, w_kv, kv_scale
):
    row_count = decode_hidden.shape[0]
    prompt_rows, features = prompts.shape
    sections = lax.axis_size("section")
    local_width = kv_cache.shape[2]
    query_width = queries.shape[1]
    slots = sections * CAP
    all_rows = prompt_rows + row_count
    scale = kv_scale.reshape(1, -1)
    lengths = cache_len.reshape(1, -1)

    def moved(arrays, sign):
        return [arrays[0]] + [
            lax.ppermute(
                arrays[k], "section", [(i, (i + sign * k) % sections) for i in range(sections)]
            )
            for k in range(1, sections)
        ]

    pick, *asked = pl.pallas_call(
        select_queries,
        in_specs=[RESIDENT, RESIDENT],
        out_specs=[RESIDENT] * (1 + sections),
        out_shape=[pltpu.VMEM((slots, row_count), BF16)]
        + [pltpu.VMEM((CAP, query_width), BF16)] * sections,
        compiler_params=compiler_params(16),
        name="select_queries",
    )(in_hbm(target_row), in_hbm(queries))
    asked = moved(asked, 1)

    depth = 512
    edges = tuple(range(0, features + 1, depth))
    count = len(edges) - 1
    theirs, rows, w_mine = pl.pallas_call(
        functools.partial(project_first, edges=edges),
        in_specs=[REMAINS] * 5,
        out_specs=[RESIDENT, RESIDENT, RESIDENT],
        scratch_shapes=[
            pltpu.VMEM((features, local_width), BF16),
            pltpu.VMEM((all_rows, local_width), F32),
            pltpu.VMEM((1, local_width), F32),
            pltpu.SemaphoreType.DMA((count,)),
            pltpu.SemaphoreType.DMA((count,)),
            pltpu.SemaphoreType.DMA((count,)),
            pltpu.SemaphoreType.DMA((count,)),
            pltpu.SemaphoreType.DMA(()),
        ],
        out_shape=[
            pltpu.VMEM((all_rows, local_width), BF16),
            pltpu.VMEM((all_rows, features), BF16),
            pltpu.VMEM((features, local_width), BF16),
        ],
        compiler_params=compiler_params(16),
        name="project_first",
    )(in_hbm(prompts), in_hbm(decode_hidden), in_hbm(w_kv), in_hbm(scale), in_vmem(pick))
    other = lax.ppermute(theirs, "tp", [(0, 1), (1, 0)])
    mine, cache_here, queries_here = pl.pallas_call(
        functools.partial(project_second, block=all_rows // 2),
        in_specs=[RESIDENT, RESIDENT, REMAINS, REMAINS, REMAINS],
        out_specs=[RESIDENT, RESIDENT, RESIDENT],
        scratch_shapes=[
            pltpu.VMEM((1, local_width), F32),
            pltpu.SemaphoreType.DMA(()),
            pltpu.SemaphoreType.DMA(()),
            pltpu.SemaphoreType.DMA(()),
        ],
        out_shape=[
            pltpu.VMEM((all_rows, local_width), BF16),
            pltpu.VMEM(kv_cache.shape, BF16),
            pltpu.VMEM(queries.shape, BF16),
        ],
        compiler_params=compiler_params(16),
        name="project_second",
    )(in_vmem(rows), in_vmem(w_mine), in_hbm(scale), in_hbm(kv_cache), in_hbm(queries))

    answer_width = query_width + 3 * STATS
    answers = pl.pallas_call(
        functools.partial(attend_arrived, row_count=row_count),
        in_specs=[RESIDENT] * (4 + sections),
        out_specs=[RESIDENT] * sections,
        out_shape=[pltpu.VMEM((CAP, answer_width), BF16)] * sections,
        compiler_params=compiler_params(24),
        name="attend_arrived",
    )(in_hbm(target_row), in_hbm(span_len), in_vmem(mine), in_vmem(other), *map(in_vmem, asked))
    after = answers[0]
    answers = moved(answers, -1)

    block = 32
    cached, slot_out, slot_lse = pl.pallas_call(
        functools.partial(attend_cache, block_rows=block),
        grid=(row_count // block,),
        in_specs=[RESIDENT] * 6 + [REMAINS],
        out_specs=[RESIDENT] * 3,
        out_shape=[
            pltpu.VMEM((row_count, query_width), BF16),
            pltpu.VMEM((slots, query_width), F32),
            pltpu.VMEM((slots, STATS), F32),
        ],
        compiler_params=compiler_params(24),
        name="attend_cache",
    )(
        in_vmem(queries_here),
        in_vmem(cache_here),
        in_hbm(lengths),
        in_vmem(mine),
        in_vmem(other),
        in_vmem(pick),
        in_vmem(after),
    )

    return pl.pallas_call(
        merge,
        in_specs=[RESIDENT] * (4 + sections),
        out_specs=RESIDENT,
        out_shape=jax.ShapeDtypeStruct((row_count, query_width), BF16),
        compiler_params=compiler_params(24),
        name="merge",
    )(*map(in_vmem, (pick, cached, slot_out, slot_lse, *answers)))


def solution(mesh):
    in_specs = (
        P(("groups", "section"), "tp"),
        P(("groups", "section"), "tp"),
        P(("groups", "section"), "tp"),
        P(("groups", "section"), None, "tp"),
        P(("groups", "section")),
        P("groups", None),
        P("groups", None),
        P("tp", None),
        P(),
    )
    out_specs = P(("groups", "section"), "tp")
    return jax.shard_map(shards, mesh=mesh, in_specs=in_specs, out_specs=out_specs, check_vma=False)
```

time: 74.8 us -> 49.7 us (0.66)
  blocking collectives: 33.5 us -> 0 us
  starting transfers between devices: 6.03 us -> 22.1 us
  local copies, waits for them, and re-layouts: 9.44 us -> 0 us
  Pallas kernels: 23.2 us -> 24.6 us
    all_gather x1 -> x0, blocking collectives: 33.5 us -> none  [shards(): asked = lax.all_gather(asked, 'section', axis=0, tiled=True)]
    ppermute x0 -> x14, starting transfers between devices: none -> 21.6 us  [moved(): lax.ppermute(arrays[k], 'section', [(i, (i + sign * k) % sections) for i...]
    unnamed x20 -> x0, local copies, waits for them, and re-layouts: 9.44 us -> none
    all_to_all x1 -> x0, starting transfers between devices: 5.51 us -> none  [shards(): answers = lax.all_to_all(answers, 'section', 0, 0)]
    ppermute x0 -> x14, waiting for transfers between devices: none -> 2.62 us  [moved(): lax.ppermute(arrays[k], 'section', [(i, (i + sign * k) % sections) for i...]
    all_to_all x1 -> x0, waiting for transfers between devices: 2.06 us -> none  [shards(): answers = lax.all_to_all(answers, 'section', 0, 0)]
    pallas_call x5, Pallas kernels: 20.9 us -> 22.8 us  [the longest x1 9.92 us: shards(): pl.pallas_call(functools.partial(project_first, edges=edges), in_specs=[R...]
  transfers between devices with their start and end apart: 2 -> 15, of which waited for: 1 -> 2; matrix products, arithmetic and copies ran while one was open for 0% -> 0% of each run, Pallas kernels for 13% -> 20%
where the time goes in v3:
time: 49.7 us; the launch traced here: 49.4 us
  Pallas kernels  24.6 us (49%)
  starting transfers between devices  22.1 us (44%)
  waiting for transfers between devices  2.63 us (5%)
    ppermute x14, starting transfers between devices, moved(): lax.ppermute(arrays[k], 'section', [(i, (i + sign * k) % sections) for i...  21.6 us
    pallas_call x1, Pallas kernels, shards(): pl.pallas_call(functools.partial(project_first, edges=edges), in_specs=[R...  9.92 us
    pallas_call x1, Pallas kernels, shards(): pl.pallas_call(functools.partial(project_second, block=all_rows // 2), in...  6.27 us
    pallas_call x1, Pallas kernels, shards(): pl.pallas_call(functools.partial(attend_cache, block_rows=block), grid=(r...  3.63 us
    ppermute x14, waiting for transfers between devices, moved(): lax.ppermute(arrays[k], 'section', [(i, (i + sign * k) % sections) for i...  2.62 us
    pallas_call x1, Pallas kernels, shards(): pl.pallas_call(functools.partial(attend_arrived, row_count=row_count), in...  1.86 us
    pallas_call x1, Pallas kernels, shards(): pl.pallas_call(select_queries, in_specs=[RESIDENT, RESIDENT], out_specs=[...  1.56 us
    pallas_call x1, Pallas kernels, shards(): pl.pallas_call(merge, in_specs=[RESIDENT] * (4 + sections), out_specs=RES...  1.37 us
  transfers between devices with their start and end apart: 15, of which 2 were waited for; matrix products, arithmetic and copies ran while one was open for 0% of the time, Pallas kernels for 20%

profile of v3, /device:TPU:0, one launch (start us, length us, event | category | flops | bytes accessed | tf_op | source)
XLA Modules:
  0.0 49.4 jit_solution(6898132490066866409)
XLA Ops:
  0.0 1.6 %select_queries.1 = (bf16[16,128]{1,0:T(8,128)(2,1)S(1)}, bf16[2,3072]{1,0:T(2,128)(2,1)S(1)}, bf16[2,3072]{1,0:T(2,128)(2,1)S(1)}, bf16[2,3072]{1,0:T(2,128)(2,...) custom-call(s32[8,12]{1,0:T(8,128)} %target_ref.3, ...), custom_call_target="tpu_custom_call" | custom-call | tf_op jit(solution)/shard_map/select_queries/pallas_call | solution.py:426
  1.6 9.9 %project_first.1 = (bf16[896,512]{1,0:T(8,128)(2,1)S(1)}, bf16[896,6144]{1,0:T(8,128)(2,1)S(1)}, bf16[6144,512]{1,0:T(8,128)(2,1)S(1)}) custom-call(bf16[768,6144]{1,0:T(8,128)(2,1)} %prompts_ref.1, bf16[128,6144]{1,0:T(8,128)(2,1)} %hidden_ref.1, bf16[6144,1024]{1,0:T(8,128)(2,1)} %w_ref.1, f32[1,1024]{1,0:T(1,128)} %bitcast.2, ...), custom_call_target="tpu_custom_call" | custom-call | tf_op jit(solution)/shard_map/project_first/pallas_call | solution.py:440
  11.5 0.5 %collective-permute-start = (bf16[896,512]{1,0:T(8,128)(2,1)S(1)}, bf16[896,512]{1,0:T(8,128)(2,1)S(1)}, u32[]{:S(2)}, u32[]{:S(2)}) collective-permute-start(bf16[896,512]{1,0:T(8,128)(2,1)S(1)} %get-tuple-element.37), channel_id=1, source_target_pairs={{0,1},{1,0},{2,3},{3,2},{4,5},{5,4},{6,7},{7,6},{8,9},{9,8},{10,11... | collective-permute-start | bytes 2752520 | tf_op jit(solution)/shard_map/ppermute | solution.py:462
  12.0 2.6 %collective-permute-start.1 = (bf16[2,3072]{1,0:T(2,128)(2,1)S(1)}, bf16[2,3072]{1,0:T(2,128)(2,1)S(1)}, u32[]{:S(2)}, u32[]{:S(2)}) collective-permute-start(bf16[2,3072]{1,0:T(2,128)(2,1)S(1)} %get-tuple-element.39), channel_id=1, source_target_pairs={{0,2},{2,4},{4,6},{6,8},{8,10},{10,12},{12,14},{14,0},{1,3},{3,5},... | collective-permute-start | bytes 36872 | tf_op jit(solution)/shard_map/ppermute | solution.py:420
  14.6 1.6 %collective-permute-start.2 = (bf16[2,3072]{1,0:T(2,128)(2,1)S(1)}, bf16[2,3072]{1,0:T(2,128)(2,1)S(1)}, u32[]{:S(2)}, u32[]{:S(2)}) collective-permute-start(bf16[2,3072]{1,0:T(2,128)(2,1)S(1)} %get-tuple-element.40), channel_id=1, source_target_pairs={{0,4},{2,6},{4,8},{6,10},{8,12},{10,14},{12,0},{14,2},{1,5},{3,7},... | collective-permute-start | bytes 36872 | tf_op jit(solution)/shard_map/ppermute | solution.py:420
  16.2 2.5 %collective-permute-start.3 = (bf16[2,3072]{1,0:T(2,128)(2,1)S(1)}, bf16[2,3072]{1,0:T(2,128)(2,1)S(1)}, u32[]{:S(2)}, u32[]{:S(2)}) collective-permute-start(bf16[2,3072]{1,0:T(2,128)(2,1)S(1)} %get-tuple-element.41), channel_id=1, source_target_pairs={{0,6},{2,8},{4,10},{6,12},{8,14},{10,0},{12,2},{14,4},{1,7},{3,9},... | collective-permute-start | bytes 36872 | tf_op jit(solution)/shard_map/ppermute | solution.py:420
  18.7 1.2 %collective-permute-start.4 = (bf16[2,3072]{1,0:T(2,128)(2,1)S(1)}, bf16[2,3072]{1,0:T(2,128)(2,1)S(1)}, u32[]{:S(2)}, u32[]{:S(2)}) collective-permute-start(bf16[2,3072]{1,0:T(2,128)(2,1)S(1)} %get-tuple-element.42), channel_id=1, source_target_pairs={{0,8},{2,10},{4,12},{6,14},{8,0},{10,2},{12,4},{14,6},{1,9},{3,11}... | collective-permute-start | bytes 36872 | tf_op jit(solution)/shard_map/ppermute | solution.py:420
  19.9 0.0 collective-permute-done.1.refs_1_
  19.9 2.6 %collective-permute-start.5 = (bf16[2,3072]{1,0:T(2,128)(2,1)S(1)}, bf16[2,3072]{1,0:T(2,128)(2,1)S(1)}, u32[]{:S(2)}, u32[]{:S(2)}) collective-permute-start(bf16[2,3072]{1,0:T(2,128)(2,1)S(1)} %get-tuple-element.43), channel_id=1, source_target_pairs={{0,10},{2,12},{4,14},{6,0},{8,2},{10,4},{12,6},{14,8},{1,11},{3,13... | collective-permute-start | bytes 36872 | tf_op jit(solution)/shard_map/ppermute | solution.py:420
  22.6 1.4 %collective-permute-start.6 = (bf16[2,3072]{1,0:T(2,128)(2,1)S(1)}, bf16[2,3072]{1,0:T(2,128)(2,1)S(1)}, u32[]{:S(2)}, u32[]{:S(2)}) collective-permute-start(bf16[2,3072]{1,0:T(2,128)(2,1)S(1)} %get-tuple-element.44), channel_id=1, source_target_pairs={{0,12},{2,14},{4,0},{6,2},{8,4},{10,6},{12,8},{14,10},{1,13},{3,15... | collective-permute-start | bytes 36872 | tf_op jit(solution)/shard_map/ppermute | solution.py:420
  23.9 1.4 %collective-permute-start.7 = (bf16[2,3072]{1,0:T(2,128)(2,1)S(1)}, bf16[2,3072]{1,0:T(2,128)(2,1)S(1)}, u32[]{:S(2)}, u32[]{:S(2)}) collective-permute-start(bf16[2,3072]{1,0:T(2,128)(2,1)S(1)} %get-tuple-element.45), channel_id=1, source_target_pairs={{0,14},{2,0},{4,2},{6,4},{8,6},{10,8},{12,10},{14,12},{1,15},{3,1}... | collective-permute-start | bytes 36872 | tf_op jit(solution)/shard_map/ppermute | solution.py:420
  25.3 6.3 %project_second.1 = (bf16[896,512]{1,0:T(8,128)(2,1)S(1)}, bf16[128,32,512]{2,1,0:T(8,128)(2,1)S(1)}, bf16[128,3072]{1,0:T(8,128)(2,1)S(1)}) custom-call(bf16[896,6144]{1,0:T(8,128)(2,1)S(1)} %get-tuple-element.32.rows_ref, bf16[6144,512]{1,0:T(8,128)(2,1)S(1)} %get-tuple-element.33.w_ref, f32[1,1024]{1,0:T(1,128)} %bitcast.3, ...), custom_call_target="tpu_custom_call" | custom-call | tf_op jit(solution)/shard_map/project_second/pallas_call | solution.py:463
  31.7 1.9 %attend_arrived.1 = (bf16[2,3456]{1,0:T(2,128)(2,1)S(1)}, bf16[2,3456]{1,0:T(2,128)(2,1)S(1)}, bf16[2,3456]{1,0:T(2,128)(2,1)S(1)}, bf16[2,3456]{1,0:T(2,128)(2,...) custom-call(s32[8,12]{1,0:T(8,128)} %target_ref.3, ...), custom_call_target="tpu_custom_call" | custom-call | tf_op jit(solution)/shard_map/attend_arrived/pallas_call | solution.py:483
  33.5 0.6 %collective-permute-start.8 = (bf16[2,3456]{1,0:T(2,128)(2,1)S(1)}, bf16[2,3456]{1,0:T(2,128)(2,1)S(1)}, u32[]{:S(2)}, u32[]{:S(2)}) collective-permute-start(bf16[2,3456]{1,0:T(2,128)(2,1)S(1)} %get-tuple-element.50), channel_id=1, source_target_pairs={{0,14},{2,0},{4,2},{6,4},{8,6},{10,8},{12,10},{14,12},{1,15},{3,1}... | collective-permute-start | bytes 41480 | tf_op jit(solution)/shard_map/ppermute | solution.py:420
  34.1 1.3 %collective-permute-start.9 = (bf16[2,3456]{1,0:T(2,128)(2,1)S(1)}, bf16[2,3456]{1,0:T(2,128)(2,1)S(1)}, u32[]{:S(2)}, u32[]{:S(2)}) collective-permute-start(bf16[2,3456]{1,0:T(2,128)(2,1)S(1)} %get-tuple-element.51), channel_id=1, source_target_pairs={{0,12},{2,14},{4,0},{6,2},{8,4},{10,6},{12,8},{14,10},{1,13},{3,15... | collective-permute-start | bytes 41480 | tf_op jit(solution)/shard_map/ppermute | solution.py:420
  35.5 1.7 %collective-permute-start.10 = (bf16[2,3456]{1,0:T(2,128)(2,1)S(1)}, bf16[2,3456]{1,0:T(2,128)(2,1)S(1)}, u32[]{:S(2)}, u32[]{:S(2)}) collective-permute-start(bf16[2,3456]{1,0:T(2,128)(2,1)S(1)} %get-tuple-element.52), channel_id=1, source_target_pairs={{0,10},{2,12},{4,14},{6,0},{8,2},{10,4},{12,6},{14,8},{1,11},{3,13... | collective-permute-start | bytes 41480 | tf_op jit(solution)/shard_map/ppermute | solution.py:420
  37.2 1.2 %collective-permute-start.11 = (bf16[2,3456]{1,0:T(2,128)(2,1)S(1)}, bf16[2,3456]{1,0:T(2,128)(2,1)S(1)}, u32[]{:S(2)}, u32[]{:S(2)}) collective-permute-start(bf16[2,3456]{1,0:T(2,128)(2,1)S(1)} %get-tuple-element.53), channel_id=1, source_target_pairs={{0,8},{2,10},{4,12},{6,14},{8,0},{10,2},{12,4},{14,6},{1,9},{3,11}... | collective-permute-start | bytes 41480 | tf_op jit(solution)/shard_map/ppermute | solution.py:420
  38.4 1.6 %collective-permute-start.12 = (bf16[2,3456]{1,0:T(2,128)(2,1)S(1)}, bf16[2,3456]{1,0:T(2,128)(2,1)S(1)}, u32[]{:S(2)}, u32[]{:S(2)}) collective-permute-start(bf16[2,3456]{1,0:T(2,128)(2,1)S(1)} %get-tuple-element.54), channel_id=1, source_target_pairs={{0,6},{2,8},{4,10},{6,12},{8,14},{10,0},{12,2},{14,4},{1,7},{3,9},... | collective-permute-start | bytes 41480 | tf_op jit(solution)/shard_map/ppermute | solution.py:420
  40.1 1.6 %collective-permute-start.13 = (bf16[2,3456]{1,0:T(2,128)(2,1)S(1)}, bf16[2,3456]{1,0:T(2,128)(2,1)S(1)}, u32[]{:S(2)}, u32[]{:S(2)}) collective-permute-start(bf16[2,3456]{1,0:T(2,128)(2,1)S(1)} %get-tuple-element.55), channel_id=1, source_target_pairs={{0,4},{2,6},{4,8},{6,10},{8,12},{10,14},{12,0},{14,2},{1,5},{3,7},... | collective-permute-start | bytes 41480 | tf_op jit(solution)/shard_map/ppermute | solution.py:420
  41.7 0.1 collective-permute-start.14
  41.8 3.6 %attend_cache.1 = (bf16[128,3072]{1,0:T(8,128)(2,1)S(1)}, f32[16,3072]{1,0:T(8,128)S(1)}, f32[16,128]{1,0:T(8,128)S(1)}) custom-call(bf16[128,3072]{1,0:T(8,128)(2,1)S(1)} %get-tuple-element.34.queries_ref, bf16[128,32,512]{2,1,0:T(8,128)(2,1)S(1)} %get-tuple-element.35.cache_ref, s32[1,128]{1,0:T(1,128)} %bitcast.4, ...), custom_call_target="tpu_custom_call" | custom-call | tf_op jit(solution)/shard_map/attend_cache/pallas_call | solution.py:495
  45.5 0.1 collective-permute-done.13.refs_6_
  45.6 2.5 %collective-permute-done.14.refs_7_ = bf16[2,3456]{1,0:T(2,128)(2,1)S(1)} collective-permute-done((bf16[2,3456]{1,0:T(2,128)(2,1)S(1)}, bf16[2,3456]{1,0:T(2,128)(2,1)S(1)}, u32[]{:S(2)}, u32[]{:S(2)}) %collective-permute-start.14) | collective-permute-done | bytes 13856 | tf_op jit(solution)/shard_map/ppermute | solution.py:420
  48.1 1.4 %merge.1 = bf16[128,3072]{1,0:T(8,128)(2,1)} custom-call(bf16[16,128]{1,0:T(8,128)(2,1)S(1)} %get-tuple-element.31.after_ref.pick_ref, bf16[128,3072]{1,0:T(8,128)(2,1)S(1)} %get-tuple-element.47.cached_ref, f32[16,3072]{1,0:T(8,128)S(1)} %get-tuple-element.48.slot_out_ref, f32[16,128]{1,0:T(8,128)S(1)} %get-tuple-element.49.slot_lse_ref, ...), custom_call_target="tpu_custom_call" | custom-call | tf_op jit(solution)/shard_map/merge/pallas_call | solution.py:517
  (12 shorter events, 0.0 us)
Async XLA Ops:
  11.5 20.2 %collective-permute-start = (bf16[896,512]{1,0:T(8,128)(2,1)S(1)}, bf16[896,512]{1,0:T(8,128)(2,1)S(1)}, u32[]{:S(2)}, u32[]{:S(2)}) collective-permute-start(bf16[896,512]{1,0:T(8,128)(2,1)S(1)} %get-tuple-element.37), channel_id=1, source_target_pairs={{0,1},{1,0},{2,3},{3,2},{4,5},{5,4},{6,7},{7,6},{8,9},{9,8},{10,11... | collective-permute-start | bytes 2752520 | tf_op jit(solution)/shard_map/ppermute | solution.py:462
  12.0 7.9 %collective-permute-start.1 = (bf16[2,3072]{1,0:T(2,128)(2,1)S(1)}, bf16[2,3072]{1,0:T(2,128)(2,1)S(1)}, u32[]{:S(2)}, u32[]{:S(2)}) collective-permute-start(bf16[2,3072]{1,0:T(2,128)(2,1)S(1)} %get-tuple-element.39), channel_id=1, source_target_pairs={{0,2},{2,4},{4,6},{6,8},{8,10},{10,12},{12,14},{14,0},{1,3},{3,5},... | collective-permute-start | bytes 36872 | tf_op jit(solution)/shard_map/ppermute | solution.py:420
  14.6 8.0 %collective-permute-start.2 = (bf16[2,3072]{1,0:T(2,128)(2,1)S(1)}, bf16[2,3072]{1,0:T(2,128)(2,1)S(1)}, u32[]{:S(2)}, u32[]{:S(2)}) collective-permute-start(bf16[2,3072]{1,0:T(2,128)(2,1)S(1)} %get-tuple-element.40), channel_id=1, source_target_pairs={{0,4},{2,6},{4,8},{6,10},{8,12},{10,14},{12,0},{14,2},{1,5},{3,7},... | collective-permute-start | bytes 36872 | tf_op jit(solution)/shard_map/ppermute | solution.py:420
  16.2 7.8 %collective-permute-start.3 = (bf16[2,3072]{1,0:T(2,128)(2,1)S(1)}, bf16[2,3072]{1,0:T(2,128)(2,1)S(1)}, u32[]{:S(2)}, u32[]{:S(2)}) collective-permute-start(bf16[2,3072]{1,0:T(2,128)(2,1)S(1)} %get-tuple-element.41), channel_id=1, source_target_pairs={{0,6},{2,8},{4,10},{6,12},{8,14},{10,0},{12,2},{14,4},{1,7},{3,9},... | collective-permute-start | bytes 36872 | tf_op jit(solution)/shard_map/ppermute | solution.py:420
  18.7 12.9 %collective-permute-start.4 = (bf16[2,3072]{1,0:T(2,128)(2,1)S(1)}, bf16[2,3072]{1,0:T(2,128)(2,1)S(1)}, u32[]{:S(2)}, u32[]{:S(2)}) collective-permute-start(bf16[2,3072]{1,0:T(2,128)(2,1)S(1)} %get-tuple-element.42), channel_id=1, source_target_pairs={{0,8},{2,10},{4,12},{6,14},{8,0},{10,2},{12,4},{14,6},{1,9},{3,11}... | collective-permute-start | bytes 36872 | tf_op jit(solution)/shard_map/ppermute | solution.py:420
  19.9 11.7 %collective-permute-start.5 = (bf16[2,3072]{1,0:T(2,128)(2,1)S(1)}, bf16[2,3072]{1,0:T(2,128)(2,1)S(1)}, u32[]{:S(2)}, u32[]{:S(2)}) collective-permute-start(bf16[2,3072]{1,0:T(2,128)(2,1)S(1)} %get-tuple-element.43), channel_id=1, source_target_pairs={{0,10},{2,12},{4,14},{6,0},{8,2},{10,4},{12,6},{14,8},{1,11},{3,13... | collective-permute-start | bytes 36872 | tf_op jit(solution)/shard_map/ppermute | solution.py:420
  22.6 9.1 %collective-permute-start.6 = (bf16[2,3072]{1,0:T(2,128)(2,1)S(1)}, bf16[2,3072]{1,0:T(2,128)(2,1)S(1)}, u32[]{:S(2)}, u32[]{:S(2)}) collective-permute-start(bf16[2,3072]{1,0:T(2,128)(2,1)S(1)} %get-tuple-element.44), channel_id=1, source_target_pairs={{0,12},{2,14},{4,0},{6,2},{8,4},{10,6},{12,8},{14,10},{1,13},{3,15... | collective-permute-start | bytes 36872 | tf_op jit(solution)/shard_map/ppermute | solution.py:420
  23.9 7.7 %collective-permute-start.7 = (bf16[2,3072]{1,0:T(2,128)(2,1)S(1)}, bf16[2,3072]{1,0:T(2,128)(2,1)S(1)}, u32[]{:S(2)}, u32[]{:S(2)}) collective-permute-start(bf16[2,3072]{1,0:T(2,128)(2,1)S(1)} %get-tuple-element.45), channel_id=1, source_target_pairs={{0,14},{2,0},{4,2},{6,4},{8,6},{10,8},{12,10},{14,12},{1,15},{3,1}... | collective-permute-start | bytes 36872 | tf_op jit(solution)/shard_map/ppermute | solution.py:420
  33.5 6.5 %collective-permute-start.8 = (bf16[2,3456]{1,0:T(2,128)(2,1)S(1)}, bf16[2,3456]{1,0:T(2,128)(2,1)S(1)}, u32[]{:S(2)}, u32[]{:S(2)}) collective-permute-start(bf16[2,3456]{1,0:T(2,128)(2,1)S(1)} %get-tuple-element.50), channel_id=1, source_target_pairs={{0,14},{2,0},{4,2},{6,4},{8,6},{10,8},{12,10},{14,12},{1,15},{3,1}... | collective-permute-start | bytes 41480 | tf_op jit(solution)/shard_map/ppermute | solution.py:420
  34.1 7.5 %collective-permute-start.9 = (bf16[2,3456]{1,0:T(2,128)(2,1)S(1)}, bf16[2,3456]{1,0:T(2,128)(2,1)S(1)}, u32[]{:S(2)}, u32[]{:S(2)}) collective-permute-start(bf16[2,3456]{1,0:T(2,128)(2,1)S(1)} %get-tuple-element.51), channel_id=1, source_target_pairs={{0,12},{2,14},{4,0},{6,2},{8,4},{10,6},{12,8},{14,10},{1,13},{3,15... | collective-permute-start | bytes 41480 | tf_op jit(solution)/shard_map/ppermute | solution.py:420
  35.5 10.0 %collective-permute-start.10 = (bf16[2,3456]{1,0:T(2,128)(2,1)S(1)}, bf16[2,3456]{1,0:T(2,128)(2,1)S(1)}, u32[]{:S(2)}, u32[]{:S(2)}) collective-permute-start(bf16[2,3456]{1,0:T(2,128)(2,1)S(1)} %get-tuple-element.52), channel_id=1, source_target_pairs={{0,10},{2,12},{4,14},{6,0},{8,2},{10,4},{12,6},{14,8},{1,11},{3,13... | collective-permute-start | bytes 41480 | tf_op jit(solution)/shard_map/ppermute | solution.py:420
  37.2 8.2 %collective-permute-start.11 = (bf16[2,3456]{1,0:T(2,128)(2,1)S(1)}, bf16[2,3456]{1,0:T(2,128)(2,1)S(1)}, u32[]{:S(2)}, u32[]{:S(2)}) collective-permute-start(bf16[2,3456]{1,0:T(2,128)(2,1)S(1)} %get-tuple-element.53), channel_id=1, source_target_pairs={{0,8},{2,10},{4,12},{6,14},{8,0},{10,2},{12,4},{14,6},{1,9},{3,11}... | collective-permute-start | bytes 41480 | tf_op jit(solution)/shard_map/ppermute | solution.py:420
  38.4 7.0 %collective-permute-start.12 = (bf16[2,3456]{1,0:T(2,128)(2,1)S(1)}, bf16[2,3456]{1,0:T(2,128)(2,1)S(1)}, u32[]{:S(2)}, u32[]{:S(2)}) collective-permute-start(bf16[2,3456]{1,0:T(2,128)(2,1)S(1)} %get-tuple-element.54), channel_id=1, source_target_pairs={{0,6},{2,8},{4,10},{6,12},{8,14},{10,0},{12,2},{14,4},{1,7},{3,9},... | collective-permute-start | bytes 41480 | tf_op jit(solution)/shard_map/ppermute | solution.py:420
  40.1 5.5 %collective-permute-start.13 = (bf16[2,3456]{1,0:T(2,128)(2,1)S(1)}, bf16[2,3456]{1,0:T(2,128)(2,1)S(1)}, u32[]{:S(2)}, u32[]{:S(2)}) collective-permute-start(bf16[2,3456]{1,0:T(2,128)(2,1)S(1)} %get-tuple-element.55), channel_id=1, source_target_pairs={{0,4},{2,6},{4,8},{6,10},{8,12},{10,14},{12,0},{14,2},{1,5},{3,7},... | collective-permute-start | bytes 41480 | tf_op jit(solution)/shard_map/ppermute | solution.py:420
  41.7 6.4 %collective-permute-start.14 = (bf16[2,3456]{1,0:T(2,128)(2,1)S(1)}, bf16[2,3456]{1,0:T(2,128)(2,1)S(1)}, u32[]{:S(2)}, u32[]{:S(2)}) collective-permute-start(bf16[2,3456]{1,0:T(2,128)(2,1)S(1)} %get-tuple-element.56), channel_id=1, source_target_pairs={{0,2},{2,4},{4,6},{6,8},{8,10},{10,12},{12,14},{14,0},{1,3},{3,5},... | collective-permute-start | bytes 41480 | tf_op jit(solution)/shard_map/ppermute | solution.py:420

commit v4 on v3

--- a/solution.py
+++ b/solution.py
@@ -26,7 +26,7 @@
     return (iota(shape, dim) == index).astype(F32).astype(BF16)
 
 
-def select_queries(target_ref, queries_ref, pick_ref, *asked_refs):
+def select_queries(target_ref, queries_ref, pick_ref, asked_ref):
     sections, requests = target_ref.shape
     row_count = queries_ref.shape[0]
     slots = sections * CAP
@@ -34,8 +34,8 @@
     slot_id = iota((slots, requests), 0)
     table = jnp.zeros((slots, requests), jnp.int32)
     for k in range(sections):
-        row = target_ref[pl.ds(lax.rem(position + k, sections), 1), :]
-        table = jnp.where((slot_id >= k * CAP) & (slot_id < (k + 1) * CAP), row, table)
+        mine = (slot_id >= k * CAP) & (slot_id < (k + 1) * CAP)
+        table = jnp.where(mine, target_ref[k : k + 1, :], table)
     local = table - position * row_count
     here = (local >= 0) & (local < row_count)
     square = (requests, requests)
@@ -50,7 +50,25 @@
     pick_ref[...] = pick
     asked = jnp.dot(pick, queries_ref[...], preferred_element_type=F32).astype(BF16)
     for k in range(sections):
-        asked_refs[k][...] = asked[k * CAP : (k + 1) * CAP]
+        asked_ref[k] = asked[k * CAP : (k + 1) * CAP]
+
+
+def spans(edges):
+    return [slice(a, b) for a, b in zip(edges[:-1], edges[1:])]
+
+
+def accumulate(rows_ref, w_ref, total_ref, out_ref, scale_ref, chunks, waits, scale_copy):
+    for c, at in enumerate(chunks):
+        for copy in waits[c]:
+            copy.wait()
+        part = jnp.dot(rows_ref[:, at], w_ref[at, :], preferred_element_type=F32)
+        if c == 0:
+            total_ref[...] = part
+        elif c < len(chunks) - 1:
+            total_ref[...] += part
+        else:
+            scale_copy.wait()
+            out_ref[...] = ((total_ref[...] + part) * scale_ref[...]).astype(BF16)
 
 
 def project_first(
@@ -68,7 +86,7 @@
     row_sems,
     hidden_sems,
     theirs_sems,
-    mine_sems,
+    mine_sem,
     scale_sem,
     *,
     edges,
@@ -78,7 +96,7 @@
     tp = lax.axis_index("tp")
     theirs = pl.ds(pl.multiple_of((1 - tp) * width, width), width)
     mine = pl.ds(pl.multiple_of(tp * width, width), width)
-    chunks = [slice(a, b) for a, b in zip(edges[:-1], edges[1:])]
+    chunks = spans(edges)
     waits = []
     for c, at in enumerate(chunks):
         copies = [
@@ -95,30 +113,20 @@
         for copy in copies:
             copy.start()
         waits.append(copies)
-    later = [
-        pltpu.make_async_copy(w_ref.at[at, mine], w_mine_ref.at[at, :], mine_sems.at[c])
-        for c, at in enumerate(chunks)
-    ]
-    later.append(pltpu.make_async_copy(scale_ref.at[:, theirs], scale_here_ref, scale_sem))
-    for copy in later:
-        copy.start()
-    for c, at in enumerate(chunks):
-        for copy in waits[c]:
-            copy.wait()
-        part = jnp.dot(rows_ref[:, at], w_theirs_ref[at, :], preferred_element_type=F32)
-        if c == 0:
-            total_ref[...] = part
-        elif c < len(chunks) - 1:
-            total_ref[...] += part
-        else:
-            later[-1].wait()
-            out_ref[...] = ((total_ref[...] + part) * scale_here_ref[...]).astype(BF16)
-    for copy in later[:-1]:
-        copy.wait()
+    scale_copy = pltpu.make_async_copy(scale_ref.at[:, theirs], scale_here_ref, scale_sem)
+    head = pl.ds(0, w_mine_ref.shape[0])
+    mine_copy = pltpu.make_async_copy(w_ref.at[head, mine], w_mine_ref, mine_sem)
+    scale_copy.start()
+    mine_copy.start()
+    accumulate(
+        rows_ref, w_theirs_ref, total_ref, out_ref, scale_here_ref, chunks, waits, scale_copy
+    )
+    mine_copy.wait()
 
 
 def project_second(
     rows_ref,
+    w_head_ref,
     w_ref,
     scale_ref,
     cache_ref,
@@ -126,29 +134,32 @@
     out_ref,
     cache_here_ref,
     queries_here_ref,
+    w_tail_ref,
+    total_ref,
     scale_here_ref,
+    tail_sem,
     scale_sem,
     cache_sem,
     queries_sem,
-    *,
-    block,
 ):
     width = out_ref.shape[1]
     mine = pl.ds(pl.multiple_of(lax.axis_index("tp") * width, width), width)
+    head = w_head_ref.shape[0]
+    tail = pl.ds(head, w_tail_ref.shape[0])
     copies = [
+        pltpu.make_async_copy(w_ref.at[tail, mine], w_tail_ref, tail_sem),
         pltpu.make_async_copy(scale_ref.at[:, mine], scale_here_ref, scale_sem),
         pltpu.make_async_copy(queries_ref, queries_here_ref, queries_sem),
         pltpu.make_async_copy(cache_ref, cache_here_ref, cache_sem),
     ]
     for copy in copies:
         copy.start()
-    for m in range(0, rows_ref.shape[0], block):
-        at = slice(m, m + block)
-        total = jnp.dot(rows_ref[at, :], w_ref[...], preferred_element_type=F32)
-        if m == 0:
-            copies[0].wait()
-        out_ref[at, :] = (total * scale_here_ref[...]).astype(BF16)
-    for copy in copies[1:]:
+    total_ref[...] = jnp.dot(rows_ref[:, :head], w_head_ref[...], preferred_element_type=F32)
+    copies[0].wait()
+    copies[1].wait()
+    part = jnp.dot(rows_ref[:, head:], w_tail_ref[...], preferred_element_type=F32)
+    out_ref[...] = ((total_ref[...] + part) * scale_here_ref[...]).astype(BF16)
+    for copy in copies[2:]:
         copy.wait()
 
 
@@ -175,26 +186,26 @@
         iota((padded, requests), 1) < iota((padded, requests), 0)
     )
     rank_col = jnp.sum(before.astype(F32), axis=1, keepdims=True).astype(jnp.int32)
-    back = position - section_col.astype(jnp.int32)
-    back = jnp.where(back < 0, back + sections, back)
     real = iota((padded, 1), 0) < requests
-    return jnp.where(real, back * CAP + rank_col, -1), span_col.astype(jnp.int32)
-
-
-def attend_arrived(target_ref, span_ref, mine_ref, other_ref, *refs, row_count):
+    slot_col = jnp.where(real, section_col.astype(jnp.int32) * CAP + rank_col, -1)
+    return slot_col, span_col.astype(jnp.int32)
+
+
+def attend_arrived(
+    target_ref, span_ref, mine_ref, other_ref, asked_ref, out_ref, *, row_count
+):
     sections, requests = target_ref.shape
-    asked_refs, out_refs = refs[:sections], refs[sections:]
     slots = sections * CAP
     padded = -(-requests // 16) * 16
     prompt_rows = mine_ref.shape[0] - row_count
     span_rows = prompt_rows // requests
     kv_heads = mine_ref.shape[1] // (2 * HD)
-    group = asked_refs[0].shape[1] // (kv_heads * HD)
+    group = asked_ref.shape[2] // (kv_heads * HD)
     slot_col, span_col = request_slots(target_ref, span_ref, row_count, padded)
     slot_of = one_hot((padded, slots), 1, slot_col)
     key = iota((padded, prompt_rows), 1) - iota((padded, prompt_rows), 0) * span_rows
     bias = jnp.where((key >= 0) & (key < span_col), 0.0, MASKED)
-    asked = jnp.concatenate([ref[...].astype(F32) for ref in asked_refs], axis=0).astype(BF16)
+    asked = jnp.concatenate([asked_ref[s].astype(F32) for s in range(sections)], axis=0).astype(BF16)
     rows = jnp.dot(slot_of, asked, preferred_element_type=F32).astype(BF16)
     kv = (
         mine_ref[:prompt_rows, :].astype(F32) + other_ref[:prompt_rows, :].astype(F32)
@@ -233,8 +244,8 @@
             lse = jnp.where(lane == h * group + i, head_lse[i], lse)
     result = jnp.concatenate(pieces + list(split_bf16(lse)), axis=1).astype(BF16)
     answers = lax.dot_general(slot_of, result, TRANSPOSED, preferred_element_type=F32).astype(BF16)
-    for k in range(sections):
-        out_refs[k][...] = answers[k * CAP : (k + 1) * CAP]
+    for s in range(sections):
+        out_ref[s] = answers[s * CAP : (s + 1) * CAP]
 
 
 def attend_cache(
@@ -354,11 +365,10 @@
         slot_lse_ref[...] += slot_lse
 
 
-def merge(pick_ref, cached_ref, slot_out_ref, slot_lse_ref, *refs):
-    arrived_refs, out_ref = refs[:-1], refs[-1]
+def merge(pick_ref, cached_ref, slot_out_ref, slot_lse_ref, arrived_ref, out_ref):
     width = cached_ref.shape[1]
     pick = pick_ref[...]
-    arrived = jnp.concatenate([ref[...].astype(F32) for ref in arrived_refs], axis=0)
+    arrived = jnp.concatenate([arrived_ref[s].astype(F32) for s in range(arrived_ref.shape[0])], axis=0)
     arrived_lse = (
         arrived[:, width : width + STATS]
         + arrived[:, width + STATS : width + 2 * STATS]
@@ -415,29 +425,23 @@
     scale = kv_scale.reshape(1, -1)
     lengths = cache_len.reshape(1, -1)
 
-    def moved(arrays, sign):
-        return [arrays[0]] + [
-            lax.ppermute(
-                arrays[k], "section", [(i, (i + sign * k) % sections) for i in range(sections)]
-            )
-            for k in range(1, sections)
-        ]
-
-    pick, *asked = pl.pallas_call(
+    pick, asked = pl.pallas_call(
         select_queries,
         in_specs=[RESIDENT, RESIDENT],
-        out_specs=[RESIDENT] * (1 + sections),
-        out_shape=[pltpu.VMEM((slots, row_count), BF16)]
-        + [pltpu.VMEM((CAP, query_width), BF16)] * sections,
+        out_specs=[RESIDENT] * 2,
+        out_shape=[
+            pltpu.VMEM((slots, row_count), BF16),
+            pltpu.VMEM((sections, CAP, query_width), BF16),
+        ],
         compiler_params=compiler_params(16),
         name="select_queries",
     )(in_hbm(target_row), in_hbm(queries))
-    asked = moved(asked, 1)
-
-    depth = 512
-    edges = tuple(range(0, features + 1, depth))
+    asked = lax.all_to_all(asked, "section", 0, 0)
+
+    edges = (0, 256, 768, 1536, 2560, 4096, features)
     count = len(edges) - 1
-    theirs, rows, w_mine = pl.pallas_call(
+    head = features // 3
+    theirs, rows, w_head = pl.pallas_call(
         functools.partial(project_first, edges=edges),
         in_specs=[REMAINS] * 5,
         out_specs=[RESIDENT, RESIDENT, RESIDENT],
@@ -448,24 +452,27 @@
             pltpu.SemaphoreType.DMA((count,)),
             pltpu.SemaphoreType.DMA((count,)),
             pltpu.SemaphoreType.DMA((count,)),
-            pltpu.SemaphoreType.DMA((count,)),
+            pltpu.SemaphoreType.DMA(()),
             pltpu.SemaphoreType.DMA(()),
         ],
         out_shape=[
             pltpu.VMEM((all_rows, local_width), BF16),
             pltpu.VMEM((all_rows, features), BF16),
-            pltpu.VMEM((features, local_width), BF16),
+            pltpu.VMEM((head, local_width), BF16),
         ],
         compiler_params=compiler_params(16),
         name="project_first",
-    )(in_hbm(prompts), in_hbm(decode_hidden), in_hbm(w_kv), in_hbm(scale), in_vmem(pick))
+    )(in_hbm(prompts), in_hbm(decode_hidden), in_hbm(w_kv), in_hbm(scale), in_vmem(asked))
     other = lax.ppermute(theirs, "tp", [(0, 1), (1, 0)])
     mine, cache_here, queries_here = pl.pallas_call(
-        functools.partial(project_second, block=all_rows // 2),
-        in_specs=[RESIDENT, RESIDENT, REMAINS, REMAINS, REMAINS],
+        project_second,
+        in_specs=[RESIDENT, RESIDENT] + [REMAINS] * 4,
         out_specs=[RESIDENT, RESIDENT, RESIDENT],
         scratch_shapes=[
+            pltpu.VMEM((features - head, local_width), BF16),
+            pltpu.VMEM((all_rows, local_width), F32),
             pltpu.VMEM((1, local_width), F32),
+            pltpu.SemaphoreType.DMA(()),
             pltpu.SemaphoreType.DMA(()),
             pltpu.SemaphoreType.DMA(()),
             pltpu.SemaphoreType.DMA(()),
@@ -477,19 +484,26 @@
         ],
         compiler_params=compiler_params(16),
         name="project_second",
-    )(in_vmem(rows), in_vmem(w_mine), in_hbm(scale), in_hbm(kv_cache), in_hbm(queries))
+    )(
+        in_vmem(rows),
+        in_vmem(w_head),
+        in_hbm(w_kv),
+        in_hbm(scale),
+        in_hbm(kv_cache),
+        in_hbm(queries),
+    )
 
     answer_width = query_width + 3 * STATS
     answers = pl.pallas_call(
         functools.partial(attend_arrived, row_count=row_count),
-        in_specs=[RESIDENT] * (4 + sections),
-        out_specs=[RESIDENT] * sections,
-        out_shape=[pltpu.VMEM((CAP, answer_width), BF16)] * sections,
+        in_specs=[RESIDENT] * 5,
+        out_specs=RESIDENT,
+        out_shape=pltpu.VMEM((sections, CAP, answer_width), BF16),
         compiler_params=compiler_params(24),
         name="attend_arrived",
-    )(in_hbm(target_row), in_hbm(span_len), in_vmem(mine), in_vmem(other), *map(in_vmem, asked))
-    after = answers[0]
-    answers = moved(answers, -1)
+    )(in_hbm(target_row), in_hbm(span_len), in_vmem(mine), in_vmem(other), in_vmem(asked))
+    after = answers
+    answers = lax.all_to_all(answers, "section", 0, 0)
 
     block = 32
     cached, slot_out, slot_lse = pl.pallas_call(
@@ -516,12 +530,12 @@
 
     return pl.pallas_call(
         merge,
-        in_specs=[RESIDENT] * (4 + sections),
+        in_specs=[RESIDENT] * 5,
         out_specs=RESIDENT,
         out_shape=jax.ShapeDtypeStruct((row_count, query_width), BF16),
         compiler_params=compiler_params(24),
         name="merge",
-    )(*map(in_vmem, (pick, cached, slot_out, slot_lse, *answers)))
+    )(*map(in_vmem, (pick, cached, slot_out, slot_lse, answers)))
 
 
 def solution(mesh):

time: 49.7 us -> 50.4 us (1.014)
  starting transfers between devices: 22.1 us -> 3.44 us
  blocking collectives: 0 us -> 14.2 us
  local copies, waits for them, and re-layouts: 0 us -> 5.72 us
  waiting for transfers between devices: 2.63 us -> 1.06 us
  Pallas kernels: 24.6 us -> 25.5 us
    ppermute x14 -> x0, starting transfers between devices: 21.6 us -> none  [moved(): lax.ppermute(arrays[k], 'section', [(i, (i + sign * k) % sections) for i...]
    all_to_all x0 -> x1, blocking collectives: none -> 14.2 us  [shards(): asked = lax.all_to_all(asked, 'section', 0, 0)]
    unnamed x0 -> x8, local copies, waits for them, and re-layouts: none -> 5.72 us
    all_to_all x0 -> x1, starting transfers between devices: none -> 3.36 us  [shards(): answers = lax.all_to_all(answers, 'section', 0, 0)]
    ppermute x14 -> x0, waiting for transfers between devices: 2.62 us -> none  [moved(): lax.ppermute(arrays[k], 'section', [(i, (i + sign * k) % sections) for i...]
    pallas_call x2, Pallas kernels: 7.64 us -> 9.12 us  [the longest x1 7.76 us: shards(): pl.pallas_call(project_second, in_specs=[RESIDENT, RESIDENT] + [REMAINS]...]
    pallas_call x1, Pallas kernels: 9.92 us -> 8.64 us  [shards(): pl.pallas_call(functools.partial(project_first, edges=edges), in_specs=[R...]
    all_to_all x0 -> x1, waiting for transfers between devices: none -> 1.06 us  [shards(): answers = lax.all_to_all(answers, 'section', 0, 0)]
  transfers between devices with their start and end apart: 15 -> 2, of which waited for: 2 -> 1; matrix products, arithmetic and copies ran while one was open for 0% -> 0% of each run, Pallas kernels for 20% -> 23%
where the time goes in v4:
time: 50.4 us; the launch traced here: 50 us
  Pallas kernels  25.5 us (51%)
  blocking collectives  14.2 us (28%)
  local copies, waits for them, and re-layouts  5.72 us (11%)
  starting transfers between devices  3.44 us (7%)
  waiting for transfers between devices  1.06 us (2%)
    all_to_all x1, blocking collectives, shards(): asked = lax.all_to_all(asked, 'section', 0, 0)  14.2 us
    pallas_call x1, Pallas kernels, shards(): pl.pallas_call(functools.partial(project_first, edges=edges), in_specs=[R...  8.64 us
    pallas_call x1, Pallas kernels, shards(): pl.pallas_call(project_second, in_specs=[RESIDENT, RESIDENT] + [REMAINS]...  7.76 us
    unnamed x8, local copies, waits for them, and re-layouts  5.72 us
    pallas_call x1, Pallas kernels, shards(): pl.pallas_call(functools.partial(attend_cache, block_rows=block), grid=(r...  3.75 us
    all_to_all x1, starting transfers between devices, shards(): answers = lax.all_to_all(answers, 'section', 0, 0)  3.36 us
    pallas_call x1, Pallas kernels, shards(): pl.pallas_call(functools.partial(attend_arrived, row_count=row_count), in...  2.44 us
    pallas_call x1, Pallas kernels, shards(): pl.pallas_call(select_queries, in_specs=[RESIDENT, RESIDENT], out_specs=[...  1.55 us
  transfers between devices with their start and end apart: 2, of which 1 were waited for; matrix products, arithmetic and copies ran while one was open for 0% of the time, Pallas kernels for 23%

profile of v4, /device:TPU:0, one launch (start us, length us, event | category | flops | bytes accessed | tf_op | source)
XLA Modules:
  0.0 50.0 jit_solution(5585823928382470142)
XLA Ops:
  0.0 1.5 %select_queries.1 = (bf16[16,128]{1,0:T(8,128)(2,1)S(1)}, bf16[8,2,3072]{2,1,0:T(2,128)(2,1)S(1)}) custom-call(s32[8,12]{1,0:T(8,128)} %target_ref.3, bf16[128,3072]{1,0:T(8,128)(2,1)} %queries_ref.3), custom_call_target="tpu_custom_call" | custom-call | tf_op jit(solution)/shard_map/select_queries/pallas_call | solution.py:428
  1.6 14.2 %all_to_all.10.after_ref.asked_ref = bf16[8,2,3072]{2,1,0:T(2,128)(2,1)S(1)} all-to-all(bf16[8,2,3072]{2,1,0:T(2,128)(2,1)S(1)} %get-tuple-element.17), channel_id=1, replica_groups=mesh['groups'=2,'section'=8,'tp'=2] {'section'}, dimensions={0} | all-to-all | bytes 196608 | tf_op jit(solution)/shard_map/all_to_all | solution.py:439
  15.8 8.6 %project_first.1 = (bf16[896,512]{1,0:T(8,128)(2,1)S(1)}, bf16[896,6144]{1,0:T(8,128)(2,1)S(1)}, bf16[2048,512]{1,0:T(8,128)(2,1)S(1)}) custom-call(bf16[768,6144]{1,0:T(8,128)(2,1)} %prompts_ref.1, bf16[128,6144]{1,0:T(8,128)(2,1)} %hidden_ref.1, bf16[6144,1024]{1,0:T(8,128)(2,1)} %w_ref.3, f32[1,1024]{1,0:T(1,128)} %bitcast.2, ...), custom_call_target="tpu_custom_call" | custom-call | tf_op jit(solution)/shard_map/project_first/pallas_call | solution.py:444
  24.4 0.1 collective-permute-start
  24.5 7.8 %project_second.1 = (bf16[896,512]{1,0:T(8,128)(2,1)S(1)}, bf16[128,32,512]{2,1,0:T(8,128)(2,1)S(1)}, bf16[128,3072]{1,0:T(8,128)(2,1)S(1)}) custom-call(bf16[896,6144]{1,0:T(8,128)(2,1)S(1)} %get-tuple-element.18.rows_ref, bf16[2048,512]{1,0:T(8,128)(2,1)S(1)} %get-tuple-element.19.w_head_ref, bf16[6144,1024]{1,0:T(8,128)(2,1)} %w_ref.3, ...), custom_call_target="tpu_custom_call" | custom-call | tf_op jit(solution)/shard_map/project_second/pallas_call | solution.py:467
  32.3 0.0 copy-start
  32.3 1.9 %copy-done = bf16[128,32,512]{2,1,0:T(8,128)(2,1)} copy-done((bf16[128,32,512]{2,1,0:T(8,128)(2,1)}, bf16[128,32,512]{2,1,0:T(8,128)(2,1)S(1)}, u32[]{:S(2)}) %copy-start) | copy-done | bytes 4194328
  34.2 0.0 collective-permute-done.other_ref
  34.2 2.4 %attend_arrived.1.after_ref = bf16[8,2,3456]{2,1,0:T(2,128)(2,1)} custom-call(s32[8,12]{1,0:T(8,128)} %target_ref.3, s32[8,12]{1,0:T(8,128)} %span_ref.1, bf16[896,512]{1,0:T(8,128)(2,1)S(1)} %get-tuple-element.22.mine_ref, bf16[896,512]{1,0:T(8,128)(2,1)S(1)} %collective-permute-done.other_ref, bf16[8,2,3072]{2,1,0:T(2,128)(2,1)S(1)} %all_to_all.10.after_ref.asked_ref), custom_call_target="tpu_custom_call" | custom-call | tf_op jit(solution)/shard_map/attend_arrived/pallas_call | solution.py:497
  36.7 3.4 %all-to-all-start.1 = ((bf16[8,2,3456]{2,1,0:T(2,128)(2,1)}), bf16[8,2,3456]{2,1,0:T(2,128)(2,1)S(1)}, u32[]{:S(2)}, u32[]{:S(2)}) async-start(bf16[8,2,3456]{2,1,0:T(2,128)(2,1)} %attend_arrived.1.after_ref), calls=%async_computation.1 | async-start | bytes 221184 | tf_op jit(solution)/shard_map/all_to_all | solution.py:506
  40.0 0.0 copy-start.1
  40.0 2.2 %copy-done.1 = bf16[128,32,512]{2,1,0:T(8,128)(2,1)S(1)} copy-done((bf16[128,32,512]{2,1,0:T(8,128)(2,1)S(1)}, bf16[128,32,512]{2,1,0:T(8,128)(2,1)}, u32[]{:S(2)}) %copy-start.1) | copy-done | bytes 4194328
  42.2 3.8 %attend_cache.1 = (bf16[128,3072]{1,0:T(8,128)(2,1)S(1)}, f32[16,3072]{1,0:T(8,128)S(1)}, f32[16,128]{1,0:T(8,128)S(1)}) custom-call(bf16[128,3072]{1,0:T(8,128)(2,1)S(1)} %get-tuple-element.20.queries_ref, bf16[128,32,512]{2,1,0:T(8,128)(2,1)S(1)} %copy-done.1, s32[1,128]{1,0:T(1,128)} %bitcast.4, bf16[896,512]{1,0:T(8,128)(2,1)S(1)} %get-tuple-element.22.mine_ref, ...), custom_call_target="tpu_custom_call" | custom-call | tf_op jit(solution)/shard_map/attend_cache/pallas_call | solution.py:509
  46.0 0.0 copy-start.2
  46.0 0.7 %copy-done.2 = f32[16,3072]{1,0:T(8,128)} copy-done((f32[16,3072]{1,0:T(8,128)}, f32[16,3072]{1,0:T(8,128)S(1)}, u32[]{:S(2)}) %copy-start.2) | copy-done | bytes 196632
  46.7 1.1 %all-to-all-done.1.arrived_ref = bf16[8,2,3456]{2,1,0:T(2,128)(2,1)S(1)} async-done(((bf16[8,2,3456]{2,1,0:T(2,128)(2,1)}), bf16[8,2,3456]{2,1,0:T(2,128)(2,1)S(1)}, u32[]{:S(2)}, u32[]{:S(2)}) %all-to-all-start.1) | async-done | bytes 110624 | tf_op jit(solution)/shard_map/all_to_all | solution.py:506
  47.7 0.0 copy-start.3
  47.7 0.9 %copy-done.3 = f32[16,3072]{1,0:T(8,128)S(1)} copy-done((f32[16,3072]{1,0:T(8,128)S(1)}, f32[16,3072]{1,0:T(8,128)}, u32[]{:S(2)}) %copy-start.3) | copy-done | bytes 196632
  48.6 1.4 %merge.1 = bf16[128,3072]{1,0:T(8,128)(2,1)} custom-call(bf16[16,128]{1,0:T(8,128)(2,1)S(1)} %get-tuple-element.16.pick_ref, bf16[128,3072]{1,0:T(8,128)(2,1)S(1)} %get-tuple-element.24.cached_ref, f32[16,3072]{1,0:T(8,128)S(1)} %copy-done.3, f32[16,128]{1,0:T(8,128)S(1)} %get-tuple-element.26.slot_lse_ref, bf16[8,2,3456]{2,1,0:T(2,128)(2,1)S(1)} %all-to-all-done.1.arrived_ref), custom_call_target="tpu_custom_call" | custom-call | tf_op jit(solution)/shard_map/merge/pallas_call | solution.py:531
Async XLA Ops:
  24.4 9.8 %collective-permute-start = (bf16[896,512]{1,0:T(8,128)(2,1)S(1)}, bf16[896,512]{1,0:T(8,128)(2,1)S(1)}, u32[]{:S(2)}, u32[]{:S(2)}) collective-permute-start(bf16[896,512]{1,0:T(8,128)(2,1)S(1)} %get-tuple-element.23), channel_id=1, source_target_pairs={{0,1},{1,0},{2,3},{3,2},{4,5},{5,4},{6,7},{7,6},{8,9},{9,8},{10,11... | collective-permute-start | bytes 2752520 | tf_op jit(solution)/shard_map/ppermute | solution.py:466
  32.3 1.9 %copy-start = (bf16[128,32,512]{2,1,0:T(8,128)(2,1)}, bf16[128,32,512]{2,1,0:T(8,128)(2,1)S(1)}, u32[]{:S(2)}) copy-start(bf16[128,32,512]{2,1,0:T(8,128)(2,1)S(1)} %get-tuple-element.21.cache_ref) | copy-start | bytes 12582916
  36.7 11.1 %all-to-all-start.1 = ((bf16[8,2,3456]{2,1,0:T(2,128)(2,1)}), bf16[8,2,3456]{2,1,0:T(2,128)(2,1)S(1)}, u32[]{:S(2)}, u32[]{:S(2)}) async-start(bf16[8,2,3456]{2,1,0:T(2,128)(2,1)} %attend_arrived.1.after_ref), calls=%async_computation.1 | async-start | bytes 221184 | tf_op jit(solution)/shard_map/all_to_all | solution.py:506
  40.0 2.2 %copy-start.1 = (bf16[128,32,512]{2,1,0:T(8,128)(2,1)S(1)}, bf16[128,32,512]{2,1,0:T(8,128)(2,1)}, u32[]{:S(2)}) copy-start(bf16[128,32,512]{2,1,0:T(8,128)(2,1)} %copy-done) | copy-start | bytes 12582916
  46.0 0.7 %copy-start.2 = (f32[16,3072]{1,0:T(8,128)}, f32[16,3072]{1,0:T(8,128)S(1)}, u32[]{:S(2)}) copy-start(f32[16,3072]{1,0:T(8,128)S(1)} %get-tuple-element.25.slot_out_ref) | copy-start | bytes 589828
  47.7 0.9 %copy-start.3 = (f32[16,3072]{1,0:T(8,128)S(1)}, f32[16,3072]{1,0:T(8,128)}, u32[]{:S(2)}) copy-start(f32[16,3072]{1,0:T(8,128)} %copy-done.2) | copy-start | bytes 589828

commit v5 on v4

--- a/solution.py
+++ b/solution.py
@@ -57,18 +57,22 @@
     return [slice(a, b) for a, b in zip(edges[:-1], edges[1:])]
 
 
-def accumulate(rows_ref, w_ref, total_ref, out_ref, scale_ref, chunks, waits, scale_copy):
+def accumulate(
+    rows_ref, w_ref, total_ref, out_ref, scale_ref, chunks, block, waits, scale_copy
+):
     for c, at in enumerate(chunks):
         for copy in waits[c]:
             copy.wait()
-        part = jnp.dot(rows_ref[:, at], w_ref[at, :], preferred_element_type=F32)
-        if c == 0:
-            total_ref[...] = part
-        elif c < len(chunks) - 1:
-            total_ref[...] += part
-        else:
+        if c == len(chunks) - 1:
             scale_copy.wait()
-            out_ref[...] = ((total_ref[...] + part) * scale_ref[...]).astype(BF16)
+        for m in spans(range(0, rows_ref.shape[0] + 1, block)):
+            part = jnp.dot(rows_ref[m, at], w_ref[at, :], preferred_element_type=F32)
+            if c == 0:
+                total_ref[m, :] = part
+            elif c < len(chunks) - 1:
+                total_ref[m, :] += part
+            else:
+                out_ref[m, :] = ((total_ref[m, :] + part) * scale_ref[...]).astype(BF16)
 
 
 def project_first(
@@ -90,12 +94,14 @@
     scale_sem,
     *,
     edges,
+    block,
 ):
     prompt_rows = prompts_ref.shape[0]
     width = out_ref.shape[1]
     tp = lax.axis_index("tp")
     theirs = pl.ds(pl.multiple_of((1 - tp) * width, width), width)
-    mine = pl.ds(pl.multiple_of(tp * width, width), width)
+    half = w_mine_ref.shape[1]
+    mine = pl.ds(pl.multiple_of(tp * width, half), half)
     chunks = spans(edges)
     waits = []
     for c, at in enumerate(chunks):
@@ -114,12 +120,11 @@
             copy.start()
         waits.append(copies)
     scale_copy = pltpu.make_async_copy(scale_ref.at[:, theirs], scale_here_ref, scale_sem)
-    head = pl.ds(0, w_mine_ref.shape[0])
-    mine_copy = pltpu.make_async_copy(w_ref.at[head, mine], w_mine_ref, mine_sem)
+    mine_copy = pltpu.make_async_copy(w_ref.at[:, mine], w_mine_ref, mine_sem)
     scale_copy.start()
     mine_copy.start()
     accumulate(
-        rows_ref, w_theirs_ref, total_ref, out_ref, scale_here_ref, chunks, waits, scale_copy
+        rows_ref, w_theirs_ref, total_ref, out_ref, scale_here_ref, chunks, block, waits, scale_copy
     )
     mine_copy.wait()
 
@@ -129,38 +134,32 @@
     w_head_ref,
     w_ref,
     scale_ref,
-    cache_ref,
-    queries_ref,
     out_ref,
-    cache_here_ref,
-    queries_here_ref,
     w_tail_ref,
-    total_ref,
     scale_here_ref,
     tail_sem,
     scale_sem,
-    cache_sem,
-    queries_sem,
+    *,
+    block,
 ):
     width = out_ref.shape[1]
-    mine = pl.ds(pl.multiple_of(lax.axis_index("tp") * width, width), width)
-    head = w_head_ref.shape[0]
-    tail = pl.ds(head, w_tail_ref.shape[0])
-    copies = [
-        pltpu.make_async_copy(w_ref.at[tail, mine], w_tail_ref, tail_sem),
-        pltpu.make_async_copy(scale_ref.at[:, mine], scale_here_ref, scale_sem),
-        pltpu.make_async_copy(queries_ref, queries_here_ref, queries_sem),
-        pltpu.make_async_copy(cache_ref, cache_here_ref, cache_sem),
-    ]
-    for copy in copies:
-        copy.start()
-    total_ref[...] = jnp.dot(rows_ref[:, :head], w_head_ref[...], preferred_element_type=F32)
-    copies[0].wait()
-    copies[1].wait()
-    part = jnp.dot(rows_ref[:, head:], w_tail_ref[...], preferred_element_type=F32)
-    out_ref[...] = ((total_ref[...] + part) * scale_here_ref[...]).astype(BF16)
-    for copy in copies[2:]:
-        copy.wait()
+    half = w_head_ref.shape[1]
+    tp = lax.axis_index("tp")
+    mine = pl.ds(pl.multiple_of(tp * width, width), width)
+    tail = pl.ds(pl.multiple_of(tp * width + half, half), half)
+    tail_copy = pltpu.make_async_copy(w_ref.at[:, tail], w_tail_ref, tail_sem)
+    scale_copy = pltpu.make_async_copy(scale_ref.at[:, mine], scale_here_ref, scale_sem)
+    tail_copy.start()
+    scale_copy.start()
+    for part_ref, copy, first in ((w_head_ref, scale_copy, 0), (w_tail_ref, tail_copy, half)):
+        at = slice(first, first + half)
+        if copy is tail_copy:
+            copy.wait()
+        for m in spans(range(0, rows_ref.shape[0] + 1, block)):
+            total = jnp.dot(rows_ref[m, :], part_ref[...], preferred_element_type=F32)
+            if copy is scale_copy and m.start == 0:
+                copy.wait()
+            out_ref[m, at] = (total * scale_here_ref[:, at]).astype(BF16)
 
 
 def split_bf16(x):
@@ -262,7 +261,8 @@
     *,
     block_rows,
 ):
-    row_count, cache_rows, width = cache_ref.shape
+    cache_rows, width = cache_ref.shape[1:]
+    row_count = len_ref.shape[1]
     kv_heads = width // (2 * HD)
     group = queries_ref.shape[1] // (kv_heads * HD)
     unit = 8
@@ -270,7 +270,7 @@
     first_row = pl.multiple_of(pl.program_id(0) * block_rows, block_rows)
     block = pl.ds(first_row, block_rows)
     own_block = pl.ds(first_row + (mine_ref.shape[0] - row_count), block_rows)
-    queries = queries_ref[block, :].astype(F32)
+    queries = queries_ref[...].astype(F32)
     own = mine_ref[own_block, :].astype(F32) + other_ref[own_block, :].astype(F32)
     own = own.astype(BF16).astype(F32)
     key = iota((unit, keys_of), 1) - iota((unit, keys_of), 0) * cache_rows
@@ -280,7 +280,7 @@
     units = range(block_rows // unit)
 
     def rows_of(u):
-        return pl.ds(first_row + u * unit, unit)
+        return slice(u * unit, (u + 1) * unit)
 
     pairs = [(u, h) for u in units for h in range(kv_heads)]
     bias = []
@@ -440,9 +440,15 @@
 
     edges = (0, 256, 768, 1536, 2560, 4096, features)
     count = len(edges) - 1
-    head = features // 3
+    half = local_width // 2
+    block = all_rows // 2
+    cost = pl.CostEstimate(
+        flops=2 * all_rows * features * local_width,
+        bytes_accessed=2 * features * (all_rows + local_width),
+        transcendentals=0,
+    )
     theirs, rows, w_head = pl.pallas_call(
-        functools.partial(project_first, edges=edges),
+        functools.partial(project_first, edges=edges, block=block),
         in_specs=[REMAINS] * 5,
         out_specs=[RESIDENT, RESIDENT, RESIDENT],
         scratch_shapes=[
@@ -458,40 +464,28 @@
         out_shape=[
             pltpu.VMEM((all_rows, local_width), BF16),
             pltpu.VMEM((all_rows, features), BF16),
-            pltpu.VMEM((head, local_width), BF16),
+            pltpu.VMEM((features, half), BF16),
         ],
         compiler_params=compiler_params(16),
+        cost_estimate=cost,
         name="project_first",
-    )(in_hbm(prompts), in_hbm(decode_hidden), in_hbm(w_kv), in_hbm(scale), in_vmem(asked))
+    )(in_hbm(prompts), in_hbm(decode_hidden), in_hbm(w_kv), in_hbm(scale), in_vmem(pick))
     other = lax.ppermute(theirs, "tp", [(0, 1), (1, 0)])
-    mine, cache_here, queries_here = pl.pallas_call(
-        project_second,
-        in_specs=[RESIDENT, RESIDENT] + [REMAINS] * 4,
-        out_specs=[RESIDENT, RESIDENT, RESIDENT],
+    mine = pl.pallas_call(
+        functools.partial(project_second, block=block),
+        in_specs=[RESIDENT, RESIDENT, REMAINS, REMAINS],
+        out_specs=RESIDENT,
         scratch_shapes=[
-            pltpu.VMEM((features - head, local_width), BF16),
-            pltpu.VMEM((all_rows, local_width), F32),
+            pltpu.VMEM((features, local_width - half), BF16),
             pltpu.VMEM((1, local_width), F32),
             pltpu.SemaphoreType.DMA(()),
             pltpu.SemaphoreType.DMA(()),
-            pltpu.SemaphoreType.DMA(()),
-            pltpu.SemaphoreType.DMA(()),
         ],
-        out_shape=[
-            pltpu.VMEM((all_rows, local_width), BF16),
-            pltpu.VMEM(kv_cache.shape, BF16),
-            pltpu.VMEM(queries.shape, BF16),
-        ],
+        out_shape=pltpu.VMEM((all_rows, local_width), BF16),
         compiler_params=compiler_params(16),
+        cost_estimate=cost,
         name="project_second",
-    )(
-        in_vmem(rows),
-        in_vmem(w_head),
-        in_hbm(w_kv),
-        in_hbm(scale),
-        in_hbm(kv_cache),
-        in_hbm(queries),
-    )
+    )(in_vmem(rows), in_vmem(w_head), in_hbm(w_kv), in_hbm(scale))
 
     answer_width = query_width + 3 * STATS
     answers = pl.pallas_call(
@@ -509,7 +503,12 @@
     cached, slot_out, slot_lse = pl.pallas_call(
         functools.partial(attend_cache, block_rows=block),
         grid=(row_count // block,),
-        in_specs=[RESIDENT] * 6 + [REMAINS],
+        in_specs=[
+            pl.BlockSpec((block, query_width), lambda b: (b, 0)),
+            pl.BlockSpec((block, *kv_cache.shape[1:]), lambda b: (b, 0, 0)),
+        ]
+        + [RESIDENT] * 4
+        + [REMAINS],
         out_specs=[RESIDENT] * 3,
         out_shape=[
             pltpu.VMEM((row_count, query_width), BF16),
@@ -519,8 +518,8 @@
         compiler_params=compiler_params(24),
         name="attend_cache",
     )(
-        in_vmem(queries_here),
-        in_vmem(cache_here),
+        in_hbm(queries),
+        in_hbm(kv_cache),
         in_hbm(lengths),
         in_vmem(mine),
         in_vmem(other),

time: 50.4 us -> 56.7 us (1.12)
  blocking collectives: 14.2 us -> 0 us
  starting transfers between devices: 3.44 us -> 13.3 us
  local copies, waits for them, and re-layouts: 5.72 us -> 11.9 us
  Pallas kernels: 25.5 us -> 28.8 us
  waiting for transfers between devices: 1.06 us -> 2.18 us
    all_to_all x1 -> x0, blocking collectives: 14.2 us -> none  [shards(): asked = lax.all_to_all(asked, 'section', 0, 0)]
    all_to_all x0 -> x1, starting transfers between devices: none -> 6.83 us  [shards(): asked = lax.all_to_all(asked, 'section', 0, 0)]
    unnamed x8, local copies, waits for them, and re-layouts: 5.72 us -> 11.9 us
    all_to_all x1, starting transfers between devices: 3.36 us -> 6 us  [shards(): answers = lax.all_to_all(answers, 'section', 0, 0)]
    pallas_call x2, Pallas kernels: 16.4 us -> 17.8 us  [the longest x1 9 us: shards(): pl.pallas_call(functools.partial(project_second, block=block), in_specs=[...]
    pallas_call x1, Pallas kernels: 3.75 us -> 5.02 us  [shards(): pl.pallas_call(functools.partial(attend_cache, block_rows=block), grid=(r...]
    all_to_all x1, waiting for transfers between devices: 1.06 us -> 2.18 us  [shards(): answers = lax.all_to_all(answers, 'section', 0, 0)]
    pallas_call x1, Pallas kernels: 1.55 us -> 2.2 us  [shards(): pl.pallas_call(select_queries, in_specs=[RESIDENT, RESIDENT], out_specs=[...]
  transfers between devices with their start and end apart: 2 -> 3, of which waited for: 1 -> 1; matrix products, arithmetic and copies ran while one was open for 0% -> 0% of each run, Pallas kernels for 23% -> 25%
where the time goes in v5:
time: 56.7 us; the launch traced here: 56.2 us
  Pallas kernels  28.8 us (51%)
  starting transfers between devices  13.3 us (23%)
  local copies, waits for them, and re-layouts  11.9 us (21%)
  waiting for transfers between devices  2.18 us (4%)
    unnamed x8, local copies, waits for them, and re-layouts  11.9 us
    pallas_call x1, Pallas kernels, shards(): pl.pallas_call(functools.partial(project_second, block=block), in_specs=[...  9 us
    pallas_call x1, Pallas kernels, shards(): pl.pallas_call(functools.partial(project_first, edges=edges, block=block)...  8.77 us
    all_to_all x1, starting transfers between devices, shards(): asked = lax.all_to_all(asked, 'section', 0, 0)  6.83 us
    all_to_all x1, starting transfers between devices, shards(): answers = lax.all_to_all(answers, 'section', 0, 0)  6 us
    pallas_call x1, Pallas kernels, shards(): pl.pallas_call(functools.partial(attend_cache, block_rows=block), grid=(r...  5.02 us
    pallas_call x1, Pallas kernels, shards(): pl.pallas_call(functools.partial(attend_arrived, row_count=row_count), in...  2.45 us
    pallas_call x1, Pallas kernels, shards(): pl.pallas_call(select_queries, in_specs=[RESIDENT, RESIDENT], out_specs=[...  2.2 us
  transfers between devices with their start and end apart: 3, of which 1 were waited for; matrix products, arithmetic and copies ran while one was open for 0% of the time, Pallas kernels for 25%

profile of v5, /device:TPU:0, one launch (start us, length us, event | category | flops | bytes accessed | tf_op | source)
XLA Modules:
  0.0 56.2 jit_solution(14402839426691876059)
XLA Ops:
  0.0 2.2 %select_queries.1 = (bf16[16,128]{1,0:T(8,128)(2,1)S(1)}, bf16[8,2,3072]{2,1,0:T(2,128)(2,1)}) custom-call(s32[8,12]{1,0:T(8,128)} %target_ref.3, bf16[128,3072]{1,0:T(8,128)(2,1)} %queries_ref.3), custom_call_target="tpu_custom_call" | custom-call | tf_op jit(solution)/shard_map/select_queries/pallas_call | solution.py:428
  2.2 8.8 %project_first.1 = (bf16[896,512]{1,0:T(8,128)(2,1)S(1)}, bf16[896,6144]{1,0:T(8,128)(2,1)S(1)}, bf16[6144,256]{1,0:T(8,128)(2,1)S(1)}) custom-call(bf16[768,6144]{1,0:T(8,128)(2,1)} %prompts_ref.1, bf16[128,6144]{1,0:T(8,128)(2,1)} %hidden_ref.1, bf16[6144,1024]{1,0:T(8,128)(2,1)} %w_ref.3, f32[1,1024]{1,0:T(1,128)} %bitcast.2, ...), custom_call_target="tpu_custom_call" | custom-call | flops 5637144576 | bytes 17301504 | tf_op jit(solution)/shard_map/project_first/pallas_call | solution.py:450
  11.0 0.0 copy-start
  11.0 4.2 %copy-done = bf16[896,6144]{1,0:T(8,128)(2,1)} copy-done((bf16[896,6144]{1,0:T(8,128)(2,1)}, bf16[896,6144]{1,0:T(8,128)(2,1)S(1)}, u32[]{:S(2)}) %copy-start) | copy-done | bytes 11010072
  15.2 0.0 copy-start.2
  15.2 1.7 %copy-done.2 = bf16[6144,256]{1,0:T(8,128)(2,1)} copy-done((bf16[6144,256]{1,0:T(8,128)(2,1)}, bf16[6144,256]{1,0:T(8,128)(2,1)S(1)}, u32[]{:S(2)}) %copy-start.2) | copy-done | bytes 3145752
  16.9 0.5 collective-permute-start
  17.3 6.8 %all-to-all-start = ((bf16[8,2,3072]{2,1,0:T(2,128)(2,1)}), bf16[8,2,3072]{2,1,0:T(2,128)(2,1)S(1)}, u32[]{:S(2)}, u32[]{:S(2)}) async-start(bf16[8,2,3072]{2,1,0:T(2,128)(2,1)} %get-tuple-element.17), calls=%async_computation | async-start | bytes 196608 | tf_op jit(solution)/shard_map/all_to_all | solution.py:439
  24.2 0.0 copy-start.1
  24.2 4.1 %copy-done.1 = bf16[896,6144]{1,0:T(8,128)(2,1)S(1)} copy-done((bf16[896,6144]{1,0:T(8,128)(2,1)S(1)}, bf16[896,6144]{1,0:T(8,128)(2,1)}, u32[]{:S(2)}) %copy-start.1) | copy-done | bytes 11010072
  28.3 0.0 copy-start.3
  28.3 1.9 %copy-done.3 = bf16[6144,256]{1,0:T(8,128)(2,1)S(1)} copy-done((bf16[6144,256]{1,0:T(8,128)(2,1)S(1)}, bf16[6144,256]{1,0:T(8,128)(2,1)}, u32[]{:S(2)}) %copy-start.3) | copy-done | bytes 3145752
  30.2 9.0 %project_second.1.mine_ref = bf16[896,512]{1,0:T(8,128)(2,1)S(1)} custom-call(bf16[896,6144]{1,0:T(8,128)(2,1)S(1)} %copy-done.1, bf16[6144,256]{1,0:T(8,128)(2,1)S(1)} %copy-done.3, bf16[6144,1024]{1,0:T(8,128)(2,1)} %w_ref.3, f32[1,1024]{1,0:T(1,128)} %bitcast.3), custom_call_target="tpu_custom_call" | custom-call | flops 5637144576 | bytes 17301504 | tf_op jit(solution)/shard_map/project_second/pallas_call | solution.py:474
  39.2 0.0 all-to-all-done.asked_ref
  39.2 0.0 collective-permute-done.other_ref
  39.2 2.5 %attend_arrived.1.after_ref = bf16[8,2,3456]{2,1,0:T(2,128)(2,1)} custom-call(s32[8,12]{1,0:T(8,128)} %target_ref.3, s32[8,12]{1,0:T(8,128)} %span_ref.1, bf16[896,512]{1,0:T(8,128)(2,1)S(1)} %project_second.1.mine_ref, bf16[896,512]{1,0:T(8,128)(2,1)S(1)} %collective-permute-done.other_ref, bf16[8,2,3072]{2,1,0:T(2,128)(2,1)S(1)} %all-to-all-done.asked_ref), custom_call_target="tpu_custom_call" | custom-call | tf_op jit(solution)/shard_map/attend_arrived/pallas_call | solution.py:491
  41.7 6.0 %all-to-all-start.1 = ((bf16[8,2,3456]{2,1,0:T(2,128)(2,1)}), bf16[8,2,3456]{2,1,0:T(2,128)(2,1)S(1)}, u32[]{:S(2)}, u32[]{:S(2)}) async-start(bf16[8,2,3456]{2,1,0:T(2,128)(2,1)} %attend_arrived.1.after_ref), calls=%async_computation.1 | async-start | bytes 221184 | tf_op jit(solution)/shard_map/all_to_all | solution.py:500
  47.7 5.0 %attend_cache.1 = (bf16[128,3072]{1,0:T(8,128)(2,1)S(1)}, f32[16,3072]{1,0:T(8,128)S(1)}, f32[16,128]{1,0:T(8,128)S(1)}) custom-call(bf16[128,3072]{1,0:T(8,128)(2,1)} %queries_ref.3, bf16[128,32,512]{2,1,0:T(8,128)(2,1)} %cache_ref.1, s32[1,128]{1,0:T(1,128)} %bitcast.4, bf16[896,512]{1,0:T(8,128)(2,1)S(1)} %project_second.1.mine_ref, ...), custom_call_target="tpu_custom_call" | custom-call | tf_op jit(solution)/shard_map/attend_cache/pallas_call | solution.py:503
  52.7 2.2 %all-to-all-done.1.arrived_ref = bf16[8,2,3456]{2,1,0:T(2,128)(2,1)S(1)} async-done(((bf16[8,2,3456]{2,1,0:T(2,128)(2,1)}), bf16[8,2,3456]{2,1,0:T(2,128)(2,1)S(1)}, u32[]{:S(2)}, u32[]{:S(2)}) %all-to-all-start.1) | async-done | bytes 110624 | tf_op jit(solution)/shard_map/all_to_all | solution.py:500
  54.9 1.4 %merge.1 = bf16[128,3072]{1,0:T(8,128)(2,1)} custom-call(bf16[16,128]{1,0:T(8,128)(2,1)S(1)} %get-tuple-element.13.after_ref.pick_ref, bf16[128,3072]{1,0:T(8,128)(2,1)S(1)} %get-tuple-element.18.cached_ref, f32[16,3072]{1,0:T(8,128)S(1)} %get-tuple-element.19.slot_out_ref, f32[16,128]{1,0:T(8,128)S(1)} %get-tuple-element.20.slot_lse_ref, ...), custom_call_target="tpu_custom_call" | custom-call | tf_op jit(solution)/shard_map/merge/pallas_call | solution.py:530
Async XLA Ops:
  11.0 4.2 %copy-start = (bf16[896,6144]{1,0:T(8,128)(2,1)}, bf16[896,6144]{1,0:T(8,128)(2,1)S(1)}, u32[]{:S(2)}) copy-start(bf16[896,6144]{1,0:T(8,128)(2,1)S(1)} %get-tuple-element.14.rows_ref) | copy-start | bytes 33030148
  15.2 1.7 %copy-start.2 = (bf16[6144,256]{1,0:T(8,128)(2,1)}, bf16[6144,256]{1,0:T(8,128)(2,1)S(1)}, u32[]{:S(2)}) copy-start(bf16[6144,256]{1,0:T(8,128)(2,1)S(1)} %get-tuple-element.15.w_head_ref) | copy-start | bytes 9437188
  16.9 22.3 %collective-permute-start = (bf16[896,512]{1,0:T(8,128)(2,1)S(1)}, bf16[896,512]{1,0:T(8,128)(2,1)S(1)}, u32[]{:S(2)}, u32[]{:S(2)}) collective-permute-start(bf16[896,512]{1,0:T(8,128)(2,1)S(1)} %get-tuple-element.16), channel_id=1, source_target_pairs={{0,1},{1,0},{2,3},{3,2},{4,5},{5,4},{6,7},{7,6},{8,9},{9,8},{10,11... | collective-permute-start | bytes 2752520 | tf_op jit(solution)/shard_map/ppermute | solution.py:473
  17.3 21.9 %all-to-all-start = ((bf16[8,2,3072]{2,1,0:T(2,128)(2,1)}), bf16[8,2,3072]{2,1,0:T(2,128)(2,1)S(1)}, u32[]{:S(2)}, u32[]{:S(2)}) async-start(bf16[8,2,3072]{2,1,0:T(2,128)(2,1)} %get-tuple-element.17), calls=%async_computation | async-start | bytes 196608 | tf_op jit(solution)/shard_map/all_to_all | solution.py:439
  24.2 4.1 %copy-start.1 = (bf16[896,6144]{1,0:T(8,128)(2,1)S(1)}, bf16[896,6144]{1,0:T(8,128)(2,1)}, u32[]{:S(2)}) copy-start(bf16[896,6144]{1,0:T(8,128)(2,1)} %copy-done) | copy-start | bytes 33030148
  28.3 1.9 %copy-start.3 = (bf16[6144,256]{1,0:T(8,128)(2,1)S(1)}, bf16[6144,256]{1,0:T(8,128)(2,1)}, u32[]{:S(2)}) copy-start(bf16[6144,256]{1,0:T(8,128)(2,1)} %copy-done.2) | copy-start | bytes 9437188
  41.7 13.2 %all-to-all-start.1 = ((bf16[8,2,3456]{2,1,0:T(2,128)(2,1)}), bf16[8,2,3456]{2,1,0:T(2,128)(2,1)S(1)}, u32[]{:S(2)}, u32[]{:S(2)}) async-start(bf16[8,2,3456]{2,1,0:T(2,128)(2,1)} %attend_arrived.1.after_ref), calls=%async_computation.1 | async-start | bytes 221184 | tf_op jit(solution)/shard_map/all_to_all | solution.py:500

commit v6 on v5

--- a/solution.py
+++ b/solution.py
@@ -57,58 +57,31 @@
     return [slice(a, b) for a, b in zip(edges[:-1], edges[1:])]
 
 
-def accumulate(
-    rows_ref, w_ref, total_ref, out_ref, scale_ref, chunks, block, waits, scale_copy
-):
-    for c, at in enumerate(chunks):
-        for copy in waits[c]:
-            copy.wait()
-        if c == len(chunks) - 1:
-            scale_copy.wait()
-        for m in spans(range(0, rows_ref.shape[0] + 1, block)):
-            part = jnp.dot(rows_ref[m, at], w_ref[at, :], preferred_element_type=F32)
-            if c == 0:
-                total_ref[m, :] = part
-            elif c < len(chunks) - 1:
-                total_ref[m, :] += part
-            else:
-                out_ref[m, :] = ((total_ref[m, :] + part) * scale_ref[...]).astype(BF16)
-
-
-def project_first(
+def project(
     prompts_ref,
     hidden_ref,
     w_ref,
     scale_ref,
     after_ref,
-    out_ref,
+    mine_ref,
+    theirs_ref,
     rows_ref,
-    w_mine_ref,
-    w_theirs_ref,
+    w_here_ref,
     total_ref,
-    scale_here_ref,
     row_sems,
     hidden_sems,
-    theirs_sems,
-    mine_sem,
-    scale_sem,
+    w_sems,
     *,
     edges,
     block,
 ):
     prompt_rows = prompts_ref.shape[0]
-    width = out_ref.shape[1]
-    tp = lax.axis_index("tp")
-    theirs = pl.ds(pl.multiple_of((1 - tp) * width, width), width)
-    half = w_mine_ref.shape[1]
-    mine = pl.ds(pl.multiple_of(tp * width, half), half)
+    width = mine_ref.shape[1]
     chunks = spans(edges)
     waits = []
     for c, at in enumerate(chunks):
         copies = [
-            pltpu.make_async_copy(
-                w_ref.at[at, theirs], w_theirs_ref.at[at, :], theirs_sems.at[c]
-            ),
+            pltpu.make_async_copy(w_ref.at[at, :], w_here_ref.at[at, :], w_sems.at[c]),
             pltpu.make_async_copy(
                 prompts_ref.at[:, at], rows_ref.at[:prompt_rows, at], row_sems.at[c]
             ),
@@ -119,47 +92,26 @@
         for copy in copies:
             copy.start()
         waits.append(copies)
-    scale_copy = pltpu.make_async_copy(scale_ref.at[:, theirs], scale_here_ref, scale_sem)
-    mine_copy = pltpu.make_async_copy(w_ref.at[:, mine], w_mine_ref, mine_sem)
-    scale_copy.start()
-    mine_copy.start()
-    accumulate(
-        rows_ref, w_theirs_ref, total_ref, out_ref, scale_here_ref, chunks, block, waits, scale_copy
-    )
-    mine_copy.wait()
-
-
-def project_second(
-    rows_ref,
-    w_head_ref,
-    w_ref,
-    scale_ref,
-    out_ref,
-    w_tail_ref,
-    scale_here_ref,
-    tail_sem,
-    scale_sem,
-    *,
-    block,
-):
-    width = out_ref.shape[1]
-    half = w_head_ref.shape[1]
-    tp = lax.axis_index("tp")
-    mine = pl.ds(pl.multiple_of(tp * width, width), width)
-    tail = pl.ds(pl.multiple_of(tp * width + half, half), half)
-    tail_copy = pltpu.make_async_copy(w_ref.at[:, tail], w_tail_ref, tail_sem)
-    scale_copy = pltpu.make_async_copy(scale_ref.at[:, mine], scale_here_ref, scale_sem)
-    tail_copy.start()
-    scale_copy.start()
-    for part_ref, copy, first in ((w_head_ref, scale_copy, 0), (w_tail_ref, tail_copy, half)):
-        at = slice(first, first + half)
-        if copy is tail_copy:
+    for c, at in enumerate(chunks[:-1]):
+        for copy in waits[c]:
             copy.wait()
         for m in spans(range(0, rows_ref.shape[0] + 1, block)):
-            total = jnp.dot(rows_ref[m, :], part_ref[...], preferred_element_type=F32)
-            if copy is scale_copy and m.start == 0:
-                copy.wait()
-            out_ref[m, at] = (total * scale_here_ref[:, at]).astype(BF16)
+            part = jnp.dot(rows_ref[m, at], w_here_ref[at, :], preferred_element_type=F32)
+            if c == 0:
+                total_ref[m, :] = part
+            else:
+                total_ref[m, :] += part
+    for copy in waits[-1]:
+        copy.wait()
+    first = lax.axis_index("tp") == 0
+    for m in spans(range(0, rows_ref.shape[0] + 1, block)):
+        part = jnp.dot(
+            rows_ref[m, chunks[-1]], w_here_ref[chunks[-1], :], preferred_element_type=F32
+        )
+        term = ((total_ref[m, :] + part) * scale_ref[...]).astype(BF16)
+        low, high = term[:, :width], term[:, width:]
+        mine_ref[m, :] = jnp.where(first, low, high)
+        theirs_ref[m, :] = jnp.where(first, high, low)
 
 
 def split_bf16(x):
@@ -191,7 +143,7 @@
 
 
 def attend_arrived(
-    target_ref, span_ref, mine_ref, other_ref, asked_ref, out_ref, *, row_count
+    target_ref, span_ref, mine_ref, other_ref, asked_ref, after_ref, out_ref, *, row_count
 ):
     sections, requests = target_ref.shape
     slots = sections * CAP
@@ -260,6 +212,7 @@
     slot_lse_ref,
     *,
     block_rows,
+    first_block,
 ):
     cache_rows, width = cache_ref.shape[1:]
     row_count = len_ref.shape[1]
@@ -267,8 +220,9 @@
     group = queries_ref.shape[1] // (kv_heads * HD)
     unit = 8
     keys_of = unit * cache_rows
-    first_row = pl.multiple_of(pl.program_id(0) * block_rows, block_rows)
-    block = pl.ds(first_row, block_rows)
+    step = pl.program_id(0)
+    block = pl.ds(pl.multiple_of(step * block_rows, block_rows), block_rows)
+    first_row = pl.multiple_of((step + first_block) * block_rows, block_rows)
     own_block = pl.ds(first_row + (mine_ref.shape[0] - row_count), block_rows)
     queries = queries_ref[...].astype(F32)
     own = mine_ref[own_block, :].astype(F32) + other_ref[own_block, :].astype(F32)
@@ -354,27 +308,31 @@
         jnp.dot(pick, part.astype(BF16), preferred_element_type=F32) for part in split_bf16(lse)
     )
 
-    @pl.when(pl.program_id(0) == 0)
+    @pl.when(step == 0)
     def _():
         slot_out_ref[...] = slot_out
         slot_lse_ref[...] = slot_lse
 
-    @pl.when(pl.program_id(0) > 0)
+    @pl.when(step > 0)
     def _():
         slot_out_ref[...] += slot_out
         slot_lse_ref[...] += slot_lse
 
 
-def merge(pick_ref, cached_ref, slot_out_ref, slot_lse_ref, arrived_ref, out_ref):
-    width = cached_ref.shape[1]
+def merge(pick_ref, *refs):
+    parts, arrived_ref, out_ref = refs[:-2], refs[-2], refs[-1]
+    cached_refs, slot_out_refs, slot_lse_refs = parts[0::3], parts[1::3], parts[2::3]
+    width = out_ref.shape[1]
     pick = pick_ref[...]
-    arrived = jnp.concatenate([arrived_ref[s].astype(F32) for s in range(arrived_ref.shape[0])], axis=0)
+    arrived = jnp.concatenate(
+        [arrived_ref[s].astype(F32) for s in range(arrived_ref.shape[0])], axis=0
+    )
     arrived_lse = (
         arrived[:, width : width + STATS]
         + arrived[:, width + STATS : width + 2 * STATS]
         + arrived[:, width + 2 * STATS :]
     )
-    cached_lse = slot_lse_ref[...]
+    cached_lse = sum(ref[...] for ref in slot_lse_refs)
     largest = jnp.maximum(cached_lse, arrived_lse)
     cached_weight = jnp.exp2(cached_lse - largest)
     arrived_weight = jnp.exp2(arrived_lse - largest)
@@ -387,13 +345,18 @@
     for i in range(width // HD):
         at = slice(i * HD, (i + 1) * HD)
         merged = (
-            slot_out_ref[:, at] * cached_weight[:, i : i + 1]
+            sum(ref[:, at] for ref in slot_out_refs) * cached_weight[:, i : i + 1]
             + arrived[:, at] * arrived_weight[:, i : i + 1]
         )
         placed = lax.dot_general(
             pick, merged.astype(BF16), TRANSPOSED, preferred_element_type=F32
         )
-        out_ref[:, at] = jnp.where(has > 0.5, placed, cached_ref[:, at].astype(F32)).astype(BF16)
+        row = 0
+        for ref in cached_refs:
+            rows = slice(row, row + ref.shape[0])
+            kept = ref[:, at].astype(F32)
+            out_ref[rows, at] = jnp.where(has[rows] > 0.5, placed[rows], kept).astype(BF16)
+            row += ref.shape[0]
 
 
 def compiler_params(megabytes):
@@ -438,103 +401,90 @@
     )(in_hbm(target_row), in_hbm(queries))
     asked = lax.all_to_all(asked, "section", 0, 0)
 
-    edges = (0, 256, 768, 1536, 2560, 4096, features)
+    edges = (0, 512, 1152, 1920, 2944, 4224, features)
     count = len(edges) - 1
-    half = local_width // 2
-    block = all_rows // 2
-    cost = pl.CostEstimate(
-        flops=2 * all_rows * features * local_width,
-        bytes_accessed=2 * features * (all_rows + local_width),
-        transcendentals=0,
-    )
-    theirs, rows, w_head = pl.pallas_call(
-        functools.partial(project_first, edges=edges, block=block),
-        in_specs=[REMAINS] * 5,
-        out_specs=[RESIDENT, RESIDENT, RESIDENT],
+    mine, theirs = pl.pallas_call(
+        functools.partial(project, edges=edges, block=all_rows // 2),
+        in_specs=[REMAINS] * 3 + [RESIDENT, REMAINS],
+        out_specs=[RESIDENT, RESIDENT],
         scratch_shapes=[
-            pltpu.VMEM((features, local_width), BF16),
-            pltpu.VMEM((all_rows, local_width), F32),
-            pltpu.VMEM((1, local_width), F32),
+            pltpu.VMEM((all_rows, features), BF16),
+            pltpu.VMEM(w_kv.shape, BF16),
+            pltpu.VMEM((all_rows, w_kv.shape[1]), F32),
             pltpu.SemaphoreType.DMA((count,)),
             pltpu.SemaphoreType.DMA((count,)),
             pltpu.SemaphoreType.DMA((count,)),
-            pltpu.SemaphoreType.DMA(()),
-            pltpu.SemaphoreType.DMA(()),
         ],
-        out_shape=[
-            pltpu.VMEM((all_rows, local_width), BF16),
-            pltpu.VMEM((all_rows, features), BF16),
-            pltpu.VMEM((features, half), BF16),
-        ],
-        compiler_params=compiler_params(16),
-        cost_estimate=cost,
-        name="project_first",
+        out_shape=[pltpu.VMEM((all_rows, local_width), BF16)] * 2,
+        compiler_params=compiler_params(44),
+        name="project",
     )(in_hbm(prompts), in_hbm(decode_hidden), in_hbm(w_kv), in_hbm(scale), in_vmem(pick))
     other = lax.ppermute(theirs, "tp", [(0, 1), (1, 0)])
-    mine = pl.pallas_call(
-        functools.partial(project_second, block=block),
-        in_specs=[RESIDENT, RESIDENT, REMAINS, REMAINS],
-        out_specs=RESIDENT,
-        scratch_shapes=[
-            pltpu.VMEM((features, local_width - half), BF16),
-            pltpu.VMEM((1, local_width), F32),
-            pltpu.SemaphoreType.DMA(()),
-            pltpu.SemaphoreType.DMA(()),
-        ],
-        out_shape=pltpu.VMEM((all_rows, local_width), BF16),
-        compiler_params=compiler_params(16),
-        cost_estimate=cost,
-        name="project_second",
-    )(in_vmem(rows), in_vmem(w_head), in_hbm(w_kv), in_hbm(scale))
+
+    block = 32
+    calls = 2
+    call_rows = row_count // calls
+
+    def cache_share(call, after):
+        first_block = call * call_rows // block
+        return pl.pallas_call(
+            functools.partial(attend_cache, block_rows=block, first_block=first_block),
+            grid=(call_rows // block,),
+            in_specs=[
+                pl.BlockSpec((block, query_width), lambda b: (first_block + b, 0)),
+                pl.BlockSpec((block, *kv_cache.shape[1:]), lambda b: (first_block + b, 0, 0)),
+            ]
+            + [RESIDENT] * 4
+            + [REMAINS],
+            out_specs=[RESIDENT] * 3,
+            out_shape=[
+                pltpu.VMEM((call_rows, query_width), BF16),
+                pltpu.VMEM((slots, query_width), F32),
+                pltpu.VMEM((slots, STATS), F32),
+            ],
+            compiler_params=compiler_params(24),
+            name="attend_cache",
+        )(
+            in_hbm(queries),
+            in_hbm(kv_cache),
+            in_hbm(lengths),
+            in_vmem(mine),
+            in_vmem(other),
+            in_vmem(pick),
+            in_vmem(after),
+        )
+
+    shares = cache_share(0, pick)
 
     answer_width = query_width + 3 * STATS
     answers = pl.pallas_call(
         functools.partial(attend_arrived, row_count=row_count),
-        in_specs=[RESIDENT] * 5,
+        in_specs=[RESIDENT] * 5 + [REMAINS],
         out_specs=RESIDENT,
         out_shape=pltpu.VMEM((sections, CAP, answer_width), BF16),
         compiler_params=compiler_params(24),
         name="attend_arrived",
-    )(in_hbm(target_row), in_hbm(span_len), in_vmem(mine), in_vmem(other), in_vmem(asked))
+    )(
+        in_hbm(target_row),
+        in_hbm(span_len),
+        in_vmem(mine),
+        in_vmem(other),
+        in_vmem(asked),
+        in_vmem(shares[2]),
+    )
     after = answers
     answers = lax.all_to_all(answers, "section", 0, 0)
-
-    block = 32
-    cached, slot_out, slot_lse = pl.pallas_call(
-        functools.partial(attend_cache, block_rows=block),
-        grid=(row_count // block,),
-        in_specs=[
-            pl.BlockSpec((block, query_width), lambda b: (b, 0)),
-            pl.BlockSpec((block, *kv_cache.shape[1:]), lambda b: (b, 0, 0)),
-        ]
-        + [RESIDENT] * 4
-        + [REMAINS],
-        out_specs=[RESIDENT] * 3,
-        out_shape=[
-            pltpu.VMEM((row_count, query_width), BF16),
-            pltpu.VMEM((slots, query_width), F32),
-            pltpu.VMEM((slots, STATS), F32),
-        ],
-        compiler_params=compiler_params(24),
-        name="attend_cache",
-    )(
-        in_hbm(queries),
-        in_hbm(kv_cache),
-        in_hbm(lengths),
-        in_vmem(mine),
-        in_vmem(other),
-        in_vmem(pick),
-        in_vmem(after),
-    )
+    for call in range(1, calls):
+        shares = [*shares, *cache_share(call, after)]
 
     return pl.pallas_call(
         merge,
-        in_specs=[RESIDENT] * 5,
+        in_specs=[RESIDENT] * (2 + len(shares)),
         out_specs=RESIDENT,
         out_shape=jax.ShapeDtypeStruct((row_count, query_width), BF16),
         compiler_params=compiler_params(24),
         name="merge",
-    )(*map(in_vmem, (pick, cached, slot_out, slot_lse, answers)))
+    )(*map(in_vmem, (pick, *shares, answers)))
 
 
 def solution(mesh):

time: 56.7 us -> 47.6 us (0.84)
  local copies, waits for them, and re-layouts: 11.9 us -> 0 us
  waiting for transfers between devices: 2.18 us -> 8.51 us
  starting transfers between devices: 13.3 us -> 10.7 us
  Pallas kernels: 28.8 us -> 27.8 us
    unnamed x8 -> x0, local copies, waits for them, and re-layouts: 11.9 us -> none
    all_to_all x1, waiting for transfers between devices: 0.01 us -> 4.26 us  [shards(): asked = lax.all_to_all(asked, 'section', 0, 0)]
    all_to_all x1, starting transfers between devices: 6 us -> 3.37 us  [shards(): answers = lax.all_to_all(answers, 'section', 0, 0)]
    all_to_all x1, waiting for transfers between devices: 2.18 us -> 4.25 us  [shards(): answers = lax.all_to_all(answers, 'section', 0, 0)]
    pallas_call x4, Pallas kernels: 24.1 us -> 23.1 us  [the longest x1 16 us: shards(): pl.pallas_call(functools.partial(project, edges=edges, block=all_rows //...]
  transfers between devices with their start and end apart: 3 -> 3, of which waited for: 1 -> 2; matrix products, arithmetic and copies ran while one was open for 0% -> 0% of each run, Pallas kernels for 25% -> 12%
where the time goes in v6:
time: 47.6 us; the launch traced here: 47.1 us
  Pallas kernels  27.8 us (58%)
  starting transfers between devices  10.7 us (22%)
  waiting for transfers between devices  8.51 us (18%)
    pallas_call x1, Pallas kernels, shards(): pl.pallas_call(functools.partial(project, edges=edges, block=all_rows //...  16 us
    all_to_all x1, starting transfers between devices, shards(): asked = lax.all_to_all(asked, 'section', 0, 0)  6.86 us
    pallas_call x2, Pallas kernels, cache_share(): pl.pallas_call(functools.partial(attend_cache, block_rows=block, first_bl...  5.76 us
    all_to_all x1, waiting for transfers between devices, shards(): asked = lax.all_to_all(asked, 'section', 0, 0)  4.26 us
    all_to_all x1, waiting for transfers between devices, shards(): answers = lax.all_to_all(answers, 'section', 0, 0)  4.25 us
    all_to_all x1, starting transfers between devices, shards(): answers = lax.all_to_all(answers, 'section', 0, 0)  3.37 us
    pallas_call x1, Pallas kernels, shards(): pl.pallas_call(functools.partial(attend_arrived, row_count=row_count), in...  2.45 us
    pallas_call x1, Pallas kernels, shards(): pl.pallas_call(select_queries, in_specs=[RESIDENT, RESIDENT], out_specs=[...  2.2 us
  transfers between devices with their start and end apart: 3, of which 2 were waited for; matrix products, arithmetic and copies ran while one was open for 0% of the time, Pallas kernels for 12%

profile of v6, /device:TPU:0, one launch (start us, length us, event | category | flops | bytes accessed | tf_op | source)
XLA Modules:
  0.0 47.1 jit_solution(5673481593891569166)
XLA Ops:
  0.0 2.2 %select_queries.1 = (bf16[16,128]{1,0:T(8,128)(2,1)S(1)}, bf16[8,2,3072]{2,1,0:T(2,128)(2,1)}) custom-call(s32[8,12]{1,0:T(8,128)} %target_ref.3, bf16[128,3072]{1,0:T(8,128)(2,1)} %queries_ref.5), custom_call_target="tpu_custom_call" | custom-call | tf_op jit(solution)/shard_map/select_queries/pallas_call | solution.py:391
  2.2 16.0 %project.1 = (bf16[896,512]{1,0:T(8,128)(2,1)S(1)}, bf16[896,512]{1,0:T(8,128)(2,1)S(1)}) custom-call(bf16[768,6144]{1,0:T(8,128)(2,1)} %prompts_ref.1, bf16[128,6144]{1,0:T(8,128)(2,1)} %hidden_ref.1, bf16[6144,1024]{1,0:T(8,128)(2,1)} %w_ref.1, f32[1,1024]{1,0:T(1,128)} %bitcast.2, bf16[16,128]{1,0:T(8,128)(2,1)S(1)} %get-tuple-element.15.after_ref.pick_ref), custom_call_target="tpu_custom_call" | custom-call | tf_op jit(solution)/shard_map/project/pallas_call | solution.py:406
  18.2 0.5 %collective-permute-start = (bf16[896,512]{1,0:T(8,128)(2,1)S(1)}, bf16[896,512]{1,0:T(8,128)(2,1)S(1)}, u32[]{:S(2)}, u32[]{:S(2)}) collective-permute-start(bf16[896,512]{1,0:T(8,128)(2,1)S(1)} %get-tuple-element.17), channel_id=1, source_target_pairs={{0,1},{1,0},{2,3},{3,2},{4,5},{5,4},{6,7},{7,6},{8,9},{9,8},{10,11... | collective-permute-start | bytes 2752520 | tf_op jit(solution)/shard_map/ppermute | solution.py:422
  18.7 6.9 %all-to-all-start = ((bf16[8,2,3072]{2,1,0:T(2,128)(2,1)}), bf16[8,2,3072]{2,1,0:T(2,128)(2,1)S(1)}, u32[]{:S(2)}, u32[]{:S(2)}) async-start(bf16[8,2,3072]{2,1,0:T(2,128)(2,1)} %get-tuple-element.21), calls=%async_computation | async-start | bytes 196608 | tf_op jit(solution)/shard_map/all_to_all | solution.py:402
  25.6 0.0 collective-permute-done.other_ref
  25.6 2.9 %attend_cache.2 = (bf16[64,3072]{1,0:T(8,128)(2,1)S(1)}, f32[16,3072]{1,0:T(8,128)S(1)}, f32[16,128]{1,0:T(8,128)S(1)}) custom-call(bf16[128,3072]{1,0:T(8,128)(2,1)} %queries_ref.5, bf16[128,32,512]{2,1,0:T(8,128)(2,1)} %cache_ref.3, s32[1,128]{1,0:T(1,128)} %bitcast.3, bf16[896,512]{1,0:T(8,128)(2,1)S(1)} %get-tuple-element.16.mine_ref, ...), custom_call_target="tpu_custom_call" | custom-call | tf_op jit(solution)/shard_map/attend_cache/pallas_call | solution.py:430
  28.5 4.3 %all-to-all-done.asked_ref = bf16[8,2,3072]{2,1,0:T(2,128)(2,1)S(1)} async-done(((bf16[8,2,3072]{2,1,0:T(2,128)(2,1)}), bf16[8,2,3072]{2,1,0:T(2,128)(2,1)S(1)}, u32[]{:S(2)}, u32[]{:S(2)}) %all-to-all-start) | async-done | bytes 98336 | tf_op jit(solution)/shard_map/all_to_all | solution.py:402
  32.8 2.5 %attend_arrived.1.after_ref = bf16[8,2,3456]{2,1,0:T(2,128)(2,1)} custom-call(s32[8,12]{1,0:T(8,128)} %target_ref.3, s32[8,12]{1,0:T(8,128)} %span_ref.1, bf16[896,512]{1,0:T(8,128)(2,1)S(1)} %get-tuple-element.16.mine_ref, bf16[896,512]{1,0:T(8,128)(2,1)S(1)} %collective-permute-done.other_ref, bf16[8,2,3072]{2,1,0:T(2,128)(2,1)S(1)} %all-to-all-done.asked_ref, ...), custom_call_target="tpu_custom_call" | custom-call | tf_op jit(solution)/shard_map/attend_arrived/pallas_call | solution.py:460
  35.2 3.4 %all-to-all-start.1 = ((bf16[8,2,3456]{2,1,0:T(2,128)(2,1)}), bf16[8,2,3456]{2,1,0:T(2,128)(2,1)S(1)}, u32[]{:S(2)}, u32[]{:S(2)}) async-start(bf16[8,2,3456]{2,1,0:T(2,128)(2,1)} %attend_arrived.1.after_ref), calls=%async_computation.1 | async-start | bytes 221184 | tf_op jit(solution)/shard_map/all_to_all | solution.py:476
  38.6 2.9 %attend_cache.3 = (bf16[64,3072]{1,0:T(8,128)(2,1)S(1)}, f32[16,3072]{1,0:T(8,128)S(1)}, f32[16,128]{1,0:T(8,128)S(1)}) custom-call(bf16[128,3072]{1,0:T(8,128)(2,1)} %queries_ref.5, bf16[128,32,512]{2,1,0:T(8,128)(2,1)} %cache_ref.3, s32[1,128]{1,0:T(1,128)} %bitcast.4, bf16[896,512]{1,0:T(8,128)(2,1)S(1)} %get-tuple-element.16.mine_ref, ...), custom_call_target="tpu_custom_call" | custom-call | tf_op jit(solution)/shard_map/attend_cache/pallas_call | solution.py:430
  41.5 4.2 %all-to-all-done.1.refs_6_ = bf16[8,2,3456]{2,1,0:T(2,128)(2,1)S(1)} async-done(((bf16[8,2,3456]{2,1,0:T(2,128)(2,1)}), bf16[8,2,3456]{2,1,0:T(2,128)(2,1)S(1)}, u32[]{:S(2)}, u32[]{:S(2)}) %all-to-all-start.1) | async-done | bytes 110624 | tf_op jit(solution)/shard_map/all_to_all | solution.py:476
  45.7 1.4 %merge.1 = bf16[128,3072]{1,0:T(8,128)(2,1)} custom-call(bf16[16,128]{1,0:T(8,128)(2,1)S(1)} %get-tuple-element.15.after_ref.pick_ref, bf16[64,3072]{1,0:T(8,128)(2,1)S(1)} %get-tuple-element.18.refs_0_, f32[16,3072]{1,0:T(8,128)S(1)} %get-tuple-element.19.refs_1_, f32[16,128]{1,0:T(8,128)S(1)} %get-tuple-element.20.after_ref.refs_2_, ...), custom_call_target="tpu_custom_call" | custom-call | tf_op jit(solution)/shard_map/merge/pallas_call | solution.py:480
Async XLA Ops:
  18.2 7.4 %collective-permute-start = (bf16[896,512]{1,0:T(8,128)(2,1)S(1)}, bf16[896,512]{1,0:T(8,128)(2,1)S(1)}, u32[]{:S(2)}, u32[]{:S(2)}) collective-permute-start(bf16[896,512]{1,0:T(8,128)(2,1)S(1)} %get-tuple-element.17), channel_id=1, source_target_pairs={{0,1},{1,0},{2,3},{3,2},{4,5},{5,4},{6,7},{7,6},{8,9},{9,8},{10,11... | collective-permute-start | bytes 2752520 | tf_op jit(solution)/shard_map/ppermute | solution.py:422
  18.7 14.0 %all-to-all-start = ((bf16[8,2,3072]{2,1,0:T(2,128)(2,1)}), bf16[8,2,3072]{2,1,0:T(2,128)(2,1)S(1)}, u32[]{:S(2)}, u32[]{:S(2)}) async-start(bf16[8,2,3072]{2,1,0:T(2,128)(2,1)} %get-tuple-element.21), calls=%async_computation | async-start | bytes 196608 | tf_op jit(solution)/shard_map/all_to_all | solution.py:402
  35.2 10.5 %all-to-all-start.1 = ((bf16[8,2,3456]{2,1,0:T(2,128)(2,1)}), bf16[8,2,3456]{2,1,0:T(2,128)(2,1)S(1)}, u32[]{:S(2)}, u32[]{:S(2)}) async-start(bf16[8,2,3456]{2,1,0:T(2,128)(2,1)} %attend_arrived.1.after_ref), calls=%async_computation.1 | async-start | bytes 221184 | tf_op jit(solution)/shard_map/all_to_all | solution.py:476

commit v7 on v6

--- a/solution.py
+++ b/solution.py
@@ -48,9 +48,7 @@
     row = jnp.max(jnp.where(chosen, local.astype(F32), -1.0), axis=1, keepdims=True)
     pick = one_hot((slots, row_count), 1, row.astype(jnp.int32))
     pick_ref[...] = pick
-    asked = jnp.dot(pick, queries_ref[...], preferred_element_type=F32).astype(BF16)
-    for k in range(sections):
-        asked_ref[k] = asked[k * CAP : (k + 1) * CAP]
+    asked_ref[...] = jnp.dot(pick, queries_ref[...], preferred_element_type=F32).astype(BF16)
 
 
 def spans(edges):
@@ -138,8 +136,8 @@
     )
     rank_col = jnp.sum(before.astype(F32), axis=1, keepdims=True).astype(jnp.int32)
     real = iota((padded, 1), 0) < requests
-    slot_col = jnp.where(real, section_col.astype(jnp.int32) * CAP + rank_col, -1)
-    return slot_col, span_col.astype(jnp.int32)
+    section_col = jnp.where(real, section_col.astype(jnp.int32), -1)
+    return section_col, rank_col, span_col.astype(jnp.int32)
 
 
 def attend_arrived(
@@ -151,13 +149,16 @@
     prompt_rows = mine_ref.shape[0] - row_count
     span_rows = prompt_rows // requests
     kv_heads = mine_ref.shape[1] // (2 * HD)
-    group = asked_ref.shape[2] // (kv_heads * HD)
-    slot_col, span_col = request_slots(target_ref, span_ref, row_count, padded)
-    slot_of = one_hot((padded, slots), 1, slot_col)
+    group = asked_ref.shape[1] // (kv_heads * HD)
+    section_col, rank_col, span_col = request_slots(target_ref, span_ref, row_count, padded)
+    slot = jnp.where(section_col >= 0, section_col * CAP + rank_col, -1)
+    slot_of = one_hot((padded, slots), 1, slot)
+    asked_slot = section_col * slots + lax.axis_index("section") * CAP + rank_col
+    asked_slot = jnp.where(section_col >= 0, asked_slot, -1)
+    asked_slot_of = one_hot((padded, sections * slots), 1, asked_slot)
     key = iota((padded, prompt_rows), 1) - iota((padded, prompt_rows), 0) * span_rows
     bias = jnp.where((key >= 0) & (key < span_col), 0.0, MASKED)
-    asked = jnp.concatenate([asked_ref[s].astype(F32) for s in range(sections)], axis=0).astype(BF16)
-    rows = jnp.dot(slot_of, asked, preferred_element_type=F32).astype(BF16)
+    rows = jnp.dot(asked_slot_of, asked_ref[...], preferred_element_type=F32).astype(BF16)
     kv = (
         mine_ref[:prompt_rows, :].astype(F32) + other_ref[:prompt_rows, :].astype(F32)
     ).astype(BF16)
@@ -394,12 +395,12 @@
         out_specs=[RESIDENT] * 2,
         out_shape=[
             pltpu.VMEM((slots, row_count), BF16),
-            pltpu.VMEM((sections, CAP, query_width), BF16),
+            jax.ShapeDtypeStruct((slots, query_width), BF16),
         ],
         compiler_params=compiler_params(16),
         name="select_queries",
     )(in_hbm(target_row), in_hbm(queries))
-    asked = lax.all_to_all(asked, "section", 0, 0)
+    asked = lax.all_gather(asked, "section", axis=0, tiled=True)
 
     edges = (0, 512, 1152, 1920, 2944, 4224, features)
     count = len(edges) - 1
@@ -419,6 +420,7 @@
         compiler_params=compiler_params(44),
         name="project",
     )(in_hbm(prompts), in_hbm(decode_hidden), in_hbm(w_kv), in_hbm(scale), in_vmem(pick))
+    theirs, asked = lax.optimization_barrier((theirs, asked))
     other = lax.ppermute(theirs, "tp", [(0, 1), (1, 0)])
 
     block = 32
@@ -451,10 +453,10 @@
             in_vmem(mine),
             in_vmem(other),
             in_vmem(pick),
-            in_vmem(after),
-        )
-
-    shares = cache_share(0, pick)
+            after,
+        )
+
+    shares = cache_share(0, in_hbm(asked))
 
     answer_width = query_width + 3 * STATS
     answers = pl.pallas_call(
@@ -469,7 +471,7 @@
         in_hbm(span_len),
         in_vmem(mine),
         in_vmem(other),
-        in_vmem(asked),
+        in_hbm(asked),
         in_vmem(shares[2]),
     )
     after = answers

time: 47.6 us -> 76.4 us (1.61)
  blocking collectives: 0 us -> 36 us
  starting transfers between devices: 10.7 us -> 5.64 us
  waiting for transfers between devices: 8.51 us -> 6.79 us
    all_gather x0 -> x1, blocking collectives: none -> 36 us  [shards(): asked = lax.all_gather(asked, 'section', axis=0, tiled=True)]
    all_to_all x1 -> x0, starting transfers between devices: 6.86 us -> none  [shards(): asked = lax.all_to_all(asked, 'section', 0, 0)]
    all_to_all x1 -> x0, waiting for transfers between devices: 4.26 us -> none  [shards(): asked = lax.all_to_all(asked, 'section', 0, 0)]
    ppermute x1, waiting for transfers between devices: 0.01 us -> 2.46 us  [shards(): other = lax.ppermute(theirs, 'tp', [(0, 1), (1, 0)])]
    all_to_all x1, starting transfers between devices: 3.37 us -> 5.57 us  [shards(): answers = lax.all_to_all(answers, 'section', 0, 0)]
  transfers between devices with their start and end apart: 3 -> 2, of which waited for: 2 -> 2; matrix products, arithmetic and copies ran while one was open for 0% -> 0% of each run, Pallas kernels for 12% -> 4%
where the time goes in v7:
time: 76.4 us; the launch traced here: 76.1 us
  blocking collectives  36 us (47%)
  Pallas kernels  27.6 us (36%)
  waiting for transfers between devices  6.79 us (9%)
  starting transfers between devices  5.64 us (7%)
    all_gather x1, blocking collectives, shards(): asked = lax.all_gather(asked, 'section', axis=0, tiled=True)  36 us
    pallas_call x1, Pallas kernels, shards(): pl.pallas_call(functools.partial(project, edges=edges, block=all_rows //...  16 us
    pallas_call x2, Pallas kernels, cache_share(): pl.pallas_call(functools.partial(attend_cache, block_rows=block, first_bl...  5.73 us
    all_to_all x1, starting transfers between devices, shards(): answers = lax.all_to_all(answers, 'section', 0, 0)  5.57 us
    all_to_all x1, waiting for transfers between devices, shards(): answers = lax.all_to_all(answers, 'section', 0, 0)  4.33 us
    pallas_call x1, Pallas kernels, shards(): pl.pallas_call(functools.partial(attend_arrived, row_count=row_count), in...  2.92 us
    ppermute x1, waiting for transfers between devices, shards(): other = lax.ppermute(theirs, 'tp', [(0, 1), (1, 0)])  2.46 us
    pallas_call x1, Pallas kernels, shards(): pl.pallas_call(select_queries, in_specs=[RESIDENT, RESIDENT], out_specs=[...  1.54 us
  transfers between devices with their start and end apart: 2, of which 2 were waited for; matrix products, arithmetic and copies ran while one was open for 0% of the time, Pallas kernels for 4%

profile of v7, /device:TPU:0, one launch (start us, length us, event | category | flops | bytes accessed | tf_op | source)
XLA Modules:
  0.0 76.1 jit_solution(2699303085686506401)
XLA Ops:
  0.0 1.5 %select_queries.1 = (bf16[16,128]{1,0:T(8,128)(2,1)S(1)}, bf16[16,3072]{1,0:T(8,128)(2,1)S(1)}) custom-call(s32[8,12]{1,0:T(8,128)} %target_ref.3, bf16[128,3072]{1,0:T(8,128)(2,1)} %queries_ref.5), custom_call_target="tpu_custom_call" | custom-call | tf_op jit(solution)/shard_map/select_queries/pallas_call | solution.py:392
  1.5 36.0 %all_gather.3.after_ref.asked_ref = bf16[128,3072]{1,0:T(8,128)(2,1)} all-gather(bf16[16,3072]{1,0:T(8,128)(2,1)S(1)} %get-tuple-element.20), channel_id=1, replica_groups=mesh['groups'=2,'section'=8,'tp'=2] {'section'}, dimensions={0}, use_global_device_ids=true | all-gather | bytes 884736 | tf_op jit(solution)/shard_map/all_gather | solution.py:403
  37.6 16.0 %project.1 = (bf16[896,512]{1,0:T(8,128)(2,1)S(1)}, bf16[896,512]{1,0:T(8,128)(2,1)S(1)}) custom-call(bf16[768,6144]{1,0:T(8,128)(2,1)} %prompts_ref.1, bf16[128,6144]{1,0:T(8,128)(2,1)} %hidden_ref.1, bf16[6144,1024]{1,0:T(8,128)(2,1)} %w_ref.1, f32[1,1024]{1,0:T(1,128)} %bitcast.2, bf16[16,128]{1,0:T(8,128)(2,1)S(1)} %get-tuple-element.17.after_ref.pick_ref), custom_call_target="tpu_custom_call" | custom-call | tf_op jit(solution)/shard_map/project/pallas_call | solution.py:407
  53.6 0.1 collective-permute-start
  53.7 2.5 %collective-permute-done.other_ref = bf16[896,512]{1,0:T(8,128)(2,1)S(1)} collective-permute-done((bf16[896,512]{1,0:T(8,128)(2,1)S(1)}, bf16[896,512]{1,0:T(8,128)(2,1)S(1)}, u32[]{:S(2)}, u32[]{:S(2)}) %collective-permute-start) | collective-permute-done | bytes 917536 | tf_op jit(solution)/shard_map/ppermute | solution.py:424
  56.1 2.9 %attend_cache.2 = (bf16[64,3072]{1,0:T(8,128)(2,1)S(1)}, f32[16,3072]{1,0:T(8,128)S(1)}, f32[16,128]{1,0:T(8,128)S(1)}) custom-call(bf16[128,3072]{1,0:T(8,128)(2,1)} %queries_ref.5, bf16[128,32,512]{2,1,0:T(8,128)(2,1)} %cache_ref.3, s32[1,128]{1,0:T(1,128)} %bitcast.3, bf16[896,512]{1,0:T(8,128)(2,1)S(1)} %get-tuple-element.18.mine_ref, ...), custom_call_target="tpu_custom_call" | custom-call | tf_op jit(solution)/shard_map/attend_cache/pallas_call | solution.py:432
  59.0 2.9 %attend_arrived.1.after_ref = bf16[8,2,3456]{2,1,0:T(2,128)(2,1)} custom-call(s32[8,12]{1,0:T(8,128)} %target_ref.3, s32[8,12]{1,0:T(8,128)} %span_ref.1, bf16[896,512]{1,0:T(8,128)(2,1)S(1)} %get-tuple-element.18.mine_ref, bf16[896,512]{1,0:T(8,128)(2,1)S(1)} %collective-permute-done.other_ref, bf16[128,3072]{1,0:T(8,128)(2,1)} %all_gather.3.after_ref.asked_ref, ...), custom_call_target="tpu_custom_call" | custom-call | tf_op jit(solution)/shard_map/attend_arrived/pallas_call | solution.py:462
  61.9 5.6 %all-to-all-start = ((bf16[8,2,3456]{2,1,0:T(2,128)(2,1)}), bf16[8,2,3456]{2,1,0:T(2,128)(2,1)S(1)}, u32[]{:S(2)}, u32[]{:S(2)}) async-start(bf16[8,2,3456]{2,1,0:T(2,128)(2,1)} %attend_arrived.1.after_ref), calls=%async_computation | async-start | bytes 221184 | tf_op jit(solution)/shard_map/all_to_all | solution.py:478
  67.5 2.9 %attend_cache.3 = (bf16[64,3072]{1,0:T(8,128)(2,1)S(1)}, f32[16,3072]{1,0:T(8,128)S(1)}, f32[16,128]{1,0:T(8,128)S(1)}) custom-call(bf16[128,3072]{1,0:T(8,128)(2,1)} %queries_ref.5, bf16[128,32,512]{2,1,0:T(8,128)(2,1)} %cache_ref.3, s32[1,128]{1,0:T(1,128)} %bitcast.4, bf16[896,512]{1,0:T(8,128)(2,1)S(1)} %get-tuple-element.18.mine_ref, ...), custom_call_target="tpu_custom_call" | custom-call | tf_op jit(solution)/shard_map/attend_cache/pallas_call | solution.py:432
  70.4 4.3 %all-to-all-done.refs_6_ = bf16[8,2,3456]{2,1,0:T(2,128)(2,1)S(1)} async-done(((bf16[8,2,3456]{2,1,0:T(2,128)(2,1)}), bf16[8,2,3456]{2,1,0:T(2,128)(2,1)S(1)}, u32[]{:S(2)}, u32[]{:S(2)}) %all-to-all-start) | async-done | bytes 110624 | tf_op jit(solution)/shard_map/all_to_all | solution.py:478
  74.7 1.4 %merge.1 = bf16[128,3072]{1,0:T(8,128)(2,1)} custom-call(bf16[16,128]{1,0:T(8,128)(2,1)S(1)} %get-tuple-element.17.after_ref.pick_ref, bf16[64,3072]{1,0:T(8,128)(2,1)S(1)} %get-tuple-element.23.refs_0_, f32[16,3072]{1,0:T(8,128)S(1)} %get-tuple-element.24.refs_1_, f32[16,128]{1,0:T(8,128)S(1)} %get-tuple-element.25.after_ref.refs_2_, ...), custom_call_target="tpu_custom_call" | custom-call | tf_op jit(solution)/shard_map/merge/pallas_call | solution.py:482
Async XLA Ops:
  53.6 2.5 %collective-permute-start = (bf16[896,512]{1,0:T(8,128)(2,1)S(1)}, bf16[896,512]{1,0:T(8,128)(2,1)S(1)}, u32[]{:S(2)}, u32[]{:S(2)}) collective-permute-start(bf16[896,512]{1,0:T(8,128)(2,1)S(1)} %get-tuple-element.21), channel_id=1, source_target_pairs={{0,1},{1,0},{2,3},{3,2},{4,5},{5,4},{6,7},{7,6},{8,9},{9,8},{10,11... | collective-permute-start | bytes 2752520 | tf_op jit(solution)/shard_map/ppermute | solution.py:424
  61.9 12.8 %all-to-all-start = ((bf16[8,2,3456]{2,1,0:T(2,128)(2,1)}), bf16[8,2,3456]{2,1,0:T(2,128)(2,1)S(1)}, u32[]{:S(2)}, u32[]{:S(2)}) async-start(bf16[8,2,3456]{2,1,0:T(2,128)(2,1)} %attend_arrived.1.after_ref), calls=%async_computation | async-start | bytes 221184 | tf_op jit(solution)/shard_map/all_to_all | solution.py:478

commit v8 on v6

--- a/solution.py
+++ b/solution.py
@@ -143,7 +143,7 @@
 
 
 def attend_arrived(
-    target_ref, span_ref, mine_ref, other_ref, asked_ref, after_ref, out_ref, *, row_count
+    target_ref, span_ref, mine_ref, other_ref, asked_ref, out_ref, *, row_count
 ):
     sections, requests = target_ref.shape
     slots = sections * CAP
@@ -419,10 +419,11 @@
         compiler_params=compiler_params(44),
         name="project",
     )(in_hbm(prompts), in_hbm(decode_hidden), in_hbm(w_kv), in_hbm(scale), in_vmem(pick))
+    theirs, asked = lax.optimization_barrier((theirs, asked))
     other = lax.ppermute(theirs, "tp", [(0, 1), (1, 0)])
 
     block = 32
-    calls = 2
+    calls = 1
     call_rows = row_count // calls
 
     def cache_share(call, after):
@@ -454,12 +455,10 @@
             in_vmem(after),
         )
 
-    shares = cache_share(0, pick)
-
     answer_width = query_width + 3 * STATS
     answers = pl.pallas_call(
         functools.partial(attend_arrived, row_count=row_count),
-        in_specs=[RESIDENT] * 5 + [REMAINS],
+        in_specs=[RESIDENT] * 5,
         out_specs=RESIDENT,
         out_shape=pltpu.VMEM((sections, CAP, answer_width), BF16),
         compiler_params=compiler_params(24),
@@ -470,12 +469,12 @@
         in_vmem(mine),
         in_vmem(other),
         in_vmem(asked),
-        in_vmem(shares[2]),
     )
     after = answers
     answers = lax.all_to_all(answers, "section", 0, 0)
-    for call in range(1, calls):
-        shares = [*shares, *cache_share(call, after)]
+    shares = []
+    for call in range(calls):
+        shares += cache_share(call, after)
 
     return pl.pallas_call(
         merge,

time: 47.6 us -> 45.6 us (0.958)
  waiting for transfers between devices: 8.51 us -> 4.65 us
  starting transfers between devices: 10.7 us -> 13.3 us
  Pallas kernels: 27.8 us -> 27.1 us
    all_to_all x1, waiting for transfers between devices: 4.26 us -> 0.01 us  [shards(): asked = lax.all_to_all(asked, 'section', 0, 0)]
    all_to_all x1, starting transfers between devices: 3.37 us -> 5.98 us  [shards(): answers = lax.all_to_all(answers, 'section', 0, 0)]
    ppermute x1, waiting for transfers between devices: 0.01 us -> 2.46 us  [shards(): other = lax.ppermute(theirs, 'tp', [(0, 1), (1, 0)])]
    all_to_all x1, waiting for transfers between devices: 4.25 us -> 2.19 us  [shards(): answers = lax.all_to_all(answers, 'section', 0, 0)]
    pallas_call x2 -> x1, Pallas kernels: 5.76 us -> 5.01 us  [cache_share(): pl.pallas_call(functools.partial(attend_cache, block_rows=block, first_bl...]
  transfers between devices with their start and end apart: 3 -> 3, of which waited for: 2 -> 2; matrix products, arithmetic and copies ran while one was open for 0% -> 0% of each run, Pallas kernels for 12% -> 47%
where the time goes in v8:
time: 45.6 us; the launch traced here: 45.1 us
  Pallas kernels  27.1 us (59%)
  starting transfers between devices  13.3 us (29%)
  waiting for transfers between devices  4.65 us (10%)
    pallas_call x1, Pallas kernels, shards(): pl.pallas_call(functools.partial(project, edges=edges, block=all_rows //...  16 us
    all_to_all x1, starting transfers between devices, shards(): asked = lax.all_to_all(asked, 'section', 0, 0)  7.28 us
    all_to_all x1, starting transfers between devices, shards(): answers = lax.all_to_all(answers, 'section', 0, 0)  5.98 us
    pallas_call x1, Pallas kernels, cache_share(): pl.pallas_call(functools.partial(attend_cache, block_rows=block, first_bl...  5.01 us
    ppermute x1, waiting for transfers between devices, shards(): other = lax.ppermute(theirs, 'tp', [(0, 1), (1, 0)])  2.46 us
    pallas_call x1, Pallas kernels, shards(): pl.pallas_call(functools.partial(attend_arrived, row_count=row_count), in...  2.46 us
    pallas_call x1, Pallas kernels, shards(): pl.pallas_call(select_queries, in_specs=[RESIDENT, RESIDENT], out_specs=[...  2.2 us
    all_to_all x1, waiting for transfers between devices, shards(): answers = lax.all_to_all(answers, 'section', 0, 0)  2.19 us
  transfers between devices with their start and end apart: 3, of which 2 were waited for; matrix products, arithmetic and copies ran while one was open for 0% of the time, Pallas kernels for 47%

profile of v8, /device:TPU:0, one launch (start us, length us, event | category | flops | bytes accessed | tf_op | source)
XLA Modules:
  0.0 45.1 jit_solution(6956017391682158185)
XLA Ops:
  0.0 2.2 %select_queries.1 = (bf16[16,128]{1,0:T(8,128)(2,1)S(1)}, bf16[8,2,3072]{2,1,0:T(2,128)(2,1)}) custom-call(s32[8,12]{1,0:T(8,128)} %target_ref.3, bf16[128,3072]{1,0:T(8,128)(2,1)} %queries_ref.3), custom_call_target="tpu_custom_call" | custom-call | tf_op jit(solution)/shard_map/select_queries/pallas_call | solution.py:391
  2.2 7.3 %all-to-all-start = ((bf16[8,2,3072]{2,1,0:T(2,128)(2,1)}), bf16[8,2,3072]{2,1,0:T(2,128)(2,1)S(1)}, u32[]{:S(2)}, u32[]{:S(2)}) async-start(bf16[8,2,3072]{2,1,0:T(2,128)(2,1)} %get-tuple-element.17), calls=%async_computation | async-start | bytes 196608 | tf_op jit(solution)/shard_map/all_to_all | solution.py:402
  9.5 16.0 %project.1 = (bf16[896,512]{1,0:T(8,128)(2,1)S(1)}, bf16[896,512]{1,0:T(8,128)(2,1)S(1)}) custom-call(bf16[768,6144]{1,0:T(8,128)(2,1)} %prompts_ref.1, bf16[128,6144]{1,0:T(8,128)(2,1)} %hidden_ref.1, bf16[6144,1024]{1,0:T(8,128)(2,1)} %w_ref.1, f32[1,1024]{1,0:T(1,128)} %bitcast.2, bf16[16,128]{1,0:T(8,128)(2,1)S(1)} %get-tuple-element.14.after_ref.pick_ref), custom_call_target="tpu_custom_call" | custom-call | tf_op jit(solution)/shard_map/project/pallas_call | solution.py:406
  25.5 0.0 all-to-all-done.asked_ref
  25.5 0.1 collective-permute-start
  25.6 2.5 %collective-permute-done.other_ref = bf16[896,512]{1,0:T(8,128)(2,1)S(1)} collective-permute-done((bf16[896,512]{1,0:T(8,128)(2,1)S(1)}, bf16[896,512]{1,0:T(8,128)(2,1)S(1)}, u32[]{:S(2)}, u32[]{:S(2)}) %collective-permute-start) | collective-permute-done | bytes 917536 | tf_op jit(solution)/shard_map/ppermute | solution.py:423
  28.1 2.5 %attend_arrived.1.after_ref = bf16[8,2,3456]{2,1,0:T(2,128)(2,1)} custom-call(s32[8,12]{1,0:T(8,128)} %target_ref.3, s32[8,12]{1,0:T(8,128)} %span_ref.1, bf16[896,512]{1,0:T(8,128)(2,1)S(1)} %get-tuple-element.15.mine_ref, bf16[896,512]{1,0:T(8,128)(2,1)S(1)} %collective-permute-done.other_ref, bf16[8,2,3072]{2,1,0:T(2,128)(2,1)S(1)} %all-to-all-done.asked_ref), custom_call_target="tpu_custom_call" | custom-call | tf_op jit(solution)/shard_map/attend_arrived/pallas_call | solution.py:459
  30.5 6.0 %all-to-all-start.1 = ((bf16[8,2,3456]{2,1,0:T(2,128)(2,1)}), bf16[8,2,3456]{2,1,0:T(2,128)(2,1)S(1)}, u32[]{:S(2)}, u32[]{:S(2)}) async-start(bf16[8,2,3456]{2,1,0:T(2,128)(2,1)} %attend_arrived.1.after_ref), calls=%async_computation.1 | async-start | bytes 221184 | tf_op jit(solution)/shard_map/all_to_all | solution.py:474
  36.5 5.0 %attend_cache.1 = (bf16[128,3072]{1,0:T(8,128)(2,1)S(1)}, f32[16,3072]{1,0:T(8,128)S(1)}, f32[16,128]{1,0:T(8,128)S(1)}) custom-call(bf16[128,3072]{1,0:T(8,128)(2,1)} %queries_ref.3, bf16[128,32,512]{2,1,0:T(8,128)(2,1)} %cache_ref.1, s32[1,128]{1,0:T(1,128)} %bitcast.3, bf16[896,512]{1,0:T(8,128)(2,1)S(1)} %get-tuple-element.15.mine_ref, ...), custom_call_target="tpu_custom_call" | custom-call | tf_op jit(solution)/shard_map/attend_cache/pallas_call | solution.py:431
  41.5 2.2 %all-to-all-done.1.refs_3_ = bf16[8,2,3456]{2,1,0:T(2,128)(2,1)S(1)} async-done(((bf16[8,2,3456]{2,1,0:T(2,128)(2,1)}), bf16[8,2,3456]{2,1,0:T(2,128)(2,1)S(1)}, u32[]{:S(2)}, u32[]{:S(2)}) %all-to-all-start.1) | async-done | bytes 110624 | tf_op jit(solution)/shard_map/all_to_all | solution.py:474
  43.7 1.4 %merge.1 = bf16[128,3072]{1,0:T(8,128)(2,1)} custom-call(bf16[16,128]{1,0:T(8,128)(2,1)S(1)} %get-tuple-element.14.after_ref.pick_ref, bf16[128,3072]{1,0:T(8,128)(2,1)S(1)} %get-tuple-element.20.refs_0_, f32[16,3072]{1,0:T(8,128)S(1)} %get-tuple-element.21.refs_1_, f32[16,128]{1,0:T(8,128)S(1)} %get-tuple-element.22.refs_2_, ...), custom_call_target="tpu_custom_call" | custom-call | tf_op jit(solution)/shard_map/merge/pallas_call | solution.py:479
Async XLA Ops:
  2.2 23.3 %all-to-all-start = ((bf16[8,2,3072]{2,1,0:T(2,128)(2,1)}), bf16[8,2,3072]{2,1,0:T(2,128)(2,1)S(1)}, u32[]{:S(2)}, u32[]{:S(2)}) async-start(bf16[8,2,3072]{2,1,0:T(2,128)(2,1)} %get-tuple-element.17), calls=%async_computation | async-start | bytes 196608 | tf_op jit(solution)/shard_map/all_to_all | solution.py:402
  25.5 2.5 %collective-permute-start = (bf16[896,512]{1,0:T(8,128)(2,1)S(1)}, bf16[896,512]{1,0:T(8,128)(2,1)S(1)}, u32[]{:S(2)}, u32[]{:S(2)}) collective-permute-start(bf16[896,512]{1,0:T(8,128)(2,1)S(1)} %get-tuple-element.18), channel_id=1, source_target_pairs={{0,1},{1,0},{2,3},{3,2},{4,5},{5,4},{6,7},{7,6},{8,9},{9,8},{10,11... | collective-permute-start | bytes 2752520 | tf_op jit(solution)/shard_map/ppermute | solution.py:423
  30.5 13.2 %all-to-all-start.1 = ((bf16[8,2,3456]{2,1,0:T(2,128)(2,1)}), bf16[8,2,3456]{2,1,0:T(2,128)(2,1)S(1)}, u32[]{:S(2)}, u32[]{:S(2)}) async-start(bf16[8,2,3456]{2,1,0:T(2,128)(2,1)} %attend_arrived.1.after_ref), calls=%async_computation.1 | async-start | bytes 221184 | tf_op jit(solution)/shard_map/all_to_all | solution.py:474

commit v9 on v8

--- a/solution.py
+++ b/solution.py
@@ -12,6 +12,7 @@
 CAP = 2
 STATS = 128
 MASKED = -1e30
+PITCH = 8
 LOG2_SCALE = HD ** (-0.5) * math.log2(math.e)
 F32 = jnp.float32
 BF16 = jnp.bfloat16
@@ -26,16 +27,15 @@
     return (iota(shape, dim) == index).astype(F32).astype(BF16)
 
 
-def select_queries(target_ref, queries_ref, pick_ref, asked_ref):
+def pick_rows(target_ref, row_count, pitch):
     sections, requests = target_ref.shape
-    row_count = queries_ref.shape[0]
-    slots = sections * CAP
+    shape = (sections * pitch, requests)
     position = lax.axis_index("section")
-    slot_id = iota((slots, requests), 0)
-    table = jnp.zeros((slots, requests), jnp.int32)
-    for k in range(sections):
-        mine = (slot_id >= k * CAP) & (slot_id < (k + 1) * CAP)
-        table = jnp.where(mine, target_ref[k : k + 1, :], table)
+    slot_id = iota(shape, 0)
+    table = jnp.zeros(shape, jnp.int32)
+    for s in range(sections):
+        mine = (slot_id >= s * pitch) & (slot_id < (s + 1) * pitch)
+        table = jnp.where(mine, target_ref[s : s + 1, :], table)
     local = table - position * row_count
     here = (local >= 0) & (local < row_count)
     square = (requests, requests)
@@ -44,13 +44,44 @@
         (iota(square, 0) < iota(square, 1)).astype(F32).astype(BF16),
         preferred_element_type=F32,
     )
-    chosen = here & (earlier == lax.rem(slot_id, CAP).astype(F32))
+    chosen = here & (earlier == lax.rem(slot_id, pitch).astype(F32))
     row = jnp.max(jnp.where(chosen, local.astype(F32), -1.0), axis=1, keepdims=True)
-    pick = one_hot((slots, row_count), 1, row.astype(jnp.int32))
-    pick_ref[...] = pick
-    asked = jnp.dot(pick, queries_ref[...], preferred_element_type=F32).astype(BF16)
-    for k in range(sections):
-        asked_ref[k] = asked[k * CAP : (k + 1) * CAP]
+    return one_hot((shape[0], row_count), 1, row.astype(jnp.int32))
+
+
+def select_queries(
+    target_ref,
+    queries_ref,
+    prompts_ref,
+    hidden_ref,
+    w_ref,
+    pick_ref,
+    asked_ref,
+    rows_ref,
+    w_head_ref,
+    queries_here_ref,
+    sems,
+):
+    sections = target_ref.shape[0]
+    row_count = queries_ref.shape[0]
+    prompt_rows = prompts_ref.shape[0]
+    depth = w_head_ref.shape[0]
+    copies = [
+        pltpu.make_async_copy(queries_ref, queries_here_ref, sems.at[0]),
+        pltpu.make_async_copy(w_ref.at[:depth, :], w_head_ref, sems.at[1]),
+        pltpu.make_async_copy(prompts_ref.at[:, :depth], rows_ref.at[:prompt_rows, :], sems.at[2]),
+        pltpu.make_async_copy(hidden_ref.at[:, :depth], rows_ref.at[prompt_rows:, :], sems.at[3]),
+    ]
+    for copy in copies:
+        copy.start()
+    pick = pick_rows(target_ref, row_count, PITCH)
+    pick_ref[...] = pick_rows(target_ref, row_count, CAP)
+    copies[0].wait()
+    asked = jnp.dot(pick, queries_here_ref[...], preferred_element_type=F32)
+    for s in range(sections):
+        asked_ref[s] = asked[s * PITCH : s * PITCH + CAP].astype(BF16)
+    for copy in copies[1:]:
+        copy.wait()
 
 
 def spans(edges):
@@ -58,11 +89,12 @@
 
 
 def project(
+    rows_head_ref,
+    w_head_ref,
     prompts_ref,
     hidden_ref,
     w_ref,
     scale_ref,
-    after_ref,
     mine_ref,
     theirs_ref,
     rows_ref,
@@ -77,39 +109,41 @@
 ):
     prompt_rows = prompts_ref.shape[0]
     width = mine_ref.shape[1]
+    head = w_head_ref.shape[0]
     chunks = spans(edges)
     waits = []
     for c, at in enumerate(chunks):
+        there = slice(head + at.start, head + at.stop)
         copies = [
-            pltpu.make_async_copy(w_ref.at[at, :], w_here_ref.at[at, :], w_sems.at[c]),
+            pltpu.make_async_copy(w_ref.at[there, :], w_here_ref.at[at, :], w_sems.at[c]),
             pltpu.make_async_copy(
-                prompts_ref.at[:, at], rows_ref.at[:prompt_rows, at], row_sems.at[c]
+                prompts_ref.at[:, there], rows_ref.at[:prompt_rows, at], row_sems.at[c]
             ),
             pltpu.make_async_copy(
-                hidden_ref.at[:, at], rows_ref.at[prompt_rows:, at], hidden_sems.at[c]
+                hidden_ref.at[:, there], rows_ref.at[prompt_rows:, at], hidden_sems.at[c]
             ),
         ]
         for copy in copies:
             copy.start()
         waits.append(copies)
-    for c, at in enumerate(chunks[:-1]):
+    first = lax.axis_index("tp") == 0
+    blocks = spans(range(0, total_ref.shape[0] + 1, block))
+    halves = (slice(0, width), slice(width, 2 * width))
+    for m in blocks:
+        for n in halves:
+            total_ref[m, n] = jnp.dot(
+                rows_head_ref[m, :], w_head_ref[:, n], preferred_element_type=F32
+            )
+    for c, at in enumerate(chunks):
         for copy in waits[c]:
             copy.wait()
-        for m in spans(range(0, rows_ref.shape[0] + 1, block)):
-            part = jnp.dot(rows_ref[m, at], w_here_ref[at, :], preferred_element_type=F32)
-            if c == 0:
-                total_ref[m, :] = part
-            else:
-                total_ref[m, :] += part
-    for copy in waits[-1]:
-        copy.wait()
-    first = lax.axis_index("tp") == 0
-    for m in spans(range(0, rows_ref.shape[0] + 1, block)):
-        part = jnp.dot(
-            rows_ref[m, chunks[-1]], w_here_ref[chunks[-1], :], preferred_element_type=F32
-        )
-        term = ((total_ref[m, :] + part) * scale_ref[...]).astype(BF16)
-        low, high = term[:, :width], term[:, width:]
+        for m in blocks:
+            for n in halves:
+                total_ref[m, n] += jnp.dot(
+                    rows_ref[m, at], w_here_ref[at, n], preferred_element_type=F32
+                )
+    for m in blocks:
+        low, high = ((total_ref[m, n] * scale_ref[:, n]).astype(BF16) for n in halves)
         mine_ref[m, :] = jnp.where(first, low, high)
         theirs_ref[m, :] = jnp.where(first, high, low)
 
@@ -138,26 +172,37 @@
     )
     rank_col = jnp.sum(before.astype(F32), axis=1, keepdims=True).astype(jnp.int32)
     real = iota((padded, 1), 0) < requests
-    slot_col = jnp.where(real, section_col.astype(jnp.int32) * CAP + rank_col, -1)
-    return slot_col, span_col.astype(jnp.int32)
-
-
-def attend_arrived(
-    target_ref, span_ref, mine_ref, other_ref, asked_ref, out_ref, *, row_count
+    section_col = jnp.where(real, section_col.astype(jnp.int32), -1)
+    return section_col, rank_col, span_col.astype(jnp.int32)
+
+
+def prepare_arrived(
+    target_ref, span_ref, asked_ref, rows_ref, slot_of_ref, bias_ref, *, row_count
 ):
     sections, requests = target_ref.shape
-    slots = sections * CAP
-    padded = -(-requests // 16) * 16
-    prompt_rows = mine_ref.shape[0] - row_count
+    padded, prompt_rows = bias_ref.shape
     span_rows = prompt_rows // requests
+    section_col, rank_col, span_col = request_slots(target_ref, span_ref, row_count, padded)
+    slot = jnp.where(section_col >= 0, section_col * PITCH + rank_col, -1)
+    slot_of_ref[...] = one_hot((padded, sections * PITCH), 1, slot)
+    slot = jnp.where(section_col >= 0, section_col * CAP + rank_col, -1)
+    asked = jnp.concatenate([asked_ref[s].astype(F32) for s in range(sections)], axis=0)
+    rows_ref[...] = jnp.dot(
+        one_hot((padded, sections * CAP), 1, slot),
+        asked.astype(BF16),
+        preferred_element_type=F32,
+    ).astype(BF16)
+    key = iota((padded, prompt_rows), 1) - iota((padded, prompt_rows), 0) * span_rows
+    bias_ref[...] = jnp.where((key >= 0) & (key < span_col), 0.0, MASKED)
+
+
+def attend_arrived(rows_ref, slot_of_ref, bias_ref, mine_ref, other_ref, out_ref):
+    padded, prompt_rows = bias_ref.shape
     kv_heads = mine_ref.shape[1] // (2 * HD)
-    group = asked_ref.shape[2] // (kv_heads * HD)
-    slot_col, span_col = request_slots(target_ref, span_ref, row_count, padded)
-    slot_of = one_hot((padded, slots), 1, slot_col)
-    key = iota((padded, prompt_rows), 1) - iota((padded, prompt_rows), 0) * span_rows
-    bias = jnp.where((key >= 0) & (key < span_col), 0.0, MASKED)
-    asked = jnp.concatenate([asked_ref[s].astype(F32) for s in range(sections)], axis=0).astype(BF16)
-    rows = jnp.dot(slot_of, asked, preferred_element_type=F32).astype(BF16)
+    group = rows_ref.shape[1] // (kv_heads * HD)
+    rows = rows_ref[...]
+    slot_of = slot_of_ref[...]
+    bias = bias_ref[...]
     kv = (
         mine_ref[:prompt_rows, :].astype(F32) + other_ref[:prompt_rows, :].astype(F32)
     ).astype(BF16)
@@ -194,9 +239,9 @@
             pieces.append(values[i])
             lse = jnp.where(lane == h * group + i, head_lse[i], lse)
     result = jnp.concatenate(pieces + list(split_bf16(lse)), axis=1).astype(BF16)
-    answers = lax.dot_general(slot_of, result, TRANSPOSED, preferred_element_type=F32).astype(BF16)
-    for s in range(sections):
-        out_ref[s] = answers[s * CAP : (s + 1) * CAP]
+    answers = lax.dot_general(slot_of, result, TRANSPOSED, preferred_element_type=F32)
+    for s in range(out_ref.shape[0]):
+        out_ref[s] = answers[s * PITCH : s * PITCH + CAP].astype(BF16)
 
 
 def attend_cache(
@@ -388,28 +433,33 @@
     scale = kv_scale.reshape(1, -1)
     lengths = cache_len.reshape(1, -1)
 
-    pick, asked = pl.pallas_call(
+    depth = 512
+    pick, asked, rows_head, w_head = pl.pallas_call(
         select_queries,
-        in_specs=[RESIDENT, RESIDENT],
-        out_specs=[RESIDENT] * 2,
+        in_specs=[RESIDENT] + [REMAINS] * 4,
+        out_specs=[RESIDENT] * 4,
         out_shape=[
             pltpu.VMEM((slots, row_count), BF16),
-            pltpu.VMEM((sections, CAP, query_width), BF16),
+            jax.ShapeDtypeStruct((sections, CAP, query_width), BF16),
+            pltpu.VMEM((all_rows, depth), BF16),
+            pltpu.VMEM((depth, w_kv.shape[1]), BF16),
         ],
+        scratch_shapes=[pltpu.VMEM(queries.shape, BF16), pltpu.SemaphoreType.DMA((4,))],
         compiler_params=compiler_params(16),
         name="select_queries",
-    )(in_hbm(target_row), in_hbm(queries))
+    )(in_hbm(target_row), in_hbm(queries), in_hbm(prompts), in_hbm(decode_hidden), in_hbm(w_kv))
     asked = lax.all_to_all(asked, "section", 0, 0)
 
-    edges = (0, 512, 1152, 1920, 2944, 4224, features)
+    rest = features - depth
+    edges = (0, 512, 1408, 2816, 4096, rest)
     count = len(edges) - 1
     mine, theirs = pl.pallas_call(
         functools.partial(project, edges=edges, block=all_rows // 2),
-        in_specs=[REMAINS] * 3 + [RESIDENT, REMAINS],
+        in_specs=[RESIDENT] * 2 + [REMAINS] * 3 + [RESIDENT],
         out_specs=[RESIDENT, RESIDENT],
         scratch_shapes=[
-            pltpu.VMEM((all_rows, features), BF16),
-            pltpu.VMEM(w_kv.shape, BF16),
+            pltpu.VMEM((all_rows, rest), BF16),
+            pltpu.VMEM((rest, w_kv.shape[1]), BF16),
             pltpu.VMEM((all_rows, w_kv.shape[1]), F32),
             pltpu.SemaphoreType.DMA((count,)),
             pltpu.SemaphoreType.DMA((count,)),
@@ -418,7 +468,14 @@
         out_shape=[pltpu.VMEM((all_rows, local_width), BF16)] * 2,
         compiler_params=compiler_params(44),
         name="project",
-    )(in_hbm(prompts), in_hbm(decode_hidden), in_hbm(w_kv), in_hbm(scale), in_vmem(pick))
+    )(
+        in_vmem(rows_head),
+        in_vmem(w_head),
+        in_hbm(prompts),
+        in_hbm(decode_hidden),
+        in_hbm(w_kv),
+        in_hbm(scale),
+    )
     theirs, asked = lax.optimization_barrier((theirs, asked))
     other = lax.ppermute(theirs, "tp", [(0, 1), (1, 0)])
 
@@ -452,24 +509,31 @@
             in_vmem(mine),
             in_vmem(other),
             in_vmem(pick),
-            in_vmem(after),
-        )
-
+            after,
+        )
+
+    padded = -(-span_len.shape[1] // 16) * 16
+    prepared = pl.pallas_call(
+        functools.partial(prepare_arrived, row_count=row_count),
+        in_specs=[RESIDENT] * 3,
+        out_specs=[RESIDENT] * 3,
+        out_shape=[
+            pltpu.VMEM((padded, query_width), BF16),
+            pltpu.VMEM((padded, sections * PITCH), BF16),
+            pltpu.VMEM((padded, prompt_rows), F32),
+        ],
+        compiler_params=compiler_params(16),
+        name="prepare_arrived",
+    )(in_hbm(target_row), in_hbm(span_len), in_vmem(asked))
     answer_width = query_width + 3 * STATS
     answers = pl.pallas_call(
-        functools.partial(attend_arrived, row_count=row_count),
+        attend_arrived,
         in_specs=[RESIDENT] * 5,
         out_specs=RESIDENT,
-        out_shape=pltpu.VMEM((sections, CAP, answer_width), BF16),
+        out_shape=jax.ShapeDtypeStruct((sections, CAP, answer_width), BF16),
         compiler_params=compiler_params(24),
         name="attend_arrived",
-    )(
-        in_hbm(target_row),
-        in_hbm(span_len),
-        in_vmem(mine),
-        in_vmem(other),
-        in_vmem(asked),
-    )
+    )(*map(in_vmem, (*prepared, mine, other)))
     after = answers
     answers = lax.all_to_all(answers, "section", 0, 0)
     shares = []

time: 45.6 us -> 46.6 us (1.022)
  local copies, waits for them, and re-layouts: 0 us -> 0.93 us
  Pallas kernels: 27.1 us -> 28 us
  waiting for transfers between devices: 4.65 us -> 3.84 us
    pallas_call x2 -> x3, Pallas kernels: 4.66 us -> 5.62 us  [the longest x1 3.07 us: shards(): pl.pallas_call(select_queries, in_specs=[RESIDENT] + [REMAINS] * 4, out_s...]
    unnamed x0 -> x2, local copies, waits for them, and re-layouts: none -> 0.93 us
    ppermute x1, waiting for transfers between devices: 2.46 us -> 1.65 us  [shards(): other = lax.ppermute(theirs, 'tp', [(0, 1), (1, 0)])]
  transfers between devices with their start and end apart: 3 -> 3, of which waited for: 2 -> 2; matrix products, arithmetic and copies ran while one was open for 0% -> 0% of each run, Pallas kernels for 47% -> 48%
where the time goes in v9:
time: 46.6 us; the launch traced here: 46.1 us
  Pallas kernels  28 us (60%)
  starting transfers between devices  13.3 us (29%)
  waiting for transfers between devices  3.84 us (8%)
  local copies, waits for them, and re-layouts  0.93 us (2%)
    pallas_call x1, Pallas kernels, shards(): pl.pallas_call(functools.partial(project, edges=edges, block=all_rows //...  16 us
    all_to_all x1, starting transfers between devices, shards(): asked = lax.all_to_all(asked, 'section', 0, 0)  7.29 us
    all_to_all x1, starting transfers between devices, shards(): answers = lax.all_to_all(answers, 'section', 0, 0)  6 us
    pallas_call x1, Pallas kernels, cache_share(): pl.pallas_call(functools.partial(attend_cache, block_rows=block, first_bl...  5.01 us
    pallas_call x1, Pallas kernels, shards(): pl.pallas_call(select_queries, in_specs=[RESIDENT] + [REMAINS] * 4, out_s...  3.07 us
    all_to_all x1, waiting for transfers between devices, shards(): answers = lax.all_to_all(answers, 'section', 0, 0)  2.19 us
    ppermute x1, waiting for transfers between devices, shards(): other = lax.ppermute(theirs, 'tp', [(0, 1), (1, 0)])  1.65 us
    pallas_call x1, Pallas kernels, shards(): pl.pallas_call(attend_arrived, in_specs=[RESIDENT] * 5, out_specs=RESIDEN...  1.53 us
  transfers between devices with their start and end apart: 3, of which 2 were waited for; matrix products, arithmetic and copies ran while one was open for 0% of the time, Pallas kernels for 48%

profile of v9, /device:TPU:0, one launch (start us, length us, event | category | flops | bytes accessed | tf_op | source)
XLA Modules:
  0.0 46.1 jit_solution(14260338237109221440)
XLA Ops:
  0.0 3.1 %select_queries.1 = (bf16[16,128]{1,0:T(8,128)(2,1)S(1)}, bf16[8,2,3072]{2,1,0:T(2,128)(2,1)}, bf16[896,512]{1,0:T(8,128)(2,1)S(1)}, bf16[512,1024]{1,0:T(8,128)(2,1)S(1)}) custom-call(s32[8,12]{1,0:T(8,128)} %target_ref.3, bf16[128,3072]{1,0:T(8,128)(2,1)} %queries_ref.3, bf16[768,6144]{1,0:T(8,128)(2,1)} %prompts_ref.3, bf16[128,6144]{1,0:T(8,128)(2,1)} %hidden_ref.3, ...), custom_call_target="tpu_custom_call" | custom-call | tf_op jit(solution)/shard_map/select_queries/pallas_call | solution.py:437
  3.1 7.3 %all-to-all-start = ((bf16[8,2,3072]{2,1,0:T(2,128)(2,1)}), bf16[8,2,3072]{2,1,0:T(2,128)(2,1)S(1)}, u32[]{:S(2)}, u32[]{:S(2)}) async-start(bf16[8,2,3072]{2,1,0:T(2,128)(2,1)} %get-tuple-element.24), calls=%async_computation | async-start | bytes 196608 | tf_op jit(solution)/shard_map/all_to_all | solution.py:451
  10.4 16.0 %project.1 = (bf16[896,512]{1,0:T(8,128)(2,1)S(1)}, bf16[896,512]{1,0:T(8,128)(2,1)S(1)}) custom-call(bf16[896,512]{1,0:T(8,128)(2,1)S(1)} %get-tuple-element.20.rows_head_ref, bf16[512,1024]{1,0:T(8,128)(2,1)S(1)} %get-tuple-element.21.w_head_ref, bf16[768,6144]{1,0:T(8,128)(2,1)} %prompts_ref.3, bf16[128,6144]{1,0:T(8,128)(2,1)} %hidden_ref.3, ...), custom_call_target="tpu_custom_call" | custom-call | tf_op jit(solution)/shard_map/project/pallas_call | solution.py:456
  26.4 0.0 copy-start
  26.4 0.9 %copy-done = bf16[896,512]{1,0:T(8,128)(2,1)} copy-done((bf16[896,512]{1,0:T(8,128)(2,1)}, bf16[896,512]{1,0:T(8,128)(2,1)S(1)}, u32[]{:S(2)}) %copy-start) | copy-done | bytes 917528
  27.3 0.0 all-to-all-done.asked_ref
  27.3 0.0 collective-permute-start
  27.3 1.0 %prepare_arrived.1 = (bf16[16,3072]{1,0:T(8,128)(2,1)S(1)}, bf16[16,64]{1,0:T(8,128)(2,1)S(1)}, f32[16,768]{1,0:T(8,128)S(1)}) custom-call(s32[8,12]{1,0:T(8,128)} %target_ref.3, s32[8,12]{1,0:T(8,128)} %span_ref.1, bf16[8,2,3072]{2,1,0:T(2,128)(2,1)S(1)} %all-to-all-done.asked_ref), custom_call_target="tpu_custom_call" | custom-call | tf_op jit(solution)/shard_map/prepare_arrived/pallas_call | solution.py:516
  28.3 1.7 %collective-permute-done.other_ref = bf16[896,512]{1,0:T(8,128)(2,1)S(1)} collective-permute-done((bf16[896,512]{1,0:T(8,128)(2,1)}, bf16[896,512]{1,0:T(8,128)(2,1)S(1)}, u32[]{:S(2)}, u32[]{:S(2)}) %collective-permute-start) | collective-permute-done | bytes 917536 | tf_op jit(solution)/shard_map/ppermute | solution.py:480
  30.0 1.5 %attend_arrived.1.after_ref = bf16[8,2,3456]{2,1,0:T(2,128)(2,1)} custom-call(bf16[16,3072]{1,0:T(8,128)(2,1)S(1)} %get-tuple-element.27.rows_ref, bf16[16,64]{1,0:T(8,128)(2,1)S(1)} %get-tuple-element.28.slot_of_ref, f32[16,768]{1,0:T(8,128)S(1)} %get-tuple-element.29.bias_ref, bf16[896,512]{1,0:T(8,128)(2,1)S(1)} %get-tuple-element.22.mine_ref, ...), custom_call_target="tpu_custom_call" | custom-call | tf_op jit(solution)/shard_map/attend_arrived/pallas_call | solution.py:529
  31.5 6.0 %all-to-all-start.1 = ((bf16[8,2,3456]{2,1,0:T(2,128)(2,1)}), bf16[8,2,3456]{2,1,0:T(2,128)(2,1)S(1)}, u32[]{:S(2)}, u32[]{:S(2)}) async-start(bf16[8,2,3456]{2,1,0:T(2,128)(2,1)} %attend_arrived.1.after_ref), calls=%async_computation.1 | async-start | bytes 221184 | tf_op jit(solution)/shard_map/all_to_all | solution.py:538
  37.5 5.0 %attend_cache.1 = (bf16[128,3072]{1,0:T(8,128)(2,1)S(1)}, f32[16,3072]{1,0:T(8,128)S(1)}, f32[16,128]{1,0:T(8,128)S(1)}) custom-call(bf16[128,3072]{1,0:T(8,128)(2,1)} %queries_ref.3, bf16[128,32,512]{2,1,0:T(8,128)(2,1)} %cache_ref.1, s32[1,128]{1,0:T(1,128)} %bitcast.3, bf16[896,512]{1,0:T(8,128)(2,1)S(1)} %get-tuple-element.22.mine_ref, ...), custom_call_target="tpu_custom_call" | custom-call | tf_op jit(solution)/shard_map/attend_cache/pallas_call | solution.py:488
  42.5 2.2 %all-to-all-done.1.refs_3_ = bf16[8,2,3456]{2,1,0:T(2,128)(2,1)S(1)} async-done(((bf16[8,2,3456]{2,1,0:T(2,128)(2,1)}), bf16[8,2,3456]{2,1,0:T(2,128)(2,1)S(1)}, u32[]{:S(2)}, u32[]{:S(2)}) %all-to-all-start.1) | async-done | bytes 110624 | tf_op jit(solution)/shard_map/all_to_all | solution.py:538
  44.7 1.4 %merge.1 = bf16[128,3072]{1,0:T(8,128)(2,1)} custom-call(bf16[16,128]{1,0:T(8,128)(2,1)S(1)} %get-tuple-element.19.pick_ref, bf16[128,3072]{1,0:T(8,128)(2,1)S(1)} %get-tuple-element.30.refs_0_, f32[16,3072]{1,0:T(8,128)S(1)} %get-tuple-element.31.refs_1_, f32[16,128]{1,0:T(8,128)S(1)} %get-tuple-element.32.refs_2_, ...), custom_call_target="tpu_custom_call" | custom-call | tf_op jit(solution)/shard_map/merge/pallas_call | solution.py:543
Async XLA Ops:
  3.1 24.2 %all-to-all-start = ((bf16[8,2,3072]{2,1,0:T(2,128)(2,1)}), bf16[8,2,3072]{2,1,0:T(2,128)(2,1)S(1)}, u32[]{:S(2)}, u32[]{:S(2)}) async-start(bf16[8,2,3072]{2,1,0:T(2,128)(2,1)} %get-tuple-element.24), calls=%async_computation | async-start | bytes 196608 | tf_op jit(solution)/shard_map/all_to_all | solution.py:451
  26.4 0.9 %copy-start = (bf16[896,512]{1,0:T(8,128)(2,1)}, bf16[896,512]{1,0:T(8,128)(2,1)S(1)}, u32[]{:S(2)}) copy-start(bf16[896,512]{1,0:T(8,128)(2,1)S(1)} %get-tuple-element.25) | copy-start | bytes 2752516
  27.3 2.7 %collective-permute-start = (bf16[896,512]{1,0:T(8,128)(2,1)}, bf16[896,512]{1,0:T(8,128)(2,1)S(1)}, u32[]{:S(2)}, u32[]{:S(2)}) collective-permute-start(bf16[896,512]{1,0:T(8,128)(2,1)} %copy-done), channel_id=1, source_target_pairs={{0,1},{1,0},{2,3},{3,2},{4,5},{5,4},{6,7},{7,6},{8,9},{9,8},{10,11... | collective-permute-start | bytes 2752520 | tf_op jit(solution)/shard_map/ppermute | solution.py:480
  31.5 13.2 %all-to-all-start.1 = ((bf16[8,2,3456]{2,1,0:T(2,128)(2,1)}), bf16[8,2,3456]{2,1,0:T(2,128)(2,1)S(1)}, u32[]{:S(2)}, u32[]{:S(2)}) async-start(bf16[8,2,3456]{2,1,0:T(2,128)(2,1)} %attend_arrived.1.after_ref), calls=%async_computation.1 | async-start | bytes 221184 | tf_op jit(solution)/shard_map/all_to_all | solution.py:538

commit v10 on v9

--- a/solution.py
+++ b/solution.py
@@ -49,103 +49,106 @@
     return one_hot((shape[0], row_count), 1, row.astype(jnp.int32))
 
 
-def select_queries(
-    target_ref,
-    queries_ref,
-    prompts_ref,
-    hidden_ref,
-    w_ref,
-    pick_ref,
-    asked_ref,
-    rows_ref,
-    w_head_ref,
-    queries_here_ref,
-    sems,
-):
-    sections = target_ref.shape[0]
+def select_queries(target_ref, queries_ref, pick_ref, asked_ref, queries_here_ref, sem):
     row_count = queries_ref.shape[0]
-    prompt_rows = prompts_ref.shape[0]
-    depth = w_head_ref.shape[0]
-    copies = [
-        pltpu.make_async_copy(queries_ref, queries_here_ref, sems.at[0]),
-        pltpu.make_async_copy(w_ref.at[:depth, :], w_head_ref, sems.at[1]),
-        pltpu.make_async_copy(prompts_ref.at[:, :depth], rows_ref.at[:prompt_rows, :], sems.at[2]),
-        pltpu.make_async_copy(hidden_ref.at[:, :depth], rows_ref.at[prompt_rows:, :], sems.at[3]),
-    ]
-    for copy in copies:
-        copy.start()
+    copy = pltpu.make_async_copy(queries_ref, queries_here_ref, sem)
+    copy.start()
     pick = pick_rows(target_ref, row_count, PITCH)
     pick_ref[...] = pick_rows(target_ref, row_count, CAP)
-    copies[0].wait()
+    copy.wait()
     asked = jnp.dot(pick, queries_here_ref[...], preferred_element_type=F32)
-    for s in range(sections):
+    for s in range(asked_ref.shape[0]):
         asked_ref[s] = asked[s * PITCH : s * PITCH + CAP].astype(BF16)
-    for copy in copies[1:]:
-        copy.wait()
 
 
 def spans(edges):
     return [slice(a, b) for a, b in zip(edges[:-1], edges[1:])]
 
 
-def project(
-    rows_head_ref,
-    w_head_ref,
+def project_first(
     prompts_ref,
     hidden_ref,
     w_ref,
     scale_ref,
-    mine_ref,
     theirs_ref,
+    total_mine_ref,
     rows_ref,
-    w_here_ref,
+    w_mine_ref,
+    w_theirs_ref,
     total_ref,
+    scale_here_ref,
     row_sems,
     hidden_sems,
-    w_sems,
+    theirs_sems,
+    mine_sems,
+    scale_sem,
     *,
     edges,
-    block,
+    head,
 ):
     prompt_rows = prompts_ref.shape[0]
-    width = mine_ref.shape[1]
-    head = w_head_ref.shape[0]
+    features, width = w_mine_ref.shape
+    tp = lax.axis_index("tp")
+    theirs = pl.ds(pl.multiple_of((1 - tp) * width, width), width)
+    mine = pl.ds(pl.multiple_of(tp * width, width), width)
     chunks = spans(edges)
     waits = []
     for c, at in enumerate(chunks):
-        there = slice(head + at.start, head + at.stop)
         copies = [
-            pltpu.make_async_copy(w_ref.at[there, :], w_here_ref.at[at, :], w_sems.at[c]),
             pltpu.make_async_copy(
-                prompts_ref.at[:, there], rows_ref.at[:prompt_rows, at], row_sems.at[c]
+                w_ref.at[at, theirs], w_theirs_ref.at[at, :], theirs_sems.at[c]
             ),
             pltpu.make_async_copy(
-                hidden_ref.at[:, there], rows_ref.at[prompt_rows:, at], hidden_sems.at[c]
+                prompts_ref.at[:, at], rows_ref.at[:prompt_rows, at], row_sems.at[c]
+            ),
+            pltpu.make_async_copy(
+                hidden_ref.at[:, at], rows_ref.at[prompt_rows:, at], hidden_sems.at[c]
             ),
         ]
         for copy in copies:
             copy.start()
         waits.append(copies)
-    first = lax.axis_index("tp") == 0
-    blocks = spans(range(0, total_ref.shape[0] + 1, block))
-    halves = (slice(0, width), slice(width, 2 * width))
-    for m in blocks:
-        for n in halves:
-            total_ref[m, n] = jnp.dot(
-                rows_head_ref[m, :], w_head_ref[:, n], preferred_element_type=F32
-            )
+    later = [
+        pltpu.make_async_copy(scale_ref.at[:, theirs], scale_here_ref, scale_sem),
+        pltpu.make_async_copy(
+            w_ref.at[:head, mine], w_mine_ref.at[:head, :], mine_sems.at[0]
+        ),
+        pltpu.make_async_copy(
+            w_ref.at[head:, mine], w_mine_ref.at[head:, :], mine_sems.at[1]
+        ),
+    ]
+    for copy in later:
+        copy.start()
     for c, at in enumerate(chunks):
         for copy in waits[c]:
             copy.wait()
-        for m in blocks:
-            for n in halves:
-                total_ref[m, n] += jnp.dot(
-                    rows_ref[m, at], w_here_ref[at, n], preferred_element_type=F32
-                )
-    for m in blocks:
-        low, high = ((total_ref[m, n] * scale_ref[:, n]).astype(BF16) for n in halves)
-        mine_ref[m, :] = jnp.where(first, low, high)
-        theirs_ref[m, :] = jnp.where(first, high, low)
+        part = jnp.dot(rows_ref[:, at], w_theirs_ref[at, :], preferred_element_type=F32)
+        if c == 0:
+            total_ref[...] = part
+        elif c < len(chunks) - 1:
+            total_ref[...] += part
+        else:
+            later[0].wait()
+            theirs_ref[...] = ((total_ref[...] + part) * scale_here_ref[...]).astype(BF16)
+    later[1].wait()
+    total_mine_ref[...] = jnp.dot(
+        rows_ref[:, :head], w_mine_ref[:head, :], preferred_element_type=F32
+    )
+    later[2].wait()
+
+
+def project_second(
+    rows_ref, w_mine_ref, total_ref, scale_ref, out_ref, scale_here_ref, scale_sem, *, head, block
+):
+    width = out_ref.shape[1]
+    mine = pl.ds(pl.multiple_of(lax.axis_index("tp") * width, width), width)
+    copy = pltpu.make_async_copy(scale_ref.at[:, mine], scale_here_ref, scale_sem)
+    copy.start()
+    for m in spans(range(0, out_ref.shape[0] + 1, block)):
+        part = jnp.dot(rows_ref[m, head:], w_mine_ref[head:, :], preferred_element_type=F32)
+        if m.start == 0:
+            copy.wait()
+        out_ref[m, :] = ((total_ref[m, :] + part) * scale_here_ref[...]).astype(BF16)
 
 
 def split_bf16(x):
@@ -433,51 +436,57 @@
     scale = kv_scale.reshape(1, -1)
     lengths = cache_len.reshape(1, -1)
 
-    depth = 512
-    pick, asked, rows_head, w_head = pl.pallas_call(
+    pick, asked = pl.pallas_call(
         select_queries,
-        in_specs=[RESIDENT] + [REMAINS] * 4,
-        out_specs=[RESIDENT] * 4,
+        in_specs=[RESIDENT, REMAINS],
+        out_specs=[RESIDENT] * 2,
         out_shape=[
             pltpu.VMEM((slots, row_count), BF16),
             jax.ShapeDtypeStruct((sections, CAP, query_width), BF16),
-            pltpu.VMEM((all_rows, depth), BF16),
-            pltpu.VMEM((depth, w_kv.shape[1]), BF16),
         ],
-        scratch_shapes=[pltpu.VMEM(queries.shape, BF16), pltpu.SemaphoreType.DMA((4,))],
+        scratch_shapes=[pltpu.VMEM(queries.shape, BF16), pltpu.SemaphoreType.DMA(())],
         compiler_params=compiler_params(16),
         name="select_queries",
-    )(in_hbm(target_row), in_hbm(queries), in_hbm(prompts), in_hbm(decode_hidden), in_hbm(w_kv))
+    )(in_hbm(target_row), in_hbm(queries))
     asked = lax.all_to_all(asked, "section", 0, 0)
 
-    rest = features - depth
-    edges = (0, 512, 1408, 2816, 4096, rest)
+    edges = (0, 256, 768, 1536, 2560, 4096, features)
     count = len(edges) - 1
-    mine, theirs = pl.pallas_call(
-        functools.partial(project, edges=edges, block=all_rows // 2),
-        in_specs=[RESIDENT] * 2 + [REMAINS] * 3 + [RESIDENT],
-        out_specs=[RESIDENT, RESIDENT],
+    head = features // 3
+    theirs, total_mine, rows, w_mine = pl.pallas_call(
+        functools.partial(project_first, edges=edges, head=head),
+        in_specs=[REMAINS] * 4,
+        out_specs=[RESIDENT] * 4,
         scratch_shapes=[
-            pltpu.VMEM((all_rows, rest), BF16),
-            pltpu.VMEM((rest, w_kv.shape[1]), BF16),
-            pltpu.VMEM((all_rows, w_kv.shape[1]), F32),
+            pltpu.VMEM((features, local_width), BF16),
+            pltpu.VMEM((all_rows, local_width), F32),
+            pltpu.VMEM((1, local_width), F32),
             pltpu.SemaphoreType.DMA((count,)),
             pltpu.SemaphoreType.DMA((count,)),
             pltpu.SemaphoreType.DMA((count,)),
+            pltpu.SemaphoreType.DMA((2,)),
+            pltpu.SemaphoreType.DMA(()),
         ],
-        out_shape=[pltpu.VMEM((all_rows, local_width), BF16)] * 2,
-        compiler_params=compiler_params(44),
-        name="project",
-    )(
-        in_vmem(rows_head),
-        in_vmem(w_head),
-        in_hbm(prompts),
-        in_hbm(decode_hidden),
-        in_hbm(w_kv),
-        in_hbm(scale),
-    )
+        out_shape=[
+            pltpu.VMEM((all_rows, local_width), BF16),
+            pltpu.VMEM((all_rows, local_width), F32),
+            pltpu.VMEM((all_rows, features), BF16),
+            pltpu.VMEM((features, local_width), BF16),
+        ],
+        compiler_params=compiler_params(16),
+        name="project_first",
+    )(in_hbm(prompts), in_hbm(decode_hidden), in_hbm(w_kv), in_hbm(scale))
     theirs, asked = lax.optimization_barrier((theirs, asked))
     other = lax.ppermute(theirs, "tp", [(0, 1), (1, 0)])
+    mine = pl.pallas_call(
+        functools.partial(project_second, head=head, block=all_rows // 2),
+        in_specs=[RESIDENT] * 3 + [REMAINS],
+        out_specs=RESIDENT,
+        scratch_shapes=[pltpu.VMEM((1, local_width), F32), pltpu.SemaphoreType.DMA(())],
+        out_shape=pltpu.VMEM((all_rows, local_width), BF16),
+        compiler_params=compiler_params(16),
+        name="project_second",
+    )(*map(in_vmem, (rows, w_mine, total_mine)), in_hbm(scale))
 
     block = 32
     calls = 1

time: 46.6 us -> 59.6 us (1.28)
  local copies, waits for them, and re-layouts: 0.93 us -> 16.5 us
  waiting for transfers between devices: 3.84 us -> 2.33 us
  Pallas kernels: 28 us -> 26.9 us
    unnamed x2 -> x12, local copies, waits for them, and re-layouts: 0.93 us -> 16.5 us
    ppermute x1, waiting for transfers between devices: 1.65 us -> 0.01 us  [shards(): other = lax.ppermute(theirs, 'tp', [(0, 1), (1, 0)])]
    pallas_call x2 -> x3, Pallas kernels: 19 us -> 18 us  [the longest x1 10.9 us: shards(): pl.pallas_call(functools.partial(project_first, edges=edges, head=head),...]
  transfers between devices with their start and end apart: 3 -> 3, of which waited for: 2 -> 1; matrix products, arithmetic and copies ran while one was open for 0% -> 0% of each run, Pallas kernels for 48% -> 36%
where the time goes in v10:
time: 59.6 us; the launch traced here: 59 us
  Pallas kernels  26.9 us (45%)
  local copies, waits for them, and re-layouts  16.5 us (28%)
  starting transfers between devices  13.3 us (22%)
  waiting for transfers between devices  2.33 us (4%)
    unnamed x12, local copies, waits for them, and re-layouts  16.5 us
    pallas_call x1, Pallas kernels, shards(): pl.pallas_call(functools.partial(project_first, edges=edges, head=head),...  10.9 us
    all_to_all x1, starting transfers between devices, shards(): asked = lax.all_to_all(asked, 'section', 0, 0)  7.29 us
    all_to_all x1, starting transfers between devices, shards(): answers = lax.all_to_all(answers, 'section', 0, 0)  5.99 us
    pallas_call x1, Pallas kernels, cache_share(): pl.pallas_call(functools.partial(attend_cache, block_rows=block, first_bl...  5.01 us
    pallas_call x1, Pallas kernels, shards(): pl.pallas_call(functools.partial(project_second, head=head, block=all_row...  4.27 us
    pallas_call x1, Pallas kernels, shards(): pl.pallas_call(select_queries, in_specs=[RESIDENT, REMAINS], out_specs=[R...  2.74 us
    all_to_all x1, waiting for transfers between devices, shards(): answers = lax.all_to_all(answers, 'section', 0, 0)  2.33 us
  transfers between devices with their start and end apart: 3, of which 1 were waited for; matrix products, arithmetic and copies ran while one was open for 0% of the time, Pallas kernels for 36%

profile of v10, /device:TPU:0, one launch (start us, length us, event | category | flops | bytes accessed | tf_op | source)
XLA Modules:
  0.0 59.0 jit_solution(13471318257152367092)
XLA Ops:
  0.0 2.7 %select_queries.1 = (bf16[16,128]{1,0:T(8,128)(2,1)S(1)}, bf16[8,2,3072]{2,1,0:T(2,128)(2,1)}) custom-call(s32[8,12]{1,0:T(8,128)} %target_ref.3, bf16[128,3072]{1,0:T(8,128)(2,1)} %queries_ref.3), custom_call_target="tpu_custom_call" | custom-call | tf_op jit(solution)/shard_map/select_queries/pallas_call | solution.py:439
  2.7 7.3 %all-to-all-start = ((bf16[8,2,3072]{2,1,0:T(2,128)(2,1)}), bf16[8,2,3072]{2,1,0:T(2,128)(2,1)S(1)}, u32[]{:S(2)}, u32[]{:S(2)}) async-start(bf16[8,2,3072]{2,1,0:T(2,128)(2,1)} %get-tuple-element.24), calls=%async_computation | async-start | bytes 196608 | tf_op jit(solution)/shard_map/all_to_all | solution.py:451
  10.0 10.9 %project_first.1 = (bf16[896,512]{1,0:T(8,128)(2,1)S(1)}, f32[896,512]{1,0:T(8,128)S(1)}, bf16[896,6144]{1,0:T(8,128)(2,1)S(1)}, bf16[6144,512]{1,0:T(8,128)(2,1)S(1)}) custom-call(bf16[768,6144]{1,0:T(8,128)(2,1)} %prompts_ref.1, bf16[128,6144]{1,0:T(8,128)(2,1)} %hidden_ref.1, bf16[6144,1024]{1,0:T(8,128)(2,1)} %w_ref.1, f32[1,1024]{1,0:T(1,128)} %bitcast.2), custom_call_target="tpu_custom_call" | custom-call | tf_op jit(solution)/shard_map/project_first/pallas_call | solution.py:456
  21.0 0.0 copy-start
  21.0 4.2 %copy-done = bf16[896,6144]{1,0:T(8,128)(2,1)} copy-done((bf16[896,6144]{1,0:T(8,128)(2,1)}, bf16[896,6144]{1,0:T(8,128)(2,1)S(1)}, u32[]{:S(2)}) %copy-start) | copy-done | bytes 11010072
  25.2 0.0 copy-start.2
  25.2 2.6 %copy-done.2 = bf16[6144,512]{1,0:T(8,128)(2,1)} copy-done((bf16[6144,512]{1,0:T(8,128)(2,1)}, bf16[6144,512]{1,0:T(8,128)(2,1)S(1)}, u32[]{:S(2)}) %copy-start.2) | copy-done | bytes 6291480
  27.8 0.0 copy-start.4
  27.8 1.3 %copy-done.4 = f32[896,512]{1,0:T(8,128)} copy-done((f32[896,512]{1,0:T(8,128)}, f32[896,512]{1,0:T(8,128)S(1)}, u32[]{:S(2)}) %copy-start.4) | copy-done | bytes 1835032
  29.1 0.0 all-to-all-done.asked_ref
  29.1 0.0 collective-permute-start
  29.1 0.0 copy-start.1
  29.1 4.1 %copy-done.1 = bf16[896,6144]{1,0:T(8,128)(2,1)S(1)} copy-done((bf16[896,6144]{1,0:T(8,128)(2,1)S(1)}, bf16[896,6144]{1,0:T(8,128)(2,1)}, u32[]{:S(2)}) %copy-start.1) | copy-done | bytes 11010072
  33.2 0.0 copy-start.3
  33.2 2.8 %copy-done.3 = bf16[6144,512]{1,0:T(8,128)(2,1)S(1)} copy-done((bf16[6144,512]{1,0:T(8,128)(2,1)S(1)}, bf16[6144,512]{1,0:T(8,128)(2,1)}, u32[]{:S(2)}) %copy-start.3) | copy-done | bytes 6291480
  36.0 1.5 %copy-done.5 = f32[896,512]{1,0:T(8,128)S(1)} copy-done((f32[896,512]{1,0:T(8,128)S(1)}, f32[896,512]{1,0:T(8,128)}, u32[]{:S(2)}) %copy-start.5) | copy-done | bytes 1835032
  37.5 4.3 %project_second.1.mine_ref = bf16[896,512]{1,0:T(8,128)(2,1)S(1)} custom-call(bf16[896,6144]{1,0:T(8,128)(2,1)S(1)} %copy-done.1, bf16[6144,512]{1,0:T(8,128)(2,1)S(1)} %copy-done.3, f32[896,512]{1,0:T(8,128)S(1)} %copy-done.5, f32[1,1024]{1,0:T(1,128)} %bitcast.3), custom_call_target="tpu_custom_call" | custom-call | tf_op jit(solution)/shard_map/project_second/pallas_call | solution.py:481
  41.8 1.0 %prepare_arrived.1 = (bf16[16,3072]{1,0:T(8,128)(2,1)S(1)}, bf16[16,64]{1,0:T(8,128)(2,1)S(1)}, f32[16,768]{1,0:T(8,128)S(1)}) custom-call(s32[8,12]{1,0:T(8,128)} %target_ref.3, s32[8,12]{1,0:T(8,128)} %span_ref.1, bf16[8,2,3072]{2,1,0:T(2,128)(2,1)S(1)} %all-to-all-done.asked_ref), custom_call_target="tpu_custom_call" | custom-call | tf_op jit(solution)/shard_map/prepare_arrived/pallas_call | solution.py:525
  42.8 0.0 collective-permute-done.other_ref
  42.8 1.5 %attend_arrived.1.after_ref = bf16[8,2,3456]{2,1,0:T(2,128)(2,1)} custom-call(bf16[16,3072]{1,0:T(8,128)(2,1)S(1)} %get-tuple-element.27.rows_ref, bf16[16,64]{1,0:T(8,128)(2,1)S(1)} %get-tuple-element.28.slot_of_ref, f32[16,768]{1,0:T(8,128)S(1)} %get-tuple-element.29.bias_ref, bf16[896,512]{1,0:T(8,128)(2,1)S(1)} %project_second.1.mine_ref, ...), custom_call_target="tpu_custom_call" | custom-call | tf_op jit(solution)/shard_map/attend_arrived/pallas_call | solution.py:538
  44.3 6.0 %all-to-all-start.1 = ((bf16[8,2,3456]{2,1,0:T(2,128)(2,1)}), bf16[8,2,3456]{2,1,0:T(2,128)(2,1)S(1)}, u32[]{:S(2)}, u32[]{:S(2)}) async-start(bf16[8,2,3456]{2,1,0:T(2,128)(2,1)} %attend_arrived.1.after_ref), calls=%async_computation.1 | async-start | bytes 221184 | tf_op jit(solution)/shard_map/all_to_all | solution.py:547
  50.3 5.0 %attend_cache.1 = (bf16[128,3072]{1,0:T(8,128)(2,1)S(1)}, f32[16,3072]{1,0:T(8,128)S(1)}, f32[16,128]{1,0:T(8,128)S(1)}) custom-call(bf16[128,3072]{1,0:T(8,128)(2,1)} %queries_ref.3, bf16[128,32,512]{2,1,0:T(8,128)(2,1)} %cache_ref.1, s32[1,128]{1,0:T(1,128)} %bitcast.4, bf16[896,512]{1,0:T(8,128)(2,1)S(1)} %project_second.1.mine_ref, ...), custom_call_target="tpu_custom_call" | custom-call | tf_op jit(solution)/shard_map/attend_cache/pallas_call | solution.py:497
  55.3 2.3 %all-to-all-done.1.refs_3_ = bf16[8,2,3456]{2,1,0:T(2,128)(2,1)S(1)} async-done(((bf16[8,2,3456]{2,1,0:T(2,128)(2,1)}), bf16[8,2,3456]{2,1,0:T(2,128)(2,1)S(1)}, u32[]{:S(2)}, u32[]{:S(2)}) %all-to-all-start.1) | async-done | bytes 110624 | tf_op jit(solution)/shard_map/all_to_all | solution.py:547
  57.7 1.4 %merge.1 = bf16[128,3072]{1,0:T(8,128)(2,1)} custom-call(bf16[16,128]{1,0:T(8,128)(2,1)S(1)} %get-tuple-element.19.pick_ref, bf16[128,3072]{1,0:T(8,128)(2,1)S(1)} %get-tuple-element.30.refs_0_, f32[16,3072]{1,0:T(8,128)S(1)} %get-tuple-element.31.refs_1_, f32[16,128]{1,0:T(8,128)S(1)} %get-tuple-element.32.refs_2_, ...), custom_call_target="tpu_custom_call" | custom-call | tf_op jit(solution)/shard_map/merge/pallas_call | solution.py:552
  (1 shorter events, 0.0 us)
Async XLA Ops:
  2.7 26.3 %all-to-all-start = ((bf16[8,2,3072]{2,1,0:T(2,128)(2,1)}), bf16[8,2,3072]{2,1,0:T(2,128)(2,1)S(1)}, u32[]{:S(2)}, u32[]{:S(2)}) async-start(bf16[8,2,3072]{2,1,0:T(2,128)(2,1)} %get-tuple-element.24), calls=%async_computation | async-start | bytes 196608 | tf_op jit(solution)/shard_map/all_to_all | solution.py:451
  21.0 4.2 %copy-start = (bf16[896,6144]{1,0:T(8,128)(2,1)}, bf16[896,6144]{1,0:T(8,128)(2,1)S(1)}, u32[]{:S(2)}) copy-start(bf16[896,6144]{1,0:T(8,128)(2,1)S(1)} %get-tuple-element.20.rows_ref) | copy-start | bytes 33030148
  25.2 2.6 %copy-start.2 = (bf16[6144,512]{1,0:T(8,128)(2,1)}, bf16[6144,512]{1,0:T(8,128)(2,1)S(1)}, u32[]{:S(2)}) copy-start(bf16[6144,512]{1,0:T(8,128)(2,1)S(1)} %get-tuple-element.21.w_mine_ref) | copy-start | bytes 18874372
  27.8 1.3 %copy-start.4 = (f32[896,512]{1,0:T(8,128)}, f32[896,512]{1,0:T(8,128)S(1)}, u32[]{:S(2)}) copy-start(f32[896,512]{1,0:T(8,128)S(1)} %get-tuple-element.22.total_ref) | copy-start | bytes 5505028
  29.1 13.7 %collective-permute-start = (bf16[896,512]{1,0:T(8,128)(2,1)S(1)}, bf16[896,512]{1,0:T(8,128)(2,1)S(1)}, u32[]{:S(2)}, u32[]{:S(2)}) collective-permute-start(bf16[896,512]{1,0:T(8,128)(2,1)S(1)} %get-tuple-element.25), channel_id=1, source_target_pairs={{0,1},{1,0},{2,3},{3,2},{4,5},{5,4},{6,7},{7,6},{8,9},{9,8},{10,11... | collective-permute-start | bytes 2752520 | tf_op jit(solution)/shard_map/ppermute | solution.py:480
  29.1 4.1 %copy-start.1 = (bf16[896,6144]{1,0:T(8,128)(2,1)S(1)}, bf16[896,6144]{1,0:T(8,128)(2,1)}, u32[]{:S(2)}) copy-start(bf16[896,6144]{1,0:T(8,128)(2,1)} %copy-done) | copy-start | bytes 33030148
  33.2 2.8 %copy-start.3 = (bf16[6144,512]{1,0:T(8,128)(2,1)S(1)}, bf16[6144,512]{1,0:T(8,128)(2,1)}, u32[]{:S(2)}) copy-start(bf16[6144,512]{1,0:T(8,128)(2,1)} %copy-done.2) | copy-start | bytes 18874372
  36.0 1.5 %copy-start.5 = (f32[896,512]{1,0:T(8,128)S(1)}, f32[896,512]{1,0:T(8,128)}, u32[]{:S(2)}) copy-start(f32[896,512]{1,0:T(8,128)} %copy-done.4) | copy-start | bytes 5505028
  44.3 13.3 %all-to-all-start.1 = ((bf16[8,2,3456]{2,1,0:T(2,128)(2,1)}), bf16[8,2,3456]{2,1,0:T(2,128)(2,1)S(1)}, u32[]{:S(2)}, u32[]{:S(2)}) async-start(bf16[8,2,3456]{2,1,0:T(2,128)(2,1)} %attend_arrived.1.after_ref), calls=%async_computation.1 | async-start | bytes 221184 | tf_op jit(solution)/shard_map/all_to_all | solution.py:547

commit v11 on v10

--- a/solution.py
+++ b/solution.py
@@ -12,6 +12,7 @@
 CAP = 2
 STATS = 128
 MASKED = -1e30
+LSE_PITCH = 40
 PITCH = 8
 LOG2_SCALE = HD ** (-0.5) * math.log2(math.e)
 F32 = jnp.float32
@@ -49,29 +50,25 @@
     return one_hot((shape[0], row_count), 1, row.astype(jnp.int32))
 
 
-def select_queries(target_ref, queries_ref, pick_ref, asked_ref, queries_here_ref, sem):
-    row_count = queries_ref.shape[0]
-    copy = pltpu.make_async_copy(queries_ref, queries_here_ref, sem)
-    copy.start()
-    pick = pick_rows(target_ref, row_count, PITCH)
-    pick_ref[...] = pick_rows(target_ref, row_count, CAP)
-    copy.wait()
-    asked = jnp.dot(pick, queries_here_ref[...], preferred_element_type=F32)
+def select_queries(target_ref, queries_ref, pick_ref, asked_ref):
+    pick = pick_rows(target_ref, queries_ref.shape[0], CAP)
+    pick_ref[...] = pick
+    asked = jnp.dot(pick, queries_ref[...], preferred_element_type=F32).astype(BF16)
     for s in range(asked_ref.shape[0]):
-        asked_ref[s] = asked[s * PITCH : s * PITCH + CAP].astype(BF16)
+        asked_ref[s] = asked[s * CAP : (s + 1) * CAP]
 
 
 def spans(edges):
     return [slice(a, b) for a, b in zip(edges[:-1], edges[1:])]
 
 
-def project_first(
+def project(
     prompts_ref,
     hidden_ref,
     w_ref,
     scale_ref,
+    mine_ref,
     theirs_ref,
-    total_mine_ref,
     rows_ref,
     w_mine_ref,
     w_theirs_ref,
@@ -80,14 +77,14 @@
     row_sems,
     hidden_sems,
     theirs_sems,
-    mine_sems,
-    scale_sem,
+    mine_sem,
+    scale_sems,
     *,
     edges,
-    head,
+    block,
 ):
     prompt_rows = prompts_ref.shape[0]
-    features, width = w_mine_ref.shape
+    width = mine_ref.shape[1]
     tp = lax.axis_index("tp")
     theirs = pl.ds(pl.multiple_of((1 - tp) * width, width), width)
     mine = pl.ds(pl.multiple_of(tp * width, width), width)
@@ -109,13 +106,11 @@
             copy.start()
         waits.append(copies)
     later = [
-        pltpu.make_async_copy(scale_ref.at[:, theirs], scale_here_ref, scale_sem),
         pltpu.make_async_copy(
-            w_ref.at[:head, mine], w_mine_ref.at[:head, :], mine_sems.at[0]
+            scale_ref.at[:, theirs], scale_here_ref.at[0], scale_sems.at[0]
         ),
-        pltpu.make_async_copy(
-            w_ref.at[head:, mine], w_mine_ref.at[head:, :], mine_sems.at[1]
-        ),
+        pltpu.make_async_copy(scale_ref.at[:, mine], scale_here_ref.at[1], scale_sems.at[1]),
+        pltpu.make_async_copy(w_ref.at[:, mine], w_mine_ref, mine_sem),
     ]
     for copy in later:
         copy.start()
@@ -129,26 +124,12 @@
             total_ref[...] += part
         else:
             later[0].wait()
-            theirs_ref[...] = ((total_ref[...] + part) * scale_here_ref[...]).astype(BF16)
-    later[1].wait()
-    total_mine_ref[...] = jnp.dot(
-        rows_ref[:, :head], w_mine_ref[:head, :], preferred_element_type=F32
-    )
-    later[2].wait()
-
-
-def project_second(
-    rows_ref, w_mine_ref, total_ref, scale_ref, out_ref, scale_here_ref, scale_sem, *, head, block
-):
-    width = out_ref.shape[1]
-    mine = pl.ds(pl.multiple_of(lax.axis_index("tp") * width, width), width)
-    copy = pltpu.make_async_copy(scale_ref.at[:, mine], scale_here_ref, scale_sem)
-    copy.start()
-    for m in spans(range(0, out_ref.shape[0] + 1, block)):
-        part = jnp.dot(rows_ref[m, head:], w_mine_ref[head:, :], preferred_element_type=F32)
-        if m.start == 0:
-            copy.wait()
-        out_ref[m, :] = ((total_ref[m, :] + part) * scale_here_ref[...]).astype(BF16)
+            theirs_ref[...] = ((total_ref[...] + part) * scale_here_ref[0]).astype(BF16)
+    for copy in later[1:]:
+        copy.wait()
+    for m in spans(range(0, rows_ref.shape[0] + 1, block)):
+        total = jnp.dot(rows_ref[m, :], w_mine_ref[...], preferred_element_type=F32)
+        mine_ref[m, :] = (total * scale_here_ref[1]).astype(BF16)
 
 
 def split_bf16(x):
@@ -241,7 +222,9 @@
         for i in range(group):
             pieces.append(values[i])
             lse = jnp.where(lane == h * group + i, head_lse[i], lse)
-    result = jnp.concatenate(pieces + list(split_bf16(lse)), axis=1).astype(BF16)
+    high, middle, low = split_bf16(lse)
+    stats = high + pltpu.roll(middle, LSE_PITCH, 1) + pltpu.roll(low, 2 * LSE_PITCH, 1)
+    result = jnp.concatenate(pieces + [stats], axis=1).astype(BF16)
     answers = lax.dot_general(slot_of, result, TRANSPOSED, preferred_element_type=F32)
     for s in range(out_ref.shape[0]):
         out_ref[s] = answers[s * PITCH : s * PITCH + CAP].astype(BF16)
@@ -375,10 +358,11 @@
     arrived = jnp.concatenate(
         [arrived_ref[s].astype(F32) for s in range(arrived_ref.shape[0])], axis=0
     )
+    stats = arrived[:, width:]
     arrived_lse = (
-        arrived[:, width : width + STATS]
-        + arrived[:, width + STATS : width + 2 * STATS]
-        + arrived[:, width + 2 * STATS :]
+        stats
+        + pltpu.roll(stats, STATS - LSE_PITCH, 1)
+        + pltpu.roll(stats, STATS - 2 * LSE_PITCH, 1)
     )
     cached_lse = sum(ref[...] for ref in slot_lse_refs)
     largest = jnp.maximum(cached_lse, arrived_lse)
@@ -438,13 +422,12 @@
 
     pick, asked = pl.pallas_call(
         select_queries,
-        in_specs=[RESIDENT, REMAINS],
+        in_specs=[RESIDENT, RESIDENT],
         out_specs=[RESIDENT] * 2,
         out_shape=[
             pltpu.VMEM((slots, row_count), BF16),
             jax.ShapeDtypeStruct((sections, CAP, query_width), BF16),
         ],
-        scratch_shapes=[pltpu.VMEM(queries.shape, BF16), pltpu.SemaphoreType.DMA(())],
         compiler_params=compiler_params(16),
         name="select_queries",
     )(in_hbm(target_row), in_hbm(queries))
@@ -452,42 +435,28 @@
 
     edges = (0, 256, 768, 1536, 2560, 4096, features)
     count = len(edges) - 1
-    head = features // 3
-    theirs, total_mine, rows, w_mine = pl.pallas_call(
-        functools.partial(project_first, edges=edges, head=head),
+    mine, theirs = pl.pallas_call(
+        functools.partial(project, edges=edges, block=all_rows // 2),
         in_specs=[REMAINS] * 4,
-        out_specs=[RESIDENT] * 4,
+        out_specs=[RESIDENT] * 2,
         scratch_shapes=[
+            pltpu.VMEM((all_rows, features), BF16),
+            pltpu.VMEM((features, local_width), BF16),
             pltpu.VMEM((features, local_width), BF16),
             pltpu.VMEM((all_rows, local_width), F32),
-            pltpu.VMEM((1, local_width), F32),
+            pltpu.VMEM((2, 1, local_width), F32),
             pltpu.SemaphoreType.DMA((count,)),
             pltpu.SemaphoreType.DMA((count,)),
             pltpu.SemaphoreType.DMA((count,)),
+            pltpu.SemaphoreType.DMA(()),
             pltpu.SemaphoreType.DMA((2,)),
-            pltpu.SemaphoreType.DMA(()),
         ],
-        out_shape=[
-            pltpu.VMEM((all_rows, local_width), BF16),
-            pltpu.VMEM((all_rows, local_width), F32),
-            pltpu.VMEM((all_rows, features), BF16),
-            pltpu.VMEM((features, local_width), BF16),
-        ],
-        compiler_params=compiler_params(16),
-        name="project_first",
+        out_shape=[pltpu.VMEM((all_rows, local_width), BF16)] * 2,
+        compiler_params=compiler_params(44),
+        name="project",
     )(in_hbm(prompts), in_hbm(decode_hidden), in_hbm(w_kv), in_hbm(scale))
     theirs, asked = lax.optimization_barrier((theirs, asked))
     other = lax.ppermute(theirs, "tp", [(0, 1), (1, 0)])
-    mine = pl.pallas_call(
-        functools.partial(project_second, head=head, block=all_rows // 2),
-        in_specs=[RESIDENT] * 3 + [REMAINS],
-        out_specs=RESIDENT,
-        scratch_shapes=[pltpu.VMEM((1, local_width), F32), pltpu.SemaphoreType.DMA(())],
-        out_shape=pltpu.VMEM((all_rows, local_width), BF16),
-        compiler_params=compiler_params(16),
-        name="project_second",
-    )(*map(in_vmem, (rows, w_mine, total_mine)), in_hbm(scale))
-
     block = 32
     calls = 1
     call_rows = row_count // calls
@@ -534,7 +503,7 @@
         compiler_params=compiler_params(16),
         name="prepare_arrived",
     )(in_hbm(target_row), in_hbm(span_len), in_vmem(asked))
-    answer_width = query_width + 3 * STATS
+    answer_width = query_width + STATS
     answers = pl.pallas_call(
         attend_arrived,
         in_specs=[RESIDENT] * 5,

time: 59.6 us -> 43.1 us (0.72)
  local copies, waits for them, and re-layouts: 16.5 us -> 0 us
  waiting for transfers between devices: 2.33 us -> 3.56 us
  Pallas kernels: 26.9 us -> 25.7 us
    unnamed x12 -> x0, local copies, waits for them, and re-layouts: 16.5 us -> none
    ppermute x1, waiting for transfers between devices: 0.01 us -> 1.43 us  [shards(): other = lax.ppermute(theirs, 'tp', [(0, 1), (1, 0)])]
    pallas_call x3 -> x2, Pallas kernels: 18 us -> 16.7 us  [the longest x1 14.5 us: shards(): pl.pallas_call(functools.partial(project, edges=edges, block=all_rows //...]
  transfers between devices with their start and end apart: 3 -> 3, of which waited for: 1 -> 2; matrix products, arithmetic and copies ran while one was open for 0% -> 0% of each run, Pallas kernels for 36% -> 48%
where the time goes in v11:
time: 43.1 us; the launch traced here: 42.6 us
  Pallas kernels  25.7 us (60%)
  starting transfers between devices  13.3 us (31%)
  waiting for transfers between devices  3.56 us (8%)
    pallas_call x1, Pallas kernels, shards(): pl.pallas_call(functools.partial(project, edges=edges, block=all_rows //...  14.5 us
    all_to_all x1, starting transfers between devices, shards(): asked = lax.all_to_all(asked, 'section', 0, 0)  7.28 us
    all_to_all x1, starting transfers between devices, shards(): answers = lax.all_to_all(answers, 'section', 0, 0)  6 us
    pallas_call x1, Pallas kernels, cache_share(): pl.pallas_call(functools.partial(attend_cache, block_rows=block, first_bl...  5.01 us
    pallas_call x1, Pallas kernels, shards(): pl.pallas_call(select_queries, in_specs=[RESIDENT, RESIDENT], out_specs=[...  2.2 us
    all_to_all x1, waiting for transfers between devices, shards(): answers = lax.all_to_all(answers, 'section', 0, 0)  2.13 us
    pallas_call x1, Pallas kernels, shards(): pl.pallas_call(attend_arrived, in_specs=[RESIDENT] * 5, out_specs=RESIDEN...  1.53 us
    ppermute x1, waiting for transfers between devices, shards(): other = lax.ppermute(theirs, 'tp', [(0, 1), (1, 0)])  1.43 us
  transfers between devices with their start and end apart: 3, of which 2 were waited for; matrix products, arithmetic and copies ran while one was open for 0% of the time, Pallas kernels for 48%

profile of v11, /device:TPU:0, one launch (start us, length us, event | category | flops | bytes accessed | tf_op | source)
XLA Modules:
  0.0 42.6 jit_solution(12396495495760852173)
XLA Ops:
  0.0 2.2 %select_queries.1 = (bf16[16,128]{1,0:T(8,128)(2,1)S(1)}, bf16[8,2,3072]{2,1,0:T(2,128)(2,1)}) custom-call(s32[8,12]{1,0:T(8,128)} %target_ref.3, bf16[128,3072]{1,0:T(8,128)(2,1)} %queries_ref.3), custom_call_target="tpu_custom_call" | custom-call | tf_op jit(solution)/shard_map/select_queries/pallas_call | solution.py:423
  2.2 7.3 %all-to-all-start = ((bf16[8,2,3072]{2,1,0:T(2,128)(2,1)}), bf16[8,2,3072]{2,1,0:T(2,128)(2,1)S(1)}, u32[]{:S(2)}, u32[]{:S(2)}) async-start(bf16[8,2,3072]{2,1,0:T(2,128)(2,1)} %get-tuple-element.20), calls=%async_computation | async-start | bytes 196608 | tf_op jit(solution)/shard_map/all_to_all | solution.py:434
  9.5 14.5 %project.1 = (bf16[896,512]{1,0:T(8,128)(2,1)S(1)}, bf16[896,512]{1,0:T(8,128)(2,1)S(1)}) custom-call(bf16[768,6144]{1,0:T(8,128)(2,1)} %prompts_ref.1, bf16[128,6144]{1,0:T(8,128)(2,1)} %hidden_ref.1, bf16[6144,1024]{1,0:T(8,128)(2,1)} %w_ref.1, f32[1,1024]{1,0:T(1,128)} %bitcast.2), custom_call_target="tpu_custom_call" | custom-call | tf_op jit(solution)/shard_map/project/pallas_call | solution.py:438
  24.0 0.0 all-to-all-done.asked_ref
  24.0 0.1 collective-permute-start
  24.1 1.0 %prepare_arrived.1 = (bf16[16,3072]{1,0:T(8,128)(2,1)S(1)}, bf16[16,64]{1,0:T(8,128)(2,1)S(1)}, f32[16,768]{1,0:T(8,128)S(1)}) custom-call(s32[8,12]{1,0:T(8,128)} %target_ref.3, s32[8,12]{1,0:T(8,128)} %span_ref.1, bf16[8,2,3072]{2,1,0:T(2,128)(2,1)S(1)} %all-to-all-done.asked_ref), custom_call_target="tpu_custom_call" | custom-call | tf_op jit(solution)/shard_map/prepare_arrived/pallas_call | solution.py:494
  25.1 1.4 %collective-permute-done.other_ref = bf16[896,512]{1,0:T(8,128)(2,1)S(1)} collective-permute-done((bf16[896,512]{1,0:T(8,128)(2,1)S(1)}, bf16[896,512]{1,0:T(8,128)(2,1)S(1)}, u32[]{:S(2)}, u32[]{:S(2)}) %collective-permute-start) | collective-permute-done | bytes 917536 | tf_op jit(solution)/shard_map/ppermute | solution.py:459
  26.5 1.5 %attend_arrived.1.after_ref = bf16[8,2,3200]{2,1,0:T(2,128)(2,1)} custom-call(bf16[16,3072]{1,0:T(8,128)(2,1)S(1)} %get-tuple-element.23.rows_ref, bf16[16,64]{1,0:T(8,128)(2,1)S(1)} %get-tuple-element.24.slot_of_ref, f32[16,768]{1,0:T(8,128)S(1)} %get-tuple-element.25.bias_ref, bf16[896,512]{1,0:T(8,128)(2,1)S(1)} %get-tuple-element.18.mine_ref, ...), custom_call_target="tpu_custom_call" | custom-call | tf_op jit(solution)/shard_map/attend_arrived/pallas_call | solution.py:507
  28.1 6.0 %all-to-all-start.1 = ((bf16[8,2,3200]{2,1,0:T(2,128)(2,1)}), bf16[8,2,3200]{2,1,0:T(2,128)(2,1)S(1)}, u32[]{:S(2)}, u32[]{:S(2)}) async-start(bf16[8,2,3200]{2,1,0:T(2,128)(2,1)} %attend_arrived.1.after_ref), calls=%async_computation.1 | async-start | bytes 204800 | tf_op jit(solution)/shard_map/all_to_all | solution.py:516
  34.1 5.0 %attend_cache.1 = (bf16[128,3072]{1,0:T(8,128)(2,1)S(1)}, f32[16,3072]{1,0:T(8,128)S(1)}, f32[16,128]{1,0:T(8,128)S(1)}) custom-call(bf16[128,3072]{1,0:T(8,128)(2,1)} %queries_ref.3, bf16[128,32,512]{2,1,0:T(8,128)(2,1)} %cache_ref.1, s32[1,128]{1,0:T(1,128)} %bitcast.3, bf16[896,512]{1,0:T(8,128)(2,1)S(1)} %get-tuple-element.18.mine_ref, ...), custom_call_target="tpu_custom_call" | custom-call | tf_op jit(solution)/shard_map/attend_cache/pallas_call | solution.py:466
  39.1 2.1 %all-to-all-done.1.refs_3_ = bf16[8,2,3200]{2,1,0:T(2,128)(2,1)S(1)} async-done(((bf16[8,2,3200]{2,1,0:T(2,128)(2,1)}), bf16[8,2,3200]{2,1,0:T(2,128)(2,1)S(1)}, u32[]{:S(2)}, u32[]{:S(2)}) %all-to-all-start.1) | async-done | bytes 102432 | tf_op jit(solution)/shard_map/all_to_all | solution.py:516
  41.2 1.4 %merge.1 = bf16[128,3072]{1,0:T(8,128)(2,1)} custom-call(bf16[16,128]{1,0:T(8,128)(2,1)S(1)} %get-tuple-element.17.pick_ref, bf16[128,3072]{1,0:T(8,128)(2,1)S(1)} %get-tuple-element.26.refs_0_, f32[16,3072]{1,0:T(8,128)S(1)} %get-tuple-element.27.refs_1_, f32[16,128]{1,0:T(8,128)S(1)} %get-tuple-element.28.refs_2_, ...), custom_call_target="tpu_custom_call" | custom-call | tf_op jit(solution)/shard_map/merge/pallas_call | solution.py:521
Async XLA Ops:
  2.2 21.8 %all-to-all-start = ((bf16[8,2,3072]{2,1,0:T(2,128)(2,1)}), bf16[8,2,3072]{2,1,0:T(2,128)(2,1)S(1)}, u32[]{:S(2)}, u32[]{:S(2)}) async-start(bf16[8,2,3072]{2,1,0:T(2,128)(2,1)} %get-tuple-element.20), calls=%async_computation | async-start | bytes 196608 | tf_op jit(solution)/shard_map/all_to_all | solution.py:434
  24.0 2.5 %collective-permute-start = (bf16[896,512]{1,0:T(8,128)(2,1)S(1)}, bf16[896,512]{1,0:T(8,128)(2,1)S(1)}, u32[]{:S(2)}, u32[]{:S(2)}) collective-permute-start(bf16[896,512]{1,0:T(8,128)(2,1)S(1)} %get-tuple-element.21), channel_id=1, source_target_pairs={{0,1},{1,0},{2,3},{3,2},{4,5},{5,4},{6,7},{7,6},{8,9},{9,8},{10,11... | collective-permute-start | bytes 2752520 | tf_op jit(solution)/shard_map/ppermute | solution.py:459
  28.1 13.1 %all-to-all-start.1 = ((bf16[8,2,3200]{2,1,0:T(2,128)(2,1)}), bf16[8,2,3200]{2,1,0:T(2,128)(2,1)S(1)}, u32[]{:S(2)}, u32[]{:S(2)}) async-start(bf16[8,2,3200]{2,1,0:T(2,128)(2,1)} %attend_arrived.1.after_ref), calls=%async_computation.1 | async-start | bytes 204800 | tf_op jit(solution)/shard_map/all_to_all | solution.py:516

commit v12 on v11

--- a/solution.py
+++ b/solution.py
@@ -50,12 +50,17 @@
     return one_hot((shape[0], row_count), 1, row.astype(jnp.int32))
 
 
-def select_queries(target_ref, queries_ref, pick_ref, asked_ref):
+def select_queries(target_ref, queries_ref, pick_ref, *refs):
+    asked_refs, asked_ref = refs[:-1], refs[-1]
+    sections = target_ref.shape[0]
+    position = lax.axis_index("section")
     pick = pick_rows(target_ref, queries_ref.shape[0], CAP)
     pick_ref[...] = pick
-    asked = jnp.dot(pick, queries_ref[...], preferred_element_type=F32).astype(BF16)
-    for s in range(asked_ref.shape[0]):
+    asked = jnp.dot(pick, queries_ref[...], preferred_element_type=F32)
+    for s in range(sections):
         asked_ref[s] = asked[s * CAP : (s + 1) * CAP]
+    for k in range(sections):
+        asked_refs[k][...] = asked_ref[position ^ k].astype(BF16)
 
 
 def spans(edges):
@@ -161,16 +166,18 @@
 
 
 def prepare_arrived(
-    target_ref, span_ref, asked_ref, rows_ref, slot_of_ref, bias_ref, *, row_count
+    target_ref, span_ref, *refs, row_count
 ):
     sections, requests = target_ref.shape
+    asked_refs, (rows_ref, slot_of_ref, bias_ref) = refs[:sections], refs[sections:]
     padded, prompt_rows = bias_ref.shape
     span_rows = prompt_rows // requests
     section_col, rank_col, span_col = request_slots(target_ref, span_ref, row_count, padded)
     slot = jnp.where(section_col >= 0, section_col * PITCH + rank_col, -1)
     slot_of_ref[...] = one_hot((padded, sections * PITCH), 1, slot)
-    slot = jnp.where(section_col >= 0, section_col * CAP + rank_col, -1)
-    asked = jnp.concatenate([asked_ref[s].astype(F32) for s in range(sections)], axis=0)
+    step = section_col ^ lax.axis_index("section")
+    slot = jnp.where(section_col >= 0, step * CAP + rank_col, -1)
+    asked = jnp.concatenate([ref[...].astype(F32) for ref in asked_refs], axis=0)
     rows_ref[...] = jnp.dot(
         one_hot((padded, sections * CAP), 1, slot),
         asked.astype(BF16),
@@ -420,23 +427,24 @@
     scale = kv_scale.reshape(1, -1)
     lengths = cache_len.reshape(1, -1)
 
-    pick, asked = pl.pallas_call(
+    pick, *asked = pl.pallas_call(
         select_queries,
         in_specs=[RESIDENT, RESIDENT],
-        out_specs=[RESIDENT] * 2,
-        out_shape=[
-            pltpu.VMEM((slots, row_count), BF16),
-            jax.ShapeDtypeStruct((sections, CAP, query_width), BF16),
-        ],
+        out_specs=[RESIDENT] * (1 + sections),
+        out_shape=[pltpu.VMEM((slots, row_count), BF16)]
+        + [pltpu.VMEM((CAP, query_width), BF16)] * sections,
+        scratch_shapes=[pltpu.VMEM((sections, CAP, query_width), F32)],
         compiler_params=compiler_params(16),
         name="select_queries",
     )(in_hbm(target_row), in_hbm(queries))
-    asked = lax.all_to_all(asked, "section", 0, 0)
+    for k in range(1, sections):
+        pairs = [(s, k ^ s) for s in range(sections)]
+        asked[k] = lax.ppermute(asked[k], "section", pairs)
 
     edges = (0, 256, 768, 1536, 2560, 4096, features)
     count = len(edges) - 1
     mine, theirs = pl.pallas_call(
-        functools.partial(project, edges=edges, block=all_rows // 2),
+        functools.partial(project, edges=edges, block=all_rows // 4),
         in_specs=[REMAINS] * 4,
         out_specs=[RESIDENT] * 2,
         scratch_shapes=[
@@ -455,7 +463,7 @@
         compiler_params=compiler_params(44),
         name="project",
     )(in_hbm(prompts), in_hbm(decode_hidden), in_hbm(w_kv), in_hbm(scale))
-    theirs, asked = lax.optimization_barrier((theirs, asked))
+    theirs, *asked = lax.optimization_barrier((theirs, *asked))
     other = lax.ppermute(theirs, "tp", [(0, 1), (1, 0)])
     block = 32
     calls = 1
@@ -493,7 +501,7 @@
     padded = -(-span_len.shape[1] // 16) * 16
     prepared = pl.pallas_call(
         functools.partial(prepare_arrived, row_count=row_count),
-        in_specs=[RESIDENT] * 3,
+        in_specs=[RESIDENT] * (2 + sections),
         out_specs=[RESIDENT] * 3,
         out_shape=[
             pltpu.VMEM((padded, query_width), BF16),
@@ -502,7 +510,7 @@
         ],
         compiler_params=compiler_params(16),
         name="prepare_arrived",
-    )(in_hbm(target_row), in_hbm(span_len), in_vmem(asked))
+    )(in_hbm(target_row), in_hbm(span_len), *map(in_vmem, asked))
     answer_width = query_width + STATS
     answers = pl.pallas_call(
         attend_arrived,

time: 43.1 us -> 47.7 us (1.11)
  starting transfers between devices: 13.3 us -> 18.6 us
  Pallas kernels: 25.7 us -> 25.1 us
    ppermute x0 -> x7, starting transfers between devices: none -> 12.5 us  [shards(): asked[k] = lax.ppermute(asked[k], 'section', pairs)]
    all_to_all x1 -> x0, starting transfers between devices: 7.28 us -> none  [shards(): asked = lax.all_to_all(asked, 'section', 0, 0)]
    pallas_call x1, Pallas kernels: 2.2 us -> 1.64 us  [shards(): pl.pallas_call(select_queries, in_specs=[RESIDENT, RESIDENT], out_specs=[...]
  transfers between devices with their start and end apart: 3 -> 9, of which waited for: 2 -> 2; matrix products, arithmetic and copies ran while one was open for 0% -> 0% of each run, Pallas kernels for 48% -> 43%
where the time goes in v12:
time: 47.7 us; the launch traced here: 47.3 us
  Pallas kernels  25.1 us (53%)
  starting transfers between devices  18.6 us (39%)
  waiting for transfers between devices  3.58 us (8%)
    pallas_call x1, Pallas kernels, shards(): pl.pallas_call(functools.partial(project, edges=edges, block=all_rows //...  14.5 us
    ppermute x7, starting transfers between devices, shards(): asked[k] = lax.ppermute(asked[k], 'section', pairs)  12.5 us
    all_to_all x1, starting transfers between devices, shards(): answers = lax.all_to_all(answers, 'section', 0, 0)  5.99 us
    pallas_call x1, Pallas kernels, cache_share(): pl.pallas_call(functools.partial(attend_cache, block_rows=block, first_bl...  5.01 us
    all_to_all x1, waiting for transfers between devices, shards(): answers = lax.all_to_all(answers, 'section', 0, 0)  2.13 us
    pallas_call x1, Pallas kernels, shards(): pl.pallas_call(select_queries, in_specs=[RESIDENT, RESIDENT], out_specs=[...  1.64 us
    pallas_call x1, Pallas kernels, shards(): pl.pallas_call(attend_arrived, in_specs=[RESIDENT] * 5, out_specs=RESIDEN...  1.54 us
    ppermute x1, waiting for transfers between devices, shards(): other = lax.ppermute(theirs, 'tp', [(0, 1), (1, 0)])  1.43 us
  transfers between devices with their start and end apart: 9, of which 2 were waited for; matrix products, arithmetic and copies ran while one was open for 0% of the time, Pallas kernels for 43%

profile of v12, /device:TPU:0, one launch (start us, length us, event | category | flops | bytes accessed | tf_op | source)
XLA Modules:
  0.0 47.3 jit_solution(9321543934509040914)
XLA Ops:
  0.0 1.6 %select_queries.1 = (bf16[16,128]{1,0:T(8,128)(2,1)S(1)}, bf16[2,3072]{1,0:T(2,128)(2,1)S(1)}, bf16[2,3072]{1,0:T(2,128)(2,1)S(1)}, bf16[2,3072]{1,0:T(2,128)(2,...) custom-call(s32[8,12]{1,0:T(8,128)} %target_ref.3, ...), custom_call_target="tpu_custom_call" | custom-call | tf_op jit(solution)/shard_map/select_queries/pallas_call | solution.py:430
  1.6 3.0 %collective-permute-start = (bf16[2,3072]{1,0:T(2,128)(2,1)S(1)}, bf16[2,3072]{1,0:T(2,128)(2,1)S(1)}, u32[]{:S(2)}, u32[]{:S(2)}) collective-permute-start(bf16[2,3072]{1,0:T(2,128)(2,1)S(1)} %get-tuple-element.35), channel_id=1, source_target_pairs={{0,2},{2,0},{4,6},{6,4},{8,10},{10,8},{12,14},{14,12},{1,3},{3,1},... | collective-permute-start | bytes 36872 | tf_op jit(solution)/shard_map/ppermute | solution.py:442
  4.7 1.6 %collective-permute-start.1 = (bf16[2,3072]{1,0:T(2,128)(2,1)S(1)}, bf16[2,3072]{1,0:T(2,128)(2,1)S(1)}, u32[]{:S(2)}, u32[]{:S(2)}) collective-permute-start(bf16[2,3072]{1,0:T(2,128)(2,1)S(1)} %get-tuple-element.36), channel_id=1, source_target_pairs={{0,4},{2,6},{4,0},{6,2},{8,12},{10,14},{12,8},{14,10},{1,5},{3,7},... | collective-permute-start | bytes 36872 | tf_op jit(solution)/shard_map/ppermute | solution.py:442
  6.3 0.0 collective-permute-start.2
  6.3 3.0 %collective-permute-start.3 = (bf16[2,3072]{1,0:T(2,128)(2,1)S(1)}, bf16[2,3072]{1,0:T(2,128)(2,1)S(1)}, u32[]{:S(2)}, u32[]{:S(2)}) collective-permute-start(bf16[2,3072]{1,0:T(2,128)(2,1)S(1)} %get-tuple-element.38), channel_id=1, source_target_pairs={{0,8},{2,10},{4,12},{6,14},{8,0},{10,2},{12,4},{14,6},{1,9},{3,11}... | collective-permute-start | bytes 36872 | tf_op jit(solution)/shard_map/ppermute | solution.py:442
  9.2 1.3 %collective-permute-start.4 = (bf16[2,3072]{1,0:T(2,128)(2,1)S(1)}, bf16[2,3072]{1,0:T(2,128)(2,1)S(1)}, u32[]{:S(2)}, u32[]{:S(2)}) collective-permute-start(bf16[2,3072]{1,0:T(2,128)(2,1)S(1)} %get-tuple-element.39), channel_id=1, source_target_pairs={{0,10},{2,8},{4,14},{6,12},{8,2},{10,0},{12,6},{14,4},{1,11},{3,9}... | collective-permute-start | bytes 36872 | tf_op jit(solution)/shard_map/ppermute | solution.py:442
  10.5 0.0 collective-permute-done.refs_1_
  10.5 3.6 %collective-permute-start.5 = (bf16[2,3072]{1,0:T(2,128)(2,1)S(1)}, bf16[2,3072]{1,0:T(2,128)(2,1)S(1)}, u32[]{:S(2)}, u32[]{:S(2)}) collective-permute-start(bf16[2,3072]{1,0:T(2,128)(2,1)S(1)} %get-tuple-element.40), channel_id=1, source_target_pairs={{0,12},{2,14},{4,8},{6,10},{8,4},{10,6},{12,0},{14,2},{1,13},{3,15... | collective-permute-start | bytes 36872 | tf_op jit(solution)/shard_map/ppermute | solution.py:442
  14.1 0.0 collective-permute-done.1.refs_2_
  14.1 0.0 collective-permute-start.6
  14.2 14.5 %project.1 = (bf16[896,512]{1,0:T(8,128)(2,1)S(1)}, bf16[896,512]{1,0:T(8,128)(2,1)S(1)}) custom-call(bf16[768,6144]{1,0:T(8,128)(2,1)} %prompts_ref.1, bf16[128,6144]{1,0:T(8,128)(2,1)} %hidden_ref.1, bf16[6144,1024]{1,0:T(8,128)(2,1)} %w_ref.1, f32[1,1024]{1,0:T(1,128)} %bitcast.2), custom_call_target="tpu_custom_call" | custom-call | tf_op jit(solution)/shard_map/project/pallas_call | solution.py:446
  28.6 0.0 collective-permute-done.2.refs_3_
  28.7 0.0 collective-permute-done.3.refs_4_
  28.7 0.0 collective-permute-done.4.refs_5_
  28.7 0.0 collective-permute-done.5.refs_6_
  28.7 0.0 collective-permute-done.6.refs_7_
  28.7 0.1 collective-permute-start.7
  28.8 1.0 %prepare_arrived.1 = (bf16[16,3072]{1,0:T(8,128)(2,1)S(1)}, bf16[16,64]{1,0:T(8,128)(2,1)S(1)}, f32[16,768]{1,0:T(8,128)S(1)}) custom-call(s32[8,12]{1,0:T(8,128)} %target_ref.3, s32[8,12]{1,0:T(8,128)} %span_ref.1, bf16[2,3072]{1,0:T(2,128)(2,1)S(1)} %get-tuple-element.43.refs_0_, bf16[2,3072]{1,0:T(2,128)(2,1)S(1)} %collective-permute-done.refs_1_, ...), custom_call_target="tpu_custom_call" | custom-call | tf_op jit(solution)/shard_map/prepare_arrived/pallas_call | solution.py:502
  29.8 1.4 %collective-permute-done.7.other_ref = bf16[896,512]{1,0:T(8,128)(2,1)S(1)} collective-permute-done((bf16[896,512]{1,0:T(8,128)(2,1)S(1)}, bf16[896,512]{1,0:T(8,128)(2,1)S(1)}, u32[]{:S(2)}, u32[]{:S(2)}) %collective-permute-start.7) | collective-permute-done | bytes 917536 | tf_op jit(solution)/shard_map/ppermute | solution.py:467
  31.2 1.5 %attend_arrived.1.after_ref = bf16[8,2,3200]{2,1,0:T(2,128)(2,1)} custom-call(bf16[16,3072]{1,0:T(8,128)(2,1)S(1)} %get-tuple-element.51.rows_ref, bf16[16,64]{1,0:T(8,128)(2,1)S(1)} %get-tuple-element.52.slot_of_ref, f32[16,768]{1,0:T(8,128)S(1)} %get-tuple-element.53.bias_ref, bf16[896,512]{1,0:T(8,128)(2,1)S(1)} %get-tuple-element.32.mine_ref, ...), custom_call_target="tpu_custom_call" | custom-call | tf_op jit(solution)/shard_map/attend_arrived/pallas_call | solution.py:515
  32.8 6.0 %all-to-all-start = ((bf16[8,2,3200]{2,1,0:T(2,128)(2,1)}), bf16[8,2,3200]{2,1,0:T(2,128)(2,1)S(1)}, u32[]{:S(2)}, u32[]{:S(2)}) async-start(bf16[8,2,3200]{2,1,0:T(2,128)(2,1)} %attend_arrived.1.after_ref), calls=%async_computation | async-start | bytes 204800 | tf_op jit(solution)/shard_map/all_to_all | solution.py:524
  38.8 5.0 %attend_cache.1 = (bf16[128,3072]{1,0:T(8,128)(2,1)S(1)}, f32[16,3072]{1,0:T(8,128)S(1)}, f32[16,128]{1,0:T(8,128)S(1)}) custom-call(bf16[128,3072]{1,0:T(8,128)(2,1)} %queries_ref.3, bf16[128,32,512]{2,1,0:T(8,128)(2,1)} %cache_ref.1, s32[1,128]{1,0:T(1,128)} %bitcast.3, bf16[896,512]{1,0:T(8,128)(2,1)S(1)} %get-tuple-element.32.mine_ref, ...), custom_call_target="tpu_custom_call" | custom-call | tf_op jit(solution)/shard_map/attend_cache/pallas_call | solution.py:474
  43.8 2.1 %all-to-all-done.refs_3_ = bf16[8,2,3200]{2,1,0:T(2,128)(2,1)S(1)} async-done(((bf16[8,2,3200]{2,1,0:T(2,128)(2,1)}), bf16[8,2,3200]{2,1,0:T(2,128)(2,1)S(1)}, u32[]{:S(2)}, u32[]{:S(2)}) %all-to-all-start) | async-done | bytes 102432 | tf_op jit(solution)/shard_map/all_to_all | solution.py:524
  45.9 1.4 %merge.1 = bf16[128,3072]{1,0:T(8,128)(2,1)} custom-call(bf16[16,128]{1,0:T(8,128)(2,1)S(1)} %get-tuple-element.31.pick_ref, bf16[128,3072]{1,0:T(8,128)(2,1)S(1)} %get-tuple-element.54.refs_0_, f32[16,3072]{1,0:T(8,128)S(1)} %get-tuple-element.55.refs_1_, f32[16,128]{1,0:T(8,128)S(1)} %get-tuple-element.56.refs_2_, bf16[8,2,3200]{2,1,0:T(2,128)(2,1)S(1)} %all-to-all-done.refs_3_), custom_call_target="tpu_custom_call" | custom-call | tf_op jit(solution)/shard_map/merge/pallas_call | solution.py:529
Async XLA Ops:
  1.6 8.9 %collective-permute-start = (bf16[2,3072]{1,0:T(2,128)(2,1)S(1)}, bf16[2,3072]{1,0:T(2,128)(2,1)S(1)}, u32[]{:S(2)}, u32[]{:S(2)}) collective-permute-start(bf16[2,3072]{1,0:T(2,128)(2,1)S(1)} %get-tuple-element.35), channel_id=1, source_target_pairs={{0,2},{2,0},{4,6},{6,4},{8,10},{10,8},{12,14},{14,12},{1,3},{3,1},... | collective-permute-start | bytes 36872 | tf_op jit(solution)/shard_map/ppermute | solution.py:442
  4.7 9.5 %collective-permute-start.1 = (bf16[2,3072]{1,0:T(2,128)(2,1)S(1)}, bf16[2,3072]{1,0:T(2,128)(2,1)S(1)}, u32[]{:S(2)}, u32[]{:S(2)}) collective-permute-start(bf16[2,3072]{1,0:T(2,128)(2,1)S(1)} %get-tuple-element.36), channel_id=1, source_target_pairs={{0,4},{2,6},{4,0},{6,2},{8,12},{10,14},{12,8},{14,10},{1,5},{3,7},... | collective-permute-start | bytes 36872 | tf_op jit(solution)/shard_map/ppermute | solution.py:442
  6.3 22.4 %collective-permute-start.2 = (bf16[2,3072]{1,0:T(2,128)(2,1)S(1)}, bf16[2,3072]{1,0:T(2,128)(2,1)S(1)}, u32[]{:S(2)}, u32[]{:S(2)}) collective-permute-start(bf16[2,3072]{1,0:T(2,128)(2,1)S(1)} %get-tuple-element.37), channel_id=1, source_target_pairs={{0,6},{2,4},{4,2},{6,0},{8,14},{10,12},{12,10},{14,8},{1,7},{3,5},... | collective-permute-start | bytes 36872 | tf_op jit(solution)/shard_map/ppermute | solution.py:442
  6.3 22.4 %collective-permute-start.3 = (bf16[2,3072]{1,0:T(2,128)(2,1)S(1)}, bf16[2,3072]{1,0:T(2,128)(2,1)S(1)}, u32[]{:S(2)}, u32[]{:S(2)}) collective-permute-start(bf16[2,3072]{1,0:T(2,128)(2,1)S(1)} %get-tuple-element.38), channel_id=1, source_target_pairs={{0,8},{2,10},{4,12},{6,14},{8,0},{10,2},{12,4},{14,6},{1,9},{3,11}... | collective-permute-start | bytes 36872 | tf_op jit(solution)/shard_map/ppermute | solution.py:442
  9.2 19.4 %collective-permute-start.4 = (bf16[2,3072]{1,0:T(2,128)(2,1)S(1)}, bf16[2,3072]{1,0:T(2,128)(2,1)S(1)}, u32[]{:S(2)}, u32[]{:S(2)}) collective-permute-start(bf16[2,3072]{1,0:T(2,128)(2,1)S(1)} %get-tuple-element.39), channel_id=1, source_target_pairs={{0,10},{2,8},{4,14},{6,12},{8,2},{10,0},{12,6},{14,4},{1,11},{3,9}... | collective-permute-start | bytes 36872 | tf_op jit(solution)/shard_map/ppermute | solution.py:442
  10.5 18.1 %collective-permute-start.5 = (bf16[2,3072]{1,0:T(2,128)(2,1)S(1)}, bf16[2,3072]{1,0:T(2,128)(2,1)S(1)}, u32[]{:S(2)}, u32[]{:S(2)}) collective-permute-start(bf16[2,3072]{1,0:T(2,128)(2,1)S(1)} %get-tuple-element.40), channel_id=1, source_target_pairs={{0,12},{2,14},{4,8},{6,10},{8,4},{10,6},{12,0},{14,2},{1,13},{3,15... | collective-permute-start | bytes 36872 | tf_op jit(solution)/shard_map/ppermute | solution.py:442
  14.1 14.6 %collective-permute-start.6 = (bf16[2,3072]{1,0:T(2,128)(2,1)S(1)}, bf16[2,3072]{1,0:T(2,128)(2,1)S(1)}, u32[]{:S(2)}, u32[]{:S(2)}) collective-permute-start(bf16[2,3072]{1,0:T(2,128)(2,1)S(1)} %get-tuple-element.41), channel_id=1, source_target_pairs={{0,14},{2,12},{4,10},{6,8},{8,6},{10,4},{12,2},{14,0},{1,15},{3,13... | collective-permute-start | bytes 36872 | tf_op jit(solution)/shard_map/ppermute | solution.py:442
  28.7 2.5 %collective-permute-start.7 = (bf16[896,512]{1,0:T(8,128)(2,1)S(1)}, bf16[896,512]{1,0:T(8,128)(2,1)S(1)}, u32[]{:S(2)}, u32[]{:S(2)}) collective-permute-start(bf16[896,512]{1,0:T(8,128)(2,1)S(1)} %get-tuple-element.42), channel_id=1, source_target_pairs={{0,1},{1,0},{2,3},{3,2},{4,5},{5,4},{6,7},{7,6},{8,9},{9,8},{10,11... | collective-permute-start | bytes 2752520 | tf_op jit(solution)/shard_map/ppermute | solution.py:467
  32.8 13.1 %all-to-all-start = ((bf16[8,2,3200]{2,1,0:T(2,128)(2,1)}), bf16[8,2,3200]{2,1,0:T(2,128)(2,1)S(1)}, u32[]{:S(2)}, u32[]{:S(2)}) async-start(bf16[8,2,3200]{2,1,0:T(2,128)(2,1)} %attend_arrived.1.after_ref), calls=%async_computation | async-start | bytes 204800 | tf_op jit(solution)/shard_map/all_to_all | solution.py:524

commit v13 on v11

v13 whole, which is shorter than its diff:
```python
import functools
import math

import jax
import jax.numpy as jnp
from jax import lax
from jax.experimental import pallas as pl
from jax.experimental.pallas import tpu as pltpu
from jax.sharding import PartitionSpec as P

HD = 128
CAP = 2
STATS = 128
MASKED = -1e30
LSE_PITCH = 40
PITCH = 8
LOG2_SCALE = HD ** (-0.5) * math.log2(math.e)
F32 = jnp.float32
BF16 = jnp.bfloat16
TRANSPOSED = (((0,), (0,)), ((), ()))


def iota(shape, dim):
    return lax.broadcasted_iota(jnp.int32, shape, dim)


def one_hot(shape, dim, index):
    return (iota(shape, dim) == index).astype(F32).astype(BF16)


def pick_rows(target_ref, row_count):
    sections, requests = target_ref.shape
    shape = (sections * CAP, requests)
    position = lax.axis_index("section")
    slot_id = iota(shape, 0)
    table = jnp.zeros(shape, jnp.int32)
    for k in range(sections):
        mine = (slot_id >= k * CAP) & (slot_id < (k + 1) * CAP)
        table = jnp.where(mine, target_ref[pl.ds(position ^ k, 1), :], table)
    local = table - position * row_count
    here = (local >= 0) & (local < row_count)
    square = (requests, requests)
    earlier = jnp.dot(
        here.astype(F32).astype(BF16),
        (iota(square, 0) < iota(square, 1)).astype(F32).astype(BF16),
        preferred_element_type=F32,
    )
    chosen = here & (earlier == lax.rem(slot_id, CAP).astype(F32))
    row = jnp.max(jnp.where(chosen, local.astype(F32), -1.0), axis=1, keepdims=True)
    return one_hot((shape[0], row_count), 1, row.astype(jnp.int32))


def steps_of(sections):
    steps = []
    bit = sections // 2
    while bit:
        sent = [k for k in range(sections) if k & bit]
        steps.append((bit, sent, [k for k in range(sections) if not k & bit]))
        bit //= 2
    return steps


def regroup(kept_ref, got_ref, after_ref, keep_ref, send_ref, *, steps, done):
    where = {k: (got_ref, i) for i, k in enumerate(steps[done - 1][1])}
    where |= {k: (kept_ref, i) for i, k in enumerate(steps[done - 1][2])}
    for out_ref, blocks in ((send_ref, steps[done][1]), (keep_ref, steps[done][2])):
        for i, k in enumerate(blocks):
            ref, at = where[k]
            out_ref[i] = ref[at]


def all_blocks(steps, kept_ref, got_ref):
    where = {k: got_ref[i] for i, k in enumerate(steps[-1][1])}
    where |= {k: kept_ref[i] for i, k in enumerate(steps[-1][2])}
    return jnp.concatenate([where[k].astype(F32) for k in range(len(where))], axis=0)


def select_queries(target_ref, queries_ref, pick_ref, keep_ref, send_ref):
    _, sent, kept = steps_of(target_ref.shape[0])[0]
    pick = pick_rows(target_ref, queries_ref.shape[0])
    pick_ref[...] = pick
    asked = jnp.dot(pick, queries_ref[...], preferred_element_type=F32)
    for ref, blocks in ((send_ref, sent), (keep_ref, kept)):
        for i, k in enumerate(blocks):
            ref[i] = asked[k * CAP : (k + 1) * CAP].astype(BF16)


def spans(edges):
    return [slice(a, b) for a, b in zip(edges[:-1], edges[1:])]


def load_rows(prompts_ref, hidden_ref, there, rows_ref, here, sems):
    prompt_rows = prompts_ref.shape[0]
    return [
        pltpu.make_async_copy(
            prompts_ref.at[:, there], rows_ref.at[:prompt_rows, here], sems.at[0]
        ),
        pltpu.make_async_copy(
            hidden_ref.at[:, there], rows_ref.at[prompt_rows:, here], sems.at[1]
        ),
    ]


def channels(offset, width):
    tp = lax.axis_index("tp")
    return pl.ds(pl.multiple_of(((tp + offset) & 1) * width, width), width)


def project_first(
    prompts_ref, hidden_ref, w_ref, rows_ref, w_tail_ref, total_ref, w_head_ref, sems, *, edges
):
    theirs = channels(1, total_ref.shape[1])
    chunks = spans(edges)
    head = edges[-2]
    waits = []
    for c, at in enumerate(chunks):
        here = at if at.stop <= head else slice(0, at.stop - head)
        w_here_ref = w_head_ref if at.stop <= head else w_tail_ref
        copies = load_rows(prompts_ref, hidden_ref, at, rows_ref, at, sems.at[c])
        copies.append(
            pltpu.make_async_copy(w_ref.at[at, theirs], w_here_ref.at[here, :], sems.at[c, 2])
        )
        for copy in copies:
            copy.start()
        waits.append(copies)
    for c, at in enumerate(chunks):
        for copy in waits[c]:
            copy.wait()
        if at.stop <= head:
            part = jnp.dot(rows_ref[:, at], w_head_ref[at, :], preferred_element_type=F32)
            if c == 0:
                total_ref[...] = part
            else:
                total_ref[...] += part


def project_rest(
    prompts_ref,
    hidden_ref,
    w_ref,
    scale_ref,
    rows_ref,
    w_tail_ref,
    total_ref,
    after_ref,
    theirs_ref,
    rows_rest_ref,
    w_mine_ref,
    w_rest_ref,
    scale_here_ref,
    sems,
):
    width = theirs_ref.shape[1]
    theirs, mine = channels(1, width), channels(0, width)
    depth = rows_ref.shape[1]
    head = depth - w_tail_ref.shape[0]
    rest = slice(depth, depth + rows_rest_ref.shape[1])
    copies = load_rows(prompts_ref, hidden_ref, rest, rows_rest_ref, slice(None), sems)
    copies += [
        pltpu.make_async_copy(w_ref.at[rest, theirs], w_rest_ref, sems.at[2]),
        pltpu.make_async_copy(scale_ref.at[:, theirs], scale_here_ref, sems.at[3]),
        pltpu.make_async_copy(w_ref.at[:, mine], w_mine_ref, sems.at[4]),
    ]
    for copy in copies:
        copy.start()
    total = total_ref[...] + jnp.dot(
        rows_ref[:, head:], w_tail_ref[...], preferred_element_type=F32
    )
    for copy in copies[:-1]:
        copy.wait()
    total += jnp.dot(rows_rest_ref[...], w_rest_ref[...], preferred_element_type=F32)
    theirs_ref[...] = (total * scale_here_ref[...]).astype(BF16)
    copies[-1].wait()


def project_mine(rows_ref, rows_rest_ref, w_mine_ref, scale_ref, after_ref, *refs, at, last):
    refs, (scale_here_ref, sems) = refs[:-2], refs[-2:]
    if last:
        cache_ref, queries_ref, out_ref, cache_here_ref, queries_here_ref = refs
    else:
        (out_ref,) = refs
    mine = channels(0, out_ref.shape[1])
    copies = [pltpu.make_async_copy(scale_ref.at[:, mine], scale_here_ref, sems.at[0])]
    if last:
        copies.append(pltpu.make_async_copy(queries_ref, queries_here_ref, sems.at[1]))
        copies.append(pltpu.make_async_copy(cache_ref, cache_here_ref, sems.at[2]))
    for copy in copies:
        copy.start()
    depth = rows_ref.shape[1]
    count = at.stop - at.start
    block = count // 2 if count % 32 == 0 else count
    for m in spans(range(0, count + 1, block)):
        there = slice(at.start + m.start, at.start + m.stop)
        total = jnp.dot(rows_ref[there, :], w_mine_ref[:depth, :], preferred_element_type=F32)
        total += jnp.dot(
            rows_rest_ref[there, :], w_mine_ref[depth:, :], preferred_element_type=F32
        )
        if m.start == 0:
            copies[0].wait()
        out_ref[m, :] = (total * scale_here_ref[...]).astype(BF16)
    for copy in copies[1:]:
        copy.wait()


def split_bf16(x):
    high = x.astype(BF16).astype(F32)
    middle = (x - high).astype(BF16).astype(F32)
    return high, middle, (x - high - middle).astype(BF16).astype(F32)


def request_slots(target_ref, span_ref, row_count, padded):
    sections, requests = target_ref.shape
    position = lax.axis_index("section")
    target = target_ref[pl.ds(position, 1), :].astype(F32)
    span = span_ref[pl.ds(position, 1), :].astype(F32)
    diagonal = iota((padded, requests), 0) == iota((padded, requests), 1)
    target_col = jnp.sum(jnp.where(diagonal, target, 0.0), axis=1, keepdims=True)
    span_col = jnp.sum(jnp.where(diagonal, span, 0.0), axis=1, keepdims=True)
    section_row = jnp.zeros_like(target)
    section_col = jnp.zeros_like(target_col)
    for s in range(1, sections):
        section_row = section_row + (target >= s * row_count).astype(F32)
        section_col = section_col + (target_col >= s * row_count).astype(F32)
    before = (section_row == section_col) & (
        iota((padded, requests), 1) < iota((padded, requests), 0)
    )
    rank_col = jnp.sum(before.astype(F32), axis=1, keepdims=True).astype(jnp.int32)
    real = iota((padded, 1), 0) < requests
    section_col = jnp.where(real, section_col.astype(jnp.int32), -1)
    return section_col, rank_col, span_col.astype(jnp.int32)


def prepare_arrived(
    target_ref, span_ref, kept_ref, got_ref, rows_ref, slot_of_ref, bias_ref, *, row_count
):
    sections, requests = target_ref.shape
    padded, prompt_rows = bias_ref.shape
    span_rows = prompt_rows // requests
    section_col, rank_col, span_col = request_slots(target_ref, span_ref, row_count, padded)
    block = section_col ^ lax.axis_index("section")
    slot = jnp.where(section_col >= 0, block * PITCH + rank_col, -1)
    slot_of_ref[...] = one_hot((padded, sections * PITCH), 1, slot)
    slot = jnp.where(section_col >= 0, block * CAP + rank_col, -1)
    rows_ref[...] = jnp.dot(
        one_hot((padded, sections * CAP), 1, slot),
        all_blocks(steps_of(sections), kept_ref, got_ref).astype(BF16),
        preferred_element_type=F32,
    ).astype(BF16)
    key = iota((padded, prompt_rows), 1) - iota((padded, prompt_rows), 0) * span_rows
    bias_ref[...] = jnp.where((key >= 0) & (key < span_col), 0.0, MASKED)


def attend_arrived(rows_ref, slot_of_ref, bias_ref, other_ref, *refs):
    mine_refs, (keep_ref, send_ref) = refs[:-2], refs[-2:]
    padded, prompt_rows = bias_ref.shape
    kv_heads = other_ref.shape[1] // (2 * HD)
    group = rows_ref.shape[1] // (kv_heads * HD)
    rows = rows_ref[...]
    slot_of = slot_of_ref[...]
    bias = bias_ref[...]
    mine = jnp.concatenate([ref[...] for ref in mine_refs], axis=0)
    kv = (mine[:prompt_rows].astype(F32) + other_ref[:prompt_rows, :].astype(F32)).astype(BF16)
    scores = []
    for h in range(kv_heads):
        stacked = jnp.concatenate(
            [rows[:, (h * group + i) * HD : (h * group + i + 1) * HD] for i in range(group)],
            axis=0,
        )
        keys = kv[:, h * 2 * HD : (h * 2 + 1) * HD]
        scores.append(
            lax.dot_general(
                stacked, keys, (((1,), (1,)), ((), ())), preferred_element_type=F32
            )
        )
    scores = [
        x.reshape(group, padded, prompt_rows) * LOG2_SCALE + bias[None] for x in scores
    ]
    largest = [jnp.max(x, axis=2, keepdims=True) for x in scores]
    weights = [jnp.exp2(x - y) for x, y in zip(scores, largest)]
    totals = [jnp.sum(x, axis=2, keepdims=True) for x in weights]
    lane = iota((padded, STATS), 1)
    lse = jnp.zeros((padded, STATS), F32)
    pieces = []
    for h in range(kv_heads):
        values = jnp.dot(
            weights[h].reshape(group * padded, prompt_rows).astype(BF16),
            kv[:, (h * 2 + 1) * HD : (h * 2 + 2) * HD],
            preferred_element_type=F32,
        ).reshape(group, padded, HD)
        values = values / totals[h]
        head_lse = largest[h] + jnp.log2(totals[h])
        for i in range(group):
            pieces.append(values[i])
            lse = jnp.where(lane == h * group + i, head_lse[i], lse)
    high, middle, low = split_bf16(lse)
    stats = high + pltpu.roll(middle, LSE_PITCH, 1) + pltpu.roll(low, 2 * LSE_PITCH, 1)
    result = jnp.concatenate(pieces + [stats], axis=1).astype(BF16)
    answers = lax.dot_general(slot_of, result, TRANSPOSED, preferred_element_type=F32)
    _, sent, kept = steps_of(2 * keep_ref.shape[0])[0]
    for ref, blocks in ((send_ref, sent), (keep_ref, kept)):
        for i, k in enumerate(blocks):
            ref[i] = answers[k * PITCH : k * PITCH + CAP].astype(BF16)


def attend_cache(
    queries_ref,
    cache_ref,
    len_ref,
    mine_ref,
    other_ref,
    pick_ref,
    after_ref,
    out_ref,
    slot_out_ref,
    slot_lse_ref,
    *,
    rows_at,
):
    row_count, cache_rows, width = cache_ref.shape
    first_row, block_rows = rows_at.start, rows_at.stop - rows_at.start
    kv_heads = width // (2 * HD)
    group = queries_ref.shape[1] // (kv_heads * HD)
    unit = 8
    keys_of = unit * cache_rows
    queries = queries_ref[rows_at, :].astype(F32)
    own = sum(
        ref[pl.ds(ref.shape[0] - row_count + first_row, block_rows), :].astype(F32)
        for ref in (mine_ref, other_ref)
    )
    own = own.astype(BF16).astype(F32)
    key = iota((unit, keys_of), 1) - iota((unit, keys_of), 0) * cache_rows
    lengths = len_ref[...].astype(F32)
    lane = iota((unit, STATS), 1)
    ones = jnp.ones((keys_of, HD), BF16)
    units = range(block_rows // unit)

    def rows_of(u):
        return slice(first_row + u * unit, first_row + (u + 1) * unit)

    pairs = [(u, h) for u in units for h in range(kv_heads)]
    bias = []
    for u in units:
        row = iota((unit, row_count), 0) + (first_row + u * unit)
        length = jnp.sum(
            jnp.where(iota((unit, row_count), 1) == row, lengths, 0.0), axis=1, keepdims=True
        ).astype(jnp.int32)
        bias.append(jnp.where((key >= 0) & (key < length), 0.0, MASKED))
    q, scores, own_scores = [], [], []
    for u, h in pairs:
        at = slice(u * unit, (u + 1) * unit)
        q.append(
            jnp.stack(
                [
                    queries[at, (h * group + i) * HD : (h * group + i + 1) * HD]
                    for i in range(group)
                ],
                axis=0,
            )
        )
        keys = cache_ref[rows_of(u), :, h * 2 * HD : (h * 2 + 1) * HD].reshape(keys_of, HD)
        scores.append(
            lax.dot_general(
                q[-1].reshape(group * unit, HD).astype(BF16),
                keys,
                (((1,), (1,)), ((), ())),
                preferred_element_type=F32,
            ).reshape(group, unit, keys_of)
        )
    for n, (u, h) in enumerate(pairs):
        at = slice(u * unit, (u + 1) * unit)
        own_key = own[at, h * 2 * HD : (h * 2 + 1) * HD]
        own_scores.append(jnp.sum(q[n] * own_key[None], axis=2, keepdims=True) * LOG2_SCALE)
    scores = [scores[n] * LOG2_SCALE + bias[u][None] for n, (u, h) in enumerate(pairs)]
    largest = [
        jnp.maximum(jnp.max(x, axis=2, keepdims=True), y) for x, y in zip(scores, own_scores)
    ]
    weights = [jnp.exp2(x - y).astype(BF16) for x, y in zip(scores, largest)]
    own_weights = [jnp.exp2(x - y) for x, y in zip(own_scores, largest)]
    sums = []
    for n, (u, h) in enumerate(pairs):
        at = slice(u * unit, (u + 1) * unit)
        values = cache_ref[rows_of(u), :, (h * 2 + 1) * HD : (h * 2 + 2) * HD].reshape(keys_of, HD)
        sums.append(
            jnp.dot(
                weights[n].reshape(group * unit, keys_of),
                jnp.concatenate([values, ones], axis=1),
                preferred_element_type=F32,
            ).reshape(group, unit, 2 * HD)
        )
    pieces = [[] for _ in units]
    stats = [jnp.zeros((unit, STATS), F32) for _ in units]
    for n, (u, h) in enumerate(pairs):
        at = slice(u * unit, (u + 1) * unit)
        own_value = own[at, (h * 2 + 1) * HD : (h * 2 + 2) * HD]
        total = sums[n][:, :, HD:] + own_weights[n]
        result = (sums[n][:, :, :HD] + own_weights[n] * own_value[None]) / total
        lse = largest[n] + jnp.log2(total)
        for i in range(group):
            pieces[u].append(result[i])
            stats[u] = jnp.where(lane == h * group + i, lse[i], stats[u])
    out = jnp.concatenate([jnp.concatenate(x, axis=1) for x in pieces], axis=0).astype(BF16)
    out_ref[...] = out
    here = iota((row_count, block_rows), 0) == iota((row_count, block_rows), 1) + first_row
    pick = jnp.dot(
        pick_ref[...], here.astype(F32).astype(BF16), preferred_element_type=F32
    ).astype(BF16)
    slot_out_ref[...] = jnp.dot(pick, out, preferred_element_type=F32)
    lse = jnp.concatenate(stats, axis=0)
    slot_lse_ref[...] = sum(
        jnp.dot(pick, part.astype(BF16), preferred_element_type=F32) for part in split_bf16(lse)
    )


def merge(pick_ref, *refs):
    parts, (kept_ref, got_ref, out_ref) = refs[:-3], refs[-3:]
    cached_refs, slot_out_refs, slot_lse_refs = parts[0::3], parts[1::3], parts[2::3]
    width = out_ref.shape[1]
    pick = pick_ref[...]
    arrived = all_blocks(steps_of(2 * kept_ref.shape[0]), kept_ref, got_ref)
    stats = arrived[:, width:]
    arrived_lse = (
        stats
        + pltpu.roll(stats, STATS - LSE_PITCH, 1)
        + pltpu.roll(stats, STATS - 2 * LSE_PITCH, 1)
    )
    cached_lse = sum(ref[...] for ref in slot_lse_refs)
    largest = jnp.maximum(cached_lse, arrived_lse)
    cached_weight = jnp.exp2(cached_lse - largest)
    arrived_weight = jnp.exp2(arrived_lse - largest)
    total = cached_weight + arrived_weight
    cached_weight = cached_weight / total
    arrived_weight = arrived_weight / total
    has = lax.dot_general(
        pick, jnp.ones((pick.shape[0], HD), BF16), TRANSPOSED, preferred_element_type=F32
    )
    for i in range(width // HD):
        at = slice(i * HD, (i + 1) * HD)
        merged = (
            sum(ref[:, at] for ref in slot_out_refs) * cached_weight[:, i : i + 1]
            + arrived[:, at] * arrived_weight[:, i : i + 1]
        )
        placed = lax.dot_general(
            pick, merged.astype(BF16), TRANSPOSED, preferred_element_type=F32
        )
        row = 0
        for ref in cached_refs:
            rows = slice(row, row + ref.shape[0])
            kept = ref[:, at].astype(F32)
            out_ref[rows, at] = jnp.where(has[rows] > 0.5, placed[rows], kept).astype(BF16)
            row += ref.shape[0]


def compiler_params(megabytes):
    return pltpu.CompilerParams(vmem_limit_bytes=megabytes * 1024 * 1024)


RESIDENT = pl.BlockSpec(memory_space=pltpu.VMEM)
REMAINS = pl.BlockSpec(memory_space=pl.ANY)


def in_vmem(x):
    return pltpu.with_memory_space_constraint(x, pltpu.VMEM)


def in_hbm(x):
    return pltpu.with_memory_space_constraint(x, pltpu.HBM)


def shards(
    prompts, decode_hidden, queries, kv_cache, cache_len, span_len, target_row, w_kv, kv_scale
):
    row_count = decode_hidden.shape[0]
    prompt_rows, features = prompts.shape
    sections = lax.axis_size("section")
    local_width = kv_cache.shape[2]
    query_width = queries.shape[1]
    slots = sections * CAP
    all_rows = prompt_rows + row_count
    scale = kv_scale.reshape(1, -1)
    lengths = cache_len.reshape(1, -1)

    steps = steps_of(sections)
    half = sections // 2
    prompts, decode_hidden, w_kv, scale = map(in_hbm, (prompts, decode_hidden, w_kv, scale))
    target_row, span_len, queries = map(in_hbm, (target_row, span_len, queries))
    kv_cache, lengths = map(in_hbm, (kv_cache, lengths))

    def block_pair(width):
        return [pltpu.VMEM((half, CAP, width), BF16)] * 2

    def swapped(blocks, done):
        pairs = [(i, i ^ steps[done][0]) for i in range(sections)]
        return in_vmem(lax.ppermute(blocks, "section", pairs))

    pick, keep, send = pl.pallas_call(
        select_queries,
        in_specs=[RESIDENT, RESIDENT],
        out_specs=[RESIDENT] * 3,
        out_shape=[pltpu.VMEM((slots, row_count), BF16)] + block_pair(query_width),
        compiler_params=compiler_params(16),
        name="select_queries",
    )(target_row, queries)
    got = swapped(send, 0)

    def regrouped(blocks, got, done, after):
        return pl.pallas_call(
            functools.partial(regroup, steps=steps, done=done),
            in_specs=[RESIDENT] * 2 + [REMAINS],
            out_specs=[RESIDENT] * 2,
            out_shape=block_pair(blocks.shape[2]),
            compiler_params=compiler_params(16),
            name="regroup",
        )(in_vmem(blocks), got, in_vmem(after))

    edges = (0, 256, 768, 1536, 2560, 4096)
    depth, head = edges[-1], edges[-2]
    rows, w_tail, total = pl.pallas_call(
        functools.partial(project_first, edges=edges),
        in_specs=[REMAINS] * 3,
        out_specs=[RESIDENT] * 3,
        out_shape=[
            pltpu.VMEM((all_rows, depth), BF16),
            pltpu.VMEM((depth - head, local_width), BF16),
            pltpu.VMEM((all_rows, local_width), F32),
        ],
        scratch_shapes=[
            pltpu.VMEM((head, local_width), BF16),
            pltpu.SemaphoreType.DMA((len(edges) - 1, 3)),
        ],
        compiler_params=compiler_params(12),
        name="project_first",
    )(prompts, decode_hidden, w_kv)
    keep, send = regrouped(keep, got, 1, total)
    got = swapped(send, 1)
    theirs, rows_rest, w_mine = pl.pallas_call(
        project_rest,
        in_specs=[REMAINS] * 4 + [RESIDENT] * 3 + [REMAINS],
        out_specs=[RESIDENT] * 3,
        out_shape=[
            pltpu.VMEM((all_rows, local_width), BF16),
            pltpu.VMEM((all_rows, features - depth), BF16),
            pltpu.VMEM((features, local_width), BF16),
        ],
        scratch_shapes=[
            pltpu.VMEM((features - depth, local_width), BF16),
            pltpu.VMEM((1, local_width), F32),
            pltpu.SemaphoreType.DMA((5,)),
        ],
        compiler_params=compiler_params(16),
        name="project_rest",
    )(prompts, decode_hidden, w_kv, scale, *map(in_vmem, (rows, w_tail, total, keep)))
    theirs, got = lax.optimization_barrier((theirs, got))
    got = in_vmem(got)
    other = in_vmem(lax.ppermute(theirs, "tp", [(0, 1), (1, 0)]))

    mine = []
    pieces = max(len(steps) - 2, 1)
    bounds = [all_rows * i // (16 * pieces) * 16 for i in range(pieces)] + [all_rows]
    after = theirs
    for piece, at in enumerate(spans(bounds)):
        if piece + 2 < len(steps):
            keep, send = regrouped(keep, got, piece + 2, after)
            got = swapped(send, piece + 2)
        last = piece == pieces - 1
        extra = [kv_cache, queries] if last else []
        part, *here = pl.pallas_call(
            functools.partial(project_mine, at=at, last=last),
            in_specs=[RESIDENT] * 3 + [REMAINS] * (2 + len(extra)),
            out_specs=[RESIDENT] * (1 + len(extra)),
            out_shape=[pltpu.VMEM((at.stop - at.start, local_width), BF16)]
            + [pltpu.VMEM(x.shape, BF16) for x in extra],
            scratch_shapes=[pltpu.VMEM((1, local_width), F32), pltpu.SemaphoreType.DMA((3,))],
            compiler_params=compiler_params(16),
            name="project_mine",
        )(*map(in_vmem, (rows, rows_rest, w_mine)), scale, in_vmem(keep), *extra)
        after = part
        mine.append(in_vmem(part))
    kv_here, queries_here = map(in_vmem, here)

    padded = -(-span_len.shape[1] // 16) * 16
    prepared = pl.pallas_call(
        functools.partial(prepare_arrived, row_count=row_count),
        in_specs=[RESIDENT] * 4,
        out_specs=[RESIDENT] * 3,
        out_shape=[
            pltpu.VMEM((padded, query_width), BF16),
            pltpu.VMEM((padded, sections * PITCH), BF16),
            pltpu.VMEM((padded, prompt_rows), F32),
        ],
        compiler_params=compiler_params(16),
        name="prepare_arrived",
    )(target_row, span_len, in_vmem(keep), got)
    answer_width = query_width + STATS
    keep, send = pl.pallas_call(
        attend_arrived,
        in_specs=[RESIDENT] * (4 + len(mine)),
        out_specs=[RESIDENT] * 2,
        out_shape=block_pair(answer_width),
        compiler_params=compiler_params(24),
        name="attend_arrived",
    )(*map(in_vmem, prepared), other, *mine)

    shares = []
    bounds = [row_count * i // (16 * len(steps)) * 16 for i in range(len(steps))] + [row_count]
    for done, at in enumerate(spans(bounds)):
        got = swapped(send, done)
        share = pl.pallas_call(
            functools.partial(attend_cache, rows_at=at),
            in_specs=[RESIDENT] * 6 + [REMAINS],
            out_specs=[RESIDENT] * 3,
            out_shape=[
                pltpu.VMEM((at.stop - at.start, query_width), BF16),
                pltpu.VMEM((slots, query_width), F32),
                pltpu.VMEM((slots, STATS), F32),
            ],
            compiler_params=compiler_params(24),
            name="attend_cache",
        )(queries_here, kv_here, lengths, mine[-1], other, in_vmem(pick), in_vmem(keep))
        shares += share
        if done + 1 < len(steps):
            keep, send = regrouped(keep, got, done + 1, share[2])

    return pl.pallas_call(
        merge,
        in_specs=[RESIDENT] * (3 + len(shares)),
        out_specs=RESIDENT,
        out_shape=jax.ShapeDtypeStruct((row_count, query_width), BF16),
        compiler_params=compiler_params(24),
        name="merge",
    )(*map(in_vmem, (pick, *shares, keep)), got)


def solution(mesh):
    in_specs = (
        P(("groups", "section"), "tp"),
        P(("groups", "section"), "tp"),
        P(("groups", "section"), "tp"),
        P(("groups", "section"), None, "tp"),
        P(("groups", "section")),
        P("groups", None),
        P("groups", None),
        P("tp", None),
        P(),
    )
    out_specs = P(("groups", "section"), "tp")
    return jax.shard_map(shards, mesh=mesh, in_specs=in_specs, out_specs=out_specs, check_vma=False)
```

time: 43.1 us -> 42.4 us (0.984)
  waiting for transfers between devices: 3.56 us -> 8.09 us
  starting transfers between devices: 13.3 us -> 8.95 us
  Pallas kernels: 25.7 us -> 24.9 us
    all_to_all x2 -> x0, starting transfers between devices: 13.3 us -> none  [the longest x1 7.28 us: shards(): asked = lax.all_to_all(asked, 'section', 0, 0)]
    ppermute x1 -> x7, starting transfers between devices: 0.07 us -> 8.95 us  [the longest x6 8.88 us: swapped(): return in_vmem(lax.ppermute(blocks, 'section', pairs))]
    ppermute x1 -> x7, waiting for transfers between devices: 1.43 us -> 8.09 us  [the longest x6 8.09 us: swapped(): return in_vmem(lax.ppermute(blocks, 'section', pairs))]
    all_to_all x2 -> x0, waiting for transfers between devices: 2.13 us -> none  [the longest x1 2.13 us: shards(): answers = lax.all_to_all(answers, 'section', 0, 0)]
    pallas_call x1, Pallas kernels: 2.2 us -> 1.55 us  [shards(): pl.pallas_call(select_queries, in_specs=[RESIDENT, RESIDENT], out_specs=[...]
    pallas_call x4 -> x12, Pallas kernels: 22.5 us -> 22.4 us  [the longest x1 6.09 us: shards(): pl.pallas_call(functools.partial(project_mine, at=at, last=last), in_spec...]
  transfers between devices with their start and end apart: 3 -> 7, of which waited for: 2 -> 3; matrix products, arithmetic and copies ran while one was open for 0% -> 0% of each run, Pallas kernels for 48% -> 50%
where the time goes in v13:
time: 42.4 us; the launch traced here: 42.1 us
  Pallas kernels  24.9 us (59%)
  starting transfers between devices  8.95 us (21%)
  waiting for transfers between devices  8.09 us (19%)
    ppermute x6, starting transfers between devices, swapped(): return in_vmem(lax.ppermute(blocks, 'section', pairs))  8.88 us
    ppermute x6, waiting for transfers between devices, swapped(): return in_vmem(lax.ppermute(blocks, 'section', pairs))  8.09 us
    pallas_call x1, Pallas kernels, shards(): pl.pallas_call(functools.partial(project_mine, at=at, last=last), in_spec...  6.09 us
    pallas_call x1, Pallas kernels, shards(): pl.pallas_call(project_rest, in_specs=[REMAINS] * 4 + [RESIDENT] * 3 + [R...  4.84 us
    pallas_call x3, Pallas kernels, shards(): pl.pallas_call(functools.partial(attend_cache, rows_at=at), in_specs=[RES...  4.56 us
    pallas_call x1, Pallas kernels, shards(): pl.pallas_call(functools.partial(project_first, edges=edges), in_specs=[R...  4.53 us
    pallas_call x1, Pallas kernels, shards(): pl.pallas_call(select_queries, in_specs=[RESIDENT, RESIDENT], out_specs=[...  1.55 us
    pallas_call x1, Pallas kernels, shards(): pl.pallas_call(merge, in_specs=[RESIDENT] * (3 + len(shares)), out_specs=...  1.43 us
  transfers between devices with their start and end apart: 7, of which 3 were waited for; matrix products, arithmetic and copies ran while one was open for 0% of the time, Pallas kernels for 50%

profile of v13, /device:TPU:0, one launch (start us, length us, event | category | flops | bytes accessed | tf_op | source)
XLA Modules:
  0.0 42.1 jit_solution(7936400348009307279)
XLA Ops:
  0.0 1.6 %select_queries.1 = (bf16[16,128]{1,0:T(8,128)(2,1)S(1)}, bf16[4,2,3072]{2,1,0:T(2,128)(2,1)S(1)}, bf16[4,2,3072]{2,1,0:T(2,128)(2,1)S(1)}) custom-call(s32[8,12]{1,0:T(8,128)} %target_ref.3, bf16[128,3072]{1,0:T(8,128)(2,1)} %refs_1_.1), custom_call_target="tpu_custom_call" | custom-call | tf_op jit(solution)/shard_map/select_queries/pallas_call | solution.py:495
  1.6 4.1 %collective-permute-start = (bf16[4,2,3072]{2,1,0:T(2,128)(2,1)S(1)}, bf16[4,2,3072]{2,1,0:T(2,128)(2,1)S(1)}, u32[]{:S(2)}, u32[]{:S(2)}) collective-permute-start(bf16[4,2,3072]{2,1,0:T(2,128)(2,1)S(1)} %get-tuple-element.46), channel_id=1, source_target_pairs={{0,8},{2,10},{4,12},{6,14},{8,0},{10,2},{12,4},{14,6},{1,9},{3,11}... | collective-permute-start | bytes 147464 | tf_op jit(solution)/shard_map/ppermute | solution.py:493
  5.7 4.5 %project_first.1 = (bf16[896,4096]{1,0:T(8,128)(2,1)S(1)}, bf16[1536,512]{1,0:T(8,128)(2,1)S(1)}, f32[896,512]{1,0:T(8,128)S(1)}) custom-call(bf16[768,6144]{1,0:T(8,128)(2,1)} %prompts_ref.3, bf16[128,6144]{1,0:T(8,128)(2,1)} %hidden_ref.3, bf16[6144,1024]{1,0:T(8,128)(2,1)} %w_ref.3), custom_call_target="tpu_custom_call" | custom-call | tf_op jit(solution)/shard_map/project_first/pallas_call | solution.py:517
  10.2 0.0 collective-permute-done.got_ref
  10.2 1.6 %collective-permute-start.1 = (bf16[4,2,3072]{2,1,0:T(2,128)(2,1)S(1)}, bf16[4,2,3072]{2,1,0:T(2,128)(2,1)S(1)}, u32[]{:S(2)}, u32[]{:S(2)}) collective-permute-start(bf16[4,2,3072]{2,1,0:T(2,128)(2,1)S(1)} %get-tuple-element.51), channel_id=1, source_target_pairs={{0,4},{2,6},{4,0},{6,2},{8,12},{10,14},{12,8},{14,10},{1,5},{3,7},... | collective-permute-start | bytes 147464 | tf_op jit(solution)/shard_map/ppermute | solution.py:493
  11.9 4.8 %project_rest.1 = (bf16[896,512]{1,0:T(8,128)(2,1)S(1)}, bf16[896,2048]{1,0:T(8,128)(2,1)S(1)}, bf16[6144,512]{1,0:T(8,128)(2,1)S(1)}) custom-call(bf16[768,6144]{1,0:T(8,128)(2,1)} %prompts_ref.3, bf16[128,6144]{1,0:T(8,128)(2,1)} %hidden_ref.3, bf16[6144,1024]{1,0:T(8,128)(2,1)} %w_ref.3, f32[1,1024]{1,0:T(1,128)} %bitcast.2, ...), custom_call_target="tpu_custom_call" | custom-call | tf_op jit(solution)/shard_map/project_rest/pallas_call | solution.py:535
  16.7 0.0 collective-permute-done.1.got_ref
  16.7 0.1 collective-permute-start.2
  16.8 1.6 %collective-permute-start.3 = (bf16[4,2,3072]{2,1,0:T(2,128)(2,1)S(1)}, bf16[4,2,3072]{2,1,0:T(2,128)(2,1)S(1)}, u32[]{:S(2)}, u32[]{:S(2)}) collective-permute-start(bf16[4,2,3072]{2,1,0:T(2,128)(2,1)S(1)} %get-tuple-element.58), channel_id=1, source_target_pairs={{0,2},{2,0},{4,6},{6,4},{8,10},{10,8},{12,14},{14,12},{1,3},{3,1},... | collective-permute-start | bytes 147464 | tf_op jit(solution)/shard_map/ppermute | solution.py:493
  18.4 6.1 %project_mine.1 = (bf16[896,512]{1,0:T(8,128)(2,1)S(1)}, bf16[128,32,512]{2,1,0:T(8,128)(2,1)S(1)}, bf16[128,3072]{1,0:T(8,128)(2,1)S(1)}) custom-call(bf16[896,4096]{1,0:T(8,128)(2,1)S(1)} %get-tuple-element.42.rows_ref, bf16[896,2048]{1,0:T(8,128)(2,1)S(1)} %get-tuple-element.48.rows_rest_ref, bf16[6144,512]{1,0:T(8,128)(2,1)S(1)} %get-tuple-element.49.w_mine_ref, ...), custom_call_target="tpu_custom_call" | custom-call | tf_op jit(solution)/shard_map/project_mine/pallas_call | solution.py:566
  24.5 0.0 collective-permute-done.3.got_ref
  24.5 1.0 %prepare_arrived.1 = (bf16[16,3072]{1,0:T(8,128)(2,1)S(1)}, bf16[16,64]{1,0:T(8,128)(2,1)S(1)}, f32[16,768]{1,0:T(8,128)S(1)}) custom-call(s32[8,12]{1,0:T(8,128)} %target_ref.3, s32[8,12]{1,0:T(8,128)} %span_ref.1, bf16[4,2,3072]{2,1,0:T(2,128)(2,1)S(1)} %get-tuple-element.54.after_ref.kept_ref, bf16[4,2,3072]{2,1,0:T(2,128)(2,1)S(1)} %collective-permute-done.3.got_ref), custom_call_target="tpu_custom_call" | custom-call | tf_op jit(solution)/shard_map/prepare_arrived/pallas_call | solution.py:581
  25.6 0.0 collective-permute-done.2.other_ref
  25.6 0.9 %attend_arrived.1 = (bf16[4,2,3200]{2,1,0:T(2,128)(2,1)S(1)}, bf16[4,2,3200]{2,1,0:T(2,128)(2,1)S(1)}) custom-call(bf16[16,3072]{1,0:T(8,128)(2,1)S(1)} %get-tuple-element.59.rows_ref, bf16[16,64]{1,0:T(8,128)(2,1)S(1)} %get-tuple-element.60.slot_of_ref, f32[16,768]{1,0:T(8,128)S(1)} %get-tuple-element.61.bias_ref, ...), custom_call_target="tpu_custom_call" | custom-call | tf_op jit(solution)/shard_map/attend_arrived/pallas_call | solution.py:594
  26.5 0.9 %collective-permute-start.4 = (bf16[4,2,3200]{2,1,0:T(2,128)(2,1)S(1)}, bf16[4,2,3200]{2,1,0:T(2,128)(2,1)S(1)}, u32[]{:S(2)}, u32[]{:S(2)}) collective-permute-start(bf16[4,2,3200]{2,1,0:T(2,128)(2,1)S(1)} %get-tuple-element.66), channel_id=1, source_target_pairs={{0,8},{2,10},{4,12},{6,14},{8,0},{10,2},{12,4},{14,6},{1,9},{3,11}... | collective-permute-start | bytes 153608 | tf_op jit(solution)/shard_map/ppermute | solution.py:493
  27.4 1.4 %attend_cache.3 = (bf16[32,3072]{1,0:T(8,128)(2,1)S(1)}, f32[16,3072]{1,0:T(8,128)S(1)}, f32[16,128]{1,0:T(8,128)S(1)}) custom-call(bf16[128,3072]{1,0:T(8,128)(2,1)S(1)} %get-tuple-element.55.queries_ref, bf16[128,32,512]{2,1,0:T(8,128)(2,1)S(1)} %get-tuple-element.56.cache_ref, s32[1,128]{1,0:T(1,128)} %bitcast.4, ...), custom_call_target="tpu_custom_call" | custom-call | tf_op jit(solution)/shard_map/attend_cache/pallas_call | solution.py:607
  28.7 3.6 %collective-permute-done.4.got_ref = bf16[4,2,3200]{2,1,0:T(2,128)(2,1)S(1)} collective-permute-done((bf16[4,2,3200]{2,1,0:T(2,128)(2,1)S(1)}, bf16[4,2,3200]{2,1,0:T(2,128)(2,1)S(1)}, u32[]{:S(2)}, u32[]{:S(2)}) %collective-permute-start.4) | collective-permute-done | bytes 51232 | tf_op jit(solution)/shard_map/ppermute | solution.py:493
  32.3 0.1 collective-permute-start.5
  32.4 1.6 %attend_cache.4 = (bf16[48,3072]{1,0:T(8,128)(2,1)S(1)}, f32[16,3072]{1,0:T(8,128)S(1)}, f32[16,128]{1,0:T(8,128)S(1)}) custom-call(bf16[128,3072]{1,0:T(8,128)(2,1)S(1)} %get-tuple-element.55.queries_ref, bf16[128,32,512]{2,1,0:T(8,128)(2,1)S(1)} %get-tuple-element.56.cache_ref, s32[1,128]{1,0:T(1,128)} %bitcast.5, ...), custom_call_target="tpu_custom_call" | custom-call | tf_op jit(solution)/shard_map/attend_cache/pallas_call | solution.py:607
  34.0 2.5 %collective-permute-done.5.got_ref = bf16[4,2,3200]{2,1,0:T(2,128)(2,1)S(1)} collective-permute-done((bf16[4,2,3200]{2,1,0:T(2,128)(2,1)S(1)}, bf16[4,2,3200]{2,1,0:T(2,128)(2,1)S(1)}, u32[]{:S(2)}, u32[]{:S(2)}) %collective-permute-start.5) | collective-permute-done | bytes 51232 | tf_op jit(solution)/shard_map/ppermute | solution.py:493
  36.5 0.6 %collective-permute-start.6 = (bf16[4,2,3200]{2,1,0:T(2,128)(2,1)S(1)}, bf16[4,2,3200]{2,1,0:T(2,128)(2,1)S(1)}, u32[]{:S(2)}, u32[]{:S(2)}) collective-permute-start(bf16[4,2,3200]{2,1,0:T(2,128)(2,1)S(1)} %get-tuple-element.76), channel_id=1, source_target_pairs={{0,2},{2,0},{4,6},{6,4},{8,10},{10,8},{12,14},{14,12},{1,3},{3,1},... | collective-permute-start | bytes 153608 | tf_op jit(solution)/shard_map/ppermute | solution.py:493
  37.1 1.6 %attend_cache.5 = (bf16[48,3072]{1,0:T(8,128)(2,1)S(1)}, f32[16,3072]{1,0:T(8,128)S(1)}, f32[16,128]{1,0:T(8,128)S(1)}) custom-call(bf16[128,3072]{1,0:T(8,128)(2,1)S(1)} %get-tuple-element.55.queries_ref, bf16[128,32,512]{2,1,0:T(8,128)(2,1)S(1)} %get-tuple-element.56.cache_ref, s32[1,128]{1,0:T(1,128)} %bitcast.6, ...), custom_call_target="tpu_custom_call" | custom-call | tf_op jit(solution)/shard_map/attend_cache/pallas_call | solution.py:607
  38.7 2.0 %collective-permute-done.6.refs_10_ = bf16[4,2,3200]{2,1,0:T(2,128)(2,1)S(1)} collective-permute-done((bf16[4,2,3200]{2,1,0:T(2,128)(2,1)S(1)}, bf16[4,2,3200]{2,1,0:T(2,128)(2,1)S(1)}, u32[]{:S(2)}, u32[]{:S(2)}) %collective-permute-start.6) | collective-permute-done | bytes 51232 | tf_op jit(solution)/shard_map/ppermute | solution.py:493
  40.7 1.4 %merge.1 = bf16[128,3072]{1,0:T(8,128)(2,1)} custom-call(bf16[16,128]{1,0:T(8,128)(2,1)S(1)} %get-tuple-element.41.pick_ref, bf16[32,3072]{1,0:T(8,128)(2,1)S(1)} %get-tuple-element.63.refs_0_, f32[16,3072]{1,0:T(8,128)S(1)} %get-tuple-element.64.refs_1_, f32[16,128]{1,0:T(8,128)S(1)} %get-tuple-element.65.after_ref.refs_2_, ...), custom_call_target="tpu_custom_call" | custom-call | tf_op jit(solution)/shard_map/merge/pallas_call | solution.py:623
  (4 shorter events, 0.0 us)
Async XLA Ops:
  1.6 8.6 %collective-permute-start = (bf16[4,2,3072]{2,1,0:T(2,128)(2,1)S(1)}, bf16[4,2,3072]{2,1,0:T(2,128)(2,1)S(1)}, u32[]{:S(2)}, u32[]{:S(2)}) collective-permute-start(bf16[4,2,3072]{2,1,0:T(2,128)(2,1)S(1)} %get-tuple-element.46), channel_id=1, source_target_pairs={{0,8},{2,10},{4,12},{6,14},{8,0},{10,2},{12,4},{14,6},{1,9},{3,11}... | collective-permute-start | bytes 147464 | tf_op jit(solution)/shard_map/ppermute | solution.py:493
  10.2 6.5 %collective-permute-start.1 = (bf16[4,2,3072]{2,1,0:T(2,128)(2,1)S(1)}, bf16[4,2,3072]{2,1,0:T(2,128)(2,1)S(1)}, u32[]{:S(2)}, u32[]{:S(2)}) collective-permute-start(bf16[4,2,3072]{2,1,0:T(2,128)(2,1)S(1)} %get-tuple-element.51), channel_id=1, source_target_pairs={{0,4},{2,6},{4,0},{6,2},{8,12},{10,14},{12,8},{14,10},{1,5},{3,7},... | collective-permute-start | bytes 147464 | tf_op jit(solution)/shard_map/ppermute | solution.py:493
  16.7 8.8 %collective-permute-start.2 = (bf16[896,512]{1,0:T(8,128)(2,1)S(1)}, bf16[896,512]{1,0:T(8,128)(2,1)S(1)}, u32[]{:S(2)}, u32[]{:S(2)}) collective-permute-start(bf16[896,512]{1,0:T(8,128)(2,1)S(1)} %get-tuple-element.53.after_ref), channel_id=1, source_target_pairs={{0,1},{1,0},{2,3},{3,2},{4,5},{5,4},{6,7},{7,6},{8,9},{9,8},{10,11... | collective-permute-start | bytes 2752520 | tf_op jit(solution)/shard_map/ppermute | solution.py:554
  16.8 7.7 %collective-permute-start.3 = (bf16[4,2,3072]{2,1,0:T(2,128)(2,1)S(1)}, bf16[4,2,3072]{2,1,0:T(2,128)(2,1)S(1)}, u32[]{:S(2)}, u32[]{:S(2)}) collective-permute-start(bf16[4,2,3072]{2,1,0:T(2,128)(2,1)S(1)} %get-tuple-element.58), channel_id=1, source_target_pairs={{0,2},{2,0},{4,6},{6,4},{8,10},{10,8},{12,14},{14,12},{1,3},{3,1},... | collective-permute-start | bytes 147464 | tf_op jit(solution)/shard_map/ppermute | solution.py:493
  26.5 5.8 %collective-permute-start.4 = (bf16[4,2,3200]{2,1,0:T(2,128)(2,1)S(1)}, bf16[4,2,3200]{2,1,0:T(2,128)(2,1)S(1)}, u32[]{:S(2)}, u32[]{:S(2)}) collective-permute-start(bf16[4,2,3200]{2,1,0:T(2,128)(2,1)S(1)} %get-tuple-element.66), channel_id=1, source_target_pairs={{0,8},{2,10},{4,12},{6,14},{8,0},{10,2},{12,4},{14,6},{1,9},{3,11}... | collective-permute-start | bytes 153608 | tf_op jit(solution)/shard_map/ppermute | solution.py:493
  32.3 4.2 %collective-permute-start.5 = (bf16[4,2,3200]{2,1,0:T(2,128)(2,1)S(1)}, bf16[4,2,3200]{2,1,0:T(2,128)(2,1)S(1)}, u32[]{:S(2)}, u32[]{:S(2)}) collective-permute-start(bf16[4,2,3200]{2,1,0:T(2,128)(2,1)S(1)} %get-tuple-element.71), channel_id=1, source_target_pairs={{0,4},{2,6},{4,0},{6,2},{8,12},{10,14},{12,8},{14,10},{1,5},{3,7},... | collective-permute-start | bytes 153608 | tf_op jit(solution)/shard_map/ppermute | solution.py:493
  36.5 4.2 %collective-permute-start.6 = (bf16[4,2,3200]{2,1,0:T(2,128)(2,1)S(1)}, bf16[4,2,3200]{2,1,0:T(2,128)(2,1)S(1)}, u32[]{:S(2)}, u32[]{:S(2)}) collective-permute-start(bf16[4,2,3200]{2,1,0:T(2,128)(2,1)S(1)} %get-tuple-element.76), channel_id=1, source_target_pairs={{0,2},{2,0},{4,6},{6,4},{8,10},{10,8},{12,14},{14,12},{1,3},{3,1},... | collective-permute-start | bytes 153608 | tf_op jit(solution)/shard_map/ppermute | solution.py:493

commit v14 on v13

--- a/solution.py
+++ b/solution.py
@@ -36,7 +36,8 @@
     table = jnp.zeros(shape, jnp.int32)
     for k in range(sections):
         mine = (slot_id >= k * CAP) & (slot_id < (k + 1) * CAP)
-        table = jnp.where(mine, target_ref[pl.ds(position ^ k, 1), :], table)
+        section = position ^ distance(k, lax.axis_index("tp"), sections)
+        table = jnp.where(mine, target_ref[pl.ds(section, 1), :], table)
     local = table - position * row_count
     here = (local >= 0) & (local < row_count)
     square = (requests, requests)
@@ -58,6 +59,16 @@
         steps.append((bit, sent, [k for k in range(sections) if not k & bit]))
         bit //= 2
     return steps
+
+
+def distance(block, tp, sections):
+    turned = (block << 1) & (sections - 1) | block // (sections // 2)
+    return jnp.where(tp == 0, block, turned)
+
+
+def block_at(distances, tp, sections):
+    turned = (distances >> 1) | (distances & 1) * (sections // 2)
+    return jnp.where(tp == 0, distances, turned)
 
 
 def regroup(kept_ref, got_ref, after_ref, keep_ref, send_ref, *, steps, done):
@@ -237,7 +248,9 @@
     padded, prompt_rows = bias_ref.shape
     span_rows = prompt_rows // requests
     section_col, rank_col, span_col = request_slots(target_ref, span_ref, row_count, padded)
-    block = section_col ^ lax.axis_index("section")
+    block = block_at(
+        section_col ^ lax.axis_index("section"), lax.axis_index("tp"), sections
+    )
     slot = jnp.where(section_col >= 0, block * PITCH + rank_col, -1)
     slot_of_ref[...] = one_hot((padded, sections * PITCH), 1, slot)
     slot = jnp.where(section_col >= 0, block * CAP + rank_col, -1)
@@ -472,6 +485,7 @@
     row_count = decode_hidden.shape[0]
     prompt_rows, features = prompts.shape
     sections = lax.axis_size("section")
+    tensor_parts = lax.axis_size("tp")
     local_width = kv_cache.shape[2]
     query_width = queries.shape[1]
     slots = sections * CAP
@@ -489,8 +503,14 @@
         return [pltpu.VMEM((half, CAP, width), BF16)] * 2
 
     def swapped(blocks, done):
-        pairs = [(i, i ^ steps[done][0]) for i in range(sections)]
-        return in_vmem(lax.ppermute(blocks, "section", pairs))
+        bit = steps[done][0]
+        turned = (bit << 1) & (sections - 1) or 1
+        pairs = []
+        for section in range(sections):
+            for tp in range(tensor_parts):
+                partner = section ^ (turned if tp else bit)
+                pairs.append((section * tensor_parts + tp, partner * tensor_parts + tp))
+        return in_vmem(lax.ppermute(blocks, ("section", "tp"), pairs))
 
     pick, keep, send = pl.pallas_call(
         select_queries,

time: 42.4 us -> 42.2 us (level)
  no operation moved by 1% of the time
where the time goes in v14:
time: 42.2 us; the launch traced here: 42 us
  Pallas kernels  24.9 us (59%)
  starting transfers between devices  9.05 us (21%)
  waiting for transfers between devices  7.84 us (19%)
    ppermute x6, starting transfers between devices, swapped(): return in_vmem(lax.ppermute(blocks, ('section', 'tp'), pairs))  8.98 us
    ppermute x6, waiting for transfers between devices, swapped(): return in_vmem(lax.ppermute(blocks, ('section', 'tp'), pairs))  7.84 us
    pallas_call x1, Pallas kernels, shards(): pl.pallas_call(functools.partial(project_mine, at=at, last=last), in_spec...  6.09 us
    pallas_call x1, Pallas kernels, shards(): pl.pallas_call(project_rest, in_specs=[REMAINS] * 4 + [RESIDENT] * 3 + [R...  4.84 us
    pallas_call x3, Pallas kernels, shards(): pl.pallas_call(functools.partial(attend_cache, rows_at=at), in_specs=[RES...  4.55 us
    pallas_call x1, Pallas kernels, shards(): pl.pallas_call(functools.partial(project_first, edges=edges), in_specs=[R...  4.53 us
    pallas_call x1, Pallas kernels, shards(): pl.pallas_call(select_queries, in_specs=[RESIDENT, RESIDENT], out_specs=[...  1.56 us
    pallas_call x1, Pallas kernels, shards(): pl.pallas_call(merge, in_specs=[RESIDENT] * (3 + len(shares)), out_specs=...  1.43 us
  transfers between devices with their start and end apart: 7, of which 3 were waited for; matrix products, arithmetic and copies ran while one was open for 0% of the time, Pallas kernels for 50%

profile of v14, /device:TPU:0, one launch (start us, length us, event | category | flops | bytes accessed | tf_op | source)
XLA Modules:
  0.0 42.0 jit_solution(6627613442391156788)
XLA Ops:
  0.0 1.6 %select_queries.1 = (bf16[16,128]{1,0:T(8,128)(2,1)S(1)}, bf16[4,2,3072]{2,1,0:T(2,128)(2,1)S(1)}, bf16[4,2,3072]{2,1,0:T(2,128)(2,1)S(1)}) custom-call(s32[8,12]{1,0:T(8,128)} %target_ref.3, bf16[128,3072]{1,0:T(8,128)(2,1)} %refs_1_.1), custom_call_target="tpu_custom_call" | custom-call | tf_op jit(solution)/shard_map/select_queries/pallas_call | solution.py:515
  1.6 4.1 %collective-permute-start = (bf16[4,2,3072]{2,1,0:T(2,128)(2,1)S(1)}, bf16[4,2,3072]{2,1,0:T(2,128)(2,1)S(1)}, u32[]{:S(2)}, u32[]{:S(2)}) collective-permute-start(bf16[4,2,3072]{2,1,0:T(2,128)(2,1)S(1)} %get-tuple-element.46), channel_id=1, source_target_pairs={{0,8},{1,3},{2,10},{3,1},{4,12},{5,7},{6,14},{7,5},{8,0},{9,11},{1... | collective-permute-start | bytes 147464 | tf_op jit(solution)/shard_map/ppermute | solution.py:513
  5.7 4.5 %project_first.1 = (bf16[896,4096]{1,0:T(8,128)(2,1)S(1)}, bf16[1536,512]{1,0:T(8,128)(2,1)S(1)}, f32[896,512]{1,0:T(8,128)S(1)}) custom-call(bf16[768,6144]{1,0:T(8,128)(2,1)} %prompts_ref.3, bf16[128,6144]{1,0:T(8,128)(2,1)} %hidden_ref.3, bf16[6144,1024]{1,0:T(8,128)(2,1)} %w_ref.3), custom_call_target="tpu_custom_call" | custom-call | tf_op jit(solution)/shard_map/project_first/pallas_call | solution.py:537
  10.2 0.0 collective-permute-done.got_ref
  10.2 1.6 %collective-permute-start.1 = (bf16[4,2,3072]{2,1,0:T(2,128)(2,1)S(1)}, bf16[4,2,3072]{2,1,0:T(2,128)(2,1)S(1)}, u32[]{:S(2)}, u32[]{:S(2)}) collective-permute-start(bf16[4,2,3072]{2,1,0:T(2,128)(2,1)S(1)} %get-tuple-element.51), channel_id=1, source_target_pairs={{0,4},{1,9},{2,6},{3,11},{4,0},{5,13},{6,2},{7,15},{8,12},{9,1},{1... | collective-permute-start | bytes 147464 | tf_op jit(solution)/shard_map/ppermute | solution.py:513
  11.9 4.8 %project_rest.1 = (bf16[896,512]{1,0:T(8,128)(2,1)S(1)}, bf16[896,2048]{1,0:T(8,128)(2,1)S(1)}, bf16[6144,512]{1,0:T(8,128)(2,1)S(1)}) custom-call(bf16[768,6144]{1,0:T(8,128)(2,1)} %prompts_ref.3, bf16[128,6144]{1,0:T(8,128)(2,1)} %hidden_ref.3, bf16[6144,1024]{1,0:T(8,128)(2,1)} %w_ref.3, f32[1,1024]{1,0:T(1,128)} %bitcast.2, ...), custom_call_target="tpu_custom_call" | custom-call | tf_op jit(solution)/shard_map/project_rest/pallas_call | solution.py:555
  16.7 0.0 collective-permute-done.1.got_ref
  16.7 0.1 collective-permute-start.2
  16.8 1.6 %collective-permute-start.3 = (bf16[4,2,3072]{2,1,0:T(2,128)(2,1)S(1)}, bf16[4,2,3072]{2,1,0:T(2,128)(2,1)S(1)}, u32[]{:S(2)}, u32[]{:S(2)}) collective-permute-start(bf16[4,2,3072]{2,1,0:T(2,128)(2,1)S(1)} %get-tuple-element.58), channel_id=1, source_target_pairs={{0,2},{1,5},{2,0},{3,7},{4,6},{5,1},{6,4},{7,3},{8,10},{9,13},{10,... | collective-permute-start | bytes 147464 | tf_op jit(solution)/shard_map/ppermute | solution.py:513
  18.4 6.1 %project_mine.1 = (bf16[896,512]{1,0:T(8,128)(2,1)S(1)}, bf16[128,32,512]{2,1,0:T(8,128)(2,1)S(1)}, bf16[128,3072]{1,0:T(8,128)(2,1)S(1)}) custom-call(bf16[896,4096]{1,0:T(8,128)(2,1)S(1)} %get-tuple-element.42.rows_ref, bf16[896,2048]{1,0:T(8,128)(2,1)S(1)} %get-tuple-element.48.rows_rest_ref, bf16[6144,512]{1,0:T(8,128)(2,1)S(1)} %get-tuple-element.49.w_mine_ref, ...), custom_call_target="tpu_custom_call" | custom-call | tf_op jit(solution)/shard_map/project_mine/pallas_call | solution.py:586
  24.5 0.0 collective-permute-done.3.got_ref
  24.5 1.0 %prepare_arrived.1 = (bf16[16,3072]{1,0:T(8,128)(2,1)S(1)}, bf16[16,64]{1,0:T(8,128)(2,1)S(1)}, f32[16,768]{1,0:T(8,128)S(1)}) custom-call(s32[8,12]{1,0:T(8,128)} %target_ref.3, s32[8,12]{1,0:T(8,128)} %span_ref.1, bf16[4,2,3072]{2,1,0:T(2,128)(2,1)S(1)} %get-tuple-element.54.after_ref.kept_ref, bf16[4,2,3072]{2,1,0:T(2,128)(2,1)S(1)} %collective-permute-done.3.got_ref), custom_call_target="tpu_custom_call" | custom-call | tf_op jit(solution)/shard_map/prepare_arrived/pallas_call | solution.py:601
  25.6 0.0 collective-permute-done.2.other_ref
  25.6 0.9 %attend_arrived.1 = (bf16[4,2,3200]{2,1,0:T(2,128)(2,1)S(1)}, bf16[4,2,3200]{2,1,0:T(2,128)(2,1)S(1)}) custom-call(bf16[16,3072]{1,0:T(8,128)(2,1)S(1)} %get-tuple-element.59.rows_ref, bf16[16,64]{1,0:T(8,128)(2,1)S(1)} %get-tuple-element.60.slot_of_ref, f32[16,768]{1,0:T(8,128)S(1)} %get-tuple-element.61.bias_ref, ...), custom_call_target="tpu_custom_call" | custom-call | tf_op jit(solution)/shard_map/attend_arrived/pallas_call | solution.py:614
  26.5 0.9 %collective-permute-start.4 = (bf16[4,2,3200]{2,1,0:T(2,128)(2,1)S(1)}, bf16[4,2,3200]{2,1,0:T(2,128)(2,1)S(1)}, u32[]{:S(2)}, u32[]{:S(2)}) collective-permute-start(bf16[4,2,3200]{2,1,0:T(2,128)(2,1)S(1)} %get-tuple-element.66), channel_id=1, source_target_pairs={{0,8},{1,3},{2,10},{3,1},{4,12},{5,7},{6,14},{7,5},{8,0},{9,11},{1... | collective-permute-start | bytes 153608 | tf_op jit(solution)/shard_map/ppermute | solution.py:513
  27.4 1.4 %attend_cache.3 = (bf16[32,3072]{1,0:T(8,128)(2,1)S(1)}, f32[16,3072]{1,0:T(8,128)S(1)}, f32[16,128]{1,0:T(8,128)S(1)}) custom-call(bf16[128,3072]{1,0:T(8,128)(2,1)S(1)} %get-tuple-element.55.queries_ref, bf16[128,32,512]{2,1,0:T(8,128)(2,1)S(1)} %get-tuple-element.56.cache_ref, s32[1,128]{1,0:T(1,128)} %bitcast.4, ...), custom_call_target="tpu_custom_call" | custom-call | tf_op jit(solution)/shard_map/attend_cache/pallas_call | solution.py:627
  28.7 3.2 %collective-permute-done.4.got_ref = bf16[4,2,3200]{2,1,0:T(2,128)(2,1)S(1)} collective-permute-done((bf16[4,2,3200]{2,1,0:T(2,128)(2,1)S(1)}, bf16[4,2,3200]{2,1,0:T(2,128)(2,1)S(1)}, u32[]{:S(2)}, u32[]{:S(2)}) %collective-permute-start.4) | collective-permute-done | bytes 51232 | tf_op jit(solution)/shard_map/ppermute | solution.py:513
  32.0 0.1 collective-permute-start.5
  32.1 1.6 %attend_cache.4 = (bf16[48,3072]{1,0:T(8,128)(2,1)S(1)}, f32[16,3072]{1,0:T(8,128)S(1)}, f32[16,128]{1,0:T(8,128)S(1)}) custom-call(bf16[128,3072]{1,0:T(8,128)(2,1)S(1)} %get-tuple-element.55.queries_ref, bf16[128,32,512]{2,1,0:T(8,128)(2,1)S(1)} %get-tuple-element.56.cache_ref, s32[1,128]{1,0:T(1,128)} %bitcast.5, ...), custom_call_target="tpu_custom_call" | custom-call | tf_op jit(solution)/shard_map/attend_cache/pallas_call | solution.py:627
  33.7 2.6 %collective-permute-done.5.got_ref = bf16[4,2,3200]{2,1,0:T(2,128)(2,1)S(1)} collective-permute-done((bf16[4,2,3200]{2,1,0:T(2,128)(2,1)S(1)}, bf16[4,2,3200]{2,1,0:T(2,128)(2,1)S(1)}, u32[]{:S(2)}, u32[]{:S(2)}) %collective-permute-start.5) | collective-permute-done | bytes 51232 | tf_op jit(solution)/shard_map/ppermute | solution.py:513
  36.3 0.6 %collective-permute-start.6 = (bf16[4,2,3200]{2,1,0:T(2,128)(2,1)S(1)}, bf16[4,2,3200]{2,1,0:T(2,128)(2,1)S(1)}, u32[]{:S(2)}, u32[]{:S(2)}) collective-permute-start(bf16[4,2,3200]{2,1,0:T(2,128)(2,1)S(1)} %get-tuple-element.76), channel_id=1, source_target_pairs={{0,2},{1,5},{2,0},{3,7},{4,6},{5,1},{6,4},{7,3},{8,10},{9,13},{10,... | collective-permute-start | bytes 153608 | tf_op jit(solution)/shard_map/ppermute | solution.py:513
  37.0 1.6 %attend_cache.5 = (bf16[48,3072]{1,0:T(8,128)(2,1)S(1)}, f32[16,3072]{1,0:T(8,128)S(1)}, f32[16,128]{1,0:T(8,128)S(1)}) custom-call(bf16[128,3072]{1,0:T(8,128)(2,1)S(1)} %get-tuple-element.55.queries_ref, bf16[128,32,512]{2,1,0:T(8,128)(2,1)S(1)} %get-tuple-element.56.cache_ref, s32[1,128]{1,0:T(1,128)} %bitcast.6, ...), custom_call_target="tpu_custom_call" | custom-call | tf_op jit(solution)/shard_map/attend_cache/pallas_call | solution.py:627
  38.5 2.0 %collective-permute-done.6.refs_10_ = bf16[4,2,3200]{2,1,0:T(2,128)(2,1)S(1)} collective-permute-done((bf16[4,2,3200]{2,1,0:T(2,128)(2,1)S(1)}, bf16[4,2,3200]{2,1,0:T(2,128)(2,1)S(1)}, u32[]{:S(2)}, u32[]{:S(2)}) %collective-permute-start.6) | collective-permute-done | bytes 51232 | tf_op jit(solution)/shard_map/ppermute | solution.py:513
  40.5 1.4 %merge.1 = bf16[128,3072]{1,0:T(8,128)(2,1)} custom-call(bf16[16,128]{1,0:T(8,128)(2,1)S(1)} %get-tuple-element.41.pick_ref, bf16[32,3072]{1,0:T(8,128)(2,1)S(1)} %get-tuple-element.63.refs_0_, f32[16,3072]{1,0:T(8,128)S(1)} %get-tuple-element.64.refs_1_, f32[16,128]{1,0:T(8,128)S(1)} %get-tuple-element.65.after_ref.refs_2_, ...), custom_call_target="tpu_custom_call" | custom-call | tf_op jit(solution)/shard_map/merge/pallas_call | solution.py:643
  (4 shorter events, 0.0 us)
Async XLA Ops:
  1.6 8.6 %collective-permute-start = (bf16[4,2,3072]{2,1,0:T(2,128)(2,1)S(1)}, bf16[4,2,3072]{2,1,0:T(2,128)(2,1)S(1)}, u32[]{:S(2)}, u32[]{:S(2)}) collective-permute-start(bf16[4,2,3072]{2,1,0:T(2,128)(2,1)S(1)} %get-tuple-element.46), channel_id=1, source_target_pairs={{0,8},{1,3},{2,10},{3,1},{4,12},{5,7},{6,14},{7,5},{8,0},{9,11},{1... | collective-permute-start | bytes 147464 | tf_op jit(solution)/shard_map/ppermute | solution.py:513
  10.2 6.5 %collective-permute-start.1 = (bf16[4,2,3072]{2,1,0:T(2,128)(2,1)S(1)}, bf16[4,2,3072]{2,1,0:T(2,128)(2,1)S(1)}, u32[]{:S(2)}, u32[]{:S(2)}) collective-permute-start(bf16[4,2,3072]{2,1,0:T(2,128)(2,1)S(1)} %get-tuple-element.51), channel_id=1, source_target_pairs={{0,4},{1,9},{2,6},{3,11},{4,0},{5,13},{6,2},{7,15},{8,12},{9,1},{1... | collective-permute-start | bytes 147464 | tf_op jit(solution)/shard_map/ppermute | solution.py:513
  16.7 8.8 %collective-permute-start.2 = (bf16[896,512]{1,0:T(8,128)(2,1)S(1)}, bf16[896,512]{1,0:T(8,128)(2,1)S(1)}, u32[]{:S(2)}, u32[]{:S(2)}) collective-permute-start(bf16[896,512]{1,0:T(8,128)(2,1)S(1)} %get-tuple-element.53.after_ref), channel_id=1, source_target_pairs={{0,1},{1,0},{2,3},{3,2},{4,5},{5,4},{6,7},{7,6},{8,9},{9,8},{10,11... | collective-permute-start | bytes 2752520 | tf_op jit(solution)/shard_map/ppermute | solution.py:574
  16.8 7.7 %collective-permute-start.3 = (bf16[4,2,3072]{2,1,0:T(2,128)(2,1)S(1)}, bf16[4,2,3072]{2,1,0:T(2,128)(2,1)S(1)}, u32[]{:S(2)}, u32[]{:S(2)}) collective-permute-start(bf16[4,2,3072]{2,1,0:T(2,128)(2,1)S(1)} %get-tuple-element.58), channel_id=1, source_target_pairs={{0,2},{1,5},{2,0},{3,7},{4,6},{5,1},{6,4},{7,3},{8,10},{9,13},{10,... | collective-permute-start | bytes 147464 | tf_op jit(solution)/shard_map/ppermute | solution.py:513
  26.5 5.5 %collective-permute-start.4 = (bf16[4,2,3200]{2,1,0:T(2,128)(2,1)S(1)}, bf16[4,2,3200]{2,1,0:T(2,128)(2,1)S(1)}, u32[]{:S(2)}, u32[]{:S(2)}) collective-permute-start(bf16[4,2,3200]{2,1,0:T(2,128)(2,1)S(1)} %get-tuple-element.66), channel_id=1, source_target_pairs={{0,8},{1,3},{2,10},{3,1},{4,12},{5,7},{6,14},{7,5},{8,0},{9,11},{1... | collective-permute-start | bytes 153608 | tf_op jit(solution)/shard_map/ppermute | solution.py:513
  32.0 4.3 %collective-permute-start.5 = (bf16[4,2,3200]{2,1,0:T(2,128)(2,1)S(1)}, bf16[4,2,3200]{2,1,0:T(2,128)(2,1)S(1)}, u32[]{:S(2)}, u32[]{:S(2)}) collective-permute-start(bf16[4,2,3200]{2,1,0:T(2,128)(2,1)S(1)} %get-tuple-element.71), channel_id=1, source_target_pairs={{0,4},{1,9},{2,6},{3,11},{4,0},{5,13},{6,2},{7,15},{8,12},{9,1},{1... | collective-permute-start | bytes 153608 | tf_op jit(solution)/shard_map/ppermute | solution.py:513
  36.3 4.2 %collective-permute-start.6 = (bf16[4,2,3200]{2,1,0:T(2,128)(2,1)S(1)}, bf16[4,2,3200]{2,1,0:T(2,128)(2,1)S(1)}, u32[]{:S(2)}, u32[]{:S(2)}) collective-permute-start(bf16[4,2,3200]{2,1,0:T(2,128)(2,1)S(1)} %get-tuple-element.76), channel_id=1, source_target_pairs={{0,2},{1,5},{2,0},{3,7},{4,6},{5,1},{6,4},{7,3},{8,10},{9,13},{10,... | collective-permute-start | bytes 153608 | tf_op jit(solution)/shard_map/ppermute | solution.py:513

commit v15 on v13

--- a/solution.py
+++ b/solution.py
@@ -60,13 +60,34 @@
     return steps
 
 
-def regroup(kept_ref, got_ref, after_ref, keep_ref, send_ref, *, steps, done):
-    where = {k: (got_ref, i) for i, k in enumerate(steps[done - 1][1])}
-    where |= {k: (kept_ref, i) for i, k in enumerate(steps[done - 1][2])}
-    for out_ref, blocks in ((send_ref, steps[done][1]), (keep_ref, steps[done][2])):
+def answer_steps_of(sections):
+    steps = []
+    bit = 1
+    while 4 * bit < sections:
+        sent = [k for k in range(sections) if k & bit]
+        steps.append((bit, sent, [k for k in range(sections) if not k & bit]))
+        bit *= 2
+    return steps
+
+
+def rearrange(step, kept_ref, got_ref, *out):
+    where = {k: (got_ref, i) for i, k in enumerate(step[1])}
+    where |= {k: (kept_ref, i) for i, k in enumerate(step[2])}
+    for out_ref, blocks in out:
         for i, k in enumerate(blocks):
             ref, at = where[k]
             out_ref[i] = ref[at]
+
+
+def regroup(kept_ref, got_ref, after_ref, keep_ref, send_ref, *, steps, done):
+    _, sent, kept = steps[done]
+    rearrange(steps[done - 1], kept_ref, got_ref, (send_ref, sent), (keep_ref, kept))
+
+
+def fan_out(kept_ref, got_ref, after_ref, *out_refs, step):
+    size = out_refs[0].shape[0]
+    groups = [range(m * size, (m + 1) * size) for m in range(len(out_refs))]
+    rearrange(step, kept_ref, got_ref, *zip(out_refs, groups))
 
 
 def all_blocks(steps, kept_ref, got_ref):
@@ -296,7 +317,7 @@
     stats = high + pltpu.roll(middle, LSE_PITCH, 1) + pltpu.roll(low, 2 * LSE_PITCH, 1)
     result = jnp.concatenate(pieces + [stats], axis=1).astype(BF16)
     answers = lax.dot_general(slot_of, result, TRANSPOSED, preferred_element_type=F32)
-    _, sent, kept = steps_of(2 * keep_ref.shape[0])[0]
+    _, sent, kept = answer_steps_of(2 * keep_ref.shape[0])[0]
     for ref, blocks in ((send_ref, sent), (keep_ref, kept)):
         for i, k in enumerate(blocks):
             ref[i] = answers[k * PITCH : k * PITCH + CAP].astype(BF16)
@@ -412,11 +433,13 @@
 
 
 def merge(pick_ref, *refs):
-    parts, (kept_ref, got_ref, out_ref) = refs[:-3], refs[-3:]
+    parts, group_refs, out_ref = refs[:-5], refs[-5:-1], refs[-1]
     cached_refs, slot_out_refs, slot_lse_refs = parts[0::3], parts[1::3], parts[2::3]
     width = out_ref.shape[1]
     pick = pick_ref[...]
-    arrived = all_blocks(steps_of(2 * kept_ref.shape[0]), kept_ref, got_ref)
+    arrived = jnp.concatenate(
+        [ref[i].astype(F32) for ref in group_refs for i in range(ref.shape[0])], axis=0
+    )
     stats = arrived[:, width:]
     arrived_lse = (
         stats
@@ -488,8 +511,8 @@
     def block_pair(width):
         return [pltpu.VMEM((half, CAP, width), BF16)] * 2
 
-    def swapped(blocks, done):
-        pairs = [(i, i ^ steps[done][0]) for i in range(sections)]
+    def swapped(blocks, distance):
+        pairs = [(i, i ^ distance) for i in range(sections)]
         return in_vmem(lax.ppermute(blocks, "section", pairs))
 
     pick, keep, send = pl.pallas_call(
@@ -500,9 +523,9 @@
         compiler_params=compiler_params(16),
         name="select_queries",
     )(target_row, queries)
-    got = swapped(send, 0)
-
-    def regrouped(blocks, got, done, after):
+    got = swapped(send, steps[0][0])
+
+    def regrouped(blocks, got, steps, done, after):
         return pl.pallas_call(
             functools.partial(regroup, steps=steps, done=done),
             in_specs=[RESIDENT] * 2 + [REMAINS],
@@ -530,8 +553,8 @@
         compiler_params=compiler_params(12),
         name="project_first",
     )(prompts, decode_hidden, w_kv)
-    keep, send = regrouped(keep, got, 1, total)
-    got = swapped(send, 1)
+    keep, send = regrouped(keep, got, steps, 1, total)
+    got = swapped(send, steps[1][0])
     theirs, rows_rest, w_mine = pl.pallas_call(
         project_rest,
         in_specs=[REMAINS] * 4 + [RESIDENT] * 3 + [REMAINS],
@@ -559,8 +582,8 @@
     after = theirs
     for piece, at in enumerate(spans(bounds)):
         if piece + 2 < len(steps):
-            keep, send = regrouped(keep, got, piece + 2, after)
-            got = swapped(send, piece + 2)
+            keep, send = regrouped(keep, got, steps, piece + 2, after)
+            got = swapped(send, steps[piece + 2][0])
         last = piece == pieces - 1
         extra = [kv_cache, queries] if last else []
         part, *here = pl.pallas_call(
@@ -600,10 +623,14 @@
         name="attend_arrived",
     )(*map(in_vmem, prepared), other, *mine)
 
+    steps = answer_steps_of(sections)
     shares = []
-    bounds = [row_count * i // (16 * len(steps)) * 16 for i in range(len(steps))] + [row_count]
+    calls = len(steps) + 1
+    bounds = [row_count * i // (16 * calls) * 16 for i in range(calls)] + [row_count]
     for done, at in enumerate(spans(bounds)):
-        got = swapped(send, done)
+        last = done == len(steps)
+        if not last:
+            got = swapped(send, steps[done][0])
         share = pl.pallas_call(
             functools.partial(attend_cache, rows_at=at),
             in_specs=[RESIDENT] * 6 + [REMAINS],
@@ -618,16 +645,28 @@
         )(queries_here, kv_here, lengths, mine[-1], other, in_vmem(pick), in_vmem(keep))
         shares += share
         if done + 1 < len(steps):
-            keep, send = regrouped(keep, got, done + 1, share[2])
+            keep, send = regrouped(keep, got, steps, done + 1, share[2])
+        elif not last:
+            size = sections // 4
+            keep, *sent = pl.pallas_call(
+                functools.partial(fan_out, step=steps[-1]),
+                in_specs=[RESIDENT] * 2 + [REMAINS],
+                out_specs=[RESIDENT] * 4,
+                out_shape=[pltpu.VMEM((size, CAP, answer_width), BF16)] * 4,
+                compiler_params=compiler_params(16),
+                name="fan_out",
+            )(in_vmem(keep), got, in_vmem(share[2]))
+            groups = [in_vmem(keep)]
+            groups += [swapped(blocks, (i + 1) * size) for i, blocks in enumerate(sent)]
 
     return pl.pallas_call(
         merge,
-        in_specs=[RESIDENT] * (3 + len(shares)),
+        in_specs=[RESIDENT] * (5 + len(shares)),
         out_specs=RESIDENT,
         out_shape=jax.ShapeDtypeStruct((row_count, query_width), BF16),
         compiler_params=compiler_params(24),
         name="merge",
-    )(*map(in_vmem, (pick, *shares, keep)), got)
+    )(*map(in_vmem, (pick, *shares)), *groups)
 
 
 def solution(mesh):

time: 42.4 us -> 39 us (0.920)
  waiting for transfers between devices: 8.09 us -> 2.03 us
  starting transfers between devices: 8.95 us -> 12.4 us
  Pallas kernels: 24.9 us -> 24.2 us
    ppermute x6 -> x7, waiting for transfers between devices: 8.09 us -> 2.03 us  [swapped(): return in_vmem(lax.ppermute(blocks, 'section', pairs))]
    ppermute x6 -> x7, starting transfers between devices: 8.88 us -> 12.3 us  [swapped(): return in_vmem(lax.ppermute(blocks, 'section', pairs))]
    pallas_call x3 -> x2, Pallas kernels: 4.56 us -> 3.8 us  [shards(): pl.pallas_call(functools.partial(attend_cache, rows_at=at), in_specs=[RES...]
    pallas_call x1 -> x2, Pallas kernels: 1.43 us -> 1.44 us  [the longest x1 1.43 us: shards(): pl.pallas_call(merge, in_specs=[RESIDENT] * (5 + len(shares)), out_specs=...]
  transfers between devices with their start and end apart: 7 -> 8, of which waited for: 3 -> 2; matrix products, arithmetic and copies ran while one was open for 0% -> 0% of each run, Pallas kernels for 50% -> 52%
where the time goes in v15:
time: 39 us; the launch traced here: 38.8 us
  Pallas kernels  24.2 us (62%)
  starting transfers between devices  12.4 us (32%)
  waiting for transfers between devices  2.03 us (5%)
    ppermute x7, starting transfers between devices, swapped(): return in_vmem(lax.ppermute(blocks, 'section', pairs))  12.3 us
    pallas_call x1, Pallas kernels, shards(): pl.pallas_call(functools.partial(project_mine, at=at, last=last), in_spec...  6.09 us
    pallas_call x1, Pallas kernels, shards(): pl.pallas_call(project_rest, in_specs=[REMAINS] * 4 + [RESIDENT] * 3 + [R...  4.84 us
    pallas_call x1, Pallas kernels, shards(): pl.pallas_call(functools.partial(project_first, edges=edges), in_specs=[R...  4.53 us
    pallas_call x2, Pallas kernels, shards(): pl.pallas_call(functools.partial(attend_cache, rows_at=at), in_specs=[RES...  3.8 us
    ppermute x7, waiting for transfers between devices, swapped(): return in_vmem(lax.ppermute(blocks, 'section', pairs))  2.03 us
    pallas_call x1, Pallas kernels, shards(): pl.pallas_call(select_queries, in_specs=[RESIDENT, RESIDENT], out_specs=[...  1.55 us
    pallas_call x1, Pallas kernels, shards(): pl.pallas_call(merge, in_specs=[RESIDENT] * (5 + len(shares)), out_specs=...  1.43 us
  transfers between devices with their start and end apart: 8, of which 2 were waited for; matrix products, arithmetic and copies ran while one was open for 0% of the time, Pallas kernels for 52%

profile of v15, /device:TPU:0, one launch (start us, length us, event | category | flops | bytes accessed | tf_op | source)
XLA Modules:
  0.0 38.8 jit_solution(9128912490431000168)
XLA Ops:
  0.0 1.6 %select_queries.1 = (bf16[16,128]{1,0:T(8,128)(2,1)S(1)}, bf16[4,2,3072]{2,1,0:T(2,128)(2,1)S(1)}, bf16[4,2,3072]{2,1,0:T(2,128)(2,1)S(1)}) custom-call(s32[8,12]{1,0:T(8,128)} %target_ref.3, bf16[128,3072]{1,0:T(8,128)(2,1)} %refs_1_.1), custom_call_target="tpu_custom_call" | custom-call | tf_op jit(solution)/shard_map/select_queries/pallas_call | solution.py:518
  1.6 4.1 %collective-permute-start = (bf16[4,2,3072]{2,1,0:T(2,128)(2,1)S(1)}, bf16[4,2,3072]{2,1,0:T(2,128)(2,1)S(1)}, u32[]{:S(2)}, u32[]{:S(2)}) collective-permute-start(bf16[4,2,3072]{2,1,0:T(2,128)(2,1)S(1)} %get-tuple-element.43), channel_id=1, source_target_pairs={{0,8},{2,10},{4,12},{6,14},{8,0},{10,2},{12,4},{14,6},{1,9},{3,11}... | collective-permute-start | bytes 147464 | tf_op jit(solution)/shard_map/ppermute | solution.py:516
  5.7 4.5 %project_first.1 = (bf16[896,4096]{1,0:T(8,128)(2,1)S(1)}, bf16[1536,512]{1,0:T(8,128)(2,1)S(1)}, f32[896,512]{1,0:T(8,128)S(1)}) custom-call(bf16[768,6144]{1,0:T(8,128)(2,1)} %prompts_ref.3, bf16[128,6144]{1,0:T(8,128)(2,1)} %hidden_ref.3, bf16[6144,1024]{1,0:T(8,128)(2,1)} %w_ref.3), custom_call_target="tpu_custom_call" | custom-call | tf_op jit(solution)/shard_map/project_first/pallas_call | solution.py:540
  10.2 0.0 collective-permute-done.got_ref
  10.2 1.6 %collective-permute-start.1 = (bf16[4,2,3072]{2,1,0:T(2,128)(2,1)S(1)}, bf16[4,2,3072]{2,1,0:T(2,128)(2,1)S(1)}, u32[]{:S(2)}, u32[]{:S(2)}) collective-permute-start(bf16[4,2,3072]{2,1,0:T(2,128)(2,1)S(1)} %get-tuple-element.48), channel_id=1, source_target_pairs={{0,4},{2,6},{4,0},{6,2},{8,12},{10,14},{12,8},{14,10},{1,5},{3,7},... | collective-permute-start | bytes 147464 | tf_op jit(solution)/shard_map/ppermute | solution.py:516
  11.9 4.8 %project_rest.1 = (bf16[896,512]{1,0:T(8,128)(2,1)S(1)}, bf16[896,2048]{1,0:T(8,128)(2,1)S(1)}, bf16[6144,512]{1,0:T(8,128)(2,1)S(1)}) custom-call(bf16[768,6144]{1,0:T(8,128)(2,1)} %prompts_ref.3, bf16[128,6144]{1,0:T(8,128)(2,1)} %hidden_ref.3, bf16[6144,1024]{1,0:T(8,128)(2,1)} %w_ref.3, f32[1,1024]{1,0:T(1,128)} %bitcast.2, ...), custom_call_target="tpu_custom_call" | custom-call | tf_op jit(solution)/shard_map/project_rest/pallas_call | solution.py:558
  16.7 0.0 collective-permute-done.1.got_ref
  16.7 0.1 collective-permute-start.2
  16.8 1.6 %collective-permute-start.3 = (bf16[4,2,3072]{2,1,0:T(2,128)(2,1)S(1)}, bf16[4,2,3072]{2,1,0:T(2,128)(2,1)S(1)}, u32[]{:S(2)}, u32[]{:S(2)}) collective-permute-start(bf16[4,2,3072]{2,1,0:T(2,128)(2,1)S(1)} %get-tuple-element.55), channel_id=1, source_target_pairs={{0,2},{2,0},{4,6},{6,4},{8,10},{10,8},{12,14},{14,12},{1,3},{3,1},... | collective-permute-start | bytes 147464 | tf_op jit(solution)/shard_map/ppermute | solution.py:516
  18.4 6.1 %project_mine.1 = (bf16[896,512]{1,0:T(8,128)(2,1)S(1)}, bf16[128,32,512]{2,1,0:T(8,128)(2,1)S(1)}, bf16[128,3072]{1,0:T(8,128)(2,1)S(1)}) custom-call(bf16[896,4096]{1,0:T(8,128)(2,1)S(1)} %get-tuple-element.39.rows_ref, bf16[896,2048]{1,0:T(8,128)(2,1)S(1)} %get-tuple-element.45.rows_rest_ref, bf16[6144,512]{1,0:T(8,128)(2,1)S(1)} %get-tuple-element.46.w_mine_ref, ...), custom_call_target="tpu_custom_call" | custom-call | tf_op jit(solution)/shard_map/project_mine/pallas_call | solution.py:589
  24.5 0.0 collective-permute-done.3.got_ref
  24.5 1.0 %prepare_arrived.1 = (bf16[16,3072]{1,0:T(8,128)(2,1)S(1)}, bf16[16,64]{1,0:T(8,128)(2,1)S(1)}, f32[16,768]{1,0:T(8,128)S(1)}) custom-call(s32[8,12]{1,0:T(8,128)} %target_ref.3, s32[8,12]{1,0:T(8,128)} %span_ref.1, bf16[4,2,3072]{2,1,0:T(2,128)(2,1)S(1)} %get-tuple-element.51.after_ref.kept_ref, bf16[4,2,3072]{2,1,0:T(2,128)(2,1)S(1)} %collective-permute-done.3.got_ref), custom_call_target="tpu_custom_call" | custom-call | tf_op jit(solution)/shard_map/prepare_arrived/pallas_call | solution.py:604
  25.6 0.0 collective-permute-done.2.other_ref
  25.6 0.9 %attend_arrived.1 = (bf16[4,2,3200]{2,1,0:T(2,128)(2,1)S(1)}, bf16[4,2,3200]{2,1,0:T(2,128)(2,1)S(1)}) custom-call(bf16[16,3072]{1,0:T(8,128)(2,1)S(1)} %get-tuple-element.56.rows_ref, bf16[16,64]{1,0:T(8,128)(2,1)S(1)} %get-tuple-element.57.slot_of_ref, f32[16,768]{1,0:T(8,128)S(1)} %get-tuple-element.58.bias_ref, ...), custom_call_target="tpu_custom_call" | custom-call | tf_op jit(solution)/shard_map/attend_arrived/pallas_call | solution.py:617
  26.5 0.6 %collective-permute-start.4 = (bf16[4,2,3200]{2,1,0:T(2,128)(2,1)S(1)}, bf16[4,2,3200]{2,1,0:T(2,128)(2,1)S(1)}, u32[]{:S(2)}, u32[]{:S(2)}) collective-permute-start(bf16[4,2,3200]{2,1,0:T(2,128)(2,1)S(1)} %get-tuple-element.63), channel_id=1, source_target_pairs={{0,2},{2,0},{4,6},{6,4},{8,10},{10,8},{12,14},{14,12},{1,3},{3,1},... | collective-permute-start | bytes 153608 | tf_op jit(solution)/shard_map/ppermute | solution.py:516
  27.0 1.9 %attend_cache.2 = (bf16[64,3072]{1,0:T(8,128)(2,1)S(1)}, f32[16,3072]{1,0:T(8,128)S(1)}, f32[16,128]{1,0:T(8,128)S(1)}) custom-call(bf16[128,3072]{1,0:T(8,128)(2,1)S(1)} %get-tuple-element.52.queries_ref, bf16[128,32,512]{2,1,0:T(8,128)(2,1)S(1)} %get-tuple-element.53.cache_ref, s32[1,128]{1,0:T(1,128)} %bitcast.4, ...), custom_call_target="tpu_custom_call" | custom-call | tf_op jit(solution)/shard_map/attend_cache/pallas_call | solution.py:634
  28.9 1.7 %collective-permute-done.4.got_ref = bf16[4,2,3200]{2,1,0:T(2,128)(2,1)S(1)} collective-permute-done((bf16[4,2,3200]{2,1,0:T(2,128)(2,1)S(1)}, bf16[4,2,3200]{2,1,0:T(2,128)(2,1)S(1)}, u32[]{:S(2)}, u32[]{:S(2)}) %collective-permute-start.4) | collective-permute-done | bytes 51232 | tf_op jit(solution)/shard_map/ppermute | solution.py:516
  30.7 0.5 %collective-permute-start.5 = (bf16[2,2,3200]{2,1,0:T(2,128)(2,1)S(1)}, bf16[2,2,3200]{2,1,0:T(2,128)(2,1)S(1)}, u32[]{:S(2)}, u32[]{:S(2)}) collective-permute-start(bf16[2,2,3200]{2,1,0:T(2,128)(2,1)S(1)} %get-tuple-element.68), channel_id=1, source_target_pairs={{0,4},{2,6},{4,0},{6,2},{8,12},{10,14},{12,8},{14,10},{1,5},{3,7},... | collective-permute-start | bytes 76808 | tf_op jit(solution)/shard_map/ppermute | solution.py:516
  31.2 0.5 %collective-permute-start.6 = (bf16[2,2,3200]{2,1,0:T(2,128)(2,1)S(1)}, bf16[2,2,3200]{2,1,0:T(2,128)(2,1)S(1)}, u32[]{:S(2)}, u32[]{:S(2)}) collective-permute-start(bf16[2,2,3200]{2,1,0:T(2,128)(2,1)S(1)} %get-tuple-element.69), channel_id=1, source_target_pairs={{0,8},{2,10},{4,12},{6,14},{8,0},{10,2},{12,4},{14,6},{1,9},{3,11}... | collective-permute-start | bytes 76808 | tf_op jit(solution)/shard_map/ppermute | solution.py:516
  31.6 3.5 %collective-permute-start.7 = (bf16[2,2,3200]{2,1,0:T(2,128)(2,1)S(1)}, bf16[2,2,3200]{2,1,0:T(2,128)(2,1)S(1)}, u32[]{:S(2)}, u32[]{:S(2)}) collective-permute-start(bf16[2,2,3200]{2,1,0:T(2,128)(2,1)S(1)} %get-tuple-element.70), channel_id=1, source_target_pairs={{0,12},{2,14},{4,8},{6,10},{8,4},{10,6},{12,0},{14,2},{1,13},{3,15... | collective-permute-start | bytes 76808 | tf_op jit(solution)/shard_map/ppermute | solution.py:516
  35.1 1.9 %attend_cache.3 = (bf16[64,3072]{1,0:T(8,128)(2,1)S(1)}, f32[16,3072]{1,0:T(8,128)S(1)}, f32[16,128]{1,0:T(8,128)S(1)}) custom-call(bf16[128,3072]{1,0:T(8,128)(2,1)S(1)} %get-tuple-element.52.queries_ref, bf16[128,32,512]{2,1,0:T(8,128)(2,1)S(1)} %get-tuple-element.53.cache_ref, s32[1,128]{1,0:T(1,128)} %bitcast.5, ...), custom_call_target="tpu_custom_call" | custom-call | tf_op jit(solution)/shard_map/attend_cache/pallas_call | solution.py:634
  37.0 0.0 collective-permute-done.5.refs_7_
  37.0 0.3 collective-permute-done.7.refs_9_
  37.3 1.4 %merge.1 = bf16[128,3072]{1,0:T(8,128)(2,1)} custom-call(bf16[16,128]{1,0:T(8,128)(2,1)S(1)} %get-tuple-element.38.pick_ref, bf16[64,3072]{1,0:T(8,128)(2,1)S(1)} %get-tuple-element.60.refs_0_, f32[16,3072]{1,0:T(8,128)S(1)} %get-tuple-element.61.refs_1_, f32[16,128]{1,0:T(8,128)S(1)} %get-tuple-element.62.after_ref.refs_2_, ...), custom_call_target="tpu_custom_call" | custom-call | tf_op jit(solution)/shard_map/merge/pallas_call | solution.py:662
  (4 shorter events, 0.0 us)
Async XLA Ops:
  1.6 8.6 %collective-permute-start = (bf16[4,2,3072]{2,1,0:T(2,128)(2,1)S(1)}, bf16[4,2,3072]{2,1,0:T(2,128)(2,1)S(1)}, u32[]{:S(2)}, u32[]{:S(2)}) collective-permute-start(bf16[4,2,3072]{2,1,0:T(2,128)(2,1)S(1)} %get-tuple-element.43), channel_id=1, source_target_pairs={{0,8},{2,10},{4,12},{6,14},{8,0},{10,2},{12,4},{14,6},{1,9},{3,11}... | collective-permute-start | bytes 147464 | tf_op jit(solution)/shard_map/ppermute | solution.py:516
  10.2 6.5 %collective-permute-start.1 = (bf16[4,2,3072]{2,1,0:T(2,128)(2,1)S(1)}, bf16[4,2,3072]{2,1,0:T(2,128)(2,1)S(1)}, u32[]{:S(2)}, u32[]{:S(2)}) collective-permute-start(bf16[4,2,3072]{2,1,0:T(2,128)(2,1)S(1)} %get-tuple-element.48), channel_id=1, source_target_pairs={{0,4},{2,6},{4,0},{6,2},{8,12},{10,14},{12,8},{14,10},{1,5},{3,7},... | collective-permute-start | bytes 147464 | tf_op jit(solution)/shard_map/ppermute | solution.py:516
  16.7 8.8 %collective-permute-start.2 = (bf16[896,512]{1,0:T(8,128)(2,1)S(1)}, bf16[896,512]{1,0:T(8,128)(2,1)S(1)}, u32[]{:S(2)}, u32[]{:S(2)}) collective-permute-start(bf16[896,512]{1,0:T(8,128)(2,1)S(1)} %get-tuple-element.50.after_ref), channel_id=1, source_target_pairs={{0,1},{1,0},{2,3},{3,2},{4,5},{5,4},{6,7},{7,6},{8,9},{9,8},{10,11... | collective-permute-start | bytes 2752520 | tf_op jit(solution)/shard_map/ppermute | solution.py:577
  16.8 7.7 %collective-permute-start.3 = (bf16[4,2,3072]{2,1,0:T(2,128)(2,1)S(1)}, bf16[4,2,3072]{2,1,0:T(2,128)(2,1)S(1)}, u32[]{:S(2)}, u32[]{:S(2)}) collective-permute-start(bf16[4,2,3072]{2,1,0:T(2,128)(2,1)S(1)} %get-tuple-element.55), channel_id=1, source_target_pairs={{0,2},{2,0},{4,6},{6,4},{8,10},{10,8},{12,14},{14,12},{1,3},{3,1},... | collective-permute-start | bytes 147464 | tf_op jit(solution)/shard_map/ppermute | solution.py:516
  26.5 4.2 %collective-permute-start.4 = (bf16[4,2,3200]{2,1,0:T(2,128)(2,1)S(1)}, bf16[4,2,3200]{2,1,0:T(2,128)(2,1)S(1)}, u32[]{:S(2)}, u32[]{:S(2)}) collective-permute-start(bf16[4,2,3200]{2,1,0:T(2,128)(2,1)S(1)} %get-tuple-element.63), channel_id=1, source_target_pairs={{0,2},{2,0},{4,6},{6,4},{8,10},{10,8},{12,14},{14,12},{1,3},{3,1},... | collective-permute-start | bytes 153608 | tf_op jit(solution)/shard_map/ppermute | solution.py:516
  30.7 6.4 %collective-permute-start.5 = (bf16[2,2,3200]{2,1,0:T(2,128)(2,1)S(1)}, bf16[2,2,3200]{2,1,0:T(2,128)(2,1)S(1)}, u32[]{:S(2)}, u32[]{:S(2)}) collective-permute-start(bf16[2,2,3200]{2,1,0:T(2,128)(2,1)S(1)} %get-tuple-element.68), channel_id=1, source_target_pairs={{0,4},{2,6},{4,0},{6,2},{8,12},{10,14},{12,8},{14,10},{1,5},{3,7},... | collective-permute-start | bytes 76808 | tf_op jit(solution)/shard_map/ppermute | solution.py:516
  31.2 5.9 %collective-permute-start.6 = (bf16[2,2,3200]{2,1,0:T(2,128)(2,1)S(1)}, bf16[2,2,3200]{2,1,0:T(2,128)(2,1)S(1)}, u32[]{:S(2)}, u32[]{:S(2)}) collective-permute-start(bf16[2,2,3200]{2,1,0:T(2,128)(2,1)S(1)} %get-tuple-element.69), channel_id=1, source_target_pairs={{0,8},{2,10},{4,12},{6,14},{8,0},{10,2},{12,4},{14,6},{1,9},{3,11}... | collective-permute-start | bytes 76808 | tf_op jit(solution)/shard_map/ppermute | solution.py:516
  31.6 5.7 %collective-permute-start.7 = (bf16[2,2,3200]{2,1,0:T(2,128)(2,1)S(1)}, bf16[2,2,3200]{2,1,0:T(2,128)(2,1)S(1)}, u32[]{:S(2)}, u32[]{:S(2)}) collective-permute-start(bf16[2,2,3200]{2,1,0:T(2,128)(2,1)S(1)} %get-tuple-element.70), channel_id=1, source_target_pairs={{0,12},{2,14},{4,8},{6,10},{8,4},{10,6},{12,0},{14,2},{1,13},{3,15... | collective-permute-start | bytes 76808 | tf_op jit(solution)/shard_map/ppermute | solution.py:516

commit v16 on v15

--- a/solution.py
+++ b/solution.py
@@ -128,7 +128,23 @@
 
 
 def project_first(
-    prompts_ref, hidden_ref, w_ref, rows_ref, w_tail_ref, total_ref, w_head_ref, sems, *, edges
+    prompts_ref,
+    hidden_ref,
+    w_ref,
+    target_ref,
+    span_ref,
+    len_ref,
+    rows_ref,
+    w_tail_ref,
+    total_ref,
+    target_here_ref,
+    span_here_ref,
+    len_here_ref,
+    w_head_ref,
+    sems,
+    small_sems,
+    *,
+    edges,
 ):
     theirs = channels(1, total_ref.shape[1])
     chunks = spans(edges)
@@ -144,6 +160,13 @@
         for copy in copies:
             copy.start()
         waits.append(copies)
+    small = [
+        pltpu.make_async_copy(target_ref, target_here_ref, small_sems.at[0]),
+        pltpu.make_async_copy(span_ref, span_here_ref, small_sems.at[1]),
+        pltpu.make_async_copy(len_ref, len_here_ref, small_sems.at[2]),
+    ]
+    for copy in small:
+        copy.start()
     for c, at in enumerate(chunks):
         for copy in waits[c]:
             copy.wait()
@@ -153,6 +176,8 @@
                 total_ref[...] = part
             else:
                 total_ref[...] += part
+    for copy in small:
+        copy.wait()
 
 
 def project_rest(
@@ -180,7 +205,7 @@
     copies += [
         pltpu.make_async_copy(w_ref.at[rest, theirs], w_rest_ref, sems.at[2]),
         pltpu.make_async_copy(scale_ref.at[:, theirs], scale_here_ref, sems.at[3]),
-        pltpu.make_async_copy(w_ref.at[:, mine], w_mine_ref, sems.at[4]),
+        pltpu.make_async_copy(w_ref.at[:depth, mine], w_mine_ref, sems.at[4]),
     ]
     for copy in copies:
         copy.start()
@@ -194,32 +219,40 @@
     copies[-1].wait()
 
 
-def project_mine(rows_ref, rows_rest_ref, w_mine_ref, scale_ref, after_ref, *refs, at, last):
-    refs, (scale_here_ref, sems) = refs[:-2], refs[-2:]
+def project_mine(
+    rows_ref, rows_rest_ref, w_mine_ref, w_ref, scale_ref, after_ref, *refs, at, last, row_count
+):
+    refs, (w_rest_ref, scale_here_ref, sems) = refs[:-3], refs[-3:]
     if last:
-        cache_ref, queries_ref, out_ref, cache_here_ref, queries_here_ref = refs
+        cache_ref, queries_ref, target_ref, span_ref = refs[:4]
+        out_ref, cache_here_ref, queries_here_ref, *table_refs = refs[4:]
     else:
         (out_ref,) = refs
     mine = channels(0, out_ref.shape[1])
-    copies = [pltpu.make_async_copy(scale_ref.at[:, mine], scale_here_ref, sems.at[0])]
+    depth = rows_ref.shape[1]
+    rest = pl.ds(depth, w_rest_ref.shape[0])
+    copies = [
+        pltpu.make_async_copy(w_ref.at[rest, mine], w_rest_ref, sems.at[0]),
+        pltpu.make_async_copy(scale_ref.at[:, mine], scale_here_ref, sems.at[1]),
+    ]
     if last:
-        copies.append(pltpu.make_async_copy(queries_ref, queries_here_ref, sems.at[1]))
-        copies.append(pltpu.make_async_copy(cache_ref, cache_here_ref, sems.at[2]))
+        copies.append(pltpu.make_async_copy(queries_ref, queries_here_ref, sems.at[2]))
+        copies.append(pltpu.make_async_copy(cache_ref, cache_here_ref, sems.at[3]))
     for copy in copies:
         copy.start()
-    depth = rows_ref.shape[1]
+    if last:
+        arrived_tables(target_ref, span_ref, *table_refs, row_count=row_count)
     count = at.stop - at.start
     block = count // 2 if count % 32 == 0 else count
     for m in spans(range(0, count + 1, block)):
         there = slice(at.start + m.start, at.start + m.stop)
-        total = jnp.dot(rows_ref[there, :], w_mine_ref[:depth, :], preferred_element_type=F32)
-        total += jnp.dot(
-            rows_rest_ref[there, :], w_mine_ref[depth:, :], preferred_element_type=F32
-        )
+        total = jnp.dot(rows_ref[there, :], w_mine_ref[...], preferred_element_type=F32)
         if m.start == 0:
             copies[0].wait()
+            copies[1].wait()
+        total += jnp.dot(rows_rest_ref[there, :], w_rest_ref[...], preferred_element_type=F32)
         out_ref[m, :] = (total * scale_here_ref[...]).astype(BF16)
-    for copy in copies[1:]:
+    for copy in copies[2:]:
         copy.wait()
 
 
@@ -251,32 +284,27 @@
     return section_col, rank_col, span_col.astype(jnp.int32)
 
 
-def prepare_arrived(
-    target_ref, span_ref, kept_ref, got_ref, rows_ref, slot_of_ref, bias_ref, *, row_count
-):
+def arrived_tables(target_ref, span_ref, from_slot_ref, slot_of_ref, bias_ref, *, row_count):
     sections, requests = target_ref.shape
     padded, prompt_rows = bias_ref.shape
     span_rows = prompt_rows // requests
     section_col, rank_col, span_col = request_slots(target_ref, span_ref, row_count, padded)
     block = section_col ^ lax.axis_index("section")
     slot = jnp.where(section_col >= 0, block * PITCH + rank_col, -1)
-    slot_of_ref[...] = one_hot((padded, sections * PITCH), 1, slot)
+    slot_of_ref[...] = one_hot(slot_of_ref.shape, 1, slot)
     slot = jnp.where(section_col >= 0, block * CAP + rank_col, -1)
-    rows_ref[...] = jnp.dot(
-        one_hot((padded, sections * CAP), 1, slot),
-        all_blocks(steps_of(sections), kept_ref, got_ref).astype(BF16),
-        preferred_element_type=F32,
-    ).astype(BF16)
+    from_slot_ref[...] = one_hot(from_slot_ref.shape, 1, slot)
     key = iota((padded, prompt_rows), 1) - iota((padded, prompt_rows), 0) * span_rows
     bias_ref[...] = jnp.where((key >= 0) & (key < span_col), 0.0, MASKED)
 
 
-def attend_arrived(rows_ref, slot_of_ref, bias_ref, other_ref, *refs):
+def attend_arrived(from_slot_ref, slot_of_ref, bias_ref, kept_ref, got_ref, other_ref, *refs):
     mine_refs, (keep_ref, send_ref) = refs[:-2], refs[-2:]
     padded, prompt_rows = bias_ref.shape
     kv_heads = other_ref.shape[1] // (2 * HD)
-    group = rows_ref.shape[1] // (kv_heads * HD)
-    rows = rows_ref[...]
+    group = kept_ref.shape[2] // (kv_heads * HD)
+    asked = all_blocks(steps_of(2 * kept_ref.shape[0]), kept_ref, got_ref).astype(BF16)
+    rows = jnp.dot(from_slot_ref[...], asked, preferred_element_type=F32).astype(BF16)
     slot_of = slot_of_ref[...]
     bias = bias_ref[...]
     mine = jnp.concatenate([ref[...] for ref in mine_refs], axis=0)
@@ -433,7 +461,8 @@
 
 
 def merge(pick_ref, *refs):
-    parts, group_refs, out_ref = refs[:-5], refs[-5:-1], refs[-1]
+    refs, (out_ref, out_here_ref, sems) = refs[:-3], refs[-3:]
+    parts, group_refs = refs[:-4], refs[-4:]
     cached_refs, slot_out_refs, slot_lse_refs = parts[0::3], parts[1::3], parts[2::3]
     width = out_ref.shape[1]
     pick = pick_ref[...]
@@ -456,6 +485,7 @@
     has = lax.dot_general(
         pick, jnp.ones((pick.shape[0], HD), BF16), TRANSPOSED, preferred_element_type=F32
     )
+    copies = []
     for i in range(width // HD):
         at = slice(i * HD, (i + 1) * HD)
         merged = (
@@ -469,8 +499,19 @@
         for ref in cached_refs:
             rows = slice(row, row + ref.shape[0])
             kept = ref[:, at].astype(F32)
-            out_ref[rows, at] = jnp.where(has[rows] > 0.5, placed[rows], kept).astype(BF16)
+            out_here_ref[rows, at] = jnp.where(has[rows] > 0.5, placed[rows], kept).astype(BF16)
             row += ref.shape[0]
+        ready = width * (len(copies) + 1) // sems.shape[0]
+        if at.stop == ready:
+            there = slice(width * len(copies) // sems.shape[0], ready)
+            copies.append(
+                pltpu.make_async_copy(
+                    out_here_ref.at[:, there], out_ref.at[:, there], sems.at[len(copies)]
+                )
+            )
+            copies[-1].start()
+    for copy in copies:
+        copy.wait()
 
 
 def compiler_params(megabytes):
@@ -535,24 +576,28 @@
             name="regroup",
         )(in_vmem(blocks), got, in_vmem(after))
 
-    edges = (0, 256, 768, 1536, 2560, 4096)
+    edges = (0, 256, 768, 1536, 2560, 3584)
     depth, head = edges[-1], edges[-2]
-    rows, w_tail, total = pl.pallas_call(
+    rows, w_tail, total, target_here, span_here, lengths = pl.pallas_call(
         functools.partial(project_first, edges=edges),
-        in_specs=[REMAINS] * 3,
-        out_specs=[RESIDENT] * 3,
+        in_specs=[REMAINS] * 6,
+        out_specs=[RESIDENT] * 6,
         out_shape=[
             pltpu.VMEM((all_rows, depth), BF16),
             pltpu.VMEM((depth - head, local_width), BF16),
             pltpu.VMEM((all_rows, local_width), F32),
+            pltpu.VMEM(target_row.shape, jnp.int32),
+            pltpu.VMEM(span_len.shape, jnp.int32),
+            pltpu.VMEM(lengths.shape, jnp.int32),
         ],
         scratch_shapes=[
             pltpu.VMEM((head, local_width), BF16),
             pltpu.SemaphoreType.DMA((len(edges) - 1, 3)),
+            pltpu.SemaphoreType.DMA((3,)),
         ],
         compiler_params=compiler_params(12),
         name="project_first",
-    )(prompts, decode_hidden, w_kv)
+    )(prompts, decode_hidden, w_kv, target_row, span_len, lengths)
     keep, send = regrouped(keep, got, steps, 1, total)
     got = swapped(send, steps[1][0])
     theirs, rows_rest, w_mine = pl.pallas_call(
@@ -562,7 +607,7 @@
         out_shape=[
             pltpu.VMEM((all_rows, local_width), BF16),
             pltpu.VMEM((all_rows, features - depth), BF16),
-            pltpu.VMEM((features, local_width), BF16),
+            pltpu.VMEM((depth, local_width), BF16),
         ],
         scratch_shapes=[
             pltpu.VMEM((features - depth, local_width), BF16),
@@ -585,43 +630,44 @@
             keep, send = regrouped(keep, got, steps, piece + 2, after)
             got = swapped(send, steps[piece + 2][0])
         last = piece == pieces - 1
-        extra = [kv_cache, queries] if last else []
-        part, *here = pl.pallas_call(
-            functools.partial(project_mine, at=at, last=last),
-            in_specs=[RESIDENT] * 3 + [REMAINS] * (2 + len(extra)),
-            out_specs=[RESIDENT] * (1 + len(extra)),
-            out_shape=[pltpu.VMEM((at.stop - at.start, local_width), BF16)]
-            + [pltpu.VMEM(x.shape, BF16) for x in extra],
-            scratch_shapes=[pltpu.VMEM((1, local_width), F32), pltpu.SemaphoreType.DMA((3,))],
+        padded = -(-span_len.shape[1] // 16) * 16
+        extra = [kv_cache, queries, in_vmem(target_here), in_vmem(span_here)] if last else []
+        extra_out = [
+            pltpu.VMEM(kv_cache.shape, BF16),
+            pltpu.VMEM(queries.shape, BF16),
+            pltpu.VMEM((padded, slots), BF16),
+            pltpu.VMEM((padded, sections * PITCH), BF16),
+            pltpu.VMEM((padded, prompt_rows), F32),
+        ]
+        extra_out = extra_out if last else []
+        part, *extra_out = pl.pallas_call(
+            functools.partial(project_mine, at=at, last=last, row_count=row_count),
+            in_specs=[RESIDENT] * 3
+            + [REMAINS] * 3
+            + ([REMAINS] * 2 + [RESIDENT] * 2 if last else []),
+            out_specs=[RESIDENT] * (1 + len(extra_out)),
+            out_shape=[pltpu.VMEM((at.stop - at.start, local_width), BF16)] + extra_out,
+            scratch_shapes=[
+                pltpu.VMEM((features - depth, local_width), BF16),
+                pltpu.VMEM((1, local_width), F32),
+                pltpu.SemaphoreType.DMA((4,)),
+            ],
             compiler_params=compiler_params(16),
             name="project_mine",
-        )(*map(in_vmem, (rows, rows_rest, w_mine)), scale, in_vmem(keep), *extra)
+        )(*map(in_vmem, (rows, rows_rest, w_mine)), w_kv, scale, in_vmem(keep), *extra)
         after = part
         mine.append(in_vmem(part))
-    kv_here, queries_here = map(in_vmem, here)
-
-    padded = -(-span_len.shape[1] // 16) * 16
-    prepared = pl.pallas_call(
-        functools.partial(prepare_arrived, row_count=row_count),
-        in_specs=[RESIDENT] * 4,
-        out_specs=[RESIDENT] * 3,
-        out_shape=[
-            pltpu.VMEM((padded, query_width), BF16),
-            pltpu.VMEM((padded, sections * PITCH), BF16),
-            pltpu.VMEM((padded, prompt_rows), F32),
-        ],
-        compiler_params=compiler_params(16),
-        name="prepare_arrived",
-    )(target_row, span_len, in_vmem(keep), got)
+    kv_here, queries_here, *tables = map(in_vmem, extra_out)
+
     answer_width = query_width + STATS
     keep, send = pl.pallas_call(
         attend_arrived,
-        in_specs=[RESIDENT] * (4 + len(mine)),
+        in_specs=[RESIDENT] * (6 + len(mine)),
         out_specs=[RESIDENT] * 2,
         out_shape=block_pair(answer_width),
         compiler_params=compiler_params(24),
         name="attend_arrived",
-    )(*map(in_vmem, prepared), other, *mine)
+    )(*tables, in_vmem(keep), got, other, *mine)
 
     steps = answer_steps_of(sections)
     shares = []
@@ -642,7 +688,7 @@
             ],
             compiler_params=compiler_params(24),
             name="attend_cache",
-        )(queries_here, kv_here, lengths, mine[-1], other, in_vmem(pick), in_vmem(keep))
+        )(queries_here, kv_here, in_vmem(lengths), mine[-1], other, in_vmem(pick), in_vmem(keep))
         shares += share
         if done + 1 < len(steps):
             keep, send = regrouped(keep, got, steps, done + 1, share[2])
@@ -662,8 +708,9 @@
     return pl.pallas_call(
         merge,
         in_specs=[RESIDENT] * (5 + len(shares)),
-        out_specs=RESIDENT,
+        out_specs=REMAINS,
         out_shape=jax.ShapeDtypeStruct((row_count, query_width), BF16),
+        scratch_shapes=[pltpu.VMEM((row_count, query_width), BF16), pltpu.SemaphoreType.DMA((4,))],
         compiler_params=compiler_params(24),
         name="merge",
     )(*map(in_vmem, (pick, *shares)), *groups)

time: 39 us -> 40.4 us (1.036)
  waiting for transfers between devices: 2.03 us -> 3.42 us
    ppermute x7, waiting for transfers between devices: 2.03 us -> 3.41 us  [swapped(): return in_vmem(lax.ppermute(blocks, 'section', pairs))]
    pallas_call x2, Pallas kernels: 3.8 us -> 2.53 us  [shards(): pl.pallas_call(functools.partial(attend_cache, rows_at=at), in_specs=[RES...]
    pallas_call x1, Pallas kernels: 4.84 us -> 5.87 us  [shards(): pl.pallas_call(project_rest, in_specs=[REMAINS] * 4 + [RESIDENT] * 3 + [R...]
    pallas_call x3 -> x2, Pallas kernels: 8 us -> 8.62 us  [the longest x1 7.62 us: shards(): pl.pallas_call(functools.partial(project_mine, at=at, last=last, row_coun...]
  transfers between devices with their start and end apart: 8 -> 8, of which waited for: 2 -> 2; matrix products, arithmetic and copies ran while one was open for 0% -> 0% of each run, Pallas kernels for 52% -> 51%
where the time goes in v16:
time: 40.4 us; the launch traced here: 40.2 us
  Pallas kernels  24.3 us (60%)
  starting transfers between devices  12.4 us (31%)
  waiting for transfers between devices  3.42 us (8%)
    ppermute x7, starting transfers between devices, swapped(): return in_vmem(lax.ppermute(blocks, 'section', pairs))  12.3 us
    pallas_call x1, Pallas kernels, shards(): pl.pallas_call(functools.partial(project_mine, at=at, last=last, row_coun...  7.62 us
    pallas_call x1, Pallas kernels, shards(): pl.pallas_call(project_rest, in_specs=[REMAINS] * 4 + [RESIDENT] * 3 + [R...  5.87 us
    pallas_call x1, Pallas kernels, shards(): pl.pallas_call(functools.partial(project_first, edges=edges), in_specs=[R...  4.39 us
    ppermute x7, waiting for transfers between devices, swapped(): return in_vmem(lax.ppermute(blocks, 'section', pairs))  3.41 us
    pallas_call x2, Pallas kernels, shards(): pl.pallas_call(functools.partial(attend_cache, rows_at=at), in_specs=[RES...  2.53 us
    pallas_call x1, Pallas kernels, shards(): pl.pallas_call(select_queries, in_specs=[RESIDENT, RESIDENT], out_specs=[...  1.55 us
    pallas_call x1, Pallas kernels, shards(): pl.pallas_call(merge, in_specs=[RESIDENT] * (5 + len(shares)), out_specs=...  1.3 us
  transfers between devices with their start and end apart: 8, of which 2 were waited for; matrix products, arithmetic and copies ran while one was open for 0% of the time, Pallas kernels for 51%

profile of v16, /device:TPU:0, one launch (start us, length us, event | category | flops | bytes accessed | tf_op | source)
XLA Modules:
  0.0 40.2 jit_solution(5975418649145585838)
XLA Ops:
  0.0 1.6 %select_queries.1 = (bf16[16,128]{1,0:T(8,128)(2,1)S(1)}, bf16[4,2,3072]{2,1,0:T(2,128)(2,1)S(1)}, bf16[4,2,3072]{2,1,0:T(2,128)(2,1)S(1)}) custom-call(s32[8,12]{1,0:T(8,128)} %target_ref.3, bf16[128,3072]{1,0:T(8,128)(2,1)} %refs_1_.1), custom_call_target="tpu_custom_call" | custom-call | tf_op jit(solution)/shard_map/select_queries/pallas_call | solution.py:559
  1.6 4.1 %collective-permute-start = (bf16[4,2,3072]{2,1,0:T(2,128)(2,1)S(1)}, bf16[4,2,3072]{2,1,0:T(2,128)(2,1)S(1)}, u32[]{:S(2)}, u32[]{:S(2)}) collective-permute-start(bf16[4,2,3072]{2,1,0:T(2,128)(2,1)S(1)} %get-tuple-element.46), channel_id=1, source_target_pairs={{0,8},{2,10},{4,12},{6,14},{8,0},{10,2},{12,4},{14,6},{1,9},{3,11}... | collective-permute-start | bytes 147464 | tf_op jit(solution)/shard_map/ppermute | solution.py:557
  5.7 4.4 %project_first.1 = (bf16[896,3584]{1,0:T(8,128)(2,1)S(1)}, bf16[1024,512]{1,0:T(8,128)(2,1)S(1)}, f32[896,512]{1,0:T(8,128)S(1)}, s32[8,12]{1,0:T(8,128)S(1)}, s...) custom-call(bf16[768,6144]{1,0:T(8,128)(2,1)} %prompts_ref.3, bf16[128,6144]{1,0:T(8,128)(2,1)} %hidden_ref.3, ...), custom_call_target="tpu_custom_call" | custom-call | tf_op jit(solution)/shard_map/project_first/pallas_call | solution.py:581
  10.1 0.0 collective-permute-done.got_ref
  10.1 1.6 %collective-permute-start.1 = (bf16[4,2,3072]{2,1,0:T(2,128)(2,1)S(1)}, bf16[4,2,3072]{2,1,0:T(2,128)(2,1)S(1)}, u32[]{:S(2)}, u32[]{:S(2)}) collective-permute-start(bf16[4,2,3072]{2,1,0:T(2,128)(2,1)S(1)} %get-tuple-element.51), channel_id=1, source_target_pairs={{0,4},{2,6},{4,0},{6,2},{8,12},{10,14},{12,8},{14,10},{1,5},{3,7},... | collective-permute-start | bytes 147464 | tf_op jit(solution)/shard_map/ppermute | solution.py:557
  11.7 5.9 %project_rest.1 = (bf16[896,512]{1,0:T(8,128)(2,1)S(1)}, bf16[896,2560]{1,0:T(8,128)(2,1)S(1)}, bf16[3584,512]{1,0:T(8,128)(2,1)S(1)}) custom-call(bf16[768,6144]{1,0:T(8,128)(2,1)} %prompts_ref.3, bf16[128,6144]{1,0:T(8,128)(2,1)} %hidden_ref.3, bf16[6144,1024]{1,0:T(8,128)(2,1)} %w_ref.5, f32[1,1024]{1,0:T(1,128)} %bitcast.2, ...), custom_call_target="tpu_custom_call" | custom-call | tf_op jit(solution)/shard_map/project_rest/pallas_call | solution.py:603
  17.6 0.0 collective-permute-done.1.got_ref
  17.6 0.1 collective-permute-start.2
  17.7 1.6 %collective-permute-start.3 = (bf16[4,2,3072]{2,1,0:T(2,128)(2,1)S(1)}, bf16[4,2,3072]{2,1,0:T(2,128)(2,1)S(1)}, u32[]{:S(2)}, u32[]{:S(2)}) collective-permute-start(bf16[4,2,3072]{2,1,0:T(2,128)(2,1)S(1)} %get-tuple-element.64), channel_id=1, source_target_pairs={{0,2},{2,0},{4,6},{6,4},{8,10},{10,8},{12,14},{14,12},{1,3},{3,1},... | collective-permute-start | bytes 147464 | tf_op jit(solution)/shard_map/ppermute | solution.py:557
  19.3 7.6 %project_mine.1 = (bf16[896,512]{1,0:T(8,128)(2,1)S(1)}, bf16[128,32,512]{2,1,0:T(8,128)(2,1)S(1)}, bf16[128,3072]{1,0:T(8,128)(2,1)S(1)}, bf16[16,16]{1,0:T(8,1...) custom-call(bf16[896,3584]{1,0:T(8,128)(2,1)S(1)} %get-tuple-element.42.rows_ref, ...), custom_call_target="tpu_custom_call" | custom-call | tf_op jit(solution)/shard_map/project_mine/pallas_call | solution.py:643
  26.9 0.0 collective-permute-done.3.got_ref
  26.9 0.0 collective-permute-done.2.other_ref
  27.0 1.0 %attend_arrived.1 = (bf16[4,2,3200]{2,1,0:T(2,128)(2,1)S(1)}, bf16[4,2,3200]{2,1,0:T(2,128)(2,1)S(1)}) custom-call(bf16[16,16]{1,0:T(8,128)(2,1)S(1)} %get-tuple-element.61.from_slot_ref, bf16[16,64]{1,0:T(8,128)(2,1)S(1)} %get-tuple-element.62.slot_of_ref, f32[16,768]{1,0:T(8,128)S(1)} %get-tuple-element.63.bias_ref, ...), custom_call_target="tpu_custom_call" | custom-call | tf_op jit(solution)/shard_map/attend_arrived/pallas_call | solution.py:663
  28.0 0.6 %collective-permute-start.4 = (bf16[4,2,3200]{2,1,0:T(2,128)(2,1)S(1)}, bf16[4,2,3200]{2,1,0:T(2,128)(2,1)S(1)}, u32[]{:S(2)}, u32[]{:S(2)}) collective-permute-start(bf16[4,2,3200]{2,1,0:T(2,128)(2,1)S(1)} %get-tuple-element.69), channel_id=1, source_target_pairs={{0,2},{2,0},{4,6},{6,4},{8,10},{10,8},{12,14},{14,12},{1,3},{3,1},... | collective-permute-start | bytes 153608 | tf_op jit(solution)/shard_map/ppermute | solution.py:557
  28.5 1.3 %attend_cache.2 = (bf16[64,3072]{1,0:T(8,128)(2,1)S(1)}, f32[16,3072]{1,0:T(8,128)S(1)}, f32[16,128]{1,0:T(8,128)S(1)}) custom-call(bf16[128,3072]{1,0:T(8,128)(2,1)S(1)} %get-tuple-element.57.queries_ref, bf16[128,32,512]{2,1,0:T(8,128)(2,1)S(1)} %get-tuple-element.58.cache_ref, s32[1,128]{1,0:T(1,128)S(1)} %get-tuple-element.59.len_ref, ...), custom_call_target="tpu_custom_call" | custom-call | tf_op jit(solution)/shard_map/attend_cache/pallas_call | solution.py:680
  29.8 2.3 %collective-permute-done.4.got_ref = bf16[4,2,3200]{2,1,0:T(2,128)(2,1)S(1)} collective-permute-done((bf16[4,2,3200]{2,1,0:T(2,128)(2,1)S(1)}, bf16[4,2,3200]{2,1,0:T(2,128)(2,1)S(1)}, u32[]{:S(2)}, u32[]{:S(2)}) %collective-permute-start.4) | collective-permute-done | bytes 51232 | tf_op jit(solution)/shard_map/ppermute | solution.py:557
  32.2 0.5 %collective-permute-start.5 = (bf16[2,2,3200]{2,1,0:T(2,128)(2,1)S(1)}, bf16[2,2,3200]{2,1,0:T(2,128)(2,1)S(1)}, u32[]{:S(2)}, u32[]{:S(2)}) collective-permute-start(bf16[2,2,3200]{2,1,0:T(2,128)(2,1)S(1)} %get-tuple-element.74), channel_id=1, source_target_pairs={{0,4},{2,6},{4,0},{6,2},{8,12},{10,14},{12,8},{14,10},{1,5},{3,7},... | collective-permute-start | bytes 76808 | tf_op jit(solution)/shard_map/ppermute | solution.py:557
  32.7 0.6 %collective-permute-start.6 = (bf16[2,2,3200]{2,1,0:T(2,128)(2,1)S(1)}, bf16[2,2,3200]{2,1,0:T(2,128)(2,1)S(1)}, u32[]{:S(2)}, u32[]{:S(2)}) collective-permute-start(bf16[2,2,3200]{2,1,0:T(2,128)(2,1)S(1)} %get-tuple-element.75), channel_id=1, source_target_pairs={{0,8},{2,10},{4,12},{6,14},{8,0},{10,2},{12,4},{14,6},{1,9},{3,11}... | collective-permute-start | bytes 76808 | tf_op jit(solution)/shard_map/ppermute | solution.py:557
  33.3 3.3 %collective-permute-start.7 = (bf16[2,2,3200]{2,1,0:T(2,128)(2,1)S(1)}, bf16[2,2,3200]{2,1,0:T(2,128)(2,1)S(1)}, u32[]{:S(2)}, u32[]{:S(2)}) collective-permute-start(bf16[2,2,3200]{2,1,0:T(2,128)(2,1)S(1)} %get-tuple-element.76), channel_id=1, source_target_pairs={{0,12},{2,14},{4,8},{6,10},{8,4},{10,6},{12,0},{14,2},{1,13},{3,15... | collective-permute-start | bytes 76808 | tf_op jit(solution)/shard_map/ppermute | solution.py:557
  36.6 1.3 %attend_cache.3 = (bf16[64,3072]{1,0:T(8,128)(2,1)S(1)}, f32[16,3072]{1,0:T(8,128)S(1)}, f32[16,128]{1,0:T(8,128)S(1)}) custom-call(bf16[128,3072]{1,0:T(8,128)(2,1)S(1)} %get-tuple-element.57.queries_ref, bf16[128,32,512]{2,1,0:T(8,128)(2,1)S(1)} %get-tuple-element.58.cache_ref, s32[1,128]{1,0:T(1,128)S(1)} %get-tuple-element.59.len_ref, ...), custom_call_target="tpu_custom_call" | custom-call | tf_op jit(solution)/shard_map/attend_cache/pallas_call | solution.py:680
  37.9 0.0 collective-permute-done.5.refs_7_
  37.9 0.0 collective-permute-done.6.refs_8_
  37.9 1.1 %collective-permute-done.7.refs_9_ = bf16[2,2,3200]{2,1,0:T(2,128)(2,1)S(1)} collective-permute-done((bf16[2,2,3200]{2,1,0:T(2,128)(2,1)S(1)}, bf16[2,2,3200]{2,1,0:T(2,128)(2,1)S(1)}, u32[]{:S(2)}, u32[]{:S(2)}) %collective-permute-start.7) | collective-permute-done | bytes 25632 | tf_op jit(solution)/shard_map/ppermute | solution.py:557
  38.9 1.3 %merge.1 = bf16[128,3072]{1,0:T(8,128)(2,1)} custom-call(bf16[16,128]{1,0:T(8,128)(2,1)S(1)} %get-tuple-element.41.pick_ref, bf16[64,3072]{1,0:T(8,128)(2,1)S(1)} %get-tuple-element.66.refs_0_, f32[16,3072]{1,0:T(8,128)S(1)} %get-tuple-element.67.refs_1_, f32[16,128]{1,0:T(8,128)S(1)} %get-tuple-element.68.after_ref.refs_2_, ...), custom_call_target="tpu_custom_call" | custom-call | tf_op jit(solution)/shard_map/merge/pallas_call | solution.py:708
  (3 shorter events, 0.0 us)
Async XLA Ops:
  1.6 8.5 %collective-permute-start = (bf16[4,2,3072]{2,1,0:T(2,128)(2,1)S(1)}, bf16[4,2,3072]{2,1,0:T(2,128)(2,1)S(1)}, u32[]{:S(2)}, u32[]{:S(2)}) collective-permute-start(bf16[4,2,3072]{2,1,0:T(2,128)(2,1)S(1)} %get-tuple-element.46), channel_id=1, source_target_pairs={{0,8},{2,10},{4,12},{6,14},{8,0},{10,2},{12,4},{14,6},{1,9},{3,11}... | collective-permute-start | bytes 147464 | tf_op jit(solution)/shard_map/ppermute | solution.py:557
  10.1 7.5 %collective-permute-start.1 = (bf16[4,2,3072]{2,1,0:T(2,128)(2,1)S(1)}, bf16[4,2,3072]{2,1,0:T(2,128)(2,1)S(1)}, u32[]{:S(2)}, u32[]{:S(2)}) collective-permute-start(bf16[4,2,3072]{2,1,0:T(2,128)(2,1)S(1)} %get-tuple-element.51), channel_id=1, source_target_pairs={{0,4},{2,6},{4,0},{6,2},{8,12},{10,14},{12,8},{14,10},{1,5},{3,7},... | collective-permute-start | bytes 147464 | tf_op jit(solution)/shard_map/ppermute | solution.py:557
  17.6 9.3 %collective-permute-start.2 = (bf16[896,512]{1,0:T(8,128)(2,1)S(1)}, bf16[896,512]{1,0:T(8,128)(2,1)S(1)}, u32[]{:S(2)}, u32[]{:S(2)}) collective-permute-start(bf16[896,512]{1,0:T(8,128)(2,1)S(1)} %get-tuple-element.53.after_ref), channel_id=1, source_target_pairs={{0,1},{1,0},{2,3},{3,2},{4,5},{5,4},{6,7},{7,6},{8,9},{9,8},{10,11... | collective-permute-start | bytes 2752520 | tf_op jit(solution)/shard_map/ppermute | solution.py:622
  17.7 9.2 %collective-permute-start.3 = (bf16[4,2,3072]{2,1,0:T(2,128)(2,1)S(1)}, bf16[4,2,3072]{2,1,0:T(2,128)(2,1)S(1)}, u32[]{:S(2)}, u32[]{:S(2)}) collective-permute-start(bf16[4,2,3072]{2,1,0:T(2,128)(2,1)S(1)} %get-tuple-element.64), channel_id=1, source_target_pairs={{0,2},{2,0},{4,6},{6,4},{8,10},{10,8},{12,14},{14,12},{1,3},{3,1},... | collective-permute-start | bytes 147464 | tf_op jit(solution)/shard_map/ppermute | solution.py:557
  28.0 4.2 %collective-permute-start.4 = (bf16[4,2,3200]{2,1,0:T(2,128)(2,1)S(1)}, bf16[4,2,3200]{2,1,0:T(2,128)(2,1)S(1)}, u32[]{:S(2)}, u32[]{:S(2)}) collective-permute-start(bf16[4,2,3200]{2,1,0:T(2,128)(2,1)S(1)} %get-tuple-element.69), channel_id=1, source_target_pairs={{0,2},{2,0},{4,6},{6,4},{8,10},{10,8},{12,14},{14,12},{1,3},{3,1},... | collective-permute-start | bytes 153608 | tf_op jit(solution)/shard_map/ppermute | solution.py:557
  32.2 5.7 %collective-permute-start.5 = (bf16[2,2,3200]{2,1,0:T(2,128)(2,1)S(1)}, bf16[2,2,3200]{2,1,0:T(2,128)(2,1)S(1)}, u32[]{:S(2)}, u32[]{:S(2)}) collective-permute-start(bf16[2,2,3200]{2,1,0:T(2,128)(2,1)S(1)} %get-tuple-element.74), channel_id=1, source_target_pairs={{0,4},{2,6},{4,0},{6,2},{8,12},{10,14},{12,8},{14,10},{1,5},{3,7},... | collective-permute-start | bytes 76808 | tf_op jit(solution)/shard_map/ppermute | solution.py:557
  32.7 5.2 %collective-permute-start.6 = (bf16[2,2,3200]{2,1,0:T(2,128)(2,1)S(1)}, bf16[2,2,3200]{2,1,0:T(2,128)(2,1)S(1)}, u32[]{:S(2)}, u32[]{:S(2)}) collective-permute-start(bf16[2,2,3200]{2,1,0:T(2,128)(2,1)S(1)} %get-tuple-element.75), channel_id=1, source_target_pairs={{0,8},{2,10},{4,12},{6,14},{8,0},{10,2},{12,4},{14,6},{1,9},{3,11}... | collective-permute-start | bytes 76808 | tf_op jit(solution)/shard_map/ppermute | solution.py:557
  33.3 5.7 %collective-permute-start.7 = (bf16[2,2,3200]{2,1,0:T(2,128)(2,1)S(1)}, bf16[2,2,3200]{2,1,0:T(2,128)(2,1)S(1)}, u32[]{:S(2)}, u32[]{:S(2)}) collective-permute-start(bf16[2,2,3200]{2,1,0:T(2,128)(2,1)S(1)} %get-tuple-element.76), channel_id=1, source_target_pairs={{0,12},{2,14},{4,8},{6,10},{8,4},{10,6},{12,0},{14,2},{1,13},{3,15... | collective-permute-start | bytes 76808 | tf_op jit(solution)/shard_map/ppermute | solution.py:557

commit v17 on v15

--- a/solution.py
+++ b/solution.py
@@ -128,7 +128,23 @@
 
 
 def project_first(
-    prompts_ref, hidden_ref, w_ref, rows_ref, w_tail_ref, total_ref, w_head_ref, sems, *, edges
+    prompts_ref,
+    hidden_ref,
+    w_ref,
+    target_ref,
+    span_ref,
+    len_ref,
+    rows_ref,
+    w_tail_ref,
+    total_ref,
+    target_here_ref,
+    span_here_ref,
+    len_here_ref,
+    w_head_ref,
+    sems,
+    small_sems,
+    *,
+    edges,
 ):
     theirs = channels(1, total_ref.shape[1])
     chunks = spans(edges)
@@ -144,6 +160,13 @@
         for copy in copies:
             copy.start()
         waits.append(copies)
+    small = [
+        pltpu.make_async_copy(target_ref, target_here_ref, small_sems.at[0]),
+        pltpu.make_async_copy(span_ref, span_here_ref, small_sems.at[1]),
+        pltpu.make_async_copy(len_ref, len_here_ref, small_sems.at[2]),
+    ]
+    for copy in small:
+        copy.start()
     for c, at in enumerate(chunks):
         for copy in waits[c]:
             copy.wait()
@@ -153,6 +176,8 @@
                 total_ref[...] = part
             else:
                 total_ref[...] += part
+    for copy in small:
+        copy.wait()
 
 
 def project_rest(
@@ -162,12 +187,13 @@
     scale_ref,
     rows_ref,
     w_tail_ref,
-    total_ref,
+    total_in_ref,
     after_ref,
     theirs_ref,
     rows_rest_ref,
     w_mine_ref,
     w_rest_ref,
+    total_ref,
     scale_here_ref,
     sems,
 ):
@@ -176,22 +202,37 @@
     depth = rows_ref.shape[1]
     head = depth - w_tail_ref.shape[0]
     rest = slice(depth, depth + rows_rest_ref.shape[1])
-    copies = load_rows(prompts_ref, hidden_ref, rest, rows_rest_ref, slice(None), sems)
-    copies += [
-        pltpu.make_async_copy(w_ref.at[rest, theirs], w_rest_ref, sems.at[2]),
-        pltpu.make_async_copy(scale_ref.at[:, theirs], scale_here_ref, sems.at[3]),
-        pltpu.make_async_copy(w_ref.at[:, mine], w_mine_ref, sems.at[4]),
+    size = rest.stop - rest.start
+    chunks = spans((0, size // 2, size))
+    waits = []
+    for c, at in enumerate(chunks):
+        there = slice(depth + at.start, depth + at.stop)
+        copies = load_rows(prompts_ref, hidden_ref, there, rows_rest_ref, at, sems.at[c])
+        copies.append(
+            pltpu.make_async_copy(w_ref.at[there, theirs], w_rest_ref.at[at, :], sems.at[c, 2])
+        )
+        for copy in copies:
+            copy.start()
+        waits.append(copies)
+    later = [
+        pltpu.make_async_copy(scale_ref.at[:, theirs], scale_here_ref, sems.at[2, 0]),
+        pltpu.make_async_copy(w_ref.at[:, mine], w_mine_ref, sems.at[2, 1]),
     ]
-    for copy in copies:
+    for copy in later:
         copy.start()
-    total = total_ref[...] + jnp.dot(
+    total_ref[...] = total_in_ref[...] + jnp.dot(
         rows_ref[:, head:], w_tail_ref[...], preferred_element_type=F32
     )
-    for copy in copies[:-1]:
-        copy.wait()
-    total += jnp.dot(rows_rest_ref[...], w_rest_ref[...], preferred_element_type=F32)
-    theirs_ref[...] = (total * scale_here_ref[...]).astype(BF16)
-    copies[-1].wait()
+    for c, at in enumerate(chunks):
+        for copy in waits[c]:
+            copy.wait()
+        part = jnp.dot(rows_rest_ref[:, at], w_rest_ref[at, :], preferred_element_type=F32)
+        if c < len(chunks) - 1:
+            total_ref[...] += part
+        else:
+            later[0].wait()
+            theirs_ref[...] = ((total_ref[...] + part) * scale_here_ref[...]).astype(BF16)
+    later[1].wait()
 
 
 def project_mine(rows_ref, rows_rest_ref, w_mine_ref, scale_ref, after_ref, *refs, at, last):
@@ -433,7 +474,8 @@
 
 
 def merge(pick_ref, *refs):
-    parts, group_refs, out_ref = refs[:-5], refs[-5:-1], refs[-1]
+    refs, (out_ref, out_here_ref, sems) = refs[:-3], refs[-3:]
+    parts, group_refs = refs[:-4], refs[-4:]
     cached_refs, slot_out_refs, slot_lse_refs = parts[0::3], parts[1::3], parts[2::3]
     width = out_ref.shape[1]
     pick = pick_ref[...]
@@ -456,6 +498,7 @@
     has = lax.dot_general(
         pick, jnp.ones((pick.shape[0], HD), BF16), TRANSPOSED, preferred_element_type=F32
     )
+    copies = []
     for i in range(width // HD):
         at = slice(i * HD, (i + 1) * HD)
         merged = (
@@ -469,8 +512,19 @@
         for ref in cached_refs:
             rows = slice(row, row + ref.shape[0])
             kept = ref[:, at].astype(F32)
-            out_ref[rows, at] = jnp.where(has[rows] > 0.5, placed[rows], kept).astype(BF16)
+            out_here_ref[rows, at] = jnp.where(has[rows] > 0.5, placed[rows], kept).astype(BF16)
             row += ref.shape[0]
+        ready = width * (len(copies) + 1) // sems.shape[0]
+        if at.stop == ready:
+            there = slice(width * len(copies) // sems.shape[0], ready)
+            copies.append(
+                pltpu.make_async_copy(
+                    out_here_ref.at[:, there], out_ref.at[:, there], sems.at[len(copies)]
+                )
+            )
+            copies[-1].start()
+    for copy in copies:
+        copy.wait()
 
 
 def compiler_params(megabytes):
@@ -537,22 +591,26 @@
 
     edges = (0, 256, 768, 1536, 2560, 4096)
     depth, head = edges[-1], edges[-2]
-    rows, w_tail, total = pl.pallas_call(
+    rows, w_tail, total, target_here, span_here, lengths = pl.pallas_call(
         functools.partial(project_first, edges=edges),
-        in_specs=[REMAINS] * 3,
-        out_specs=[RESIDENT] * 3,
+        in_specs=[REMAINS] * 6,
+        out_specs=[RESIDENT] * 6,
         out_shape=[
             pltpu.VMEM((all_rows, depth), BF16),
             pltpu.VMEM((depth - head, local_width), BF16),
             pltpu.VMEM((all_rows, local_width), F32),
+            pltpu.VMEM(target_row.shape, jnp.int32),
+            pltpu.VMEM(span_len.shape, jnp.int32),
+            pltpu.VMEM(lengths.shape, jnp.int32),
         ],
         scratch_shapes=[
             pltpu.VMEM((head, local_width), BF16),
             pltpu.SemaphoreType.DMA((len(edges) - 1, 3)),
+            pltpu.SemaphoreType.DMA((3,)),
         ],
         compiler_params=compiler_params(12),
         name="project_first",
-    )(prompts, decode_hidden, w_kv)
+    )(prompts, decode_hidden, w_kv, target_row, span_len, lengths)
     keep, send = regrouped(keep, got, steps, 1, total)
     got = swapped(send, steps[1][0])
     theirs, rows_rest, w_mine = pl.pallas_call(
@@ -566,8 +624,9 @@
         ],
         scratch_shapes=[
             pltpu.VMEM((features - depth, local_width), BF16),
+            pltpu.VMEM((all_rows, local_width), F32),
             pltpu.VMEM((1, local_width), F32),
-            pltpu.SemaphoreType.DMA((5,)),
+            pltpu.SemaphoreType.DMA((3, 3)),
         ],
         compiler_params=compiler_params(16),
         name="project_rest",
@@ -612,7 +671,7 @@
         ],
         compiler_params=compiler_params(16),
         name="prepare_arrived",
-    )(target_row, span_len, in_vmem(keep), got)
+    )(in_vmem(target_here), in_vmem(span_here), in_vmem(keep), got)
     answer_width = query_width + STATS
     keep, send = pl.pallas_call(
         attend_arrived,
@@ -642,7 +701,7 @@
             ],
             compiler_params=compiler_params(24),
             name="attend_cache",
-        )(queries_here, kv_here, lengths, mine[-1], other, in_vmem(pick), in_vmem(keep))
+        )(queries_here, kv_here, in_vmem(lengths), mine[-1], other, in_vmem(pick), in_vmem(keep))
         shares += share
         if done + 1 < len(steps):
             keep, send = regrouped(keep, got, steps, done + 1, share[2])
@@ -662,8 +721,9 @@
     return pl.pallas_call(
         merge,
         in_specs=[RESIDENT] * (5 + len(shares)),
-        out_specs=RESIDENT,
+        out_specs=REMAINS,
         out_shape=jax.ShapeDtypeStruct((row_count, query_width), BF16),
+        scratch_shapes=[pltpu.VMEM((row_count, query_width), BF16), pltpu.SemaphoreType.DMA((4,))],
         compiler_params=compiler_params(24),
         name="merge",
     )(*map(in_vmem, (pick, *shares)), *groups)

time: 39 us -> 38.9 us (level)
  Pallas kernels: 24.2 us -> 22.9 us
  waiting for transfers between devices: 2.03 us -> 3.28 us
    pallas_call x2, Pallas kernels: 3.8 us -> 2.51 us  [shards(): pl.pallas_call(functools.partial(attend_cache, rows_at=at), in_specs=[RES...]
    ppermute x7, waiting for transfers between devices: 2.03 us -> 3.28 us  [swapped(): return in_vmem(lax.ppermute(blocks, 'section', pairs))]
    pallas_call x1, Pallas kernels: 4.84 us -> 5.62 us  [shards(): pl.pallas_call(project_rest, in_specs=[REMAINS] * 4 + [RESIDENT] * 3 + [R...]
    pallas_call x1, Pallas kernels: 1.02 us -> 0.31 us  [shards(): pl.pallas_call(functools.partial(prepare_arrived, row_count=row_count), i...]
  transfers between devices with their start and end apart: 8 -> 8, of which waited for: 2 -> 2; matrix products, arithmetic and copies ran while one was open for 0% -> 0% of each run, Pallas kernels for 52% -> 49%
where the time goes in v17:
time: 38.9 us; the launch traced here: 38.7 us
  Pallas kernels  22.9 us (59%)
  starting transfers between devices  12.4 us (32%)
  waiting for transfers between devices  3.28 us (8%)
    ppermute x7, starting transfers between devices, swapped(): return in_vmem(lax.ppermute(blocks, 'section', pairs))  12.4 us
    pallas_call x1, Pallas kernels, shards(): pl.pallas_call(functools.partial(project_mine, at=at, last=last), in_spec...  6.09 us
    pallas_call x1, Pallas kernels, shards(): pl.pallas_call(project_rest, in_specs=[REMAINS] * 4 + [RESIDENT] * 3 + [R...  5.62 us
    pallas_call x1, Pallas kernels, shards(): pl.pallas_call(functools.partial(project_first, edges=edges), in_specs=[R...  4.57 us
    ppermute x7, waiting for transfers between devices, swapped(): return in_vmem(lax.ppermute(blocks, 'section', pairs))  3.28 us
    pallas_call x2, Pallas kernels, shards(): pl.pallas_call(functools.partial(attend_cache, rows_at=at), in_specs=[RES...  2.51 us
    pallas_call x1, Pallas kernels, shards(): pl.pallas_call(select_queries, in_specs=[RESIDENT, RESIDENT], out_specs=[...  1.55 us
    pallas_call x1, Pallas kernels, shards(): pl.pallas_call(merge, in_specs=[RESIDENT] * (5 + len(shares)), out_specs=...  1.3 us
  transfers between devices with their start and end apart: 8, of which 2 were waited for; matrix products, arithmetic and copies ran while one was open for 0% of the time, Pallas kernels for 49%

profile of v17, /device:TPU:0, one launch (start us, length us, event | category | flops | bytes accessed | tf_op | source)
XLA Modules:
  0.0 38.7 jit_solution(3527625378283428062)
XLA Ops:
  0.0 1.6 %select_queries.1 = (bf16[16,128]{1,0:T(8,128)(2,1)S(1)}, bf16[4,2,3072]{2,1,0:T(2,128)(2,1)S(1)}, bf16[4,2,3072]{2,1,0:T(2,128)(2,1)S(1)}) custom-call(s32[8,12]{1,0:T(8,128)} %target_ref.3, bf16[128,3072]{1,0:T(8,128)(2,1)} %refs_1_.1), custom_call_target="tpu_custom_call" | custom-call | tf_op jit(solution)/shard_map/select_queries/pallas_call | solution.py:572
  1.6 4.1 %collective-permute-start = (bf16[4,2,3072]{2,1,0:T(2,128)(2,1)S(1)}, bf16[4,2,3072]{2,1,0:T(2,128)(2,1)S(1)}, u32[]{:S(2)}, u32[]{:S(2)}) collective-permute-start(bf16[4,2,3072]{2,1,0:T(2,128)(2,1)S(1)} %get-tuple-element.46), channel_id=1, source_target_pairs={{0,8},{2,10},{4,12},{6,14},{8,0},{10,2},{12,4},{14,6},{1,9},{3,11}... | collective-permute-start | bytes 147464 | tf_op jit(solution)/shard_map/ppermute | solution.py:570
  5.7 4.6 %project_first.1 = (bf16[896,4096]{1,0:T(8,128)(2,1)S(1)}, bf16[1536,512]{1,0:T(8,128)(2,1)S(1)}, f32[896,512]{1,0:T(8,128)S(1)}, s32[8,12]{1,0:T(8,128)S(1)}, s...) custom-call(bf16[768,6144]{1,0:T(8,128)(2,1)} %prompts_ref.3, bf16[128,6144]{1,0:T(8,128)(2,1)} %hidden_ref.3, ...), custom_call_target="tpu_custom_call" | custom-call | tf_op jit(solution)/shard_map/project_first/pallas_call | solution.py:594
  10.2 0.0 collective-permute-done.got_ref
  10.3 1.6 %collective-permute-start.1 = (bf16[4,2,3072]{2,1,0:T(2,128)(2,1)S(1)}, bf16[4,2,3072]{2,1,0:T(2,128)(2,1)S(1)}, u32[]{:S(2)}, u32[]{:S(2)}) collective-permute-start(bf16[4,2,3072]{2,1,0:T(2,128)(2,1)S(1)} %get-tuple-element.51), channel_id=1, source_target_pairs={{0,4},{2,6},{4,0},{6,2},{8,12},{10,14},{12,8},{14,10},{1,5},{3,7},... | collective-permute-start | bytes 147464 | tf_op jit(solution)/shard_map/ppermute | solution.py:570
  11.9 5.6 %project_rest.1 = (bf16[896,512]{1,0:T(8,128)(2,1)S(1)}, bf16[896,2048]{1,0:T(8,128)(2,1)S(1)}, bf16[6144,512]{1,0:T(8,128)(2,1)S(1)}) custom-call(bf16[768,6144]{1,0:T(8,128)(2,1)} %prompts_ref.3, bf16[128,6144]{1,0:T(8,128)(2,1)} %hidden_ref.3, bf16[6144,1024]{1,0:T(8,128)(2,1)} %w_ref.3, f32[1,1024]{1,0:T(1,128)} %bitcast.2, ...), custom_call_target="tpu_custom_call" | custom-call | tf_op jit(solution)/shard_map/project_rest/pallas_call | solution.py:616
  17.5 0.0 collective-permute-done.1.got_ref
  17.6 0.1 collective-permute-start.2
  17.6 1.6 %collective-permute-start.3 = (bf16[4,2,3072]{2,1,0:T(2,128)(2,1)S(1)}, bf16[4,2,3072]{2,1,0:T(2,128)(2,1)S(1)}, u32[]{:S(2)}, u32[]{:S(2)}) collective-permute-start(bf16[4,2,3072]{2,1,0:T(2,128)(2,1)S(1)} %get-tuple-element.61), channel_id=1, source_target_pairs={{0,2},{2,0},{4,6},{6,4},{8,10},{10,8},{12,14},{14,12},{1,3},{3,1},... | collective-permute-start | bytes 147464 | tf_op jit(solution)/shard_map/ppermute | solution.py:570
  19.2 6.1 %project_mine.1 = (bf16[896,512]{1,0:T(8,128)(2,1)S(1)}, bf16[128,32,512]{2,1,0:T(8,128)(2,1)S(1)}, bf16[128,3072]{1,0:T(8,128)(2,1)S(1)}) custom-call(bf16[896,4096]{1,0:T(8,128)(2,1)S(1)} %get-tuple-element.42.rows_ref, bf16[896,2048]{1,0:T(8,128)(2,1)S(1)} %get-tuple-element.48.rows_rest_ref, bf16[6144,512]{1,0:T(8,128)(2,1)S(1)} %get-tuple-element.49.w_mine_ref, ...), custom_call_target="tpu_custom_call" | custom-call | tf_op jit(solution)/shard_map/project_mine/pallas_call | solution.py:648
  25.3 0.0 collective-permute-done.3.got_ref
  25.3 0.3 prepare_arrived.1
  25.7 0.0 collective-permute-done.2.other_ref
  25.7 0.9 %attend_arrived.1 = (bf16[4,2,3200]{2,1,0:T(2,128)(2,1)S(1)}, bf16[4,2,3200]{2,1,0:T(2,128)(2,1)S(1)}) custom-call(bf16[16,3072]{1,0:T(8,128)(2,1)S(1)} %get-tuple-element.62.rows_ref, bf16[16,64]{1,0:T(8,128)(2,1)S(1)} %get-tuple-element.63.slot_of_ref, f32[16,768]{1,0:T(8,128)S(1)} %get-tuple-element.64.bias_ref, ...), custom_call_target="tpu_custom_call" | custom-call | tf_op jit(solution)/shard_map/attend_arrived/pallas_call | solution.py:676
  26.6 0.6 %collective-permute-start.4 = (bf16[4,2,3200]{2,1,0:T(2,128)(2,1)S(1)}, bf16[4,2,3200]{2,1,0:T(2,128)(2,1)S(1)}, u32[]{:S(2)}, u32[]{:S(2)}) collective-permute-start(bf16[4,2,3200]{2,1,0:T(2,128)(2,1)S(1)} %get-tuple-element.69), channel_id=1, source_target_pairs={{0,2},{2,0},{4,6},{6,4},{8,10},{10,8},{12,14},{14,12},{1,3},{3,1},... | collective-permute-start | bytes 153608 | tf_op jit(solution)/shard_map/ppermute | solution.py:570
  27.1 1.3 %attend_cache.2 = (bf16[64,3072]{1,0:T(8,128)(2,1)S(1)}, f32[16,3072]{1,0:T(8,128)S(1)}, f32[16,128]{1,0:T(8,128)S(1)}) custom-call(bf16[128,3072]{1,0:T(8,128)(2,1)S(1)} %get-tuple-element.55.queries_ref, bf16[128,32,512]{2,1,0:T(8,128)(2,1)S(1)} %get-tuple-element.56.cache_ref, s32[1,128]{1,0:T(1,128)S(1)} %get-tuple-element.57.len_ref, ...), custom_call_target="tpu_custom_call" | custom-call | tf_op jit(solution)/shard_map/attend_cache/pallas_call | solution.py:693
  28.4 2.3 %collective-permute-done.4.got_ref = bf16[4,2,3200]{2,1,0:T(2,128)(2,1)S(1)} collective-permute-done((bf16[4,2,3200]{2,1,0:T(2,128)(2,1)S(1)}, bf16[4,2,3200]{2,1,0:T(2,128)(2,1)S(1)}, u32[]{:S(2)}, u32[]{:S(2)}) %collective-permute-start.4) | collective-permute-done | bytes 51232 | tf_op jit(solution)/shard_map/ppermute | solution.py:570
  30.8 0.5 %collective-permute-start.5 = (bf16[2,2,3200]{2,1,0:T(2,128)(2,1)S(1)}, bf16[2,2,3200]{2,1,0:T(2,128)(2,1)S(1)}, u32[]{:S(2)}, u32[]{:S(2)}) collective-permute-start(bf16[2,2,3200]{2,1,0:T(2,128)(2,1)S(1)} %get-tuple-element.74), channel_id=1, source_target_pairs={{0,4},{2,6},{4,0},{6,2},{8,12},{10,14},{12,8},{14,10},{1,5},{3,7},... | collective-permute-start | bytes 76808 | tf_op jit(solution)/shard_map/ppermute | solution.py:570
  31.3 0.4 %collective-permute-start.6 = (bf16[2,2,3200]{2,1,0:T(2,128)(2,1)S(1)}, bf16[2,2,3200]{2,1,0:T(2,128)(2,1)S(1)}, u32[]{:S(2)}, u32[]{:S(2)}) collective-permute-start(bf16[2,2,3200]{2,1,0:T(2,128)(2,1)S(1)} %get-tuple-element.75), channel_id=1, source_target_pairs={{0,8},{2,10},{4,12},{6,14},{8,0},{10,2},{12,4},{14,6},{1,9},{3,11}... | collective-permute-start | bytes 76808 | tf_op jit(solution)/shard_map/ppermute | solution.py:570
  31.7 3.5 %collective-permute-start.7 = (bf16[2,2,3200]{2,1,0:T(2,128)(2,1)S(1)}, bf16[2,2,3200]{2,1,0:T(2,128)(2,1)S(1)}, u32[]{:S(2)}, u32[]{:S(2)}) collective-permute-start(bf16[2,2,3200]{2,1,0:T(2,128)(2,1)S(1)} %get-tuple-element.76), channel_id=1, source_target_pairs={{0,12},{2,14},{4,8},{6,10},{8,4},{10,6},{12,0},{14,2},{1,13},{3,15... | collective-permute-start | bytes 76808 | tf_op jit(solution)/shard_map/ppermute | solution.py:570
  35.2 1.3 %attend_cache.3 = (bf16[64,3072]{1,0:T(8,128)(2,1)S(1)}, f32[16,3072]{1,0:T(8,128)S(1)}, f32[16,128]{1,0:T(8,128)S(1)}) custom-call(bf16[128,3072]{1,0:T(8,128)(2,1)S(1)} %get-tuple-element.55.queries_ref, bf16[128,32,512]{2,1,0:T(8,128)(2,1)S(1)} %get-tuple-element.56.cache_ref, s32[1,128]{1,0:T(1,128)S(1)} %get-tuple-element.57.len_ref, ...), custom_call_target="tpu_custom_call" | custom-call | tf_op jit(solution)/shard_map/attend_cache/pallas_call | solution.py:693
  36.5 0.0 collective-permute-done.6.refs_8_
  36.5 0.9 %collective-permute-done.7.refs_9_ = bf16[2,2,3200]{2,1,0:T(2,128)(2,1)S(1)} collective-permute-done((bf16[2,2,3200]{2,1,0:T(2,128)(2,1)S(1)}, bf16[2,2,3200]{2,1,0:T(2,128)(2,1)S(1)}, u32[]{:S(2)}, u32[]{:S(2)}) %collective-permute-start.7) | collective-permute-done | bytes 25632 | tf_op jit(solution)/shard_map/ppermute | solution.py:570
  37.4 1.3 %merge.1 = bf16[128,3072]{1,0:T(8,128)(2,1)} custom-call(bf16[16,128]{1,0:T(8,128)(2,1)S(1)} %get-tuple-element.41.pick_ref, bf16[64,3072]{1,0:T(8,128)(2,1)S(1)} %get-tuple-element.66.refs_0_, f32[16,3072]{1,0:T(8,128)S(1)} %get-tuple-element.67.refs_1_, f32[16,128]{1,0:T(8,128)S(1)} %get-tuple-element.68.after_ref.refs_2_, ...), custom_call_target="tpu_custom_call" | custom-call | tf_op jit(solution)/shard_map/merge/pallas_call | solution.py:721
  (4 shorter events, 0.0 us)
Async XLA Ops:
  1.6 8.7 %collective-permute-start = (bf16[4,2,3072]{2,1,0:T(2,128)(2,1)S(1)}, bf16[4,2,3072]{2,1,0:T(2,128)(2,1)S(1)}, u32[]{:S(2)}, u32[]{:S(2)}) collective-permute-start(bf16[4,2,3072]{2,1,0:T(2,128)(2,1)S(1)} %get-tuple-element.46), channel_id=1, source_target_pairs={{0,8},{2,10},{4,12},{6,14},{8,0},{10,2},{12,4},{14,6},{1,9},{3,11}... | collective-permute-start | bytes 147464 | tf_op jit(solution)/shard_map/ppermute | solution.py:570
  10.3 7.3 %collective-permute-start.1 = (bf16[4,2,3072]{2,1,0:T(2,128)(2,1)S(1)}, bf16[4,2,3072]{2,1,0:T(2,128)(2,1)S(1)}, u32[]{:S(2)}, u32[]{:S(2)}) collective-permute-start(bf16[4,2,3072]{2,1,0:T(2,128)(2,1)S(1)} %get-tuple-element.51), channel_id=1, source_target_pairs={{0,4},{2,6},{4,0},{6,2},{8,12},{10,14},{12,8},{14,10},{1,5},{3,7},... | collective-permute-start | bytes 147464 | tf_op jit(solution)/shard_map/ppermute | solution.py:570
  17.6 8.1 %collective-permute-start.2 = (bf16[896,512]{1,0:T(8,128)(2,1)S(1)}, bf16[896,512]{1,0:T(8,128)(2,1)S(1)}, u32[]{:S(2)}, u32[]{:S(2)}) collective-permute-start(bf16[896,512]{1,0:T(8,128)(2,1)S(1)} %get-tuple-element.53.after_ref), channel_id=1, source_target_pairs={{0,1},{1,0},{2,3},{3,2},{4,5},{5,4},{6,7},{7,6},{8,9},{9,8},{10,11... | collective-permute-start | bytes 2752520 | tf_op jit(solution)/shard_map/ppermute | solution.py:636
  17.6 7.7 %collective-permute-start.3 = (bf16[4,2,3072]{2,1,0:T(2,128)(2,1)S(1)}, bf16[4,2,3072]{2,1,0:T(2,128)(2,1)S(1)}, u32[]{:S(2)}, u32[]{:S(2)}) collective-permute-start(bf16[4,2,3072]{2,1,0:T(2,128)(2,1)S(1)} %get-tuple-element.61), channel_id=1, source_target_pairs={{0,2},{2,0},{4,6},{6,4},{8,10},{10,8},{12,14},{14,12},{1,3},{3,1},... | collective-permute-start | bytes 147464 | tf_op jit(solution)/shard_map/ppermute | solution.py:570
  26.6 4.2 %collective-permute-start.4 = (bf16[4,2,3200]{2,1,0:T(2,128)(2,1)S(1)}, bf16[4,2,3200]{2,1,0:T(2,128)(2,1)S(1)}, u32[]{:S(2)}, u32[]{:S(2)}) collective-permute-start(bf16[4,2,3200]{2,1,0:T(2,128)(2,1)S(1)} %get-tuple-element.69), channel_id=1, source_target_pairs={{0,2},{2,0},{4,6},{6,4},{8,10},{10,8},{12,14},{14,12},{1,3},{3,1},... | collective-permute-start | bytes 153608 | tf_op jit(solution)/shard_map/ppermute | solution.py:570
  30.8 5.7 %collective-permute-start.5 = (bf16[2,2,3200]{2,1,0:T(2,128)(2,1)S(1)}, bf16[2,2,3200]{2,1,0:T(2,128)(2,1)S(1)}, u32[]{:S(2)}, u32[]{:S(2)}) collective-permute-start(bf16[2,2,3200]{2,1,0:T(2,128)(2,1)S(1)} %get-tuple-element.74), channel_id=1, source_target_pairs={{0,4},{2,6},{4,0},{6,2},{8,12},{10,14},{12,8},{14,10},{1,5},{3,7},... | collective-permute-start | bytes 76808 | tf_op jit(solution)/shard_map/ppermute | solution.py:570
  31.3 5.2 %collective-permute-start.6 = (bf16[2,2,3200]{2,1,0:T(2,128)(2,1)S(1)}, bf16[2,2,3200]{2,1,0:T(2,128)(2,1)S(1)}, u32[]{:S(2)}, u32[]{:S(2)}) collective-permute-start(bf16[2,2,3200]{2,1,0:T(2,128)(2,1)S(1)} %get-tuple-element.75), channel_id=1, source_target_pairs={{0,8},{2,10},{4,12},{6,14},{8,0},{10,2},{12,4},{14,6},{1,9},{3,11}... | collective-permute-start | bytes 76808 | tf_op jit(solution)/shard_map/ppermute | solution.py:570
  31.7 5.7 %collective-permute-start.7 = (bf16[2,2,3200]{2,1,0:T(2,128)(2,1)S(1)}, bf16[2,2,3200]{2,1,0:T(2,128)(2,1)S(1)}, u32[]{:S(2)}, u32[]{:S(2)}) collective-permute-start(bf16[2,2,3200]{2,1,0:T(2,128)(2,1)S(1)} %get-tuple-element.76), channel_id=1, source_target_pairs={{0,12},{2,14},{4,8},{6,10},{8,4},{10,6},{12,0},{14,2},{1,13},{3,15... | collective-permute-start | bytes 76808 | tf_op jit(solution)/shard_map/ppermute | solution.py:570

commit v18 on v17

--- a/solution.py
+++ b/solution.py
@@ -61,13 +61,7 @@
 
 
 def answer_steps_of(sections):
-    steps = []
-    bit = 1
-    while 4 * bit < sections:
-        sent = [k for k in range(sections) if k & bit]
-        steps.append((bit, sent, [k for k in range(sections) if not k & bit]))
-        bit *= 2
-    return steps
+    return steps_of(sections)[:-2]
 
 
 def rearrange(step, kept_ref, got_ref, *out):
@@ -85,8 +79,7 @@
 
 
 def fan_out(kept_ref, got_ref, after_ref, *out_refs, step):
-    size = out_refs[0].shape[0]
-    groups = [range(m * size, (m + 1) * size) for m in range(len(out_refs))]
+    groups = [range(m, 4 * out_refs[m].shape[0], 4) for m in range(len(out_refs))]
     rearrange(step, kept_ref, got_ref, *zip(out_refs, groups))
 
 
@@ -187,13 +180,12 @@
     scale_ref,
     rows_ref,
     w_tail_ref,
-    total_in_ref,
+    total_ref,
     after_ref,
     theirs_ref,
     rows_rest_ref,
     w_mine_ref,
     w_rest_ref,
-    total_ref,
     scale_here_ref,
     sems,
 ):
@@ -202,37 +194,22 @@
     depth = rows_ref.shape[1]
     head = depth - w_tail_ref.shape[0]
     rest = slice(depth, depth + rows_rest_ref.shape[1])
-    size = rest.stop - rest.start
-    chunks = spans((0, size // 2, size))
-    waits = []
-    for c, at in enumerate(chunks):
-        there = slice(depth + at.start, depth + at.stop)
-        copies = load_rows(prompts_ref, hidden_ref, there, rows_rest_ref, at, sems.at[c])
-        copies.append(
-            pltpu.make_async_copy(w_ref.at[there, theirs], w_rest_ref.at[at, :], sems.at[c, 2])
-        )
-        for copy in copies:
-            copy.start()
-        waits.append(copies)
-    later = [
-        pltpu.make_async_copy(scale_ref.at[:, theirs], scale_here_ref, sems.at[2, 0]),
-        pltpu.make_async_copy(w_ref.at[:, mine], w_mine_ref, sems.at[2, 1]),
+    copies = load_rows(prompts_ref, hidden_ref, rest, rows_rest_ref, slice(None), sems)
+    copies += [
+        pltpu.make_async_copy(w_ref.at[rest, theirs], w_rest_ref, sems.at[2]),
+        pltpu.make_async_copy(scale_ref.at[:, theirs], scale_here_ref, sems.at[3]),
+        pltpu.make_async_copy(w_ref.at[:, mine], w_mine_ref, sems.at[4]),
     ]
-    for copy in later:
+    for copy in copies:
         copy.start()
-    total_ref[...] = total_in_ref[...] + jnp.dot(
+    total = total_ref[...] + jnp.dot(
         rows_ref[:, head:], w_tail_ref[...], preferred_element_type=F32
     )
-    for c, at in enumerate(chunks):
-        for copy in waits[c]:
-            copy.wait()
-        part = jnp.dot(rows_rest_ref[:, at], w_rest_ref[at, :], preferred_element_type=F32)
-        if c < len(chunks) - 1:
-            total_ref[...] += part
-        else:
-            later[0].wait()
-            theirs_ref[...] = ((total_ref[...] + part) * scale_here_ref[...]).astype(BF16)
-    later[1].wait()
+    for copy in copies[:-1]:
+        copy.wait()
+    total += jnp.dot(rows_rest_ref[...], w_rest_ref[...], preferred_element_type=F32)
+    theirs_ref[...] = (total * scale_here_ref[...]).astype(BF16)
+    copies[-1].wait()
 
 
 def project_mine(rows_ref, rows_rest_ref, w_mine_ref, scale_ref, after_ref, *refs, at, last):
@@ -480,7 +457,7 @@
     width = out_ref.shape[1]
     pick = pick_ref[...]
     arrived = jnp.concatenate(
-        [ref[i].astype(F32) for ref in group_refs for i in range(ref.shape[0])], axis=0
+        [ref[i].astype(F32) for i in range(group_refs[0].shape[0]) for ref in group_refs], axis=0
     )
     stats = arrived[:, width:]
     arrived_lse = (
@@ -624,9 +601,8 @@
         ],
         scratch_shapes=[
             pltpu.VMEM((features - depth, local_width), BF16),
-            pltpu.VMEM((all_rows, local_width), F32),
             pltpu.VMEM((1, local_width), F32),
-            pltpu.SemaphoreType.DMA((3, 3)),
+            pltpu.SemaphoreType.DMA((5,)),
         ],
         compiler_params=compiler_params(16),
         name="project_rest",
@@ -716,7 +692,7 @@
                 name="fan_out",
             )(in_vmem(keep), got, in_vmem(share[2]))
             groups = [in_vmem(keep)]
-            groups += [swapped(blocks, (i + 1) * size) for i, blocks in enumerate(sent)]
+            groups += [swapped(blocks, i + 1) for i, blocks in enumerate(sent)]
 
     return pl.pallas_call(
         merge,

time: 38.9 us -> 38.8 us (level)
  waiting for transfers between devices: 3.28 us -> 4.54 us
  Pallas kernels: 22.9 us -> 22.1 us
  starting transfers between devices: 12.4 us -> 11.8 us
    ppermute x7, waiting for transfers between devices: 3.28 us -> 4.54 us  [swapped(): return in_vmem(lax.ppermute(blocks, 'section', pairs))]
    pallas_call x1, Pallas kernels: 5.62 us -> 4.84 us  [shards(): pl.pallas_call(project_rest, in_specs=[REMAINS] * 4 + [RESIDENT] * 3 + [R...]
    ppermute x7, starting transfers between devices: 12.4 us -> 11.8 us  [swapped(): return in_vmem(lax.ppermute(blocks, 'section', pairs))]
  transfers between devices with their start and end apart: 8 -> 8, of which waited for: 2 -> 2; matrix products, arithmetic and copies ran while one was open for 0% -> 0% of each run, Pallas kernels for 49% -> 47%
where the time goes in v18:
time: 38.8 us; the launch traced here: 38.6 us
  Pallas kernels  22.1 us (57%)
  starting transfers between devices  11.8 us (30%)
  waiting for transfers between devices  4.54 us (12%)
    ppermute x7, starting transfers between devices, swapped(): return in_vmem(lax.ppermute(blocks, 'section', pairs))  11.8 us
    pallas_call x1, Pallas kernels, shards(): pl.pallas_call(functools.partial(project_mine, at=at, last=last), in_spec...  6.09 us
    pallas_call x1, Pallas kernels, shards(): pl.pallas_call(project_rest, in_specs=[REMAINS] * 4 + [RESIDENT] * 3 + [R...  4.84 us
    pallas_call x1, Pallas kernels, shards(): pl.pallas_call(functools.partial(project_first, edges=edges), in_specs=[R...  4.57 us
    ppermute x7, waiting for transfers between devices, swapped(): return in_vmem(lax.ppermute(blocks, 'section', pairs))  4.54 us
    pallas_call x2, Pallas kernels, shards(): pl.pallas_call(functools.partial(attend_cache, rows_at=at), in_specs=[RES...  2.5 us
    pallas_call x1, Pallas kernels, shards(): pl.pallas_call(select_queries, in_specs=[RESIDENT, RESIDENT], out_specs=[...  1.55 us
    pallas_call x1, Pallas kernels, shards(): pl.pallas_call(merge, in_specs=[RESIDENT] * (5 + len(shares)), out_specs=...  1.29 us
  transfers between devices with their start and end apart: 8, of which 2 were waited for; matrix products, arithmetic and copies ran while one was open for 0% of the time, Pallas kernels for 47%

profile of v18, /device:TPU:0, one launch (start us, length us, event | category | flops | bytes accessed | tf_op | source)
XLA Modules:
  0.0 38.6 jit_solution(16382697880306452980)
XLA Ops:
  0.0 1.6 %select_queries.1 = (bf16[16,128]{1,0:T(8,128)(2,1)S(1)}, bf16[4,2,3072]{2,1,0:T(2,128)(2,1)S(1)}, bf16[4,2,3072]{2,1,0:T(2,128)(2,1)S(1)}) custom-call(s32[8,12]{1,0:T(8,128)} %target_ref.3, bf16[128,3072]{1,0:T(8,128)(2,1)} %refs_1_.1), custom_call_target="tpu_custom_call" | custom-call | tf_op jit(solution)/shard_map/select_queries/pallas_call | solution.py:549
  1.6 4.1 %collective-permute-start = (bf16[4,2,3072]{2,1,0:T(2,128)(2,1)S(1)}, bf16[4,2,3072]{2,1,0:T(2,128)(2,1)S(1)}, u32[]{:S(2)}, u32[]{:S(2)}) collective-permute-start(bf16[4,2,3072]{2,1,0:T(2,128)(2,1)S(1)} %get-tuple-element.46), channel_id=1, source_target_pairs={{0,8},{2,10},{4,12},{6,14},{8,0},{10,2},{12,4},{14,6},{1,9},{3,11}... | collective-permute-start | bytes 147464 | tf_op jit(solution)/shard_map/ppermute | solution.py:547
  5.7 4.6 %project_first.1 = (bf16[896,4096]{1,0:T(8,128)(2,1)S(1)}, bf16[1536,512]{1,0:T(8,128)(2,1)S(1)}, f32[896,512]{1,0:T(8,128)S(1)}, s32[8,12]{1,0:T(8,128)S(1)}, s...) custom-call(bf16[768,6144]{1,0:T(8,128)(2,1)} %prompts_ref.3, bf16[128,6144]{1,0:T(8,128)(2,1)} %hidden_ref.3, ...), custom_call_target="tpu_custom_call" | custom-call | tf_op jit(solution)/shard_map/project_first/pallas_call | solution.py:571
  10.2 0.0 collective-permute-done.got_ref
  10.3 1.6 %collective-permute-start.1 = (bf16[4,2,3072]{2,1,0:T(2,128)(2,1)S(1)}, bf16[4,2,3072]{2,1,0:T(2,128)(2,1)S(1)}, u32[]{:S(2)}, u32[]{:S(2)}) collective-permute-start(bf16[4,2,3072]{2,1,0:T(2,128)(2,1)S(1)} %get-tuple-element.51), channel_id=1, source_target_pairs={{0,4},{2,6},{4,0},{6,2},{8,12},{10,14},{12,8},{14,10},{1,5},{3,7},... | collective-permute-start | bytes 147464 | tf_op jit(solution)/shard_map/ppermute | solution.py:547
  11.9 4.8 %project_rest.1 = (bf16[896,512]{1,0:T(8,128)(2,1)S(1)}, bf16[896,2048]{1,0:T(8,128)(2,1)S(1)}, bf16[6144,512]{1,0:T(8,128)(2,1)S(1)}) custom-call(bf16[768,6144]{1,0:T(8,128)(2,1)} %prompts_ref.3, bf16[128,6144]{1,0:T(8,128)(2,1)} %hidden_ref.3, bf16[6144,1024]{1,0:T(8,128)(2,1)} %w_ref.3, f32[1,1024]{1,0:T(1,128)} %bitcast.2, ...), custom_call_target="tpu_custom_call" | custom-call | tf_op jit(solution)/shard_map/project_rest/pallas_call | solution.py:593
  16.8 0.0 collective-permute-done.1.got_ref
  16.8 0.1 collective-permute-start.2
  16.9 1.6 %collective-permute-start.3 = (bf16[4,2,3072]{2,1,0:T(2,128)(2,1)S(1)}, bf16[4,2,3072]{2,1,0:T(2,128)(2,1)S(1)}, u32[]{:S(2)}, u32[]{:S(2)}) collective-permute-start(bf16[4,2,3072]{2,1,0:T(2,128)(2,1)S(1)} %get-tuple-element.61), channel_id=1, source_target_pairs={{0,2},{2,0},{4,6},{6,4},{8,10},{10,8},{12,14},{14,12},{1,3},{3,1},... | collective-permute-start | bytes 147464 | tf_op jit(solution)/shard_map/ppermute | solution.py:547
  18.5 6.1 %project_mine.1 = (bf16[896,512]{1,0:T(8,128)(2,1)S(1)}, bf16[128,32,512]{2,1,0:T(8,128)(2,1)S(1)}, bf16[128,3072]{1,0:T(8,128)(2,1)S(1)}) custom-call(bf16[896,4096]{1,0:T(8,128)(2,1)S(1)} %get-tuple-element.42.rows_ref, bf16[896,2048]{1,0:T(8,128)(2,1)S(1)} %get-tuple-element.48.rows_rest_ref, bf16[6144,512]{1,0:T(8,128)(2,1)S(1)} %get-tuple-element.49.w_mine_ref, ...), custom_call_target="tpu_custom_call" | custom-call | tf_op jit(solution)/shard_map/project_mine/pallas_call | solution.py:624
  24.6 0.0 collective-permute-done.3.got_ref
  24.6 0.3 prepare_arrived.1
  24.9 0.0 collective-permute-done.2.other_ref
  24.9 0.9 %attend_arrived.1 = (bf16[4,2,3200]{2,1,0:T(2,128)(2,1)S(1)}, bf16[4,2,3200]{2,1,0:T(2,128)(2,1)S(1)}) custom-call(bf16[16,3072]{1,0:T(8,128)(2,1)S(1)} %get-tuple-element.62.rows_ref, bf16[16,64]{1,0:T(8,128)(2,1)S(1)} %get-tuple-element.63.slot_of_ref, f32[16,768]{1,0:T(8,128)S(1)} %get-tuple-element.64.bias_ref, ...), custom_call_target="tpu_custom_call" | custom-call | tf_op jit(solution)/shard_map/attend_arrived/pallas_call | solution.py:652
  25.8 0.9 %collective-permute-start.4 = (bf16[4,2,3200]{2,1,0:T(2,128)(2,1)S(1)}, bf16[4,2,3200]{2,1,0:T(2,128)(2,1)S(1)}, u32[]{:S(2)}, u32[]{:S(2)}) collective-permute-start(bf16[4,2,3200]{2,1,0:T(2,128)(2,1)S(1)} %get-tuple-element.69), channel_id=1, source_target_pairs={{0,8},{2,10},{4,12},{6,14},{8,0},{10,2},{12,4},{14,6},{1,9},{3,11}... | collective-permute-start | bytes 153608 | tf_op jit(solution)/shard_map/ppermute | solution.py:547
  26.7 1.3 %attend_cache.2 = (bf16[64,3072]{1,0:T(8,128)(2,1)S(1)}, f32[16,3072]{1,0:T(8,128)S(1)}, f32[16,128]{1,0:T(8,128)S(1)}) custom-call(bf16[128,3072]{1,0:T(8,128)(2,1)S(1)} %get-tuple-element.55.queries_ref, bf16[128,32,512]{2,1,0:T(8,128)(2,1)S(1)} %get-tuple-element.56.cache_ref, s32[1,128]{1,0:T(1,128)S(1)} %get-tuple-element.57.len_ref, ...), custom_call_target="tpu_custom_call" | custom-call | tf_op jit(solution)/shard_map/attend_cache/pallas_call | solution.py:669
  27.9 3.7 %collective-permute-done.4.got_ref = bf16[4,2,3200]{2,1,0:T(2,128)(2,1)S(1)} collective-permute-done((bf16[4,2,3200]{2,1,0:T(2,128)(2,1)S(1)}, bf16[4,2,3200]{2,1,0:T(2,128)(2,1)S(1)}, u32[]{:S(2)}, u32[]{:S(2)}) %collective-permute-start.4) | collective-permute-done | bytes 51232 | tf_op jit(solution)/shard_map/ppermute | solution.py:547
  31.6 0.6 %collective-permute-start.5 = (bf16[2,2,3200]{2,1,0:T(2,128)(2,1)S(1)}, bf16[2,2,3200]{2,1,0:T(2,128)(2,1)S(1)}, u32[]{:S(2)}, u32[]{:S(2)}) collective-permute-start(bf16[2,2,3200]{2,1,0:T(2,128)(2,1)S(1)} %get-tuple-element.74), channel_id=1, source_target_pairs={{0,2},{2,0},{4,6},{6,4},{8,10},{10,8},{12,14},{14,12},{1,3},{3,1},... | collective-permute-start | bytes 76808 | tf_op jit(solution)/shard_map/ppermute | solution.py:547
  32.2 0.0 collective-permute-start.6
  32.2 3.0 %collective-permute-start.7 = (bf16[2,2,3200]{2,1,0:T(2,128)(2,1)S(1)}, bf16[2,2,3200]{2,1,0:T(2,128)(2,1)S(1)}, u32[]{:S(2)}, u32[]{:S(2)}) collective-permute-start(bf16[2,2,3200]{2,1,0:T(2,128)(2,1)S(1)} %get-tuple-element.76), channel_id=1, source_target_pairs={{0,6},{2,4},{4,2},{6,0},{8,14},{10,12},{12,10},{14,8},{1,7},{3,5},... | collective-permute-start | bytes 76808 | tf_op jit(solution)/shard_map/ppermute | solution.py:547
  35.2 1.2 %attend_cache.3 = (bf16[64,3072]{1,0:T(8,128)(2,1)S(1)}, f32[16,3072]{1,0:T(8,128)S(1)}, f32[16,128]{1,0:T(8,128)S(1)}) custom-call(bf16[128,3072]{1,0:T(8,128)(2,1)S(1)} %get-tuple-element.55.queries_ref, bf16[128,32,512]{2,1,0:T(8,128)(2,1)S(1)} %get-tuple-element.56.cache_ref, s32[1,128]{1,0:T(1,128)S(1)} %get-tuple-element.57.len_ref, ...), custom_call_target="tpu_custom_call" | custom-call | tf_op jit(solution)/shard_map/attend_cache/pallas_call | solution.py:669
  36.4 0.0 collective-permute-done.6.refs_8_
  36.4 0.8 %collective-permute-done.7.refs_9_ = bf16[2,2,3200]{2,1,0:T(2,128)(2,1)S(1)} collective-permute-done((bf16[2,2,3200]{2,1,0:T(2,128)(2,1)S(1)}, bf16[2,2,3200]{2,1,0:T(2,128)(2,1)S(1)}, u32[]{:S(2)}, u32[]{:S(2)}) %collective-permute-start.7) | collective-permute-done | bytes 25632 | tf_op jit(solution)/shard_map/ppermute | solution.py:547
  37.3 1.3 %merge.1 = bf16[128,3072]{1,0:T(8,128)(2,1)} custom-call(bf16[16,128]{1,0:T(8,128)(2,1)S(1)} %get-tuple-element.41.pick_ref, bf16[64,3072]{1,0:T(8,128)(2,1)S(1)} %get-tuple-element.66.refs_0_, f32[16,3072]{1,0:T(8,128)S(1)} %get-tuple-element.67.refs_1_, f32[16,128]{1,0:T(8,128)S(1)} %get-tuple-element.68.after_ref.refs_2_, ...), custom_call_target="tpu_custom_call" | custom-call | tf_op jit(solution)/shard_map/merge/pallas_call | solution.py:697
  (4 shorter events, 0.0 us)
Async XLA Ops:
  1.6 8.7 %collective-permute-start = (bf16[4,2,3072]{2,1,0:T(2,128)(2,1)S(1)}, bf16[4,2,3072]{2,1,0:T(2,128)(2,1)S(1)}, u32[]{:S(2)}, u32[]{:S(2)}) collective-permute-start(bf16[4,2,3072]{2,1,0:T(2,128)(2,1)S(1)} %get-tuple-element.46), channel_id=1, source_target_pairs={{0,8},{2,10},{4,12},{6,14},{8,0},{10,2},{12,4},{14,6},{1,9},{3,11}... | collective-permute-start | bytes 147464 | tf_op jit(solution)/shard_map/ppermute | solution.py:547
  10.3 6.5 %collective-permute-start.1 = (bf16[4,2,3072]{2,1,0:T(2,128)(2,1)S(1)}, bf16[4,2,3072]{2,1,0:T(2,128)(2,1)S(1)}, u32[]{:S(2)}, u32[]{:S(2)}) collective-permute-start(bf16[4,2,3072]{2,1,0:T(2,128)(2,1)S(1)} %get-tuple-element.51), channel_id=1, source_target_pairs={{0,4},{2,6},{4,0},{6,2},{8,12},{10,14},{12,8},{14,10},{1,5},{3,7},... | collective-permute-start | bytes 147464 | tf_op jit(solution)/shard_map/ppermute | solution.py:547
  16.8 8.1 %collective-permute-start.2 = (bf16[896,512]{1,0:T(8,128)(2,1)S(1)}, bf16[896,512]{1,0:T(8,128)(2,1)S(1)}, u32[]{:S(2)}, u32[]{:S(2)}) collective-permute-start(bf16[896,512]{1,0:T(8,128)(2,1)S(1)} %get-tuple-element.53.after_ref), channel_id=1, source_target_pairs={{0,1},{1,0},{2,3},{3,2},{4,5},{5,4},{6,7},{7,6},{8,9},{9,8},{10,11... | collective-permute-start | bytes 2752520 | tf_op jit(solution)/shard_map/ppermute | solution.py:612
  16.9 7.7 %collective-permute-start.3 = (bf16[4,2,3072]{2,1,0:T(2,128)(2,1)S(1)}, bf16[4,2,3072]{2,1,0:T(2,128)(2,1)S(1)}, u32[]{:S(2)}, u32[]{:S(2)}) collective-permute-start(bf16[4,2,3072]{2,1,0:T(2,128)(2,1)S(1)} %get-tuple-element.61), channel_id=1, source_target_pairs={{0,2},{2,0},{4,6},{6,4},{8,10},{10,8},{12,14},{14,12},{1,3},{3,1},... | collective-permute-start | bytes 147464 | tf_op jit(solution)/shard_map/ppermute | solution.py:547
  25.8 5.8 %collective-permute-start.4 = (bf16[4,2,3200]{2,1,0:T(2,128)(2,1)S(1)}, bf16[4,2,3200]{2,1,0:T(2,128)(2,1)S(1)}, u32[]{:S(2)}, u32[]{:S(2)}) collective-permute-start(bf16[4,2,3200]{2,1,0:T(2,128)(2,1)S(1)} %get-tuple-element.69), channel_id=1, source_target_pairs={{0,8},{2,10},{4,12},{6,14},{8,0},{10,2},{12,4},{14,6},{1,9},{3,11}... | collective-permute-start | bytes 153608 | tf_op jit(solution)/shard_map/ppermute | solution.py:547
  31.6 4.8 %collective-permute-start.5 = (bf16[2,2,3200]{2,1,0:T(2,128)(2,1)S(1)}, bf16[2,2,3200]{2,1,0:T(2,128)(2,1)S(1)}, u32[]{:S(2)}, u32[]{:S(2)}) collective-permute-start(bf16[2,2,3200]{2,1,0:T(2,128)(2,1)S(1)} %get-tuple-element.74), channel_id=1, source_target_pairs={{0,2},{2,0},{4,6},{6,4},{8,10},{10,8},{12,14},{14,12},{1,3},{3,1},... | collective-permute-start | bytes 76808 | tf_op jit(solution)/shard_map/ppermute | solution.py:547
  32.2 4.2 %collective-permute-start.6 = (bf16[2,2,3200]{2,1,0:T(2,128)(2,1)S(1)}, bf16[2,2,3200]{2,1,0:T(2,128)(2,1)S(1)}, u32[]{:S(2)}, u32[]{:S(2)}) collective-permute-start(bf16[2,2,3200]{2,1,0:T(2,128)(2,1)S(1)} %get-tuple-element.75), channel_id=1, source_target_pairs={{0,4},{2,6},{4,0},{6,2},{8,12},{10,14},{12,8},{14,10},{1,5},{3,7},... | collective-permute-start | bytes 76808 | tf_op jit(solution)/shard_map/ppermute | solution.py:547
  32.2 5.1 %collective-permute-start.7 = (bf16[2,2,3200]{2,1,0:T(2,128)(2,1)S(1)}, bf16[2,2,3200]{2,1,0:T(2,128)(2,1)S(1)}, u32[]{:S(2)}, u32[]{:S(2)}) collective-permute-start(bf16[2,2,3200]{2,1,0:T(2,128)(2,1)S(1)} %get-tuple-element.76), channel_id=1, source_target_pairs={{0,6},{2,4},{4,2},{6,0},{8,14},{10,12},{12,10},{14,8},{1,7},{3,5},... | collective-permute-start | bytes 76808 | tf_op jit(solution)/shard_map/ppermute | solution.py:547

commit v19 on v18

--- a/solution.py
+++ b/solution.py
@@ -61,7 +61,13 @@
 
 
 def answer_steps_of(sections):
-    return steps_of(sections)[:-2]
+    steps = []
+    bit = 1
+    while 4 * bit < sections:
+        sent = [k for k in range(sections) if k & bit]
+        steps.append((bit, sent, [k for k in range(sections) if not k & bit]))
+        bit *= 2
+    return steps
 
 
 def rearrange(step, kept_ref, got_ref, *out):
@@ -79,7 +85,8 @@
 
 
 def fan_out(kept_ref, got_ref, after_ref, *out_refs, step):
-    groups = [range(m, 4 * out_refs[m].shape[0], 4) for m in range(len(out_refs))]
+    size = out_refs[0].shape[0]
+    groups = [range(m * size, (m + 1) * size) for m in range(len(out_refs))]
     rearrange(step, kept_ref, got_ref, *zip(out_refs, groups))
 
 
@@ -89,11 +96,16 @@
     return jnp.concatenate([where[k].astype(F32) for k in range(len(where))], axis=0)
 
 
-def select_queries(target_ref, queries_ref, pick_ref, keep_ref, send_ref):
+def select_queries(
+    target_ref, queries_ref, pick_ref, keep_ref, send_ref, queries_here_ref, sem
+):
+    copy = pltpu.make_async_copy(queries_ref, queries_here_ref, sem)
+    copy.start()
     _, sent, kept = steps_of(target_ref.shape[0])[0]
     pick = pick_rows(target_ref, queries_ref.shape[0])
     pick_ref[...] = pick
-    asked = jnp.dot(pick, queries_ref[...], preferred_element_type=F32)
+    copy.wait()
+    asked = jnp.dot(pick, queries_here_ref[...], preferred_element_type=F32)
     for ref, blocks in ((send_ref, sent), (keep_ref, kept)):
         for i, k in enumerate(blocks):
             ref[i] = asked[k * CAP : (k + 1) * CAP].astype(BF16)
@@ -457,7 +469,7 @@
     width = out_ref.shape[1]
     pick = pick_ref[...]
     arrived = jnp.concatenate(
-        [ref[i].astype(F32) for i in range(group_refs[0].shape[0]) for ref in group_refs], axis=0
+        [ref[i].astype(F32) for ref in group_refs for i in range(ref.shape[0])], axis=0
     )
     stats = arrived[:, width:]
     arrived_lse = (
@@ -548,8 +560,9 @@
 
     pick, keep, send = pl.pallas_call(
         select_queries,
-        in_specs=[RESIDENT, RESIDENT],
+        in_specs=[RESIDENT, REMAINS],
         out_specs=[RESIDENT] * 3,
+        scratch_shapes=[pltpu.VMEM(queries.shape, BF16), pltpu.SemaphoreType.DMA(())],
         out_shape=[pltpu.VMEM((slots, row_count), BF16)] + block_pair(query_width),
         compiler_params=compiler_params(16),
         name="select_queries",
@@ -566,7 +579,7 @@
             name="regroup",
         )(in_vmem(blocks), got, in_vmem(after))
 
-    edges = (0, 256, 768, 1536, 2560, 4096)
+    edges = (0, 256, 768, 1536, 3072, 5120)
     depth, head = edges[-1], edges[-2]
     rows, w_tail, total, target_here, span_here, lengths = pl.pallas_call(
         functools.partial(project_first, edges=edges),
@@ -692,7 +705,7 @@
                 name="fan_out",
             )(in_vmem(keep), got, in_vmem(share[2]))
             groups = [in_vmem(keep)]
-            groups += [swapped(blocks, i + 1) for i, blocks in enumerate(sent)]
+            groups += [swapped(blocks, (i + 1) * size) for i, blocks in enumerate(sent)]
 
     return pl.pallas_call(
         merge,

time: 38.8 us -> 39.3 us (1.013)
  waiting for transfers between devices: 4.54 us -> 3.18 us
  Pallas kernels: 22.1 us -> 23.4 us
  starting transfers between devices: 11.8 us -> 12.4 us
    ppermute x7, waiting for transfers between devices: 4.54 us -> 3.17 us  [swapped(): return in_vmem(lax.ppermute(blocks, 'section', pairs))]
    pallas_call x1, Pallas kernels: 4.57 us -> 5.42 us  [shards(): pl.pallas_call(functools.partial(project_first, edges=edges), in_specs=[R...]
    ppermute x7, starting transfers between devices: 11.8 us -> 12.4 us  [swapped(): return in_vmem(lax.ppermute(blocks, 'section', pairs))]
    pallas_call x1, Pallas kernels: 1.55 us -> 2.06 us  [shards(): pl.pallas_call(select_queries, in_specs=[RESIDENT, REMAINS], out_specs=[R...]
  transfers between devices with their start and end apart: 8 -> 8, of which waited for: 2 -> 2; matrix products, arithmetic and copies ran while one was open for 0% -> 0% of each run, Pallas kernels for 47% -> 49%
where the time goes in v19:
time: 39.3 us; the launch traced here: 39.1 us
  Pallas kernels  23.4 us (60%)
  starting transfers between devices  12.4 us (32%)
  waiting for transfers between devices  3.18 us (8%)
    ppermute x7, starting transfers between devices, swapped(): return in_vmem(lax.ppermute(blocks, 'section', pairs))  12.4 us
    pallas_call x1, Pallas kernels, shards(): pl.pallas_call(functools.partial(project_mine, at=at, last=last), in_spec...  6.13 us
    pallas_call x1, Pallas kernels, shards(): pl.pallas_call(functools.partial(project_first, edges=edges), in_specs=[R...  5.42 us
    pallas_call x1, Pallas kernels, shards(): pl.pallas_call(project_rest, in_specs=[REMAINS] * 4 + [RESIDENT] * 3 + [R...  4.78 us
    ppermute x7, waiting for transfers between devices, swapped(): return in_vmem(lax.ppermute(blocks, 'section', pairs))  3.17 us
    pallas_call x2, Pallas kernels, shards(): pl.pallas_call(functools.partial(attend_cache, rows_at=at), in_specs=[RES...  2.51 us
    pallas_call x1, Pallas kernels, shards(): pl.pallas_call(select_queries, in_specs=[RESIDENT, REMAINS], out_specs=[R...  2.06 us
    pallas_call x1, Pallas kernels, shards(): pl.pallas_call(merge, in_specs=[RESIDENT] * (5 + len(shares)), out_specs=...  1.29 us
  transfers between devices with their start and end apart: 8, of which 2 were waited for; matrix products, arithmetic and copies ran while one was open for 0% of the time, Pallas kernels for 49%

profile of v19, /device:TPU:0, one launch (start us, length us, event | category | flops | bytes accessed | tf_op | source)
XLA Modules:
  0.0 39.1 jit_solution(11310904725252870528)
XLA Ops:
  0.0 2.1 %select_queries.1 = (bf16[16,128]{1,0:T(8,128)(2,1)S(1)}, bf16[4,2,3072]{2,1,0:T(2,128)(2,1)S(1)}, bf16[4,2,3072]{2,1,0:T(2,128)(2,1)S(1)}) custom-call(s32[8,12]{1,0:T(8,128)} %target_ref.3, bf16[128,3072]{1,0:T(8,128)(2,1)} %refs_1_.1), custom_call_target="tpu_custom_call" | custom-call | tf_op jit(solution)/shard_map/select_queries/pallas_call | solution.py:561
  2.1 4.1 %collective-permute-start = (bf16[4,2,3072]{2,1,0:T(2,128)(2,1)S(1)}, bf16[4,2,3072]{2,1,0:T(2,128)(2,1)S(1)}, u32[]{:S(2)}, u32[]{:S(2)}) collective-permute-start(bf16[4,2,3072]{2,1,0:T(2,128)(2,1)S(1)} %get-tuple-element.46), channel_id=1, source_target_pairs={{0,8},{2,10},{4,12},{6,14},{8,0},{10,2},{12,4},{14,6},{1,9},{3,11}... | collective-permute-start | bytes 147464 | tf_op jit(solution)/shard_map/ppermute | solution.py:559
  6.2 5.4 %project_first.1 = (bf16[896,5120]{1,0:T(8,128)(2,1)S(1)}, bf16[2048,512]{1,0:T(8,128)(2,1)S(1)}, f32[896,512]{1,0:T(8,128)S(1)}, s32[8,12]{1,0:T(8,128)S(1)}, s...) custom-call(bf16[768,6144]{1,0:T(8,128)(2,1)} %prompts_ref.3, bf16[128,6144]{1,0:T(8,128)(2,1)} %hidden_ref.3, ...), custom_call_target="tpu_custom_call" | custom-call | tf_op jit(solution)/shard_map/project_first/pallas_call | solution.py:584
  11.6 0.0 collective-permute-done.got_ref
  11.6 1.6 %collective-permute-start.1 = (bf16[4,2,3072]{2,1,0:T(2,128)(2,1)S(1)}, bf16[4,2,3072]{2,1,0:T(2,128)(2,1)S(1)}, u32[]{:S(2)}, u32[]{:S(2)}) collective-permute-start(bf16[4,2,3072]{2,1,0:T(2,128)(2,1)S(1)} %get-tuple-element.51), channel_id=1, source_target_pairs={{0,4},{2,6},{4,0},{6,2},{8,12},{10,14},{12,8},{14,10},{1,5},{3,7},... | collective-permute-start | bytes 147464 | tf_op jit(solution)/shard_map/ppermute | solution.py:559
  13.3 4.8 %project_rest.1 = (bf16[896,512]{1,0:T(8,128)(2,1)S(1)}, bf16[896,1024]{1,0:T(8,128)(2,1)S(1)}, bf16[6144,512]{1,0:T(8,128)(2,1)S(1)}) custom-call(bf16[768,6144]{1,0:T(8,128)(2,1)} %prompts_ref.3, bf16[128,6144]{1,0:T(8,128)(2,1)} %hidden_ref.3, bf16[6144,1024]{1,0:T(8,128)(2,1)} %w_ref.3, f32[1,1024]{1,0:T(1,128)} %bitcast.2, ...), custom_call_target="tpu_custom_call" | custom-call | tf_op jit(solution)/shard_map/project_rest/pallas_call | solution.py:606
  18.1 0.1 collective-permute-start.2
  18.2 1.6 %collective-permute-start.3 = (bf16[4,2,3072]{2,1,0:T(2,128)(2,1)S(1)}, bf16[4,2,3072]{2,1,0:T(2,128)(2,1)S(1)}, u32[]{:S(2)}, u32[]{:S(2)}) collective-permute-start(bf16[4,2,3072]{2,1,0:T(2,128)(2,1)S(1)} %get-tuple-element.61), channel_id=1, source_target_pairs={{0,2},{2,0},{4,6},{6,4},{8,10},{10,8},{12,14},{14,12},{1,3},{3,1},... | collective-permute-start | bytes 147464 | tf_op jit(solution)/shard_map/ppermute | solution.py:559
  19.7 6.1 %project_mine.1 = (bf16[896,512]{1,0:T(8,128)(2,1)S(1)}, bf16[128,32,512]{2,1,0:T(8,128)(2,1)S(1)}, bf16[128,3072]{1,0:T(8,128)(2,1)S(1)}) custom-call(bf16[896,5120]{1,0:T(8,128)(2,1)S(1)} %get-tuple-element.42.rows_ref, bf16[896,1024]{1,0:T(8,128)(2,1)S(1)} %get-tuple-element.48.rows_rest_ref, bf16[6144,512]{1,0:T(8,128)(2,1)S(1)} %get-tuple-element.49.w_mine_ref, ...), custom_call_target="tpu_custom_call" | custom-call | tf_op jit(solution)/shard_map/project_mine/pallas_call | solution.py:637
  25.9 0.0 collective-permute-done.3.got_ref
  25.9 0.3 prepare_arrived.1
  26.2 0.0 collective-permute-done.2.other_ref
  26.2 0.9 %attend_arrived.1 = (bf16[4,2,3200]{2,1,0:T(2,128)(2,1)S(1)}, bf16[4,2,3200]{2,1,0:T(2,128)(2,1)S(1)}) custom-call(bf16[16,3072]{1,0:T(8,128)(2,1)S(1)} %get-tuple-element.62.rows_ref, bf16[16,64]{1,0:T(8,128)(2,1)S(1)} %get-tuple-element.63.slot_of_ref, f32[16,768]{1,0:T(8,128)S(1)} %get-tuple-element.64.bias_ref, ...), custom_call_target="tpu_custom_call" | custom-call | tf_op jit(solution)/shard_map/attend_arrived/pallas_call | solution.py:665
  27.1 0.6 %collective-permute-start.4 = (bf16[4,2,3200]{2,1,0:T(2,128)(2,1)S(1)}, bf16[4,2,3200]{2,1,0:T(2,128)(2,1)S(1)}, u32[]{:S(2)}, u32[]{:S(2)}) collective-permute-start(bf16[4,2,3200]{2,1,0:T(2,128)(2,1)S(1)} %get-tuple-element.69), channel_id=1, source_target_pairs={{0,2},{2,0},{4,6},{6,4},{8,10},{10,8},{12,14},{14,12},{1,3},{3,1},... | collective-permute-start | bytes 153608 | tf_op jit(solution)/shard_map/ppermute | solution.py:559
  27.7 1.3 %attend_cache.2 = (bf16[64,3072]{1,0:T(8,128)(2,1)S(1)}, f32[16,3072]{1,0:T(8,128)S(1)}, f32[16,128]{1,0:T(8,128)S(1)}) custom-call(bf16[128,3072]{1,0:T(8,128)(2,1)S(1)} %get-tuple-element.55.queries_ref, bf16[128,32,512]{2,1,0:T(8,128)(2,1)S(1)} %get-tuple-element.56.cache_ref, s32[1,128]{1,0:T(1,128)S(1)} %get-tuple-element.57.len_ref, ...), custom_call_target="tpu_custom_call" | custom-call | tf_op jit(solution)/shard_map/attend_cache/pallas_call | solution.py:682
  29.0 2.3 %collective-permute-done.4.got_ref = bf16[4,2,3200]{2,1,0:T(2,128)(2,1)S(1)} collective-permute-done((bf16[4,2,3200]{2,1,0:T(2,128)(2,1)S(1)}, bf16[4,2,3200]{2,1,0:T(2,128)(2,1)S(1)}, u32[]{:S(2)}, u32[]{:S(2)}) %collective-permute-start.4) | collective-permute-done | bytes 51232 | tf_op jit(solution)/shard_map/ppermute | solution.py:559
  31.3 0.5 %collective-permute-start.5 = (bf16[2,2,3200]{2,1,0:T(2,128)(2,1)S(1)}, bf16[2,2,3200]{2,1,0:T(2,128)(2,1)S(1)}, u32[]{:S(2)}, u32[]{:S(2)}) collective-permute-start(bf16[2,2,3200]{2,1,0:T(2,128)(2,1)S(1)} %get-tuple-element.74), channel_id=1, source_target_pairs={{0,4},{2,6},{4,0},{6,2},{8,12},{10,14},{12,8},{14,10},{1,5},{3,7},... | collective-permute-start | bytes 76808 | tf_op jit(solution)/shard_map/ppermute | solution.py:559
  31.8 0.3 collective-permute-start.6
  32.2 3.6 %collective-permute-start.7 = (bf16[2,2,3200]{2,1,0:T(2,128)(2,1)S(1)}, bf16[2,2,3200]{2,1,0:T(2,128)(2,1)S(1)}, u32[]{:S(2)}, u32[]{:S(2)}) collective-permute-start(bf16[2,2,3200]{2,1,0:T(2,128)(2,1)S(1)} %get-tuple-element.76), channel_id=1, source_target_pairs={{0,12},{2,14},{4,8},{6,10},{8,4},{10,6},{12,0},{14,2},{1,13},{3,15... | collective-permute-start | bytes 76808 | tf_op jit(solution)/shard_map/ppermute | solution.py:559
  35.8 1.3 %attend_cache.3 = (bf16[64,3072]{1,0:T(8,128)(2,1)S(1)}, f32[16,3072]{1,0:T(8,128)S(1)}, f32[16,128]{1,0:T(8,128)S(1)}) custom-call(bf16[128,3072]{1,0:T(8,128)(2,1)S(1)} %get-tuple-element.55.queries_ref, bf16[128,32,512]{2,1,0:T(8,128)(2,1)S(1)} %get-tuple-element.56.cache_ref, s32[1,128]{1,0:T(1,128)S(1)} %get-tuple-element.57.len_ref, ...), custom_call_target="tpu_custom_call" | custom-call | tf_op jit(solution)/shard_map/attend_cache/pallas_call | solution.py:682
  37.0 0.0 collective-permute-done.5.refs_7_
  37.0 0.0 collective-permute-done.6.refs_8_
  37.0 0.8 %collective-permute-done.7.refs_9_ = bf16[2,2,3200]{2,1,0:T(2,128)(2,1)S(1)} collective-permute-done((bf16[2,2,3200]{2,1,0:T(2,128)(2,1)S(1)}, bf16[2,2,3200]{2,1,0:T(2,128)(2,1)S(1)}, u32[]{:S(2)}, u32[]{:S(2)}) %collective-permute-start.7) | collective-permute-done | bytes 25632 | tf_op jit(solution)/shard_map/ppermute | solution.py:559
  37.9 1.3 %merge.1 = bf16[128,3072]{1,0:T(8,128)(2,1)} custom-call(bf16[16,128]{1,0:T(8,128)(2,1)S(1)} %get-tuple-element.41.pick_ref, bf16[64,3072]{1,0:T(8,128)(2,1)S(1)} %get-tuple-element.66.refs_0_, f32[16,3072]{1,0:T(8,128)S(1)} %get-tuple-element.67.refs_1_, f32[16,128]{1,0:T(8,128)S(1)} %get-tuple-element.68.after_ref.refs_2_, ...), custom_call_target="tpu_custom_call" | custom-call | tf_op jit(solution)/shard_map/merge/pallas_call | solution.py:710
  (4 shorter events, 0.0 us)
Async XLA Ops:
  2.1 9.5 %collective-permute-start = (bf16[4,2,3072]{2,1,0:T(2,128)(2,1)S(1)}, bf16[4,2,3072]{2,1,0:T(2,128)(2,1)S(1)}, u32[]{:S(2)}, u32[]{:S(2)}) collective-permute-start(bf16[4,2,3072]{2,1,0:T(2,128)(2,1)S(1)} %get-tuple-element.46), channel_id=1, source_target_pairs={{0,8},{2,10},{4,12},{6,14},{8,0},{10,2},{12,4},{14,6},{1,9},{3,11}... | collective-permute-start | bytes 147464 | tf_op jit(solution)/shard_map/ppermute | solution.py:559
  11.6 6.4 %collective-permute-start.1 = (bf16[4,2,3072]{2,1,0:T(2,128)(2,1)S(1)}, bf16[4,2,3072]{2,1,0:T(2,128)(2,1)S(1)}, u32[]{:S(2)}, u32[]{:S(2)}) collective-permute-start(bf16[4,2,3072]{2,1,0:T(2,128)(2,1)S(1)} %get-tuple-element.51), channel_id=1, source_target_pairs={{0,4},{2,6},{4,0},{6,2},{8,12},{10,14},{12,8},{14,10},{1,5},{3,7},... | collective-permute-start | bytes 147464 | tf_op jit(solution)/shard_map/ppermute | solution.py:559
  18.1 8.2 %collective-permute-start.2 = (bf16[896,512]{1,0:T(8,128)(2,1)S(1)}, bf16[896,512]{1,0:T(8,128)(2,1)S(1)}, u32[]{:S(2)}, u32[]{:S(2)}) collective-permute-start(bf16[896,512]{1,0:T(8,128)(2,1)S(1)} %get-tuple-element.53.after_ref), channel_id=1, source_target_pairs={{0,1},{1,0},{2,3},{3,2},{4,5},{5,4},{6,7},{7,6},{8,9},{9,8},{10,11... | collective-permute-start | bytes 2752520 | tf_op jit(solution)/shard_map/ppermute | solution.py:625
  18.2 7.7 %collective-permute-start.3 = (bf16[4,2,3072]{2,1,0:T(2,128)(2,1)S(1)}, bf16[4,2,3072]{2,1,0:T(2,128)(2,1)S(1)}, u32[]{:S(2)}, u32[]{:S(2)}) collective-permute-start(bf16[4,2,3072]{2,1,0:T(2,128)(2,1)S(1)} %get-tuple-element.61), channel_id=1, source_target_pairs={{0,2},{2,0},{4,6},{6,4},{8,10},{10,8},{12,14},{14,12},{1,3},{3,1},... | collective-permute-start | bytes 147464 | tf_op jit(solution)/shard_map/ppermute | solution.py:559
  27.1 4.2 %collective-permute-start.4 = (bf16[4,2,3200]{2,1,0:T(2,128)(2,1)S(1)}, bf16[4,2,3200]{2,1,0:T(2,128)(2,1)S(1)}, u32[]{:S(2)}, u32[]{:S(2)}) collective-permute-start(bf16[4,2,3200]{2,1,0:T(2,128)(2,1)S(1)} %get-tuple-element.69), channel_id=1, source_target_pairs={{0,2},{2,0},{4,6},{6,4},{8,10},{10,8},{12,14},{14,12},{1,3},{3,1},... | collective-permute-start | bytes 153608 | tf_op jit(solution)/shard_map/ppermute | solution.py:559
  31.3 5.7 %collective-permute-start.5 = (bf16[2,2,3200]{2,1,0:T(2,128)(2,1)S(1)}, bf16[2,2,3200]{2,1,0:T(2,128)(2,1)S(1)}, u32[]{:S(2)}, u32[]{:S(2)}) collective-permute-start(bf16[2,2,3200]{2,1,0:T(2,128)(2,1)S(1)} %get-tuple-element.74), channel_id=1, source_target_pairs={{0,4},{2,6},{4,0},{6,2},{8,12},{10,14},{12,8},{14,10},{1,5},{3,7},... | collective-permute-start | bytes 76808 | tf_op jit(solution)/shard_map/ppermute | solution.py:559
  31.8 5.2 %collective-permute-start.6 = (bf16[2,2,3200]{2,1,0:T(2,128)(2,1)S(1)}, bf16[2,2,3200]{2,1,0:T(2,128)(2,1)S(1)}, u32[]{:S(2)}, u32[]{:S(2)}) collective-permute-start(bf16[2,2,3200]{2,1,0:T(2,128)(2,1)S(1)} %get-tuple-element.75), channel_id=1, source_target_pairs={{0,8},{2,10},{4,12},{6,14},{8,0},{10,2},{12,4},{14,6},{1,9},{3,11}... | collective-permute-start | bytes 76808 | tf_op jit(solution)/shard_map/ppermute | solution.py:559
  32.2 5.7 %collective-permute-start.7 = (bf16[2,2,3200]{2,1,0:T(2,128)(2,1)S(1)}, bf16[2,2,3200]{2,1,0:T(2,128)(2,1)S(1)}, u32[]{:S(2)}, u32[]{:S(2)}) collective-permute-start(bf16[2,2,3200]{2,1,0:T(2,128)(2,1)S(1)} %get-tuple-element.76), channel_id=1, source_target_pairs={{0,12},{2,14},{4,8},{6,10},{8,4},{10,6},{12,0},{14,2},{1,13},{3,15... | collective-permute-start | bytes 76808 | tf_op jit(solution)/shard_map/ppermute | solution.py:559

commit v20 on v19

--- a/solution.py
+++ b/solution.py
@@ -96,16 +96,11 @@
     return jnp.concatenate([where[k].astype(F32) for k in range(len(where))], axis=0)
 
 
-def select_queries(
-    target_ref, queries_ref, pick_ref, keep_ref, send_ref, queries_here_ref, sem
-):
-    copy = pltpu.make_async_copy(queries_ref, queries_here_ref, sem)
-    copy.start()
+def select_queries(target_ref, queries_ref, pick_ref, keep_ref, send_ref):
     _, sent, kept = steps_of(target_ref.shape[0])[0]
     pick = pick_rows(target_ref, queries_ref.shape[0])
     pick_ref[...] = pick
-    copy.wait()
-    asked = jnp.dot(pick, queries_here_ref[...], preferred_element_type=F32)
+    asked = jnp.dot(pick, queries_ref[...], preferred_element_type=F32)
     for ref, blocks in ((send_ref, sent), (keep_ref, kept)):
         for i, k in enumerate(blocks):
             ref[i] = asked[k * CAP : (k + 1) * CAP].astype(BF16)
@@ -560,9 +555,8 @@
 
     pick, keep, send = pl.pallas_call(
         select_queries,
-        in_specs=[RESIDENT, REMAINS],
+        in_specs=[RESIDENT, RESIDENT],
         out_specs=[RESIDENT] * 3,
-        scratch_shapes=[pltpu.VMEM(queries.shape, BF16), pltpu.SemaphoreType.DMA(())],
         out_shape=[pltpu.VMEM((slots, row_count), BF16)] + block_pair(query_width),
         compiler_params=compiler_params(16),
         name="select_queries",
@@ -579,7 +573,7 @@
             name="regroup",
         )(in_vmem(blocks), got, in_vmem(after))
 
-    edges = (0, 256, 768, 1536, 3072, 5120)
+    edges = (0, 256, 768, 1536, 2560, 4096)
     depth, head = edges[-1], edges[-2]
     rows, w_tail, total, target_here, span_here, lengths = pl.pallas_call(
         functools.partial(project_first, edges=edges),

time: 39.3 us -> 38.1 us (0.969)
  Pallas kernels: 23.4 us -> 22.1 us
    pallas_call x1, Pallas kernels: 5.42 us -> 4.57 us  [shards(): pl.pallas_call(functools.partial(project_first, edges=edges), in_specs=[R...]
    pallas_call x1, Pallas kernels: 2.06 us -> 1.55 us  [shards(): pl.pallas_call(select_queries, in_specs=[RESIDENT, RESIDENT], out_specs=[...]
  transfers between devices with their start and end apart: 8 -> 8, of which waited for: 2 -> 2; matrix products, arithmetic and copies ran while one was open for 0% -> 0% of each run, Pallas kernels for 49% -> 48%
where the time goes in v20:
time: 38.1 us; the launch traced here: 37.9 us
  Pallas kernels  22.1 us (58%)
  starting transfers between devices  12.4 us (33%)
  waiting for transfers between devices  3.28 us (9%)
    ppermute x7, starting transfers between devices, swapped(): return in_vmem(lax.ppermute(blocks, 'section', pairs))  12.4 us
    pallas_call x1, Pallas kernels, shards(): pl.pallas_call(functools.partial(project_mine, at=at, last=last), in_spec...  6.09 us
    pallas_call x1, Pallas kernels, shards(): pl.pallas_call(project_rest, in_specs=[REMAINS] * 4 + [RESIDENT] * 3 + [R...  4.84 us
    pallas_call x1, Pallas kernels, shards(): pl.pallas_call(functools.partial(project_first, edges=edges), in_specs=[R...  4.57 us
    ppermute x7, waiting for transfers between devices, swapped(): return in_vmem(lax.ppermute(blocks, 'section', pairs))  3.28 us
    pallas_call x2, Pallas kernels, shards(): pl.pallas_call(functools.partial(attend_cache, rows_at=at), in_specs=[RES...  2.51 us
    pallas_call x1, Pallas kernels, shards(): pl.pallas_call(select_queries, in_specs=[RESIDENT, RESIDENT], out_specs=[...  1.55 us
    pallas_call x1, Pallas kernels, shards(): pl.pallas_call(merge, in_specs=[RESIDENT] * (5 + len(shares)), out_specs=...  1.3 us
  transfers between devices with their start and end apart: 8, of which 2 were waited for; matrix products, arithmetic and copies ran while one was open for 0% of the time, Pallas kernels for 48%

profile of v20, /device:TPU:0, one launch (start us, length us, event | category | flops | bytes accessed | tf_op | source)
XLA Modules:
  0.0 37.9 jit_solution(11171157231522082237)
XLA Ops:
  0.0 1.6 %select_queries.1 = (bf16[16,128]{1,0:T(8,128)(2,1)S(1)}, bf16[4,2,3072]{2,1,0:T(2,128)(2,1)S(1)}, bf16[4,2,3072]{2,1,0:T(2,128)(2,1)S(1)}) custom-call(s32[8,12]{1,0:T(8,128)} %target_ref.3, bf16[128,3072]{1,0:T(8,128)(2,1)} %refs_1_.1), custom_call_target="tpu_custom_call" | custom-call | tf_op jit(solution)/shard_map/select_queries/pallas_call | solution.py:556
  1.6 4.1 %collective-permute-start = (bf16[4,2,3072]{2,1,0:T(2,128)(2,1)S(1)}, bf16[4,2,3072]{2,1,0:T(2,128)(2,1)S(1)}, u32[]{:S(2)}, u32[]{:S(2)}) collective-permute-start(bf16[4,2,3072]{2,1,0:T(2,128)(2,1)S(1)} %get-tuple-element.46), channel_id=1, source_target_pairs={{0,8},{2,10},{4,12},{6,14},{8,0},{10,2},{12,4},{14,6},{1,9},{3,11}... | collective-permute-start | bytes 147464 | tf_op jit(solution)/shard_map/ppermute | solution.py:554
  5.7 4.6 %project_first.1 = (bf16[896,4096]{1,0:T(8,128)(2,1)S(1)}, bf16[1536,512]{1,0:T(8,128)(2,1)S(1)}, f32[896,512]{1,0:T(8,128)S(1)}, s32[8,12]{1,0:T(8,128)S(1)}, s...) custom-call(bf16[768,6144]{1,0:T(8,128)(2,1)} %prompts_ref.3, bf16[128,6144]{1,0:T(8,128)(2,1)} %hidden_ref.3, ...), custom_call_target="tpu_custom_call" | custom-call | tf_op jit(solution)/shard_map/project_first/pallas_call | solution.py:578
  10.2 0.0 collective-permute-done.got_ref
  10.3 1.6 %collective-permute-start.1 = (bf16[4,2,3072]{2,1,0:T(2,128)(2,1)S(1)}, bf16[4,2,3072]{2,1,0:T(2,128)(2,1)S(1)}, u32[]{:S(2)}, u32[]{:S(2)}) collective-permute-start(bf16[4,2,3072]{2,1,0:T(2,128)(2,1)S(1)} %get-tuple-element.51), channel_id=1, source_target_pairs={{0,4},{2,6},{4,0},{6,2},{8,12},{10,14},{12,8},{14,10},{1,5},{3,7},... | collective-permute-start | bytes 147464 | tf_op jit(solution)/shard_map/ppermute | solution.py:554
  11.9 4.8 %project_rest.1 = (bf16[896,512]{1,0:T(8,128)(2,1)S(1)}, bf16[896,2048]{1,0:T(8,128)(2,1)S(1)}, bf16[6144,512]{1,0:T(8,128)(2,1)S(1)}) custom-call(bf16[768,6144]{1,0:T(8,128)(2,1)} %prompts_ref.3, bf16[128,6144]{1,0:T(8,128)(2,1)} %hidden_ref.3, bf16[6144,1024]{1,0:T(8,128)(2,1)} %w_ref.3, f32[1,1024]{1,0:T(1,128)} %bitcast.2, ...), custom_call_target="tpu_custom_call" | custom-call | tf_op jit(solution)/shard_map/project_rest/pallas_call | solution.py:600
  16.8 0.0 collective-permute-done.1.got_ref
  16.8 0.1 collective-permute-start.2
  16.9 1.6 %collective-permute-start.3 = (bf16[4,2,3072]{2,1,0:T(2,128)(2,1)S(1)}, bf16[4,2,3072]{2,1,0:T(2,128)(2,1)S(1)}, u32[]{:S(2)}, u32[]{:S(2)}) collective-permute-start(bf16[4,2,3072]{2,1,0:T(2,128)(2,1)S(1)} %get-tuple-element.61), channel_id=1, source_target_pairs={{0,2},{2,0},{4,6},{6,4},{8,10},{10,8},{12,14},{14,12},{1,3},{3,1},... | collective-permute-start | bytes 147464 | tf_op jit(solution)/shard_map/ppermute | solution.py:554
  18.5 6.1 %project_mine.1 = (bf16[896,512]{1,0:T(8,128)(2,1)S(1)}, bf16[128,32,512]{2,1,0:T(8,128)(2,1)S(1)}, bf16[128,3072]{1,0:T(8,128)(2,1)S(1)}) custom-call(bf16[896,4096]{1,0:T(8,128)(2,1)S(1)} %get-tuple-element.42.rows_ref, bf16[896,2048]{1,0:T(8,128)(2,1)S(1)} %get-tuple-element.48.rows_rest_ref, bf16[6144,512]{1,0:T(8,128)(2,1)S(1)} %get-tuple-element.49.w_mine_ref, ...), custom_call_target="tpu_custom_call" | custom-call | tf_op jit(solution)/shard_map/project_mine/pallas_call | solution.py:631
  24.6 0.0 collective-permute-done.3.got_ref
  24.6 0.3 prepare_arrived.1
  24.9 0.0 collective-permute-done.2.other_ref
  24.9 0.9 %attend_arrived.1 = (bf16[4,2,3200]{2,1,0:T(2,128)(2,1)S(1)}, bf16[4,2,3200]{2,1,0:T(2,128)(2,1)S(1)}) custom-call(bf16[16,3072]{1,0:T(8,128)(2,1)S(1)} %get-tuple-element.62.rows_ref, bf16[16,64]{1,0:T(8,128)(2,1)S(1)} %get-tuple-element.63.slot_of_ref, f32[16,768]{1,0:T(8,128)S(1)} %get-tuple-element.64.bias_ref, ...), custom_call_target="tpu_custom_call" | custom-call | tf_op jit(solution)/shard_map/attend_arrived/pallas_call | solution.py:659
  25.8 0.6 %collective-permute-start.4 = (bf16[4,2,3200]{2,1,0:T(2,128)(2,1)S(1)}, bf16[4,2,3200]{2,1,0:T(2,128)(2,1)S(1)}, u32[]{:S(2)}, u32[]{:S(2)}) collective-permute-start(bf16[4,2,3200]{2,1,0:T(2,128)(2,1)S(1)} %get-tuple-element.69), channel_id=1, source_target_pairs={{0,2},{2,0},{4,6},{6,4},{8,10},{10,8},{12,14},{14,12},{1,3},{3,1},... | collective-permute-start | bytes 153608 | tf_op jit(solution)/shard_map/ppermute | solution.py:554
  26.4 1.3 %attend_cache.2 = (bf16[64,3072]{1,0:T(8,128)(2,1)S(1)}, f32[16,3072]{1,0:T(8,128)S(1)}, f32[16,128]{1,0:T(8,128)S(1)}) custom-call(bf16[128,3072]{1,0:T(8,128)(2,1)S(1)} %get-tuple-element.55.queries_ref, bf16[128,32,512]{2,1,0:T(8,128)(2,1)S(1)} %get-tuple-element.56.cache_ref, s32[1,128]{1,0:T(1,128)S(1)} %get-tuple-element.57.len_ref, ...), custom_call_target="tpu_custom_call" | custom-call | tf_op jit(solution)/shard_map/attend_cache/pallas_call | solution.py:676
  27.6 2.3 %collective-permute-done.4.got_ref = bf16[4,2,3200]{2,1,0:T(2,128)(2,1)S(1)} collective-permute-done((bf16[4,2,3200]{2,1,0:T(2,128)(2,1)S(1)}, bf16[4,2,3200]{2,1,0:T(2,128)(2,1)S(1)}, u32[]{:S(2)}, u32[]{:S(2)}) %collective-permute-start.4) | collective-permute-done | bytes 51232 | tf_op jit(solution)/shard_map/ppermute | solution.py:554
  30.0 0.5 %collective-permute-start.5 = (bf16[2,2,3200]{2,1,0:T(2,128)(2,1)S(1)}, bf16[2,2,3200]{2,1,0:T(2,128)(2,1)S(1)}, u32[]{:S(2)}, u32[]{:S(2)}) collective-permute-start(bf16[2,2,3200]{2,1,0:T(2,128)(2,1)S(1)} %get-tuple-element.74), channel_id=1, source_target_pairs={{0,4},{2,6},{4,0},{6,2},{8,12},{10,14},{12,8},{14,10},{1,5},{3,7},... | collective-permute-start | bytes 76808 | tf_op jit(solution)/shard_map/ppermute | solution.py:554
  30.5 0.4 %collective-permute-start.6 = (bf16[2,2,3200]{2,1,0:T(2,128)(2,1)S(1)}, bf16[2,2,3200]{2,1,0:T(2,128)(2,1)S(1)}, u32[]{:S(2)}, u32[]{:S(2)}) collective-permute-start(bf16[2,2,3200]{2,1,0:T(2,128)(2,1)S(1)} %get-tuple-element.75), channel_id=1, source_target_pairs={{0,8},{2,10},{4,12},{6,14},{8,0},{10,2},{12,4},{14,6},{1,9},{3,11}... | collective-permute-start | bytes 76808 | tf_op jit(solution)/shard_map/ppermute | solution.py:554
  30.9 3.5 %collective-permute-start.7 = (bf16[2,2,3200]{2,1,0:T(2,128)(2,1)S(1)}, bf16[2,2,3200]{2,1,0:T(2,128)(2,1)S(1)}, u32[]{:S(2)}, u32[]{:S(2)}) collective-permute-start(bf16[2,2,3200]{2,1,0:T(2,128)(2,1)S(1)} %get-tuple-element.76), channel_id=1, source_target_pairs={{0,12},{2,14},{4,8},{6,10},{8,4},{10,6},{12,0},{14,2},{1,13},{3,15... | collective-permute-start | bytes 76808 | tf_op jit(solution)/shard_map/ppermute | solution.py:554
  34.4 1.3 %attend_cache.3 = (bf16[64,3072]{1,0:T(8,128)(2,1)S(1)}, f32[16,3072]{1,0:T(8,128)S(1)}, f32[16,128]{1,0:T(8,128)S(1)}) custom-call(bf16[128,3072]{1,0:T(8,128)(2,1)S(1)} %get-tuple-element.55.queries_ref, bf16[128,32,512]{2,1,0:T(8,128)(2,1)S(1)} %get-tuple-element.56.cache_ref, s32[1,128]{1,0:T(1,128)S(1)} %get-tuple-element.57.len_ref, ...), custom_call_target="tpu_custom_call" | custom-call | tf_op jit(solution)/shard_map/attend_cache/pallas_call | solution.py:676
  35.7 0.0 collective-permute-done.5.refs_7_
  35.7 0.9 %collective-permute-done.7.refs_9_ = bf16[2,2,3200]{2,1,0:T(2,128)(2,1)S(1)} collective-permute-done((bf16[2,2,3200]{2,1,0:T(2,128)(2,1)S(1)}, bf16[2,2,3200]{2,1,0:T(2,128)(2,1)S(1)}, u32[]{:S(2)}, u32[]{:S(2)}) %collective-permute-start.7) | collective-permute-done | bytes 25632 | tf_op jit(solution)/shard_map/ppermute | solution.py:554
  36.6 1.3 %merge.1 = bf16[128,3072]{1,0:T(8,128)(2,1)} custom-call(bf16[16,128]{1,0:T(8,128)(2,1)S(1)} %get-tuple-element.41.pick_ref, bf16[64,3072]{1,0:T(8,128)(2,1)S(1)} %get-tuple-element.66.refs_0_, f32[16,3072]{1,0:T(8,128)S(1)} %get-tuple-element.67.refs_1_, f32[16,128]{1,0:T(8,128)S(1)} %get-tuple-element.68.after_ref.refs_2_, ...), custom_call_target="tpu_custom_call" | custom-call | tf_op jit(solution)/shard_map/merge/pallas_call | solution.py:704
  (4 shorter events, 0.0 us)
Async XLA Ops:
  1.6 8.7 %collective-permute-start = (bf16[4,2,3072]{2,1,0:T(2,128)(2,1)S(1)}, bf16[4,2,3072]{2,1,0:T(2,128)(2,1)S(1)}, u32[]{:S(2)}, u32[]{:S(2)}) collective-permute-start(bf16[4,2,3072]{2,1,0:T(2,128)(2,1)S(1)} %get-tuple-element.46), channel_id=1, source_target_pairs={{0,8},{2,10},{4,12},{6,14},{8,0},{10,2},{12,4},{14,6},{1,9},{3,11}... | collective-permute-start | bytes 147464 | tf_op jit(solution)/shard_map/ppermute | solution.py:554
  10.3 6.5 %collective-permute-start.1 = (bf16[4,2,3072]{2,1,0:T(2,128)(2,1)S(1)}, bf16[4,2,3072]{2,1,0:T(2,128)(2,1)S(1)}, u32[]{:S(2)}, u32[]{:S(2)}) collective-permute-start(bf16[4,2,3072]{2,1,0:T(2,128)(2,1)S(1)} %get-tuple-element.51), channel_id=1, source_target_pairs={{0,4},{2,6},{4,0},{6,2},{8,12},{10,14},{12,8},{14,10},{1,5},{3,7},... | collective-permute-start | bytes 147464 | tf_op jit(solution)/shard_map/ppermute | solution.py:554
  16.8 8.1 %collective-permute-start.2 = (bf16[896,512]{1,0:T(8,128)(2,1)S(1)}, bf16[896,512]{1,0:T(8,128)(2,1)S(1)}, u32[]{:S(2)}, u32[]{:S(2)}) collective-permute-start(bf16[896,512]{1,0:T(8,128)(2,1)S(1)} %get-tuple-element.53.after_ref), channel_id=1, source_target_pairs={{0,1},{1,0},{2,3},{3,2},{4,5},{5,4},{6,7},{7,6},{8,9},{9,8},{10,11... | collective-permute-start | bytes 2752520 | tf_op jit(solution)/shard_map/ppermute | solution.py:619
  16.9 7.7 %collective-permute-start.3 = (bf16[4,2,3072]{2,1,0:T(2,128)(2,1)S(1)}, bf16[4,2,3072]{2,1,0:T(2,128)(2,1)S(1)}, u32[]{:S(2)}, u32[]{:S(2)}) collective-permute-start(bf16[4,2,3072]{2,1,0:T(2,128)(2,1)S(1)} %get-tuple-element.61), channel_id=1, source_target_pairs={{0,2},{2,0},{4,6},{6,4},{8,10},{10,8},{12,14},{14,12},{1,3},{3,1},... | collective-permute-start | bytes 147464 | tf_op jit(solution)/shard_map/ppermute | solution.py:554
  25.8 4.2 %collective-permute-start.4 = (bf16[4,2,3200]{2,1,0:T(2,128)(2,1)S(1)}, bf16[4,2,3200]{2,1,0:T(2,128)(2,1)S(1)}, u32[]{:S(2)}, u32[]{:S(2)}) collective-permute-start(bf16[4,2,3200]{2,1,0:T(2,128)(2,1)S(1)} %get-tuple-element.69), channel_id=1, source_target_pairs={{0,2},{2,0},{4,6},{6,4},{8,10},{10,8},{12,14},{14,12},{1,3},{3,1},... | collective-permute-start | bytes 153608 | tf_op jit(solution)/shard_map/ppermute | solution.py:554
  30.0 5.7 %collective-permute-start.5 = (bf16[2,2,3200]{2,1,0:T(2,128)(2,1)S(1)}, bf16[2,2,3200]{2,1,0:T(2,128)(2,1)S(1)}, u32[]{:S(2)}, u32[]{:S(2)}) collective-permute-start(bf16[2,2,3200]{2,1,0:T(2,128)(2,1)S(1)} %get-tuple-element.74), channel_id=1, source_target_pairs={{0,4},{2,6},{4,0},{6,2},{8,12},{10,14},{12,8},{14,10},{1,5},{3,7},... | collective-permute-start | bytes 76808 | tf_op jit(solution)/shard_map/ppermute | solution.py:554
  30.5 5.2 %collective-permute-start.6 = (bf16[2,2,3200]{2,1,0:T(2,128)(2,1)S(1)}, bf16[2,2,3200]{2,1,0:T(2,128)(2,1)S(1)}, u32[]{:S(2)}, u32[]{:S(2)}) collective-permute-start(bf16[2,2,3200]{2,1,0:T(2,128)(2,1)S(1)} %get-tuple-element.75), channel_id=1, source_target_pairs={{0,8},{2,10},{4,12},{6,14},{8,0},{10,2},{12,4},{14,6},{1,9},{3,11}... | collective-permute-start | bytes 76808 | tf_op jit(solution)/shard_map/ppermute | solution.py:554
  30.9 5.7 %collective-permute-start.7 = (bf16[2,2,3200]{2,1,0:T(2,128)(2,1)S(1)}, bf16[2,2,3200]{2,1,0:T(2,128)(2,1)S(1)}, u32[]{:S(2)}, u32[]{:S(2)}) collective-permute-start(bf16[2,2,3200]{2,1,0:T(2,128)(2,1)S(1)} %get-tuple-element.76), channel_id=1, source_target_pairs={{0,12},{2,14},{4,8},{6,10},{8,4},{10,6},{12,0},{14,2},{1,13},{3,15... | collective-permute-start | bytes 76808 | tf_op jit(solution)/shard_map/ppermute | solution.py:554

commit v21 on v20

--- a/solution.py
+++ b/solution.py
@@ -234,7 +234,7 @@
         copy.start()
     depth = rows_ref.shape[1]
     count = at.stop - at.start
-    block = count // 2 if count % 32 == 0 else count
+    block = count // 2 if count % 32 == 0 and count > 256 else count
     for m in spans(range(0, count + 1, block)):
         there = slice(at.start + m.start, at.start + m.stop)
         total = jnp.dot(rows_ref[there, :], w_mine_ref[:depth, :], preferred_element_type=F32)
@@ -618,9 +618,21 @@
     got = in_vmem(got)
     other = in_vmem(lax.ppermute(theirs, "tp", [(0, 1), (1, 0)]))
 
+    def own_channels(at, after, extra):
+        return pl.pallas_call(
+            functools.partial(project_mine, at=at, last=len(extra) > 0),
+            in_specs=[RESIDENT] * 3 + [REMAINS] * (2 + len(extra)),
+            out_specs=[RESIDENT] * (1 + len(extra)),
+            out_shape=[pltpu.VMEM((at.stop - at.start, local_width), BF16)]
+            + [pltpu.VMEM(x.shape, BF16) for x in extra],
+            scratch_shapes=[pltpu.VMEM((1, local_width), F32), pltpu.SemaphoreType.DMA((3,))],
+            compiler_params=compiler_params(16),
+            name="project_mine",
+        )(*map(in_vmem, (rows, rows_rest, w_mine)), scale, in_vmem(after), *extra)
+
     mine = []
     pieces = max(len(steps) - 2, 1)
-    bounds = [all_rows * i // (16 * pieces) * 16 for i in range(pieces)] + [all_rows]
+    bounds = [prompt_rows * i // (16 * pieces) * 16 for i in range(pieces)] + [prompt_rows]
     after = theirs
     for piece, at in enumerate(spans(bounds)):
         if piece + 2 < len(steps):
@@ -628,16 +640,7 @@
             got = swapped(send, steps[piece + 2][0])
         last = piece == pieces - 1
         extra = [kv_cache, queries] if last else []
-        part, *here = pl.pallas_call(
-            functools.partial(project_mine, at=at, last=last),
-            in_specs=[RESIDENT] * 3 + [REMAINS] * (2 + len(extra)),
-            out_specs=[RESIDENT] * (1 + len(extra)),
-            out_shape=[pltpu.VMEM((at.stop - at.start, local_width), BF16)]
-            + [pltpu.VMEM(x.shape, BF16) for x in extra],
-            scratch_shapes=[pltpu.VMEM((1, local_width), F32), pltpu.SemaphoreType.DMA((3,))],
-            compiler_params=compiler_params(16),
-            name="project_mine",
-        )(*map(in_vmem, (rows, rows_rest, w_mine)), scale, in_vmem(keep), *extra)
+        part, *here = own_channels(at, keep, extra)
         after = part
         mine.append(in_vmem(part))
     kv_here, queries_here = map(in_vmem, here)
@@ -665,6 +668,7 @@
         name="attend_arrived",
     )(*map(in_vmem, prepared), other, *mine)
 
+    (own_part,) = own_channels(slice(prompt_rows, all_rows), keep, [])
     steps = answer_steps_of(sections)
     shares = []
     calls = len(steps) + 1
@@ -684,7 +688,7 @@
             ],
             compiler_params=compiler_params(24),
             name="attend_cache",
-        )(queries_here, kv_here, in_vmem(lengths), mine[-1], other, in_vmem(pick), in_vmem(keep))
+        )(queries_here, kv_here, in_vmem(lengths), in_vmem(own_part), other, in_vmem(pick), in_vmem(keep))
         shares += share
         if done + 1 < len(steps):
             keep, send = regrouped(keep, got, steps, done + 1, share[2])

time: 38.1 us -> 37.3 us (0.979)
  waiting for transfers between devices: 3.28 us -> 1.71 us
  Pallas kernels: 22.1 us -> 22.8 us
    ppermute x7, waiting for transfers between devices: 3.28 us -> 1.7 us  [swapped(): return in_vmem(lax.ppermute(blocks, 'section', pairs))]
    pallas_call x1 -> x2, Pallas kernels: 6.09 us -> 6.82 us  [own_channels(): pl.pallas_call(functools.partial(project_mine, at=at, last=len(extra) > 0...]
  transfers between devices with their start and end apart: 8 -> 8, of which waited for: 2 -> 2; matrix products, arithmetic and copies ran while one was open for 0% -> 0% of each run, Pallas kernels for 48% -> 51%
where the time goes in v21:
time: 37.3 us; the launch traced here: 37.1 us
  Pallas kernels  22.8 us (61%)
  starting transfers between devices  12.4 us (33%)
  waiting for transfers between devices  1.71 us (5%)
    ppermute x7, starting transfers between devices, swapped(): return in_vmem(lax.ppermute(blocks, 'section', pairs))  12.4 us
    pallas_call x2, Pallas kernels, own_channels(): pl.pallas_call(functools.partial(project_mine, at=at, last=len(extra) > 0...  6.82 us
    pallas_call x1, Pallas kernels, shards(): pl.pallas_call(project_rest, in_specs=[REMAINS] * 4 + [RESIDENT] * 3 + [R...  4.84 us
    pallas_call x1, Pallas kernels, shards(): pl.pallas_call(functools.partial(project_first, edges=edges), in_specs=[R...  4.57 us
    pallas_call x2, Pallas kernels, shards(): pl.pallas_call(functools.partial(attend_cache, rows_at=at), in_specs=[RES...  2.53 us
    ppermute x7, waiting for transfers between devices, swapped(): return in_vmem(lax.ppermute(blocks, 'section', pairs))  1.7 us
    pallas_call x1, Pallas kernels, shards(): pl.pallas_call(select_queries, in_specs=[RESIDENT, RESIDENT], out_specs=[...  1.55 us
    pallas_call x1, Pallas kernels, shards(): pl.pallas_call(merge, in_specs=[RESIDENT] * (5 + len(shares)), out_specs=...  1.3 us
  transfers between devices with their start and end apart: 8, of which 2 were waited for; matrix products, arithmetic and copies ran while one was open for 0% of the time, Pallas kernels for 51%

profile of v21, /device:TPU:0, one launch (start us, length us, event | category | flops | bytes accessed | tf_op | source)
XLA Modules:
  0.0 37.1 jit_solution(16088692544603423040)
XLA Ops:
  0.0 1.6 %select_queries.1 = (bf16[16,128]{1,0:T(8,128)(2,1)S(1)}, bf16[4,2,3072]{2,1,0:T(2,128)(2,1)S(1)}, bf16[4,2,3072]{2,1,0:T(2,128)(2,1)S(1)}) custom-call(s32[8,12]{1,0:T(8,128)} %target_ref.3, bf16[128,3072]{1,0:T(8,128)(2,1)} %refs_1_.1), custom_call_target="tpu_custom_call" | custom-call | tf_op jit(solution)/shard_map/select_queries/pallas_call | solution.py:556
  1.6 4.1 %collective-permute-start = (bf16[4,2,3072]{2,1,0:T(2,128)(2,1)S(1)}, bf16[4,2,3072]{2,1,0:T(2,128)(2,1)S(1)}, u32[]{:S(2)}, u32[]{:S(2)}) collective-permute-start(bf16[4,2,3072]{2,1,0:T(2,128)(2,1)S(1)} %get-tuple-element.46), channel_id=1, source_target_pairs={{0,8},{2,10},{4,12},{6,14},{8,0},{10,2},{12,4},{14,6},{1,9},{3,11}... | collective-permute-start | bytes 147464 | tf_op jit(solution)/shard_map/ppermute | solution.py:554
  5.7 4.6 %project_first.1 = (bf16[896,4096]{1,0:T(8,128)(2,1)S(1)}, bf16[1536,512]{1,0:T(8,128)(2,1)S(1)}, f32[896,512]{1,0:T(8,128)S(1)}, s32[8,12]{1,0:T(8,128)S(1)}, s...) custom-call(bf16[768,6144]{1,0:T(8,128)(2,1)} %prompts_ref.3, bf16[128,6144]{1,0:T(8,128)(2,1)} %hidden_ref.3, ...), custom_call_target="tpu_custom_call" | custom-call | tf_op jit(solution)/shard_map/project_first/pallas_call | solution.py:578
  10.2 0.0 collective-permute-done.got_ref
  10.3 1.6 %collective-permute-start.1 = (bf16[4,2,3072]{2,1,0:T(2,128)(2,1)S(1)}, bf16[4,2,3072]{2,1,0:T(2,128)(2,1)S(1)}, u32[]{:S(2)}, u32[]{:S(2)}) collective-permute-start(bf16[4,2,3072]{2,1,0:T(2,128)(2,1)S(1)} %get-tuple-element.51), channel_id=1, source_target_pairs={{0,4},{2,6},{4,0},{6,2},{8,12},{10,14},{12,8},{14,10},{1,5},{3,7},... | collective-permute-start | bytes 147464 | tf_op jit(solution)/shard_map/ppermute | solution.py:554
  11.9 4.8 %project_rest.1 = (bf16[896,512]{1,0:T(8,128)(2,1)S(1)}, bf16[896,2048]{1,0:T(8,128)(2,1)S(1)}, bf16[6144,512]{1,0:T(8,128)(2,1)S(1)}) custom-call(bf16[768,6144]{1,0:T(8,128)(2,1)} %prompts_ref.3, bf16[128,6144]{1,0:T(8,128)(2,1)} %hidden_ref.3, bf16[6144,1024]{1,0:T(8,128)(2,1)} %w_ref.3, f32[1,1024]{1,0:T(1,128)} %bitcast.2, ...), custom_call_target="tpu_custom_call" | custom-call | tf_op jit(solution)/shard_map/project_rest/pallas_call | solution.py:600
  16.8 0.0 collective-permute-done.1.got_ref
  16.8 0.1 collective-permute-start.3
  16.9 1.6 %collective-permute-start.2 = (bf16[4,2,3072]{2,1,0:T(2,128)(2,1)S(1)}, bf16[4,2,3072]{2,1,0:T(2,128)(2,1)S(1)}, u32[]{:S(2)}, u32[]{:S(2)}) collective-permute-start(bf16[4,2,3072]{2,1,0:T(2,128)(2,1)S(1)} %get-tuple-element.60), channel_id=1, source_target_pairs={{0,2},{2,0},{4,6},{6,4},{8,10},{10,8},{12,14},{14,12},{1,3},{3,1},... | collective-permute-start | bytes 147464 | tf_op jit(solution)/shard_map/ppermute | solution.py:554
  18.5 5.3 %project_mine.2 = (bf16[768,512]{1,0:T(8,128)(2,1)S(1)}, bf16[128,32,512]{2,1,0:T(8,128)(2,1)S(1)}, bf16[128,3072]{1,0:T(8,128)(2,1)S(1)}) custom-call(bf16[896,4096]{1,0:T(8,128)(2,1)S(1)} %get-tuple-element.42.rows_ref, bf16[896,2048]{1,0:T(8,128)(2,1)S(1)} %get-tuple-element.48.rows_rest_ref, bf16[6144,512]{1,0:T(8,128)(2,1)S(1)} %get-tuple-element.49.w_mine_ref, ...), custom_call_target="tpu_custom_call" | custom-call | tf_op jit(solution)/shard_map/project_mine/pallas_call | solution.py:622
  23.7 0.0 collective-permute-done.2.got_ref
  23.7 0.3 prepare_arrived.1
  24.1 0.0 collective-permute-done.3.other_ref
  24.1 0.9 %attend_arrived.1 = (bf16[4,2,3200]{2,1,0:T(2,128)(2,1)S(1)}, bf16[4,2,3200]{2,1,0:T(2,128)(2,1)S(1)}) custom-call(bf16[16,3072]{1,0:T(8,128)(2,1)S(1)} %get-tuple-element.61.rows_ref, bf16[16,64]{1,0:T(8,128)(2,1)S(1)} %get-tuple-element.62.slot_of_ref, f32[16,768]{1,0:T(8,128)S(1)} %get-tuple-element.63.bias_ref, ...), custom_call_target="tpu_custom_call" | custom-call | tf_op jit(solution)/shard_map/attend_arrived/pallas_call | solution.py:662
  25.0 0.6 %collective-permute-start.4 = (bf16[4,2,3200]{2,1,0:T(2,128)(2,1)S(1)}, bf16[4,2,3200]{2,1,0:T(2,128)(2,1)S(1)}, u32[]{:S(2)}, u32[]{:S(2)}) collective-permute-start(bf16[4,2,3200]{2,1,0:T(2,128)(2,1)S(1)} %get-tuple-element.69), channel_id=1, source_target_pairs={{0,2},{2,0},{4,6},{6,4},{8,10},{10,8},{12,14},{14,12},{1,3},{3,1},... | collective-permute-start | bytes 153608 | tf_op jit(solution)/shard_map/ppermute | solution.py:554
  25.5 1.6 %project_mine.3.mine_ref = bf16[128,512]{1,0:T(8,128)(2,1)S(1)} custom-call(bf16[896,4096]{1,0:T(8,128)(2,1)S(1)} %get-tuple-element.42.rows_ref, bf16[896,2048]{1,0:T(8,128)(2,1)S(1)} %get-tuple-element.48.rows_rest_ref, bf16[6144,512]{1,0:T(8,128)(2,1)S(1)} %get-tuple-element.49.w_mine_ref, f32[1,1024]{1,0:T(1,128)} %bitcast.4, ...), custom_call_target="tpu_custom_call" | custom-call | tf_op jit(solution)/shard_map/project_mine/pallas_call | solution.py:622
  27.1 1.3 %attend_cache.2 = (bf16[64,3072]{1,0:T(8,128)(2,1)S(1)}, f32[16,3072]{1,0:T(8,128)S(1)}, f32[16,128]{1,0:T(8,128)S(1)}) custom-call(bf16[128,3072]{1,0:T(8,128)(2,1)S(1)} %get-tuple-element.55.queries_ref, bf16[128,32,512]{2,1,0:T(8,128)(2,1)S(1)} %get-tuple-element.56.cache_ref, s32[1,128]{1,0:T(1,128)S(1)} %get-tuple-element.57.len_ref, ...), custom_call_target="tpu_custom_call" | custom-call | tf_op jit(solution)/shard_map/attend_cache/pallas_call | solution.py:680
  28.4 0.8 %collective-permute-done.4.got_ref = bf16[4,2,3200]{2,1,0:T(2,128)(2,1)S(1)} collective-permute-done((bf16[4,2,3200]{2,1,0:T(2,128)(2,1)S(1)}, bf16[4,2,3200]{2,1,0:T(2,128)(2,1)S(1)}, u32[]{:S(2)}, u32[]{:S(2)}) %collective-permute-start.4) | collective-permute-done | bytes 51232 | tf_op jit(solution)/shard_map/ppermute | solution.py:554
  29.2 0.5 %collective-permute-start.5 = (bf16[2,2,3200]{2,1,0:T(2,128)(2,1)S(1)}, bf16[2,2,3200]{2,1,0:T(2,128)(2,1)S(1)}, u32[]{:S(2)}, u32[]{:S(2)}) collective-permute-start(bf16[2,2,3200]{2,1,0:T(2,128)(2,1)S(1)} %get-tuple-element.74), channel_id=1, source_target_pairs={{0,4},{2,6},{4,0},{6,2},{8,12},{10,14},{12,8},{14,10},{1,5},{3,7},... | collective-permute-start | bytes 76808 | tf_op jit(solution)/shard_map/ppermute | solution.py:554
  29.7 0.4 %collective-permute-start.6 = (bf16[2,2,3200]{2,1,0:T(2,128)(2,1)S(1)}, bf16[2,2,3200]{2,1,0:T(2,128)(2,1)S(1)}, u32[]{:S(2)}, u32[]{:S(2)}) collective-permute-start(bf16[2,2,3200]{2,1,0:T(2,128)(2,1)S(1)} %get-tuple-element.75), channel_id=1, source_target_pairs={{0,8},{2,10},{4,12},{6,14},{8,0},{10,2},{12,4},{14,6},{1,9},{3,11}... | collective-permute-start | bytes 76808 | tf_op jit(solution)/shard_map/ppermute | solution.py:554
  30.1 3.5 %collective-permute-start.7 = (bf16[2,2,3200]{2,1,0:T(2,128)(2,1)S(1)}, bf16[2,2,3200]{2,1,0:T(2,128)(2,1)S(1)}, u32[]{:S(2)}, u32[]{:S(2)}) collective-permute-start(bf16[2,2,3200]{2,1,0:T(2,128)(2,1)S(1)} %get-tuple-element.76), channel_id=1, source_target_pairs={{0,12},{2,14},{4,8},{6,10},{8,4},{10,6},{12,0},{14,2},{1,13},{3,15... | collective-permute-start | bytes 76808 | tf_op jit(solution)/shard_map/ppermute | solution.py:554
  33.6 1.3 %attend_cache.3 = (bf16[64,3072]{1,0:T(8,128)(2,1)S(1)}, f32[16,3072]{1,0:T(8,128)S(1)}, f32[16,128]{1,0:T(8,128)S(1)}) custom-call(bf16[128,3072]{1,0:T(8,128)(2,1)S(1)} %get-tuple-element.55.queries_ref, bf16[128,32,512]{2,1,0:T(8,128)(2,1)S(1)} %get-tuple-element.56.cache_ref, s32[1,128]{1,0:T(1,128)S(1)} %get-tuple-element.57.len_ref, ...), custom_call_target="tpu_custom_call" | custom-call | tf_op jit(solution)/shard_map/attend_cache/pallas_call | solution.py:680
  34.9 0.9 %collective-permute-done.7.refs_9_ = bf16[2,2,3200]{2,1,0:T(2,128)(2,1)S(1)} collective-permute-done((bf16[2,2,3200]{2,1,0:T(2,128)(2,1)S(1)}, bf16[2,2,3200]{2,1,0:T(2,128)(2,1)S(1)}, u32[]{:S(2)}, u32[]{:S(2)}) %collective-permute-start.7) | collective-permute-done | bytes 25632 | tf_op jit(solution)/shard_map/ppermute | solution.py:554
  35.8 1.3 %merge.1 = bf16[128,3072]{1,0:T(8,128)(2,1)} custom-call(bf16[16,128]{1,0:T(8,128)(2,1)S(1)} %get-tuple-element.41.pick_ref, bf16[64,3072]{1,0:T(8,128)(2,1)S(1)} %get-tuple-element.66.refs_0_, f32[16,3072]{1,0:T(8,128)S(1)} %get-tuple-element.67.refs_1_, f32[16,128]{1,0:T(8,128)S(1)} %get-tuple-element.68.after_ref.refs_2_, ...), custom_call_target="tpu_custom_call" | custom-call | tf_op jit(solution)/shard_map/merge/pallas_call | solution.py:708
  (5 shorter events, 0.0 us)
Async XLA Ops:
  1.6 8.7 %collective-permute-start = (bf16[4,2,3072]{2,1,0:T(2,128)(2,1)S(1)}, bf16[4,2,3072]{2,1,0:T(2,128)(2,1)S(1)}, u32[]{:S(2)}, u32[]{:S(2)}) collective-permute-start(bf16[4,2,3072]{2,1,0:T(2,128)(2,1)S(1)} %get-tuple-element.46), channel_id=1, source_target_pairs={{0,8},{2,10},{4,12},{6,14},{8,0},{10,2},{12,4},{14,6},{1,9},{3,11}... | collective-permute-start | bytes 147464 | tf_op jit(solution)/shard_map/ppermute | solution.py:554
  10.3 6.5 %collective-permute-start.1 = (bf16[4,2,3072]{2,1,0:T(2,128)(2,1)S(1)}, bf16[4,2,3072]{2,1,0:T(2,128)(2,1)S(1)}, u32[]{:S(2)}, u32[]{:S(2)}) collective-permute-start(bf16[4,2,3072]{2,1,0:T(2,128)(2,1)S(1)} %get-tuple-element.51), channel_id=1, source_target_pairs={{0,4},{2,6},{4,0},{6,2},{8,12},{10,14},{12,8},{14,10},{1,5},{3,7},... | collective-permute-start | bytes 147464 | tf_op jit(solution)/shard_map/ppermute | solution.py:554
  16.8 7.3 %collective-permute-start.3 = (bf16[896,512]{1,0:T(8,128)(2,1)S(1)}, bf16[896,512]{1,0:T(8,128)(2,1)S(1)}, u32[]{:S(2)}, u32[]{:S(2)}) collective-permute-start(bf16[896,512]{1,0:T(8,128)(2,1)S(1)} %get-tuple-element.53.after_ref), channel_id=1, source_target_pairs={{0,1},{1,0},{2,3},{3,2},{4,5},{5,4},{6,7},{7,6},{8,9},{9,8},{10,11... | collective-permute-start | bytes 2752520 | tf_op jit(solution)/shard_map/ppermute | solution.py:619
  16.9 6.9 %collective-permute-start.2 = (bf16[4,2,3072]{2,1,0:T(2,128)(2,1)S(1)}, bf16[4,2,3072]{2,1,0:T(2,128)(2,1)S(1)}, u32[]{:S(2)}, u32[]{:S(2)}) collective-permute-start(bf16[4,2,3072]{2,1,0:T(2,128)(2,1)S(1)} %get-tuple-element.60), channel_id=1, source_target_pairs={{0,2},{2,0},{4,6},{6,4},{8,10},{10,8},{12,14},{14,12},{1,3},{3,1},... | collective-permute-start | bytes 147464 | tf_op jit(solution)/shard_map/ppermute | solution.py:554
  25.0 4.2 %collective-permute-start.4 = (bf16[4,2,3200]{2,1,0:T(2,128)(2,1)S(1)}, bf16[4,2,3200]{2,1,0:T(2,128)(2,1)S(1)}, u32[]{:S(2)}, u32[]{:S(2)}) collective-permute-start(bf16[4,2,3200]{2,1,0:T(2,128)(2,1)S(1)} %get-tuple-element.69), channel_id=1, source_target_pairs={{0,2},{2,0},{4,6},{6,4},{8,10},{10,8},{12,14},{14,12},{1,3},{3,1},... | collective-permute-start | bytes 153608 | tf_op jit(solution)/shard_map/ppermute | solution.py:554
  29.2 5.7 %collective-permute-start.5 = (bf16[2,2,3200]{2,1,0:T(2,128)(2,1)S(1)}, bf16[2,2,3200]{2,1,0:T(2,128)(2,1)S(1)}, u32[]{:S(2)}, u32[]{:S(2)}) collective-permute-start(bf16[2,2,3200]{2,1,0:T(2,128)(2,1)S(1)} %get-tuple-element.74), channel_id=1, source_target_pairs={{0,4},{2,6},{4,0},{6,2},{8,12},{10,14},{12,8},{14,10},{1,5},{3,7},... | collective-permute-start | bytes 76808 | tf_op jit(solution)/shard_map/ppermute | solution.py:554
  29.7 5.2 %collective-permute-start.6 = (bf16[2,2,3200]{2,1,0:T(2,128)(2,1)S(1)}, bf16[2,2,3200]{2,1,0:T(2,128)(2,1)S(1)}, u32[]{:S(2)}, u32[]{:S(2)}) collective-permute-start(bf16[2,2,3200]{2,1,0:T(2,128)(2,1)S(1)} %get-tuple-element.75), channel_id=1, source_target_pairs={{0,8},{2,10},{4,12},{6,14},{8,0},{10,2},{12,4},{14,6},{1,9},{3,11}... | collective-permute-start | bytes 76808 | tf_op jit(solution)/shard_map/ppermute | solution.py:554
  30.1 5.7 %collective-permute-start.7 = (bf16[2,2,3200]{2,1,0:T(2,128)(2,1)S(1)}, bf16[2,2,3200]{2,1,0:T(2,128)(2,1)S(1)}, u32[]{:S(2)}, u32[]{:S(2)}) collective-permute-start(bf16[2,2,3200]{2,1,0:T(2,128)(2,1)S(1)} %get-tuple-element.76), channel_id=1, source_target_pairs={{0,12},{2,14},{4,8},{6,10},{8,4},{10,6},{12,0},{14,2},{1,13},{3,15... | collective-permute-start | bytes 76808 | tf_op jit(solution)/shard_map/ppermute | solution.py:554

commit v22 on v21

--- a/solution.py
+++ b/solution.py
@@ -207,11 +207,12 @@
         pltpu.make_async_copy(scale_ref.at[:, theirs], scale_here_ref, sems.at[3]),
         pltpu.make_async_copy(w_ref.at[:, mine], w_mine_ref, sems.at[4]),
     ]
-    for copy in copies:
+    for copy in copies[:-1]:
         copy.start()
     total = total_ref[...] + jnp.dot(
         rows_ref[:, head:], w_tail_ref[...], preferred_element_type=F32
     )
+    copies[-1].start()
     for copy in copies[:-1]:
         copy.wait()
     total += jnp.dot(rows_rest_ref[...], w_rest_ref[...], preferred_element_type=F32)
@@ -296,8 +297,19 @@
     bias_ref[...] = jnp.where((key >= 0) & (key < span_col), 0.0, MASKED)
 
 
-def attend_arrived(rows_ref, slot_of_ref, bias_ref, other_ref, *refs):
-    mine_refs, (keep_ref, send_ref) = refs[:-2], refs[-2:]
+def attend_arrived(target_ref, span_ref, kept_ref, got_ref, other_ref, *refs, row_count):
+    rows_ref, slot_of_ref, bias_ref = refs[-3:]
+    mine_refs, (keep_ref, send_ref) = refs[:-5], refs[-5:-3]
+    prepare_arrived(
+        target_ref,
+        span_ref,
+        kept_ref,
+        got_ref,
+        rows_ref,
+        slot_of_ref,
+        bias_ref,
+        row_count=row_count,
+    )
     padded, prompt_rows = bias_ref.shape
     kv_heads = other_ref.shape[1] // (2 * HD)
     group = rows_ref.shape[1] // (kv_heads * HD)
@@ -646,27 +658,20 @@
     kv_here, queries_here = map(in_vmem, here)
 
     padded = -(-span_len.shape[1] // 16) * 16
-    prepared = pl.pallas_call(
-        functools.partial(prepare_arrived, row_count=row_count),
-        in_specs=[RESIDENT] * 4,
-        out_specs=[RESIDENT] * 3,
-        out_shape=[
+    answer_width = query_width + STATS
+    keep, send = pl.pallas_call(
+        functools.partial(attend_arrived, row_count=row_count),
+        in_specs=[RESIDENT] * (5 + len(mine)),
+        out_specs=[RESIDENT] * 2,
+        out_shape=block_pair(answer_width),
+        scratch_shapes=[
             pltpu.VMEM((padded, query_width), BF16),
             pltpu.VMEM((padded, sections * PITCH), BF16),
             pltpu.VMEM((padded, prompt_rows), F32),
         ],
-        compiler_params=compiler_params(16),
-        name="prepare_arrived",
-    )(in_vmem(target_here), in_vmem(span_here), in_vmem(keep), got)
-    answer_width = query_width + STATS
-    keep, send = pl.pallas_call(
-        attend_arrived,
-        in_specs=[RESIDENT] * (4 + len(mine)),
-        out_specs=[RESIDENT] * 2,
-        out_shape=block_pair(answer_width),
         compiler_params=compiler_params(24),
         name="attend_arrived",
-    )(*map(in_vmem, prepared), other, *mine)
+    )(in_vmem(target_here), in_vmem(span_here), in_vmem(keep), got, other, *mine)
 
     (own_part,) = own_channels(slice(prompt_rows, all_rows), keep, [])
     steps = answer_steps_of(sections)

time: 37.3 us -> 37.3 us (level)
    pallas_call x2 -> x1, Pallas kernels: 1.21 us -> 1.19 us  [shards(): pl.pallas_call(functools.partial(attend_arrived, row_count=row_count), in...]
where the time goes in v22:
time: 37.3 us; the launch traced here: 37.1 us
  Pallas kernels  22.8 us (61%)
  starting transfers between devices  12.4 us (33%)
  waiting for transfers between devices  1.71 us (5%)
    ppermute x7, starting transfers between devices, swapped(): return in_vmem(lax.ppermute(blocks, 'section', pairs))  12.4 us
    pallas_call x2, Pallas kernels, own_channels(): pl.pallas_call(functools.partial(project_mine, at=at, last=len(extra) > 0...  6.82 us
    pallas_call x1, Pallas kernels, shards(): pl.pallas_call(project_rest, in_specs=[REMAINS] * 4 + [RESIDENT] * 3 + [R...  4.84 us
    pallas_call x1, Pallas kernels, shards(): pl.pallas_call(functools.partial(project_first, edges=edges), in_specs=[R...  4.57 us
    pallas_call x2, Pallas kernels, shards(): pl.pallas_call(functools.partial(attend_cache, rows_at=at), in_specs=[RES...  2.52 us
    ppermute x7, waiting for transfers between devices, swapped(): return in_vmem(lax.ppermute(blocks, 'section', pairs))  1.71 us
    pallas_call x1, Pallas kernels, shards(): pl.pallas_call(select_queries, in_specs=[RESIDENT, RESIDENT], out_specs=[...  1.55 us
    pallas_call x1, Pallas kernels, shards(): pl.pallas_call(merge, in_specs=[RESIDENT] * (5 + len(shares)), out_specs=...  1.3 us
  transfers between devices with their start and end apart: 8, of which 2 were waited for; matrix products, arithmetic and copies ran while one was open for 0% of the time, Pallas kernels for 51%

profile of v22, /device:TPU:0, one launch (start us, length us, event | category | flops | bytes accessed | tf_op | source)
XLA Modules:
  0.0 37.1 jit_solution(3202825195409633446)
XLA Ops:
  0.0 1.6 %select_queries.1 = (bf16[16,128]{1,0:T(8,128)(2,1)S(1)}, bf16[4,2,3072]{2,1,0:T(2,128)(2,1)S(1)}, bf16[4,2,3072]{2,1,0:T(2,128)(2,1)S(1)}) custom-call(s32[8,12]{1,0:T(8,128)} %target_ref.3, bf16[128,3072]{1,0:T(8,128)(2,1)} %refs_1_.1), custom_call_target="tpu_custom_call" | custom-call | tf_op jit(solution)/shard_map/select_queries/pallas_call | solution.py:568
  1.6 4.1 %collective-permute-start = (bf16[4,2,3072]{2,1,0:T(2,128)(2,1)S(1)}, bf16[4,2,3072]{2,1,0:T(2,128)(2,1)S(1)}, u32[]{:S(2)}, u32[]{:S(2)}) collective-permute-start(bf16[4,2,3072]{2,1,0:T(2,128)(2,1)S(1)} %get-tuple-element.43), channel_id=1, source_target_pairs={{0,8},{2,10},{4,12},{6,14},{8,0},{10,2},{12,4},{14,6},{1,9},{3,11}... | collective-permute-start | bytes 147464 | tf_op jit(solution)/shard_map/ppermute | solution.py:566
  5.7 4.6 %project_first.1 = (bf16[896,4096]{1,0:T(8,128)(2,1)S(1)}, bf16[1536,512]{1,0:T(8,128)(2,1)S(1)}, f32[896,512]{1,0:T(8,128)S(1)}, s32[8,12]{1,0:T(8,128)S(1)}, s...) custom-call(bf16[768,6144]{1,0:T(8,128)(2,1)} %prompts_ref.3, bf16[128,6144]{1,0:T(8,128)(2,1)} %hidden_ref.3, ...), custom_call_target="tpu_custom_call" | custom-call | tf_op jit(solution)/shard_map/project_first/pallas_call | solution.py:590
  10.2 0.0 collective-permute-done.got_ref
  10.3 1.6 %collective-permute-start.1 = (bf16[4,2,3072]{2,1,0:T(2,128)(2,1)S(1)}, bf16[4,2,3072]{2,1,0:T(2,128)(2,1)S(1)}, u32[]{:S(2)}, u32[]{:S(2)}) collective-permute-start(bf16[4,2,3072]{2,1,0:T(2,128)(2,1)S(1)} %get-tuple-element.48), channel_id=1, source_target_pairs={{0,4},{2,6},{4,0},{6,2},{8,12},{10,14},{12,8},{14,10},{1,5},{3,7},... | collective-permute-start | bytes 147464 | tf_op jit(solution)/shard_map/ppermute | solution.py:566
  11.9 4.8 %project_rest.1 = (bf16[896,512]{1,0:T(8,128)(2,1)S(1)}, bf16[896,2048]{1,0:T(8,128)(2,1)S(1)}, bf16[6144,512]{1,0:T(8,128)(2,1)S(1)}) custom-call(bf16[768,6144]{1,0:T(8,128)(2,1)} %prompts_ref.3, bf16[128,6144]{1,0:T(8,128)(2,1)} %hidden_ref.3, bf16[6144,1024]{1,0:T(8,128)(2,1)} %w_ref.3, f32[1,1024]{1,0:T(1,128)} %bitcast.2, ...), custom_call_target="tpu_custom_call" | custom-call | tf_op jit(solution)/shard_map/project_rest/pallas_call | solution.py:612
  16.8 0.0 collective-permute-done.1.got_ref
  16.8 0.1 collective-permute-start.3
  16.9 1.6 %collective-permute-start.2 = (bf16[4,2,3072]{2,1,0:T(2,128)(2,1)S(1)}, bf16[4,2,3072]{2,1,0:T(2,128)(2,1)S(1)}, u32[]{:S(2)}, u32[]{:S(2)}) collective-permute-start(bf16[4,2,3072]{2,1,0:T(2,128)(2,1)S(1)} %get-tuple-element.57), channel_id=1, source_target_pairs={{0,2},{2,0},{4,6},{6,4},{8,10},{10,8},{12,14},{14,12},{1,3},{3,1},... | collective-permute-start | bytes 147464 | tf_op jit(solution)/shard_map/ppermute | solution.py:566
  18.5 5.3 %project_mine.2 = (bf16[768,512]{1,0:T(8,128)(2,1)S(1)}, bf16[128,32,512]{2,1,0:T(8,128)(2,1)S(1)}, bf16[128,3072]{1,0:T(8,128)(2,1)S(1)}) custom-call(bf16[896,4096]{1,0:T(8,128)(2,1)S(1)} %get-tuple-element.39.rows_ref, bf16[896,2048]{1,0:T(8,128)(2,1)S(1)} %get-tuple-element.45.rows_rest_ref, bf16[6144,512]{1,0:T(8,128)(2,1)S(1)} %get-tuple-element.46.w_mine_ref, ...), custom_call_target="tpu_custom_call" | custom-call | tf_op jit(solution)/shard_map/project_mine/pallas_call | solution.py:634
  23.7 0.0 collective-permute-done.2.got_ref
  23.8 1.2 %attend_arrived.1 = (bf16[4,2,3200]{2,1,0:T(2,128)(2,1)S(1)}, bf16[4,2,3200]{2,1,0:T(2,128)(2,1)S(1)}) custom-call(s32[8,12]{1,0:T(8,128)S(1)} %get-tuple-element.55.target_ref, s32[8,12]{1,0:T(8,128)S(1)} %get-tuple-element.56.span_ref, bf16[4,2,3072]{2,1,0:T(2,128)(2,1)S(1)} %get-tuple-element.51.after_ref.kept_ref, ...), custom_call_target="tpu_custom_call" | custom-call | tf_op jit(solution)/shard_map/attend_arrived/pallas_call | solution.py:662
  24.9 0.6 %collective-permute-start.4 = (bf16[4,2,3200]{2,1,0:T(2,128)(2,1)S(1)}, bf16[4,2,3200]{2,1,0:T(2,128)(2,1)S(1)}, u32[]{:S(2)}, u32[]{:S(2)}) collective-permute-start(bf16[4,2,3200]{2,1,0:T(2,128)(2,1)S(1)} %get-tuple-element.63), channel_id=1, source_target_pairs={{0,2},{2,0},{4,6},{6,4},{8,10},{10,8},{12,14},{14,12},{1,3},{3,1},... | collective-permute-start | bytes 153608 | tf_op jit(solution)/shard_map/ppermute | solution.py:566
  25.5 1.6 %project_mine.3.mine_ref = bf16[128,512]{1,0:T(8,128)(2,1)S(1)} custom-call(bf16[896,4096]{1,0:T(8,128)(2,1)S(1)} %get-tuple-element.39.rows_ref, bf16[896,2048]{1,0:T(8,128)(2,1)S(1)} %get-tuple-element.45.rows_rest_ref, bf16[6144,512]{1,0:T(8,128)(2,1)S(1)} %get-tuple-element.46.w_mine_ref, f32[1,1024]{1,0:T(1,128)} %bitcast.4, ...), custom_call_target="tpu_custom_call" | custom-call | tf_op jit(solution)/shard_map/project_mine/pallas_call | solution.py:634
  27.1 1.3 %attend_cache.2 = (bf16[64,3072]{1,0:T(8,128)(2,1)S(1)}, f32[16,3072]{1,0:T(8,128)S(1)}, f32[16,128]{1,0:T(8,128)S(1)}) custom-call(bf16[128,3072]{1,0:T(8,128)(2,1)S(1)} %get-tuple-element.52.queries_ref, bf16[128,32,512]{2,1,0:T(8,128)(2,1)S(1)} %get-tuple-element.53.cache_ref, s32[1,128]{1,0:T(1,128)S(1)} %get-tuple-element.54.len_ref, ...), custom_call_target="tpu_custom_call" | custom-call | tf_op jit(solution)/shard_map/attend_cache/pallas_call | solution.py:685
  28.3 0.8 %collective-permute-done.4.got_ref = bf16[4,2,3200]{2,1,0:T(2,128)(2,1)S(1)} collective-permute-done((bf16[4,2,3200]{2,1,0:T(2,128)(2,1)S(1)}, bf16[4,2,3200]{2,1,0:T(2,128)(2,1)S(1)}, u32[]{:S(2)}, u32[]{:S(2)}) %collective-permute-start.4) | collective-permute-done | bytes 51232 | tf_op jit(solution)/shard_map/ppermute | solution.py:566
  29.1 0.5 %collective-permute-start.5 = (bf16[2,2,3200]{2,1,0:T(2,128)(2,1)S(1)}, bf16[2,2,3200]{2,1,0:T(2,128)(2,1)S(1)}, u32[]{:S(2)}, u32[]{:S(2)}) collective-permute-start(bf16[2,2,3200]{2,1,0:T(2,128)(2,1)S(1)} %get-tuple-element.68), channel_id=1, source_target_pairs={{0,4},{2,6},{4,0},{6,2},{8,12},{10,14},{12,8},{14,10},{1,5},{3,7},... | collective-permute-start | bytes 76808 | tf_op jit(solution)/shard_map/ppermute | solution.py:566
  29.6 0.4 %collective-permute-start.6 = (bf16[2,2,3200]{2,1,0:T(2,128)(2,1)S(1)}, bf16[2,2,3200]{2,1,0:T(2,128)(2,1)S(1)}, u32[]{:S(2)}, u32[]{:S(2)}) collective-permute-start(bf16[2,2,3200]{2,1,0:T(2,128)(2,1)S(1)} %get-tuple-element.69), channel_id=1, source_target_pairs={{0,8},{2,10},{4,12},{6,14},{8,0},{10,2},{12,4},{14,6},{1,9},{3,11}... | collective-permute-start | bytes 76808 | tf_op jit(solution)/shard_map/ppermute | solution.py:566
  30.1 3.5 %collective-permute-start.7 = (bf16[2,2,3200]{2,1,0:T(2,128)(2,1)S(1)}, bf16[2,2,3200]{2,1,0:T(2,128)(2,1)S(1)}, u32[]{:S(2)}, u32[]{:S(2)}) collective-permute-start(bf16[2,2,3200]{2,1,0:T(2,128)(2,1)S(1)} %get-tuple-element.70), channel_id=1, source_target_pairs={{0,12},{2,14},{4,8},{6,10},{8,4},{10,6},{12,0},{14,2},{1,13},{3,15... | collective-permute-start | bytes 76808 | tf_op jit(solution)/shard_map/ppermute | solution.py:566
  33.6 1.3 %attend_cache.3 = (bf16[64,3072]{1,0:T(8,128)(2,1)S(1)}, f32[16,3072]{1,0:T(8,128)S(1)}, f32[16,128]{1,0:T(8,128)S(1)}) custom-call(bf16[128,3072]{1,0:T(8,128)(2,1)S(1)} %get-tuple-element.52.queries_ref, bf16[128,32,512]{2,1,0:T(8,128)(2,1)S(1)} %get-tuple-element.53.cache_ref, s32[1,128]{1,0:T(1,128)S(1)} %get-tuple-element.54.len_ref, ...), custom_call_target="tpu_custom_call" | custom-call | tf_op jit(solution)/shard_map/attend_cache/pallas_call | solution.py:685
  34.8 0.0 collective-permute-done.5.refs_7_
  34.8 0.0 collective-permute-done.6.refs_8_
  34.9 0.9 %collective-permute-done.7.refs_9_ = bf16[2,2,3200]{2,1,0:T(2,128)(2,1)S(1)} collective-permute-done((bf16[2,2,3200]{2,1,0:T(2,128)(2,1)S(1)}, bf16[2,2,3200]{2,1,0:T(2,128)(2,1)S(1)}, u32[]{:S(2)}, u32[]{:S(2)}) %collective-permute-start.7) | collective-permute-done | bytes 25632 | tf_op jit(solution)/shard_map/ppermute | solution.py:566
  35.8 1.3 %merge.1 = bf16[128,3072]{1,0:T(8,128)(2,1)} custom-call(bf16[16,128]{1,0:T(8,128)(2,1)S(1)} %get-tuple-element.38.pick_ref, bf16[64,3072]{1,0:T(8,128)(2,1)S(1)} %get-tuple-element.60.refs_0_, f32[16,3072]{1,0:T(8,128)S(1)} %get-tuple-element.61.refs_1_, f32[16,128]{1,0:T(8,128)S(1)} %get-tuple-element.62.after_ref.refs_2_, ...), custom_call_target="tpu_custom_call" | custom-call | tf_op jit(solution)/shard_map/merge/pallas_call | solution.py:713
  (4 shorter events, 0.0 us)
Async XLA Ops:
  1.6 8.7 %collective-permute-start = (bf16[4,2,3072]{2,1,0:T(2,128)(2,1)S(1)}, bf16[4,2,3072]{2,1,0:T(2,128)(2,1)S(1)}, u32[]{:S(2)}, u32[]{:S(2)}) collective-permute-start(bf16[4,2,3072]{2,1,0:T(2,128)(2,1)S(1)} %get-tuple-element.43), channel_id=1, source_target_pairs={{0,8},{2,10},{4,12},{6,14},{8,0},{10,2},{12,4},{14,6},{1,9},{3,11}... | collective-permute-start | bytes 147464 | tf_op jit(solution)/shard_map/ppermute | solution.py:566
  10.3 6.5 %collective-permute-start.1 = (bf16[4,2,3072]{2,1,0:T(2,128)(2,1)S(1)}, bf16[4,2,3072]{2,1,0:T(2,128)(2,1)S(1)}, u32[]{:S(2)}, u32[]{:S(2)}) collective-permute-start(bf16[4,2,3072]{2,1,0:T(2,128)(2,1)S(1)} %get-tuple-element.48), channel_id=1, source_target_pairs={{0,4},{2,6},{4,0},{6,2},{8,12},{10,14},{12,8},{14,10},{1,5},{3,7},... | collective-permute-start | bytes 147464 | tf_op jit(solution)/shard_map/ppermute | solution.py:566
  16.8 7.0 %collective-permute-start.3 = (bf16[896,512]{1,0:T(8,128)(2,1)S(1)}, bf16[896,512]{1,0:T(8,128)(2,1)S(1)}, u32[]{:S(2)}, u32[]{:S(2)}) collective-permute-start(bf16[896,512]{1,0:T(8,128)(2,1)S(1)} %get-tuple-element.50.after_ref), channel_id=1, source_target_pairs={{0,1},{1,0},{2,3},{3,2},{4,5},{5,4},{6,7},{7,6},{8,9},{9,8},{10,11... | collective-permute-start | bytes 2752520 | tf_op jit(solution)/shard_map/ppermute | solution.py:631
  16.9 6.9 %collective-permute-start.2 = (bf16[4,2,3072]{2,1,0:T(2,128)(2,1)S(1)}, bf16[4,2,3072]{2,1,0:T(2,128)(2,1)S(1)}, u32[]{:S(2)}, u32[]{:S(2)}) collective-permute-start(bf16[4,2,3072]{2,1,0:T(2,128)(2,1)S(1)} %get-tuple-element.57), channel_id=1, source_target_pairs={{0,2},{2,0},{4,6},{6,4},{8,10},{10,8},{12,14},{14,12},{1,3},{3,1},... | collective-permute-start | bytes 147464 | tf_op jit(solution)/shard_map/ppermute | solution.py:566
  24.9 4.2 %collective-permute-start.4 = (bf16[4,2,3200]{2,1,0:T(2,128)(2,1)S(1)}, bf16[4,2,3200]{2,1,0:T(2,128)(2,1)S(1)}, u32[]{:S(2)}, u32[]{:S(2)}) collective-permute-start(bf16[4,2,3200]{2,1,0:T(2,128)(2,1)S(1)} %get-tuple-element.63), channel_id=1, source_target_pairs={{0,2},{2,0},{4,6},{6,4},{8,10},{10,8},{12,14},{14,12},{1,3},{3,1},... | collective-permute-start | bytes 153608 | tf_op jit(solution)/shard_map/ppermute | solution.py:566
  29.1 5.7 %collective-permute-start.5 = (bf16[2,2,3200]{2,1,0:T(2,128)(2,1)S(1)}, bf16[2,2,3200]{2,1,0:T(2,128)(2,1)S(1)}, u32[]{:S(2)}, u32[]{:S(2)}) collective-permute-start(bf16[2,2,3200]{2,1,0:T(2,128)(2,1)S(1)} %get-tuple-element.68), channel_id=1, source_target_pairs={{0,4},{2,6},{4,0},{6,2},{8,12},{10,14},{12,8},{14,10},{1,5},{3,7},... | collective-permute-start | bytes 76808 | tf_op jit(solution)/shard_map/ppermute | solution.py:566
  29.6 5.2 %collective-permute-start.6 = (bf16[2,2,3200]{2,1,0:T(2,128)(2,1)S(1)}, bf16[2,2,3200]{2,1,0:T(2,128)(2,1)S(1)}, u32[]{:S(2)}, u32[]{:S(2)}) collective-permute-start(bf16[2,2,3200]{2,1,0:T(2,128)(2,1)S(1)} %get-tuple-element.69), channel_id=1, source_target_pairs={{0,8},{2,10},{4,12},{6,14},{8,0},{10,2},{12,4},{14,6},{1,9},{3,11}... | collective-permute-start | bytes 76808 | tf_op jit(solution)/shard_map/ppermute | solution.py:566
  30.1 5.7 %collective-permute-start.7 = (bf16[2,2,3200]{2,1,0:T(2,128)(2,1)S(1)}, bf16[2,2,3200]{2,1,0:T(2,128)(2,1)S(1)}, u32[]{:S(2)}, u32[]{:S(2)}) collective-permute-start(bf16[2,2,3200]{2,1,0:T(2,128)(2,1)S(1)} %get-tuple-element.70), channel_id=1, source_target_pairs={{0,12},{2,14},{4,8},{6,10},{8,4},{10,6},{12,0},{14,2},{1,13},{3,15... | collective-permute-start | bytes 76808 | tf_op jit(solution)/shard_map/ppermute | solution.py:566
